TPU v7x, 32 devices: a whole 2x2x4 slice. The times are simulated.
32 devices in a mesh: gx: 4 (over y, x), gy: 8 (over z, core).
Axes of the slice: x: 2, y: 2, z: 4, core: 2. Of those that a mesh axis runs over, the one named last changes fastest.
Arguments:
- child_adjoint: float32 [32, 8, 64, 512], P(None, None, 'gy', 'gx'), may hold values from -6 to 6
- parent_adjoint: float32 [32, 8, 16, 128], P(None, None, 'gy', 'gx'), may hold values from -6 to 6
- child_rates: float32 [4, 32, 64, 512], P(None, None, 'gy', 'gx'), may hold values from 0.02 to 0.2
- child_mixing: float32 [32, 64, 512], P(None, 'gy', 'gx'), may hold values from 0.05 to 5
- child_land: int32 [64, 512], P('gy', 'gx'), may hold values 0 or 1
- parent_rates: float32 [4, 32, 16, 128], P(None, None, 'gy', 'gx'), may hold values from 0.02 to 0.2
- parent_mixing: float32 [32, 16, 128], P(None, 'gy', 'gx'), may hold values from 0.05 to 5
- parent_land: int32 [16, 128], P('gy', 'gx'), may hold values 0 or 1
- relaxation: float32 [64, 512], P('gy', 'gx'), may hold values from 0.2 to 0.9
Outputs:
- child_sensitivity: float32 [32, 8, 64, 512], P(None, None, 'gy', 'gx')
- parent_sensitivity: float32 [32, 8, 16, 128], P(None, None, 'gy', 'gx')
Inputs may be any that keep to these rules, and one draw needn't show every extreme that they name: `child_land`: 1 marks an ocean cell, 0 a land cell. `parent_land`: 1 marks an ocean cell, 0 a land cell.
All inputs are finite; a program needn't handle non-finite values. No bound on the sum of `child_land` or of `parent_land` on one device may be relied on, other than what follows from the above.
Results may differ from a plain program's by a relative error of at most 0.0001.
Values sent between devices are 32-bit elements; how exact they have to be, the bound alone decides.
No kernel may reach another device: no remote copies, remote signals or barrier semaphores. Data moves between devices by JAX's collectives and lax.ppermute only.
A program may use at most 128 MiB of HBM per device.

v0:
```python
import jax
import jax.numpy as jnp
from jax import lax
from jax.sharding import PartitionSpec as P

STEPS = 2


def passed_along(value, axis, steps):
    count = lax.axis_size(axis)
    pairs = [(source, (source + steps) % count) for source in range(count)]
    return lax.ppermute(value, axis, pairs)


def with_halo(block, sides, width):
    for axis, dim in sides:
        count = lax.axis_size(axis)
        forward = [(i, i + 1) for i in range(count - 1)]
        forward.append((count - 1, 0))
        backward = [(target, source) for source, target in forward]
        low = lax.ppermute(
            lax.slice_in_dim(block, block.shape[dim] - width, None, axis=dim), axis, forward
        )
        high = lax.ppermute(lax.slice_in_dim(block, 0, width, axis=dim), axis, backward)
        block = jnp.concatenate([low, block, high], axis=dim)
    return block


def factor_columns(mixing):
    upper_mix = jnp.concatenate([jnp.zeros_like(mixing[:1]), mixing[:-1]], axis=0)
    diagonal = 1.0 + upper_mix + mixing

    def eliminate(ratio_prev, entries):
        upper_k, diag_k, mix_k = entries
        pivot_k = diag_k - upper_k * ratio_prev
        ratio_k = mix_k / pivot_k
        return (ratio_k, (ratio_k, pivot_k))

    initial = jnp.zeros(mixing.shape[1:], jnp.float32)
    _, (ratios, pivots) = lax.scan(eliminate, initial, (upper_mix, diagonal, mixing), unroll=True)
    return (upper_mix, ratios, pivots)


def solve_columns(factors, adjoint):
    upper_mix, ratios, pivots = factors

    def forward_sweep(previous, entries):
        upper_k, pivot_k, rhs_k = entries
        solved_k = (rhs_k + upper_k[None] * previous) / pivot_k[None]
        return (solved_k, solved_k)

    initial = jnp.zeros(adjoint.shape[1:], jnp.float32)
    _, reduced = lax.scan(forward_sweep, initial, (upper_mix, pivots, adjoint), unroll=True)

    def backward_sweep(previous, entries):
        ratio_k, reduced_k = entries
        solved_k = reduced_k + ratio_k[None] * previous
        return (solved_k, solved_k)

    _, solved = lax.scan(backward_sweep, initial, (ratios, reduced), reverse=True, unroll=True)
    return solved


def transport(padded, exchange_rates, land_mask):
    centre = padded[:, :, 1:-1, 1:-1]
    summed = centre + exchange_rates[0][:, None] * (padded[:, :, 1:-1, 2:] - centre)
    summed = summed + exchange_rates[1][:, None] * (padded[:, :, 1:-1, :-2] - centre)
    summed = summed + exchange_rates[2][:, None] * (padded[:, :, 2:, 1:-1] - centre)
    summed = summed + exchange_rates[3][:, None] * (padded[:, :, :-2, 1:-1] - centre)
    return land_mask.astype(jnp.float32)[None, None] * summed


def coarsen(strip):
    depth, vectors, lines, columns = strip.shape
    return strip.reshape(depth, vectors, lines // 4, 4, columns // 4, 4).sum(axis=(3, 5)) * 0.0625


def local(
    child_adjoint,
    parent_adjoint,
    child_rates,
    child_mixing,
    child_land,
    parent_rates,
    parent_mixing,
    parent_land,
    relaxation,
):
    child_factors = factor_columns(child_mixing)
    parent_factors = factor_columns(parent_mixing)
    quarter = lax.axis_size("gy") // 4
    keep_field = 1.0 - relaxation
    child_state = child_adjoint
    parent_state = parent_adjoint
    for turn_index in range(STEPS):
        weighted = child_state * relaxation[None, None]
        feedback = passed_along(coarsen(weighted), "gy", quarter)
        child_source = child_state * keep_field[None, None]
        parent_state = parent_state + feedback
        child_solved = solve_columns(child_factors, child_source)
        child_padded = with_halo(child_solved, (("gy", 2), ("gx", 3)), 1)
        parent_solved = solve_columns(parent_factors, parent_state)
        parent_padded = with_halo(parent_solved, (("gy", 2), ("gx", 3)), 1)
        child_state = transport(child_padded, child_rates, child_land)
        parent_state = transport(parent_padded, parent_rates, parent_land)
    return (child_state, parent_state)


def solution(mesh):
    in_specs = (
        P(None, None, "gy", "gx"),
        P(None, None, "gy", "gx"),
        P(None, None, "gy", "gx"),
        P(None, "gy", "gx"),
        P("gy", "gx"),
        P(None, None, "gy", "gx"),
        P(None, "gy", "gx"),
        P("gy", "gx"),
        P("gy", "gx"),
    )
    out_specs = (P(None, None, "gy", "gx"), P(None, None, "gy", "gx"))
    return jax.shard_map(local, mesh=mesh, in_specs=in_specs, out_specs=out_specs, check_vma=False)
```

profile of v0, /device:TPU:0, one launch (start us, length us, event | category | flops | bytes accessed | tf_op | source)
XLA Modules:
  0.0 136.0 jit_solution(7425822565707523276)
XLA Ops:
  3.4 3.2 %copy.389 = f32[32,8,8,128]{0,1,3,2:T(8,128)} copy(f32[32,8,8,128]{3,2,1,0:T(8,128)S(1)} %get-tuple-element.219) | data formatting | bytes 2097152 | tf_op jit(solution)/shard_map/mul | solution.py:96
  6.6 2.8 %reduce_sum.18 = f32[32,8,2,32]{0,1,3,2:T(8,128)S(1)} reduce(f32[32,8,2,4,32,4]{0,1,5,4,3,2:T(8,128)} %bitcast.338, f32[]{:T(128)} %constant.4.clone.1), dimensions={3,5}, to_apply=%region_0.0 | reduce | flops 245760 | bytes 1114116 | tf_op jit(solution)/shard_map/reduce_sum | solution.py:75
  9.6 3.1 %collective-permute-start.8 = (f32[32,8,2,32]{3,1,2,0:T(8,128)S(1)}, f32[32,8,2,32]{3,1,2,0:T(8,128)S(1)}, u32[]{:S(2)}, u32[]{:S(2)}) collective-permute-start(f32[32,8,2,32]{3,1,2,0:T(8,128)S(1)} %broadcast_multiply_fusion.5), channel_id=1, source_target_pairs={{0,2},{1,3},{2,4},{3,5},{4,6},{5,7},{6,0},{7,1},{8,10},{9,11},{10,... | collective-permute-start | bytes 196616 | tf_op jit(solution)/shard_map/ppermute | solution.py:12
  24.1 3.5 %collective-permute-start.1 = (f32[32,8,1,128]{3,2,1,0:T(1,128)S(1)}, f32[32,8,1,128]{3,2,1,0:T(1,128)S(1)}, u32[]{:S(2)}, u32[]{:S(2)}) collective-permute-start(f32[32,8,1,128]{3,2,1,0:T(1,128)S(1)} %get-tuple-element.223), channel_id=1, source_target_pairs={{1,0},{2,1},{3,2},{4,3},{5,4},{6,5},{7,6},{0,7},{9,8},{10,9},{11,1... | collective-permute-start | bytes 393224 | tf_op jit(solution)/shard_map/ppermute | solution.py:24
  39.1 2.5 %collective-permute-done.9 = f32[32,8,1,32]{3,1,2,0:T(8,128)S(1)} collective-permute-done((f32[32,8,1,32]{3,1,2,0:T(8,128)S(1)}, f32[32,8,1,32]{3,1,2,0:T(8,128)S(1)}, u32[]{:S(2)}, u32[]{:S(2)}) %collective-permute-start.9) | collective-permute-done | bytes 32800 | tf_op jit(solution)/shard_map/ppermute | solution.py:21
  46.4 3.0 %copy.381 = f32[32,8,10,1]{0,1,3,2:T(8,128)} copy(f32[32,8,10,1]{3,2,1,0:T(8,128)} %get-tuple-element.217) | data formatting | bytes 20480 | tf_op jit(solution)/shard_map/slice | solution.py:24
  49.4 2.4 %collective-permute-start.2 = (f32[32,8,10,1]{0,1,3,2:T(8,128)}, f32[32,8,10,1]{0,1,3,2:T(8,128)}, u32[]{:S(2)}, u32[]{:S(2)}) collective-permute-start(f32[32,8,10,1]{0,1,3,2:T(8,128)} %copy.381), channel_id=1, source_target_pairs={{8,0},{16,8},{24,16},{0,24},{9,1},{17,9},{25,17},{1,25},{10,2},{18... | collective-permute-start | bytes 30728 | tf_op jit(solution)/shard_map/ppermute | solution.py:24
  53.4 2.4 %fusion.310 = (f32[32,8,4,1]{3,1,2,0:T(8,128)}, f32[32,8,4,1]{3,1,2,0:T(8,128)}) fusion(f32[32,8,4,32]{3,1,2,0:T(8,128)} %pad_maximum_fusion.18), kind=kLoop, calls=%fused_computation.870 | loop fusion | bytes 16384 | tf_op jit(solution)/shard_map/slice | solution.py:24
  55.8 2.9 %collective-permute-start.11 = (f32[32,8,4,1]{3,1,2,0:T(8,128)}, f32[32,8,4,1]{3,1,2,0:T(8,128)}, u32[]{:S(2)}, u32[]{:S(2)}) collective-permute-start(f32[32,8,4,1]{3,1,2,0:T(8,128)} %get-tuple-element.227), channel_id=1, source_target_pairs={{8,0},{16,8},{24,16},{0,24},{9,1},{17,9},{25,17},{1,25},{10,2},{18... | collective-permute-start | bytes 12296 | tf_op jit(solution)/shard_map/ppermute | solution.py:24
  58.7 2.6 %copy.382 = f32[32,8,10,1]{3,2,1,0:T(8,128)S(1)} copy(f32[32,8,10,1]{0,1,3,2:T(8,128)} %collective-permute-done.2) | data formatting | bytes 20480 | tf_op jit(solution)/shard_map/ppermute | solution.py:24
  61.3 3.6 %copy.384 = f32[32,8,10,1]{3,2,1,0:T(8,128)} copy(f32[32,8,10,1]{0,1,3,2:T(8,128)} %collective-permute-done.3) | data formatting | bytes 20480 | tf_op jit(solution)/shard_map/ppermute | solution.py:21
  65.0 5.3 %broadcast_multiply_fusion = (f32[32,8,8,128]{3,2,1,0:T(8,128)}, f32[32,8,8,128]{3,2,1,0:T(8,128)}) fusion(f32[8,128]{1,0:T(8,128)} %param.17, f32[32,8,8,128]{3,2,1,0:T(8,128)S(1)} %constant_dynamic-update-slice_fusion, f32[32,8,1,128]{3,2,1,0:T(1,128)} %copy-done.5, f32[32,8,128]{2,1,0:T(8,128)} %get-tuple-element.231, f32[32,8,1,128]{3,2,1,0:T(1,128)} %copy-done.6, ...), kind=kLoop, calls=%fused_computation.46 | loop fusion | flops 5767168 | bytes 3960832 | tf_op jit(solution)/shard_map/mul | solution.py:96
  70.2 4.3 %copy.392 = f32[32,8,8,128]{0,1,3,2:T(8,128)} copy(f32[32,8,8,128]{3,2,1,0:T(8,128)} %get-tuple-element.106) | data formatting | bytes 2097152 | tf_op jit(solution)/shard_map/mul | solution.py:96
  74.6 2.8 %reduce_sum.19 = f32[32,8,2,32]{0,1,3,2:T(8,128)S(1)} reduce(f32[32,8,2,4,32,4]{0,1,5,4,3,2:T(8,128)} %bitcast.337, f32[]{:T(128)} %constant.4.clone.1), dimensions={3,5}, to_apply=%region_1.0 | reduce | flops 245760 | bytes 1114116 | tf_op jit(solution)/shard_map/reduce_sum | solution.py:75
  80.7 5.4 %collective-permute-done.13 = f32[32,8,2,32]{3,1,2,0:T(8,128)S(1)} collective-permute-done((f32[32,8,2,32]{3,1,2,0:T(8,128)S(1)}, f32[32,8,2,32]{3,1,2,0:T(8,128)S(1)}, u32[]{:S(2)}, u32[]{:S(2)}) %collective-permute-start.13) | collective-permute-done | bytes 65568 | tf_op jit(solution)/shard_map/ppermute | solution.py:12
  89.7 3.5 %collective-permute-start.15 = (f32[32,8,1,32]{3,1,2,0:T(8,128)S(1)}, f32[32,8,1,32]{3,1,2,0:T(8,128)S(1)}, u32[]{:S(2)}, u32[]{:S(2)}) collective-permute-start(f32[32,8,1,32]{3,1,2,0:T(8,128)S(1)} %get-tuple-element.233), channel_id=1, source_target_pairs={{1,0},{2,1},{3,2},{4,3},{5,4},{6,5},{7,6},{0,7},{9,8},{10,9},{11,1... | collective-permute-start | bytes 98312 | tf_op jit(solution)/shard_map/ppermute | solution.py:24
  93.5 3.5 %collective-permute-start.5 = (f32[32,8,1,128]{3,2,1,0:T(1,128)S(1)}, f32[32,8,1,128]{3,2,1,0:T(1,128)S(1)}, u32[]{:S(2)}, u32[]{:S(2)}) collective-permute-start(f32[32,8,1,128]{3,2,1,0:T(1,128)S(1)} %get-tuple-element.221), channel_id=1, source_target_pairs={{1,0},{2,1},{3,2},{4,3},{5,4},{6,5},{7,6},{0,7},{9,8},{10,9},{11,1... | collective-permute-start | bytes 393224 | tf_op jit(solution)/shard_map/ppermute | solution.py:24
  98.2 2.9 %collective-permute-start.16 = (f32[32,8,4,1]{3,1,2,0:T(8,128)}, f32[32,8,4,1]{3,1,2,0:T(8,128)}, u32[]{:S(2)}, u32[]{:S(2)}) collective-permute-start(f32[32,8,4,1]{3,1,2,0:T(8,128)} %get-tuple-element.225), channel_id=1, source_target_pairs={{8,0},{16,8},{24,16},{0,24},{9,1},{17,9},{25,17},{1,25},{10,2},{18... | collective-permute-start | bytes 12296 | tf_op jit(solution)/shard_map/ppermute | solution.py:24
  105.0 3.0 %copy.385 = f32[32,8,10,1]{0,1,3,2:T(8,128)} copy(f32[32,8,10,1]{3,2,1,0:T(8,128)} %get-tuple-element.215) | data formatting | bytes 20480 | tf_op jit(solution)/shard_map/slice | solution.py:24
  108.0 2.9 %collective-permute-start.6 = (f32[32,8,10,1]{0,1,3,2:T(8,128)}, f32[32,8,10,1]{0,1,3,2:T(8,128)}, u32[]{:S(2)}, u32[]{:S(2)}) collective-permute-start(f32[32,8,10,1]{0,1,3,2:T(8,128)} %copy.385), channel_id=1, source_target_pairs={{8,0},{16,8},{24,16},{0,24},{9,1},{17,9},{25,17},{1,25},{10,2},{18... | collective-permute-start | bytes 30728 | tf_op jit(solution)/shard_map/ppermute | solution.py:24
  113.9 8.9 %collective-permute-done.17 = f32[32,8,4,1]{3,1,2,0:T(8,128)} collective-permute-done((f32[32,8,4,1]{3,1,2,0:T(8,128)}, f32[32,8,4,1]{3,1,2,0:T(8,128)}, u32[]{:S(2)}, u32[]{:S(2)}) %collective-permute-start.17) | collective-permute-done | bytes 4128 | tf_op jit(solution)/shard_map/ppermute | solution.py:21
  125.0 2.6 %copy.386 = f32[32,8,10,1]{3,2,1,0:T(8,128)S(1)} copy(f32[32,8,10,1]{0,1,3,2:T(8,128)} %collective-permute-done.6) | data formatting | bytes 20480 | tf_op jit(solution)/shard_map/ppermute | solution.py:24
  127.7 3.6 %copy.388 = f32[32,8,10,1]{3,2,1,0:T(8,128)} copy(f32[32,8,10,1]{0,1,3,2:T(8,128)} %collective-permute-done.7) | data formatting | bytes 20480 | tf_op jit(solution)/shard_map/ppermute | solution.py:21
  131.3 4.7 %fusion.3 = f32[32,8,8,128]{3,2,1,0:T(8,128)} fusion(f32[32,8,8,128]{3,2,1,0:T(8,128)S(1)} %constant_dynamic-update-slice_fusion.32, f32[32,8,1,128]{3,2,1,0:T(1,128)} %copy-done.14, f32[32,8,1,128]{3,2,1,0:T(1,128)} %copy-done.15, f32[32,8,10,1]{3,2,1,0:T(8,128)} %copy.388, f32[32,8,10,1]{3,2,1,0:T(8,128)S(1)} %copy.386, f32[32,8,128]{2,1,0:T(8,128)S(1)} %copy-done.3, ...), kind=kLoop, calls=%fused_computation.6 | loop fusion | flops 5505024 | bytes 2908160 | tf_op jit(solution)/shard_map/mul | solution.py:70
  (559 shorter events, 46.1 us)
Async XLA Ops:
  9.6 23.9 %collective-permute-start.8 = (f32[32,8,2,32]{3,1,2,0:T(8,128)S(1)}, f32[32,8,2,32]{3,1,2,0:T(8,128)S(1)}, u32[]{:S(2)}, u32[]{:S(2)}) collective-permute-start(f32[32,8,2,32]{3,1,2,0:T(8,128)S(1)} %broadcast_multiply_fusion.5), channel_id=1, source_target_pairs={{0,2},{1,3},{2,4},{3,5},{4,6},{5,7},{6,0},{7,1},{8,10},{9,11},{10,... | collective-permute-start | bytes 196616 | tf_op jit(solution)/shard_map/ppermute | solution.py:12
  13.4 9.9 %copy-start.48 = (f32[8,128]{1,0:T(8,128)}, f32[8,128]{1,0:T(8,128)S(1)}, u32[]{:S(2)}) copy-start(f32[8,128]{1,0:T(8,128)S(1)} %get-tuple-element.170) | copy-start | bytes 12292
  13.6 9.9 %copy-start.42 = (f32[8,128]{1,0:T(8,128)}, f32[8,128]{1,0:T(8,128)S(1)}, u32[]{:S(2)}) copy-start(f32[8,128]{1,0:T(8,128)S(1)} %get-tuple-element.179) | copy-start | bytes 12292
  13.6 9.9 %copy-start.40 = (f32[8,128]{1,0:T(8,128)}, f32[8,128]{1,0:T(8,128)S(1)}, u32[]{:S(2)}) copy-start(f32[8,128]{1,0:T(8,128)S(1)} %get-tuple-element.182) | copy-start | bytes 12292
  13.7 9.8 %copy-start.38 = (f32[8,128]{1,0:T(8,128)}, f32[8,128]{1,0:T(8,128)S(1)}, u32[]{:S(2)}) copy-start(f32[8,128]{1,0:T(8,128)S(1)} %get-tuple-element.185) | copy-start | bytes 12292
  23.4 10.1 %copy-start.20 = (f32[32,8,2,32]{3,2,1,0:T(2,128)S(1)}, f32[32,8,2,32]{3,2,1,0:T(2,128)}, u32[]{:S(2)}) copy-start(f32[32,8,2,32]{3,2,1,0:T(2,128)} %param.10) | copy-start | bytes 196612
  24.1 18.4 %collective-permute-start = (f32[32,8,1,128]{3,2,1,0:T(1,128)S(1)}, f32[32,8,1,128]{3,2,1,0:T(1,128)S(1)}, u32[]{:S(2)}, u32[]{:S(2)}) collective-permute-start(f32[32,8,1,128]{3,2,1,0:T(1,128)S(1)} %get-tuple-element.224), channel_id=1, source_target_pairs={{0,1},{1,2},{2,3},{3,4},{4,5},{5,6},{6,7},{7,0},{8,9},{9,10},{10,1... | collective-permute-start | bytes 393224 | tf_op jit(solution)/shard_map/ppermute | solution.py:21
  24.1 18.4 %collective-permute-start.1 = (f32[32,8,1,128]{3,2,1,0:T(1,128)S(1)}, f32[32,8,1,128]{3,2,1,0:T(1,128)S(1)}, u32[]{:S(2)}, u32[]{:S(2)}) collective-permute-start(f32[32,8,1,128]{3,2,1,0:T(1,128)S(1)} %get-tuple-element.223), channel_id=1, source_target_pairs={{1,0},{2,1},{3,2},{4,3},{5,4},{6,5},{7,6},{0,7},{9,8},{10,9},{11,1... | collective-permute-start | bytes 393224 | tf_op jit(solution)/shard_map/ppermute | solution.py:24
  35.3 3.8 %collective-permute-start.10 = (f32[32,8,1,32]{3,1,2,0:T(8,128)S(1)}, f32[32,8,1,32]{3,1,2,0:T(8,128)S(1)}, u32[]{:S(2)}, u32[]{:S(2)}) collective-permute-start(f32[32,8,1,32]{3,1,2,0:T(8,128)S(1)} %get-tuple-element.235), channel_id=1, source_target_pairs={{1,0},{2,1},{3,2},{4,3},{5,4},{6,5},{7,6},{0,7},{9,8},{10,9},{11,1... | collective-permute-start | bytes 98312 | tf_op jit(solution)/shard_map/ppermute | solution.py:24
  35.4 6.2 %collective-permute-start.9 = (f32[32,8,1,32]{3,1,2,0:T(8,128)S(1)}, f32[32,8,1,32]{3,1,2,0:T(8,128)S(1)}, u32[]{:S(2)}, u32[]{:S(2)}) collective-permute-start(f32[32,8,1,32]{3,1,2,0:T(8,128)S(1)} %get-tuple-element.236), channel_id=1, source_target_pairs={{0,1},{1,2},{2,3},{3,4},{4,5},{5,6},{6,7},{7,0},{8,9},{9,10},{10,1... | collective-permute-start | bytes 98312 | tf_op jit(solution)/shard_map/ppermute | solution.py:21
  49.4 9.4 %collective-permute-start.2 = (f32[32,8,10,1]{0,1,3,2:T(8,128)}, f32[32,8,10,1]{0,1,3,2:T(8,128)}, u32[]{:S(2)}, u32[]{:S(2)}) collective-permute-start(f32[32,8,10,1]{0,1,3,2:T(8,128)} %copy.381), channel_id=1, source_target_pairs={{8,0},{16,8},{24,16},{0,24},{9,1},{17,9},{25,17},{1,25},{10,2},{18... | collective-permute-start | bytes 30728 | tf_op jit(solution)/shard_map/ppermute | solution.py:24
  53.4 7.9 %collective-permute-start.3 = (f32[32,8,10,1]{0,1,3,2:T(8,128)}, f32[32,8,10,1]{0,1,3,2:T(8,128)}, u32[]{:S(2)}, u32[]{:S(2)}) collective-permute-start(f32[32,8,10,1]{0,1,3,2:T(8,128)} %copy.383), channel_id=1, source_target_pairs={{0,8},{8,16},{16,24},{24,0},{1,9},{9,17},{17,25},{25,1},{2,10},{10... | collective-permute-start | bytes 30728 | tf_op jit(solution)/shard_map/ppermute | solution.py:21
  55.8 24.9 %collective-permute-start.11 = (f32[32,8,4,1]{3,1,2,0:T(8,128)}, f32[32,8,4,1]{3,1,2,0:T(8,128)}, u32[]{:S(2)}, u32[]{:S(2)}) collective-permute-start(f32[32,8,4,1]{3,1,2,0:T(8,128)} %get-tuple-element.227), channel_id=1, source_target_pairs={{8,0},{16,8},{24,16},{0,24},{9,1},{17,9},{25,17},{1,25},{10,2},{18... | collective-permute-start | bytes 12296 | tf_op jit(solution)/shard_map/ppermute | solution.py:24
  58.7 22.0 %collective-permute-start.12 = (f32[32,8,4,1]{3,1,2,0:T(8,128)}, f32[32,8,4,1]{3,1,2,0:T(8,128)}, u32[]{:S(2)}, u32[]{:S(2)}) collective-permute-start(f32[32,8,4,1]{3,1,2,0:T(8,128)} %get-tuple-element.228), channel_id=1, source_target_pairs={{0,8},{8,16},{16,24},{24,0},{1,9},{9,17},{17,25},{25,1},{2,10},{10... | collective-permute-start | bytes 12296 | tf_op jit(solution)/shard_map/ppermute | solution.py:21
  77.9 8.2 %collective-permute-start.13 = (f32[32,8,2,32]{3,1,2,0:T(8,128)S(1)}, f32[32,8,2,32]{3,1,2,0:T(8,128)S(1)}, u32[]{:S(2)}, u32[]{:S(2)}) collective-permute-start(f32[32,8,2,32]{3,1,2,0:T(8,128)S(1)} %broadcast_multiply_fusion.4), channel_id=1, source_target_pairs={{0,2},{1,3},{2,4},{3,5},{4,6},{5,7},{6,0},{7,1},{8,10},{9,11},{10,... | collective-permute-start | bytes 196616 | tf_op jit(solution)/shard_map/ppermute | solution.py:12
  89.7 7.4 %collective-permute-start.14 = (f32[32,8,1,32]{3,1,2,0:T(8,128)S(1)}, f32[32,8,1,32]{3,1,2,0:T(8,128)S(1)}, u32[]{:S(2)}, u32[]{:S(2)}) collective-permute-start(f32[32,8,1,32]{3,1,2,0:T(8,128)S(1)} %get-tuple-element.234), channel_id=1, source_target_pairs={{0,1},{1,2},{2,3},{3,4},{4,5},{5,6},{6,7},{7,0},{8,9},{9,10},{10,1... | collective-permute-start | bytes 98312 | tf_op jit(solution)/shard_map/ppermute | solution.py:21
  89.7 7.3 %collective-permute-start.15 = (f32[32,8,1,32]{3,1,2,0:T(8,128)S(1)}, f32[32,8,1,32]{3,1,2,0:T(8,128)S(1)}, u32[]{:S(2)}, u32[]{:S(2)}) collective-permute-start(f32[32,8,1,32]{3,1,2,0:T(8,128)S(1)} %get-tuple-element.233), channel_id=1, source_target_pairs={{1,0},{2,1},{3,2},{4,3},{5,4},{6,5},{7,6},{0,7},{9,8},{10,9},{11,1... | collective-permute-start | bytes 98312 | tf_op jit(solution)/shard_map/ppermute | solution.py:24
  93.4 7.7 %collective-permute-start.4 = (f32[32,8,1,128]{3,2,1,0:T(1,128)S(1)}, f32[32,8,1,128]{3,2,1,0:T(1,128)S(1)}, u32[]{:S(2)}, u32[]{:S(2)}) collective-permute-start(f32[32,8,1,128]{3,2,1,0:T(1,128)S(1)} %get-tuple-element.222), channel_id=1, source_target_pairs={{0,1},{1,2},{2,3},{3,4},{4,5},{5,6},{6,7},{7,0},{8,9},{9,10},{10,1... | collective-permute-start | bytes 393224 | tf_op jit(solution)/shard_map/ppermute | solution.py:21
  93.5 7.7 %collective-permute-start.5 = (f32[32,8,1,128]{3,2,1,0:T(1,128)S(1)}, f32[32,8,1,128]{3,2,1,0:T(1,128)S(1)}, u32[]{:S(2)}, u32[]{:S(2)}) collective-permute-start(f32[32,8,1,128]{3,2,1,0:T(1,128)S(1)} %get-tuple-element.221), channel_id=1, source_target_pairs={{1,0},{2,1},{3,2},{4,3},{5,4},{6,5},{7,6},{0,7},{9,8},{10,9},{11,1... | collective-permute-start | bytes 393224 | tf_op jit(solution)/shard_map/ppermute | solution.py:24
  98.2 15.6 %collective-permute-start.16 = (f32[32,8,4,1]{3,1,2,0:T(8,128)}, f32[32,8,4,1]{3,1,2,0:T(8,128)}, u32[]{:S(2)}, u32[]{:S(2)}) collective-permute-start(f32[32,8,4,1]{3,1,2,0:T(8,128)} %get-tuple-element.225), channel_id=1, source_target_pairs={{8,0},{16,8},{24,16},{0,24},{9,1},{17,9},{25,17},{1,25},{10,2},{18... | collective-permute-start | bytes 12296 | tf_op jit(solution)/shard_map/ppermute | solution.py:24
  101.2 21.5 %collective-permute-start.17 = (f32[32,8,4,1]{3,1,2,0:T(8,128)}, f32[32,8,4,1]{3,1,2,0:T(8,128)}, u32[]{:S(2)}, u32[]{:S(2)}) collective-permute-start(f32[32,8,4,1]{3,1,2,0:T(8,128)} %get-tuple-element.226), channel_id=1, source_target_pairs={{0,8},{8,16},{16,24},{24,0},{1,9},{9,17},{17,25},{25,1},{2,10},{10... | collective-permute-start | bytes 12296 | tf_op jit(solution)/shard_map/ppermute | solution.py:21
  105.0 17.7 %copy-start.165 = (f32[2,32]{1,0:T(2,128)S(1)}, f32[2,32]{1,0:T(2,128)}, u32[]{:S(2)}) copy-start(f32[2,32]{1,0:T(2,128)} %convert_element_type.9) | copy-start | bytes 772
  108.0 17.0 %collective-permute-start.6 = (f32[32,8,10,1]{0,1,3,2:T(8,128)}, f32[32,8,10,1]{0,1,3,2:T(8,128)}, u32[]{:S(2)}, u32[]{:S(2)}) collective-permute-start(f32[32,8,10,1]{0,1,3,2:T(8,128)} %copy.385), channel_id=1, source_target_pairs={{8,0},{16,8},{24,16},{0,24},{9,1},{17,9},{25,17},{1,25},{10,2},{18... | collective-permute-start | bytes 30728 | tf_op jit(solution)/shard_map/ppermute | solution.py:24
  112.5 15.1 %collective-permute-start.7 = (f32[32,8,10,1]{0,1,3,2:T(8,128)}, f32[32,8,10,1]{0,1,3,2:T(8,128)}, u32[]{:S(2)}, u32[]{:S(2)}) collective-permute-start(f32[32,8,10,1]{0,1,3,2:T(8,128)} %copy.387), channel_id=1, source_target_pairs={{0,8},{8,16},{16,24},{24,0},{1,9},{9,17},{17,25},{25,1},{2,10},{10... | collective-permute-start | bytes 30728 | tf_op jit(solution)/shard_map/ppermute | solution.py:21
  (169 other events, 1006.9 us)
where the time goes:
time: 137 us; the launch traced here: 136 us
  local copies, waits for them, and re-layouts  45.3 us (33%)
  other arithmetic  41.4 us (30%)
  starting transfers between devices  25.7 us (19%)
  waiting for transfers between devices  19.3 us (14%)
  between operations  4.35 us (3%)
    ppermute x8, starting transfers between devices, with_halo(): lax.ppermute(lax.slice_in_dim(block, 0, width, axis=dim), axis, backward)  21.9 us
    slice x10, local copies, waits for them, and re-layouts, with_halo(): lax.slice_in_dim(block, 0, width, axis=dim)  14 us
    ppermute x8, waiting for transfers between devices, with_halo(): lax.ppermute(lax.slice_in_dim(block, block.shape[dim] - width, None, axis...  11.4 us
    mul x2, local copies, waits for them, and re-layouts, local(): weighted = child_state * relaxation[None, None]  7.51 us
    ppermute x2, local copies, waits for them, and re-layouts, with_halo(): lax.ppermute(lax.slice_in_dim(block, block.shape[dim] - width, None, axis...  7.28 us
    mul x2, other arithmetic, local(): weighted = child_state * relaxation[None, None]  6.72 us
    mul x16, other arithmetic, backward_sweep(): solved_k = reduced_k + ratio_k[None] * previous  6.6 us
    mul x2, other arithmetic, transport(): return land_mask.astype(jnp.float32)[None, None] * summed  6.14 us
  transfers between devices with their start and end apart: 18, of which 5 were waited for; matrix products, arithmetic and copies ran while one was open for 43% of the time, Pallas kernels for 0%

commit v1 on v0

v1 whole, which is shorter than its diff:
```python
import jax
import jax.numpy as jnp
from jax import lax
from jax.experimental import pallas as pl
from jax.experimental.pallas import tpu as pltpu
from jax.sharding import PartitionSpec as P

F32 = jnp.float32
VMEM = pl.BlockSpec(memory_space=pltpu.VMEM)
LIMIT = 40 * 1024 * 1024
LANES = 128


def shape(*dims):
    return jax.ShapeDtypeStruct(dims, F32)


def call(body, outs, scratch, operands, flops, touched):
    return pl.pallas_call(
        body,
        out_shape=outs,
        in_specs=[VMEM] * len(operands),
        out_specs=jax.tree.map(lambda _: VMEM, outs),
        scratch_shapes=scratch,
        compiler_params=pltpu.CompilerParams(vmem_limit_bytes=LIMIT),
        cost_estimate=pl.CostEstimate(flops=flops, bytes_accessed=touched, transcendentals=0),
        name=body.__name__,
    )(*operands)


def lane_index(rows=8):
    return lax.broadcasted_iota(jnp.int32, (rows, LANES), 1)


def row_index():
    return lax.broadcasted_iota(jnp.int32, (8, LANES), 0)


def minors(inner, outer):
    theta = delta = jnp.ones_like(inner[0])
    inverse = []
    for i in range(len(inner)):
        delta = theta + outer[i] * delta
        theta_next = delta + inner[i] * theta
        inverse.append(theta / theta_next)
        theta = theta_next
    return inverse


def child_factors(mix_ref, keep, a_ref, b_ref, c_ref):
    depth = mix_ref.shape[0]
    half = depth // 2
    zero = jnp.zeros_like(keep)
    top_inner = [mix_ref[i] for i in range(half)]
    top_outer = [zero] + top_inner[:-1]
    low_outer = [mix_ref[depth - 1 - i] for i in range(half)]
    low_inner = [mix_ref[depth - 2 - i] for i in range(half)]
    for levels, inner, outer in (
        (range(half), top_inner, top_outer),
        (range(depth - 1, half - 1, -1), low_inner, low_outer),
    ):
        inverse = minors(inner, outer)
        for i, k in enumerate(levels):
            a_ref[k] = inverse[i] * keep
            b_ref[k] = inverse[i] * outer[i]
            c_ref[k] = inverse[i] * inner[i]


def block_rows(source_ref, k, weights, sums_ref, i, place):
    vectors = source_ref.shape[1]
    for r in range(2):
        total = source_ref[k, :, 4 * r, :] * weights[4 * r]
        for j in range(4 * r + 1, 4 * r + 4):
            total = total + source_ref[k, :, j, :] * weights[j]
        column = (2 * place + r) * LANES
        sums_ref[pl.ds(i * vectors, vectors), column : column + LANES] = total


def block_columns(sums_ref):
    wide = sums_ref.shape[1]
    p = lax.broadcasted_iota(jnp.int32, (wide, LANES), 0)
    q = lax.broadcasted_iota(jnp.int32, (wide, LANES), 1)
    pick = jnp.where(p // 4 == q, F32(0.0625), F32(0.0))
    return jnp.dot(
        sums_ref[...], pick, precision=lax.Precision.HIGHEST, preferred_element_type=F32
    )


def child_middle(carry, c_ref, half):
    vectors = len(carry) // 2
    top, low = c_ref[half - 1], c_ref[half]
    scale = 1.0 / (1.0 - top * low)
    first = [(carry[v] + top * carry[vectors + v]) * scale for v in range(vectors)]
    second = [(carry[vectors + v] + low * carry[v]) * scale for v in range(vectors)]
    return first + second


def child_up(carry, c_ref, solved_ref, lo_rows, hi_rows, lo_cols, hi_cols):
    depth, vectors = solved_ref.shape[0], solved_ref.shape[1]
    half = depth // 2
    lane = lane_index()

    def emit(i, values, packed):
        k_low = depth - 1 - i
        packed = list(packed)
        for side, k, base in ((0, i, i * vectors), (1, k_low, (half - 1 - i) * vectors)):
            for v in range(vectors):
                x = values[side * vectors + v]
                solved_ref[k, v] = x
                at = base + v
                turned = pltpu.roll(x, (at + 1) & (LANES - 1), 1)
                packed[2 * side] = jnp.where(lane == ((at + 1) & (LANES - 1)), turned, packed[2 * side])
                packed[2 * side + 1] = jnp.where(lane == at, turned, packed[2 * side + 1])
            lo_rows[pl.ds(k * vectors, vectors), :] = solved_ref[k, :, 0, :]
            hi_rows[pl.ds(k * vectors, vectors), :] = solved_ref[k, :, 7, :]
        return packed

    values = child_middle(carry, c_ref, half)
    blank = jnp.zeros((8, LANES), F32)
    packed = emit(half - 1, values, [blank] * 4)

    def up(step, state):
        i = half - 2 - step
        k_low = depth - 1 - i
        top, low = c_ref[i], c_ref[k_low]
        values = []
        for v in range(vectors):
            values.append(solved_ref[i, v] + top * state[v])
        for v in range(vectors):
            values.append(solved_ref[k_low, v] + low * state[vectors + v])
        packed = emit(i, values, state[2 * vectors :])
        return tuple(values) + tuple(packed)

    state = lax.fori_loop(0, half - 1, up, tuple(values) + tuple(packed))
    packed = state[2 * vectors :]
    for side in range(2):
        lo_cols[8 * side : 8 * side + 8, :] = packed[2 * side]
        hi_cols[8 * side : 8 * side + 8, :] = packed[2 * side + 1]


def child_first(x_ref, mix_ref, relax_ref, sums_out, solved_ref, lo_rows, hi_rows, lo_cols, hi_cols, a_ref, b_ref, c_ref, sums_ref):
    depth, vectors = x_ref.shape[0], x_ref.shape[1]
    half = depth // 2
    child_factors(mix_ref, 1.0 - relax_ref[...], a_ref, b_ref, c_ref)
    weights = [relax_ref[j : j + 1, :] for j in range(8)]

    def down(i, carry):
        k_low = depth - 1 - i
        values = []
        for side, k in ((0, i), (1, k_low)):
            a, b = a_ref[k], b_ref[k]
            for v in range(vectors):
                y = a * x_ref[k, v] + b * carry[side * vectors + v]
                solved_ref[k, v] = y
                values.append(y)
            block_rows(x_ref, k, weights, sums_ref, i, side)
        return tuple(values)

    blank = jnp.zeros((8, LANES), F32)
    carry = lax.fori_loop(0, half, down, (blank,) * (2 * vectors))
    sums_out[...] = block_columns(sums_ref)
    child_up(carry, c_ref, solved_ref, lo_rows, hi_rows, lo_cols, hi_cols)


def child_rates_of(rates_ref, k, land):
    east, west, north, south = (rates_ref[d, k] for d in range(4))
    centre = 1.0 - (east + west + north + south)
    return [land * part for part in (centre, east, west, north, south)]


def child_cell(solved_ref, k, v, base, half_index, rates, halos, lane, row):
    north_rows, south_rows, east_cols, west_cols = halos
    vectors = solved_ref.shape[1]
    s = solved_ref[k, v]
    at = base + v
    east_edge = pltpu.roll(east_cols[half_index], (LANES - 2 - at) & (LANES - 1), 1)
    west_edge = pltpu.roll(west_cols[half_index], (LANES - at) & (LANES - 1), 1)
    line = k * vectors + v
    north_edge = jnp.broadcast_to(north_rows[pl.ds(line, 1), :], (8, LANES))
    south_edge = jnp.broadcast_to(south_rows[pl.ds(line, 1), :], (8, LANES))
    east = jnp.where(lane == LANES - 1, east_edge, pltpu.roll(s, LANES - 1, 1))
    west = jnp.where(lane == 0, west_edge, pltpu.roll(s, 1, 1))
    north = jnp.where(row == 7, north_edge, pltpu.roll(s, 7, 0))
    south = jnp.where(row == 0, south_edge, pltpu.roll(s, 1, 0))
    return (rates[0] * s + rates[1] * east) + (rates[2] * west + rates[3] * north) + rates[4] * south


def child_second(
    solved_in, a_ref, b_ref, c_ref, rates_ref, land_ref, relax_ref, north_rows, south_rows, east_ref, west_ref,
    parent_ref, pa_ref, pb_ref, pc_ref, feed_ref,
    sums_out, solved_ref, psolved_ref, lo_rows, hi_rows, lo_cols, hi_cols,
    x_ref, sums_ref,
):
    depth, vectors = solved_in.shape[0], solved_in.shape[1]
    half = depth // 2
    lane, row = lane_index(), row_index()
    land = land_ref[...].astype(F32)
    weights = [relax_ref[j : j + 1, :] for j in range(8)]
    halos = (
        north_rows,
        south_rows,
        [east_ref[8 * h : 8 * h + 8, :] for h in range(2)],
        [west_ref[8 * h : 8 * h + 8, :] for h in range(2)],
    )

    def down(i, carry):
        k_low = depth - 1 - i
        values = []
        for side, k, base in ((0, i, i * vectors), (1, k_low, (half - 1 - i) * vectors)):
            a, b = a_ref[k], b_ref[k]
            rates = child_rates_of(rates_ref, k, land)
            for v in range(vectors):
                x = child_cell(solved_in, k, v, base, side, rates, halos, lane, row)
                x_ref[k, v] = x
                y = a * x + b * carry[side * vectors + v]
                solved_ref[k, v] = y
                values.append(y)
            block_rows(x_ref, k, weights, sums_ref, i, side)
        rhs = parent_ref[i] + feed_ref[pl.ds(i * 8, 8), :]
        psolved = pa_ref[pl.ds(i, 1), :] * rhs + pb_ref[pl.ds(i, 1), :] * carry[2 * vectors]
        psolved_ref[i] = psolved
        return tuple(values) + (psolved,)

    blank = jnp.zeros((8, LANES), F32)
    carry = lax.fori_loop(0, half, down, (blank,) * (2 * vectors + 1))
    sums_out[...] = block_columns(sums_ref)
    lines = depth * vectors
    parent_up(carry[-1], pc_ref, psolved_ref, lo_rows, hi_rows, lines, lo_cols, hi_cols, 16)
    child_up(carry[:-1], c_ref, solved_ref, lo_rows, hi_rows, lo_cols, hi_cols)


def child_last(solved_in, rates_ref, land_ref, north_rows, south_rows, east_ref, west_ref, out_ref):
    depth, vectors = solved_in.shape[0], solved_in.shape[1]
    half = depth // 2
    lane, row = lane_index(), row_index()
    land = land_ref[...].astype(F32)
    halos = (
        north_rows,
        south_rows,
        [east_ref[8 * h : 8 * h + 8, :] for h in range(2)],
        [west_ref[8 * h : 8 * h + 8, :] for h in range(2)],
    )

    def level(i, _):
        for side, k in ((0, i), (1, half + i)):
            rates = child_rates_of(rates_ref, k, land)
            for v in range(vectors):
                out_ref[k, v] = child_cell(solved_in, k, v, i * vectors, side, rates, halos, lane, row)
        return 0

    lax.fori_loop(0, half, level, 0)


def parent_prepare(parent_ref, rates_ref, mix_ref, land_ref, after_ref, packed_ref, prates_ref, pa_ref, pb_ref, pc_ref, mixed):
    depth = parent_ref.shape[0]
    half = depth // 2
    places = [(h, r, 64 * h + 32 * r) for h in range(2) for r in range(2)]
    land = jnp.concatenate([land_ref[r : r + 1, :] for _ in range(2) for r in range(2)], axis=1).astype(F32)

    def level(i, _):
        for h, r, lo in places:
            k = depth - 1 - i if h else i
            packed_ref[i, :, lo : lo + 32] = parent_ref[k, :, r, :]
            mixed[pl.ds(i, 1), lo : lo + 32] = mix_ref[k, pl.ds(r, 1), :]
            for d in range(4):
                prates_ref[d + 1, pl.ds(i, 1), lo : lo + 32] = rates_ref[d, k, pl.ds(r, 1), :]
        return 0

    lax.fori_loop(0, half, level, 0)
    land = jnp.broadcast_to(land, (half, LANES))
    sides = [prates_ref[d] for d in range(1, 5)]
    prates_ref[0] = land * (1.0 - (sides[0] + sides[1] + sides[2] + sides[3]))
    for d in range(4):
        prates_ref[d + 1] = land * sides[d]
    upper = lane_index(1) < 64
    rows = [mixed[i : i + 1, :] for i in range(half)]
    inner, outer = [], []
    for i in range(half):
        nearer = rows[i + 1] if i + 1 < half else pltpu.roll(rows[i], 64, 1)
        inner.append(jnp.where(upper, rows[i], nearer))
        outer.append(jnp.where(upper, rows[i - 1] if i else jnp.zeros_like(rows[0]), rows[i]))
    inverse = minors(inner, outer)
    for i in range(half):
        pa_ref[i : i + 1, :] = inverse[i]
        pb_ref[i : i + 1, :] = inverse[i] * outer[i]
        pc_ref[i : i + 1, :] = inverse[i] * inner[i]


def parent_up(carry, pc_ref, psolved_ref, lo_rows, hi_rows, lines, lo_cols, hi_cols, cols_at):
    half = psolved_ref.shape[0]
    lane = lane_index()
    middle = pc_ref[half - 1 : half, :]
    scale = 1.0 / (1.0 - middle * pltpu.roll(middle, 64, 1))
    x = (carry + middle * pltpu.roll(carry, 64, 1)) * scale
    tiles = [None] * half
    tiles[half - 1] = x
    for i in range(half - 2, -1, -1):
        x = psolved_ref[i] + pc_ref[i : i + 1, :] * x
        tiles[i] = x
    lo = hi = jnp.zeros((8, LANES), F32)
    for i in range(half):
        psolved_ref[i] = tiles[i]
        here = (lane & 31) == i
        lo = jnp.where(here, pltpu.roll(tiles[i], i, 1) if i else tiles[i], lo)
        hi = jnp.where(here, pltpu.roll(tiles[i], (i + 97) & 127, 1), hi)
    lo_cols[cols_at : cols_at + 8, :] = lo
    hi_cols[cols_at : cols_at + 8, :] = hi
    first = (lane & 32) == 0
    for j in range(half // 2):
        one, two = tiles[j], tiles[j + half // 2]
        lo_rows[lines + 8 * j : lines + 8 * j + 8, :] = jnp.where(first, one, pltpu.roll(two, 32, 1))
        hi_rows[lines + 8 * j : lines + 8 * j + 8, :] = jnp.where(first, pltpu.roll(one, 96, 1), two)


def parent_transport(psolved_ref, prates_ref, north_rows, south_rows, lines, east, west, i):
    half = psolved_ref.shape[0]
    lane = lane_index()
    x = psolved_ref[i]
    j = i % (half // 2)
    lo = north_rows[lines + 8 * j : lines + 8 * j + 8, :]
    hi = south_rows[lines + 8 * j : lines + 8 * j + 8, :]
    if i < half // 2:
        lo = pltpu.roll(lo, 32, 1)
    else:
        hi = pltpu.roll(hi, 96, 1)
    first = (lane & 32) == 0
    to_north = jnp.where(first, pltpu.roll(x, 96, 1), lo)
    to_south = jnp.where(first, hi, pltpu.roll(x, 32, 1))
    east_edge = pltpu.roll(east, 31 - i, 1)
    west_edge = pltpu.roll(west, (LANES - i) & (LANES - 1), 1) if i else west
    column = lane & 31
    to_east = jnp.where(column == 31, east_edge, pltpu.roll(x, 127, 1))
    to_west = jnp.where(column == 0, west_edge, pltpu.roll(x, 1, 1))
    parts = [prates_ref[d, i : i + 1, :] for d in range(5)]
    return (parts[0] * x + parts[1] * to_east) + (parts[2] * to_west + parts[3] * to_north) + parts[4] * to_south


def parent_second(
    psolved_in, prates_ref, pa_ref, pb_ref, pc_ref, north_rows, south_rows, east_ref, west_ref, feed_ref,
    psolved_ref, lo_rows, hi_rows, lo_cols, hi_cols,
):
    half = psolved_in.shape[0]
    lines = north_rows.shape[0] - lo_rows.shape[0]
    east, west = east_ref[16:24, :], west_ref[16:24, :]
    y = jnp.zeros((8, LANES), F32)
    for i in range(half):
        rhs = parent_transport(psolved_in, prates_ref, north_rows, south_rows, lines, east, west, i)
        rhs = rhs + feed_ref[8 * i : 8 * i + 8, :]
        y = pa_ref[i : i + 1, :] * rhs + pb_ref[i : i + 1, :] * y
        psolved_ref[i] = y
    parent_up(y, pc_ref, psolved_ref, lo_rows, hi_rows, 0, lo_cols, hi_cols, 0)


def parent_last(psolved_in, prates_ref, north_rows, south_rows, east_ref, west_ref, out_ref):
    half = psolved_in.shape[0]
    east, west = east_ref[...], west_ref[...]
    for i in range(half):
        x = parent_transport(psolved_in, prates_ref, north_rows, south_rows, 0, east, west, i)
        for h in range(2):
            for r in range(2):
                lo = 64 * h + 32 * r
                out_ref[2 * half - 1 - i if h else i, :, r, :] = x[:, lo : lo + 32]


def passed_along(value, axis, steps):
    count = lax.axis_size(axis)
    return lax.ppermute(value, axis, [(i, (i + steps) % count) for i in range(count)])


def halos_of(lo_rows, hi_rows, lo_cols, hi_cols):
    north = passed_along(lo_rows, "gy", -1)
    south = passed_along(hi_rows, "gy", 1)
    east = passed_along(lo_cols, "gx", -1)
    west = passed_along(hi_cols, "gx", 1)
    return north, south, east, west


def local(
    child_adjoint,
    parent_adjoint,
    child_rates,
    child_mixing,
    child_land,
    parent_rates,
    parent_mixing,
    parent_land,
    relaxation,
):
    depth, vectors, lines, columns = child_adjoint.shape
    half = depth // 2
    quarter = lax.axis_size("gy") // 4
    field = shape(depth, vectors, lines, columns)
    factor = shape(depth, lines, columns)
    tiles = shape(half, vectors, LANES)
    sums = shape(half * vectors, LANES)
    count = depth * vectors
    sum_scratch = pltpu.VMEM((half * vectors, 4 * LANES), F32)

    sums1, solved, lo_r, hi_r, lo_c, hi_c, a, b, c = call(
        child_first,
        [sums, field, shape(count, LANES), shape(count, LANES), shape(16, LANES), shape(16, LANES), factor, factor, factor],
        [sum_scratch],
        [child_adjoint, child_mixing, relaxation],
        4_000_000,
        3_000_000,
    )
    halos = halos_of(lo_r, hi_r, lo_c, hi_c)
    feed = passed_along(sums1, "gy", quarter)
    packed, prates, pa, pb, pc = call(
        parent_prepare,
        [tiles, shape(5, half, LANES)] + [shape(half, LANES)] * 3,
        [pltpu.VMEM((half, LANES), F32)],
        [parent_adjoint, parent_rates, parent_mixing, parent_land, lo_c],
        1_000_000,
        3_000_000,
    )
    rows = count + half // 2 * vectors
    sums2, solved, psolved, lo_r, hi_r, lo_c, hi_c = call(
        child_second,
        [sums, field, tiles, shape(rows, LANES), shape(rows, LANES), shape(24, LANES), shape(24, LANES)],
        [pltpu.VMEM(field.shape, F32), sum_scratch],
        [solved, a, b, c, child_rates, child_land, relaxation, *halos, packed, pa, pb, pc, feed],
        8_000_000,
        3_000_000,
    )
    halos = halos_of(lo_r, hi_r, lo_c, hi_c)
    feed = passed_along(sums2, "gy", quarter)
    few = half // 2 * vectors
    psolved, lo_r, hi_r, lo_c, hi_c = call(
        parent_second,
        [tiles, shape(few, LANES), shape(few, LANES), shape(8, LANES), shape(8, LANES)],
        [],
        [psolved, prates, pa, pb, pc, *halos, feed],
        1_000_000,
        500_000,
    )
    parent_halos = halos_of(lo_r, hi_r, lo_c, hi_c)
    child_out = call(
        child_last,
        field,
        [],
        [solved, child_rates, child_land, *halos],
        4_000_000,
        3_000_000,
    )
    parent_out = call(
        parent_last,
        shape(*parent_adjoint.shape),
        [],
        [psolved, prates, *parent_halos],
        500_000,
        500_000,
    )
    return (child_out, parent_out)


def solution(mesh):
    wide = P(None, None, "gy", "gx")
    level = P(None, "gy", "gx")
    flat = P("gy", "gx")
    in_specs = (wide, wide, wide, level, flat, wide, level, flat, flat)
    return jax.shard_map(local, mesh=mesh, in_specs=in_specs, out_specs=(wide, wide), check_vma=False)
```

time: 137 us -> 42.4 us (0.31)
  local copies, waits for them, and re-layouts: 45.3 us -> 3.51 us
  other arithmetic: 41.4 us -> 0 us
  Pallas kernels: 0 us -> 14.8 us
  waiting for transfers between devices: 19.3 us -> 6.91 us
  starting transfers between devices: 25.7 us -> 16.2 us
  between operations: 4.35 us -> 0.7 us
    mul x25 -> x0, other arithmetic: 21.6 us -> none  [the longest x2 6.72 us: local(): weighted = child_state * relaxation[None, None]]
    slice x16 -> x0, local copies, waits for them, and re-layouts: 17.3 us -> none  [the longest x10 14 us: with_halo(): lax.slice_in_dim(block, 0, width, axis=dim)]
    pallas_call x0 -> x6, Pallas kernels: none -> 14.8 us  [call(): pl.pallas_call(body, out_shape=outs, in_specs=[VMEM] * len(operands), out...]
    ppermute x4 -> x0, local copies, waits for them, and re-layouts: 12.5 us -> none  [the longest x2 7.28 us: with_halo(): lax.ppermute(lax.slice_in_dim(block, block.shape[dim] - width, None, axis...]
    ppermute x18 -> x14, waiting for transfers between devices: 19.3 us -> 6.91 us  [passed_along(): lax.ppermute(value, axis, [(i, (i + steps) % count) for i in range(count)])]
    mul x6 -> x0, local copies, waits for them, and re-layouts: 10.2 us -> none  [the longest x2 7.51 us: local(): weighted = child_state * relaxation[None, None]]
    ppermute x18 -> x14, starting transfers between devices: 25.7 us -> 16.2 us  [passed_along(): lax.ppermute(value, axis, [(i, (i + steps) % count) for i in range(count)])]
    unnamed x64 -> x0, other arithmetic: 5.79 us -> none
  transfers between devices with their start and end apart: 18 -> 14, of which waited for: 5 -> 5; matrix products, arithmetic and copies ran while one was open for 43% -> 0% of each run, Pallas kernels for 0% -> 11%
where the time goes in v1:
time: 42.4 us; the launch traced here: 42.2 us
  starting transfers between devices  16.2 us (38%)
  Pallas kernels  14.8 us (35%)
  waiting for transfers between devices  6.91 us (16%)
  local copies, waits for them, and re-layouts  3.51 us (8%)
  between operations  0.7 us (2%)
    ppermute x14, starting transfers between devices, passed_along(): lax.ppermute(value, axis, [(i, (i + steps) % count) for i in range(count)])  16.2 us
    pallas_call x6, Pallas kernels, call(): pl.pallas_call(body, out_shape=outs, in_specs=[VMEM] * len(operands), out...  14.8 us
    ppermute x14, waiting for transfers between devices, passed_along(): lax.ppermute(value, axis, [(i, (i + steps) % count) for i in range(count)])  6.91 us
    unnamed x18, local copies, waits for them, and re-layouts  3.51 us
  transfers between devices with their start and end apart: 14, of which 5 were waited for; matrix products, arithmetic and copies ran while one was open for 0% of the time, Pallas kernels for 11%

profile of v1, /device:TPU:0, one launch (start us, length us, event | category | flops | bytes accessed | tf_op | source)
XLA Modules:
  0.0 42.2 jit_solution(578468763144514524)
XLA Ops:
  0.6 1.2 %copy-done.1 = f32[32,8,8,128]{3,2,1,0:T(8,128)S(1)} copy-done((f32[32,8,8,128]{3,2,1,0:T(8,128)S(1)}, f32[32,8,8,128]{3,2,1,0:T(8,128)}, u32[]{:S(2)}) %copy-start.1) | copy-done | bytes 1048600
  1.9 0.9 %copy-done.3 = f32[32,8,128]{2,1,0:T(8,128)S(1)} copy-done((f32[32,8,128]{2,1,0:T(8,128)S(1)}, f32[32,8,128]{2,1,0:T(8,128)}, u32[]{:S(2)}) %copy-start.3) | copy-done | bytes 131096
  2.8 0.7 %copy-done.6 = f32[8,128]{1,0:T(8,128)S(1)} copy-done((f32[8,128]{1,0:T(8,128)S(1)}, f32[8,128]{1,0:T(8,128)}, u32[]{:S(2)}) %copy-start.6) | copy-done | bytes 4120
  3.5 2.7 %child_first.1 = (f32[128,128]{1,0:T(8,128)S(1)}, f32[32,8,8,128]{3,2,1,0:T(8,128)S(1)}, f32[256,128]{1,0:T(8,128)S(1)}, f32[256,128]{1,0:T(8,128)S(1)}, f32[16,...) custom-call(f32[32,8,8,128]{3,2,1,0:T(8,128)S(1)} %copy-done.1, ...), custom_call_target="tpu_custom_call" | custom-call | flops 4000000 | bytes 3000000 | tf_op jit(solution)/shard_map/child_first/pallas_call | solution.py:19
  6.1 4.5 %collective-permute-start = (f32[256,128]{1,0:T(8,128)S(1)}, f32[256,128]{1,0:T(8,128)S(1)}, u32[]{:S(2)}, u32[]{:S(2)}) collective-permute-start(f32[256,128]{1,0:T(8,128)S(1)} %get-tuple-element.32), channel_id=1, source_target_pairs={{0,7},{1,0},{2,1},{3,2},{4,3},{5,4},{6,5},{7,6},{8,15},{9,8},{10,9... | collective-permute-start | bytes 393224 | tf_op jit(solution)/shard_map/ppermute | solution.py:367
  10.7 1.5 %collective-permute-start.3 = (f32[16,128]{1,0:T(8,128)S(1)}, f32[16,128]{1,0:T(8,128)S(1)}, u32[]{:S(2)}, u32[]{:S(2)}) collective-permute-start(f32[16,128]{1,0:T(8,128)S(1)} %get-tuple-element.35), channel_id=1, source_target_pairs={{0,8},{8,16},{16,24},{24,0},{1,9},{9,17},{17,25},{25,1},{2,10},{10... | collective-permute-start | bytes 24584 | tf_op jit(solution)/shard_map/ppermute | solution.py:367
  12.2 1.4 %collective-permute-start.2 = (f32[16,128]{1,0:T(8,128)S(1)}, f32[16,128]{1,0:T(8,128)S(1)}, u32[]{:S(2)}, u32[]{:S(2)}) collective-permute-start(f32[16,128]{1,0:T(8,128)S(1)} %get-tuple-element.34.after_ref), channel_id=1, source_target_pairs={{0,24},{8,0},{16,8},{24,16},{1,25},{9,1},{17,9},{25,17},{2,26},{10... | collective-permute-start | bytes 24584 | tf_op jit(solution)/shard_map/ppermute | solution.py:367
  13.7 1.6 %parent_prepare.1 = (f32[16,8,128]{2,1,0:T(8,128)S(1)}, f32[5,16,128]{2,1,0:T(8,128)S(1)}, f32[16,128]{1,0:T(8,128)S(1)}, f32[16,128]{1,0:T(8,128)S(1)}, f32[16,128]{1,0:T(8,128)S(1)}) custom-call(f32[32,8,2,32]{3,2,1,0:T(2,128)S(1)} %copy-done.2, f32[4,32,2,32]{3,2,1,0:T(2,128)S(1)} %copy-done.4, f32[32,2,32]{2,1,0:T(2,128)S(1)} %copy-done.5, ...), custom_call_target="tpu_custom_call" | custom-call | flops 1000000 | bytes 3000000 | tf_op jit(solution)/shard_map/parent_prepare/pallas_call | solution.py:19
  15.3 0.6 %collective-permute-done.2.east_ref = f32[16,128]{1,0:T(8,128)S(1)} collective-permute-done((f32[16,128]{1,0:T(8,128)S(1)}, f32[16,128]{1,0:T(8,128)S(1)}, u32[]{:S(2)}, u32[]{:S(2)}) %collective-permute-start.2) | collective-permute-done | bytes 8224 | tf_op jit(solution)/shard_map/ppermute | solution.py:367
  15.9 1.5 %collective-permute-done.4.feed_ref = f32[128,128]{1,0:T(8,128)S(1)} collective-permute-done((f32[128,128]{1,0:T(8,128)S(1)}, f32[128,128]{1,0:T(8,128)S(1)}, u32[]{:S(2)}, u32[]{:S(2)}) %collective-permute-start.4) | collective-permute-done | bytes 65568 | tf_op jit(solution)/shard_map/ppermute | solution.py:367
  17.4 0.1 collective-permute-done.1.south_rows
  17.6 0.7 %copy-done.7 = s32[8,128]{1,0:T(8,128)S(1)} copy-done((s32[8,128]{1,0:T(8,128)S(1)}, s32[8,128]{1,0:T(8,128)}, u32[]{:S(2)}) %copy-start.7) | copy-done | bytes 4120
  18.3 4.7 %child_second.1 = (f32[128,128]{1,0:T(8,128)S(1)}, f32[32,8,8,128]{3,2,1,0:T(8,128)S(1)}, f32[16,8,128]{2,1,0:T(8,128)S(1)}, f32[320,128]{1,0:T(8,128)S(1)}, f32...) custom-call(f32[32,8,8,128]{3,2,1,0:T(8,128)S(1)} %get-tuple-element.28.solved_in, ...), custom_call_target="tpu_custom_call" | custom-call | flops 8000000 | bytes 3000000 | tf_op jit(solution)/shard_map/child_second/pallas_call | solution.py:19
  23.0 0.7 %collective-permute-start.5 = (f32[320,128]{1,0:T(8,128)S(1)}, f32[320,128]{1,0:T(8,128)S(1)}, u32[]{:S(2)}, u32[]{:S(2)}) collective-permute-start(f32[320,128]{1,0:T(8,128)S(1)} %get-tuple-element.42), channel_id=1, source_target_pairs={{0,7},{1,0},{2,1},{3,2},{4,3},{5,4},{6,5},{7,6},{8,15},{9,8},{10,9... | collective-permute-start | bytes 491528 | tf_op jit(solution)/shard_map/ppermute | solution.py:367
  23.7 1.5 %collective-permute-start.9 = (f32[128,128]{1,0:T(8,128)S(1)}, f32[128,128]{1,0:T(8,128)S(1)}, u32[]{:S(2)}, u32[]{:S(2)}) collective-permute-start(f32[128,128]{1,0:T(8,128)S(1)} %get-tuple-element.48), channel_id=1, source_target_pairs={{0,2},{1,3},{2,4},{3,5},{4,6},{5,7},{6,0},{7,1},{8,10},{9,11},{10,... | collective-permute-start | bytes 196616 | tf_op jit(solution)/shard_map/ppermute | solution.py:367
  25.2 2.5 %collective-permute-start.7 = (f32[24,128]{1,0:T(8,128)S(1)}, f32[24,128]{1,0:T(8,128)S(1)}, u32[]{:S(2)}, u32[]{:S(2)}) collective-permute-start(f32[24,128]{1,0:T(8,128)S(1)} %get-tuple-element.44), channel_id=1, source_target_pairs={{0,24},{8,0},{16,8},{24,16},{1,25},{9,1},{17,9},{25,17},{2,26},{10... | collective-permute-start | bytes 36872 | tf_op jit(solution)/shard_map/ppermute | solution.py:367
  27.7 1.4 %collective-permute-done.7.east_ref = f32[24,128]{1,0:T(8,128)S(1)} collective-permute-done((f32[24,128]{1,0:T(8,128)S(1)}, f32[24,128]{1,0:T(8,128)S(1)}, u32[]{:S(2)}, u32[]{:S(2)}) %collective-permute-start.7) | collective-permute-done | bytes 12320 | tf_op jit(solution)/shard_map/ppermute | solution.py:367
  29.1 3.2 %collective-permute-done.8.west_ref = f32[24,128]{1,0:T(8,128)S(1)} collective-permute-done((f32[24,128]{1,0:T(8,128)S(1)}, f32[24,128]{1,0:T(8,128)S(1)}, u32[]{:S(2)}, u32[]{:S(2)}) %collective-permute-start.8) | collective-permute-done | bytes 12320 | tf_op jit(solution)/shard_map/ppermute | solution.py:367
  32.3 0.4 parent_second.1
  32.6 2.0 %collective-permute-start.10 = (f32[64,128]{1,0:T(8,128)S(1)}, f32[64,128]{1,0:T(8,128)S(1)}, u32[]{:S(2)}, u32[]{:S(2)}) collective-permute-start(f32[64,128]{1,0:T(8,128)S(1)} %get-tuple-element.50), channel_id=1, source_target_pairs={{0,7},{1,0},{2,1},{3,2},{4,3},{5,4},{6,5},{7,6},{8,15},{9,8},{10,9... | collective-permute-start | bytes 98312 | tf_op jit(solution)/shard_map/ppermute | solution.py:367
  34.7 0.7 %collective-permute-start.12 = (f32[8,128]{1,0:T(8,128)S(1)}, f32[8,128]{1,0:T(8,128)S(1)}, u32[]{:S(2)}, u32[]{:S(2)}) collective-permute-start(f32[8,128]{1,0:T(8,128)S(1)} %get-tuple-element.52), channel_id=1, source_target_pairs={{0,24},{8,0},{16,8},{24,16},{1,25},{9,1},{17,9},{25,17},{2,26},{10... | collective-permute-start | bytes 12296 | tf_op jit(solution)/shard_map/ppermute | solution.py:367
  35.3 1.4 %collective-permute-start.13 = (f32[8,128]{1,0:T(8,128)S(1)}, f32[8,128]{1,0:T(8,128)S(1)}, u32[]{:S(2)}, u32[]{:S(2)}) collective-permute-start(f32[8,128]{1,0:T(8,128)S(1)} %get-tuple-element.53), channel_id=1, source_target_pairs={{0,8},{8,16},{16,24},{24,0},{1,9},{9,17},{17,25},{25,1},{2,10},{10... | collective-permute-start | bytes 12296 | tf_op jit(solution)/shard_map/ppermute | solution.py:367
  36.7 3.2 %child_last.1 = f32[32,8,8,128]{3,2,1,0:T(8,128)} custom-call(f32[32,8,8,128]{3,2,1,0:T(8,128)S(1)} %get-tuple-element.41.solved_in, f32[4,32,8,128]{3,2,1,0:T(8,128)S(1)} %copy-done, s32[8,128]{1,0:T(8,128)S(1)} %copy-done.7, f32[320,128]{1,0:T(8,128)S(1)} %collective-permute-done.5.north_rows, f32[320,128]{1,0:T(8,128)S(1)} %collective-permute-done.6.south_rows, ...), custom_call_target="tpu_custom_call" | custom-call | flops 4000000 | bytes 3000000 | tf_op jit(solution)/shard_map/child_last/pallas_call | solution.py:19
  39.9 2.2 %parent_last.1 = f32[32,8,2,32]{3,2,1,0:T(2,128)} custom-call(f32[16,8,128]{2,1,0:T(8,128)S(1)} %get-tuple-element.49.psolved_in, f32[5,16,128]{2,1,0:T(8,128)S(1)} %get-tuple-element.47.prates_ref, f32[64,128]{1,0:T(8,128)S(1)} %collective-permute-done.10.north_rows, f32[64,128]{1,0:T(8,128)S(1)} %collective-permute-done.11.south_rows, ...), custom_call_target="tpu_custom_call" | custom-call | flops 500000 | bytes 500000 | tf_op jit(solution)/shard_map/parent_last/pallas_call | solution.py:19
  (28 shorter events, 0.1 us)
Async XLA Ops:
  0.6 1.2 %copy-start.1 = (f32[32,8,8,128]{3,2,1,0:T(8,128)S(1)}, f32[32,8,8,128]{3,2,1,0:T(8,128)}, u32[]{:S(2)}) copy-start(f32[32,8,8,128]{3,2,1,0:T(8,128)} %x_ref.1) | copy-start | bytes 3145732
  1.9 0.9 %copy-start.3 = (f32[32,8,128]{2,1,0:T(8,128)S(1)}, f32[32,8,128]{2,1,0:T(8,128)}, u32[]{:S(2)}) copy-start(f32[32,8,128]{2,1,0:T(8,128)} %mix_ref.2) | copy-start | bytes 393220
  2.8 0.7 %copy-start.6 = (f32[8,128]{1,0:T(8,128)S(1)}, f32[8,128]{1,0:T(8,128)}, u32[]{:S(2)}) copy-start(f32[8,128]{1,0:T(8,128)} %relax_ref.3) | copy-start | bytes 12292
  3.5 10.2 %copy-start.2 = (f32[32,8,2,32]{3,2,1,0:T(2,128)S(1)}, f32[32,8,2,32]{3,2,1,0:T(2,128)}, u32[]{:S(2)}) copy-start(f32[32,8,2,32]{3,2,1,0:T(2,128)} %parent_ref.1) | copy-start | bytes 196612
  3.5 10.2 %copy-start.4 = (f32[4,32,2,32]{3,2,1,0:T(2,128)S(1)}, f32[4,32,2,32]{3,2,1,0:T(2,128)}, u32[]{:S(2)}) copy-start(f32[4,32,2,32]{3,2,1,0:T(2,128)} %rates_ref.3) | copy-start | bytes 98308
  3.5 10.2 %copy-start.5 = (f32[32,2,32]{2,1,0:T(2,128)S(1)}, f32[32,2,32]{2,1,0:T(2,128)}, u32[]{:S(2)}) copy-start(f32[32,2,32]{2,1,0:T(2,128)} %mix_ref.3) | copy-start | bytes 24580
  3.5 14.1 %copy-start = (f32[4,32,8,128]{3,2,1,0:T(8,128)S(1)}, f32[4,32,8,128]{3,2,1,0:T(8,128)}, u32[]{:S(2)}) copy-start(f32[4,32,8,128]{3,2,1,0:T(8,128)} %rates_ref.5) | copy-start | bytes 1572868
  6.1 11.3 %collective-permute-start = (f32[256,128]{1,0:T(8,128)S(1)}, f32[256,128]{1,0:T(8,128)S(1)}, u32[]{:S(2)}, u32[]{:S(2)}) collective-permute-start(f32[256,128]{1,0:T(8,128)S(1)} %get-tuple-element.32), channel_id=1, source_target_pairs={{0,7},{1,0},{2,1},{3,2},{4,3},{5,4},{6,5},{7,6},{8,15},{9,8},{10,9... | collective-permute-start | bytes 393224 | tf_op jit(solution)/shard_map/ppermute | solution.py:367
  10.7 6.9 %collective-permute-start.1 = (f32[256,128]{1,0:T(8,128)S(1)}, f32[256,128]{1,0:T(8,128)S(1)}, u32[]{:S(2)}, u32[]{:S(2)}) collective-permute-start(f32[256,128]{1,0:T(8,128)S(1)} %get-tuple-element.33), channel_id=1, source_target_pairs={{0,1},{1,2},{2,3},{3,4},{4,5},{5,6},{6,7},{7,0},{8,9},{9,10},{10,1... | collective-permute-start | bytes 393224 | tf_op jit(solution)/shard_map/ppermute | solution.py:367
  10.7 6.7 %collective-permute-start.4 = (f32[128,128]{1,0:T(8,128)S(1)}, f32[128,128]{1,0:T(8,128)S(1)}, u32[]{:S(2)}, u32[]{:S(2)}) collective-permute-start(f32[128,128]{1,0:T(8,128)S(1)} %get-tuple-element.40), channel_id=1, source_target_pairs={{0,2},{1,3},{2,4},{3,5},{4,6},{5,7},{6,0},{7,1},{8,10},{9,11},{10,... | collective-permute-start | bytes 196616 | tf_op jit(solution)/shard_map/ppermute | solution.py:367
  10.7 3.0 %copy-start.8 = (s32[2,32]{1,0:T(2,128)S(1)}, s32[2,32]{1,0:T(2,128)}, u32[]{:S(2)}) copy-start(s32[2,32]{1,0:T(2,128)} %land_ref.3) | copy-start | bytes 772
  10.7 4.6 %collective-permute-start.3 = (f32[16,128]{1,0:T(8,128)S(1)}, f32[16,128]{1,0:T(8,128)S(1)}, u32[]{:S(2)}, u32[]{:S(2)}) collective-permute-start(f32[16,128]{1,0:T(8,128)S(1)} %get-tuple-element.35), channel_id=1, source_target_pairs={{0,8},{8,16},{16,24},{24,0},{1,9},{9,17},{17,25},{25,1},{2,10},{10... | collective-permute-start | bytes 24584 | tf_op jit(solution)/shard_map/ppermute | solution.py:367
  12.2 3.7 %collective-permute-start.2 = (f32[16,128]{1,0:T(8,128)S(1)}, f32[16,128]{1,0:T(8,128)S(1)}, u32[]{:S(2)}, u32[]{:S(2)}) collective-permute-start(f32[16,128]{1,0:T(8,128)S(1)} %get-tuple-element.34.after_ref), channel_id=1, source_target_pairs={{0,24},{8,0},{16,8},{24,16},{1,25},{9,1},{17,9},{25,17},{2,26},{10... | collective-permute-start | bytes 24584 | tf_op jit(solution)/shard_map/ppermute | solution.py:367
  17.6 0.7 %copy-start.7 = (s32[8,128]{1,0:T(8,128)S(1)}, s32[8,128]{1,0:T(8,128)}, u32[]{:S(2)}) copy-start(s32[8,128]{1,0:T(8,128)} %land_ref.5) | copy-start | bytes 12292
  23.0 9.3 %collective-permute-start.5 = (f32[320,128]{1,0:T(8,128)S(1)}, f32[320,128]{1,0:T(8,128)S(1)}, u32[]{:S(2)}, u32[]{:S(2)}) collective-permute-start(f32[320,128]{1,0:T(8,128)S(1)} %get-tuple-element.42), channel_id=1, source_target_pairs={{0,7},{1,0},{2,1},{3,2},{4,3},{5,4},{6,5},{7,6},{8,15},{9,8},{10,9... | collective-permute-start | bytes 491528 | tf_op jit(solution)/shard_map/ppermute | solution.py:367
  23.7 8.6 %collective-permute-start.6 = (f32[320,128]{1,0:T(8,128)S(1)}, f32[320,128]{1,0:T(8,128)S(1)}, u32[]{:S(2)}, u32[]{:S(2)}) collective-permute-start(f32[320,128]{1,0:T(8,128)S(1)} %get-tuple-element.43), channel_id=1, source_target_pairs={{0,1},{1,2},{2,3},{3,4},{4,5},{5,6},{6,7},{7,0},{8,9},{9,10},{10,1... | collective-permute-start | bytes 491528 | tf_op jit(solution)/shard_map/ppermute | solution.py:367
  23.7 8.6 %collective-permute-start.9 = (f32[128,128]{1,0:T(8,128)S(1)}, f32[128,128]{1,0:T(8,128)S(1)}, u32[]{:S(2)}, u32[]{:S(2)}) collective-permute-start(f32[128,128]{1,0:T(8,128)S(1)} %get-tuple-element.48), channel_id=1, source_target_pairs={{0,2},{1,3},{2,4},{3,5},{4,6},{5,7},{6,0},{7,1},{8,10},{9,11},{10,... | collective-permute-start | bytes 196616 | tf_op jit(solution)/shard_map/ppermute | solution.py:367
  25.2 3.9 %collective-permute-start.7 = (f32[24,128]{1,0:T(8,128)S(1)}, f32[24,128]{1,0:T(8,128)S(1)}, u32[]{:S(2)}, u32[]{:S(2)}) collective-permute-start(f32[24,128]{1,0:T(8,128)S(1)} %get-tuple-element.44), channel_id=1, source_target_pairs={{0,24},{8,0},{16,8},{24,16},{1,25},{9,1},{17,9},{25,17},{2,26},{10... | collective-permute-start | bytes 36872 | tf_op jit(solution)/shard_map/ppermute | solution.py:367
  27.7 4.6 %collective-permute-start.8 = (f32[24,128]{1,0:T(8,128)S(1)}, f32[24,128]{1,0:T(8,128)S(1)}, u32[]{:S(2)}, u32[]{:S(2)}) collective-permute-start(f32[24,128]{1,0:T(8,128)S(1)} %get-tuple-element.45), channel_id=1, source_target_pairs={{0,8},{8,16},{16,24},{24,0},{1,9},{9,17},{17,25},{25,1},{2,10},{10... | collective-permute-start | bytes 36872 | tf_op jit(solution)/shard_map/ppermute | solution.py:367
  32.6 7.3 %collective-permute-start.10 = (f32[64,128]{1,0:T(8,128)S(1)}, f32[64,128]{1,0:T(8,128)S(1)}, u32[]{:S(2)}, u32[]{:S(2)}) collective-permute-start(f32[64,128]{1,0:T(8,128)S(1)} %get-tuple-element.50), channel_id=1, source_target_pairs={{0,7},{1,0},{2,1},{3,2},{4,3},{5,4},{6,5},{7,6},{8,15},{9,8},{10,9... | collective-permute-start | bytes 98312 | tf_op jit(solution)/shard_map/ppermute | solution.py:367
  34.6 5.3 %collective-permute-start.11 = (f32[64,128]{1,0:T(8,128)S(1)}, f32[64,128]{1,0:T(8,128)S(1)}, u32[]{:S(2)}, u32[]{:S(2)}) collective-permute-start(f32[64,128]{1,0:T(8,128)S(1)} %get-tuple-element.51), channel_id=1, source_target_pairs={{0,1},{1,2},{2,3},{3,4},{4,5},{5,6},{6,7},{7,0},{8,9},{9,10},{10,1... | collective-permute-start | bytes 98312 | tf_op jit(solution)/shard_map/ppermute | solution.py:367
  34.7 5.2 %collective-permute-start.12 = (f32[8,128]{1,0:T(8,128)S(1)}, f32[8,128]{1,0:T(8,128)S(1)}, u32[]{:S(2)}, u32[]{:S(2)}) collective-permute-start(f32[8,128]{1,0:T(8,128)S(1)} %get-tuple-element.52), channel_id=1, source_target_pairs={{0,24},{8,0},{16,8},{24,16},{1,25},{9,1},{17,9},{25,17},{2,26},{10... | collective-permute-start | bytes 12296 | tf_op jit(solution)/shard_map/ppermute | solution.py:367
  35.3 4.6 %collective-permute-start.13 = (f32[8,128]{1,0:T(8,128)S(1)}, f32[8,128]{1,0:T(8,128)S(1)}, u32[]{:S(2)}, u32[]{:S(2)}) collective-permute-start(f32[8,128]{1,0:T(8,128)S(1)} %get-tuple-element.53), channel_id=1, source_target_pairs={{0,8},{8,16},{16,24},{24,0},{1,9},{9,17},{17,25},{25,1},{2,10},{10... | collective-permute-start | bytes 12296 | tf_op jit(solution)/shard_map/ppermute | solution.py:367

commit v2 on v1

v2 whole, which is shorter than its diff:
```python
import jax
import jax.numpy as jnp
from jax import lax
from jax.experimental import pallas as pl
from jax.experimental.pallas import tpu as pltpu
from jax.sharding import PartitionSpec as P

F32 = jnp.float32
VMEM = pl.BlockSpec(memory_space=pltpu.VMEM)
ANY = pl.BlockSpec(memory_space=pl.ANY)
LIMIT = 40 * 1024 * 1024
LANES = 128
LEVELS = 8


def shape(*dims):
    return jax.ShapeDtypeStruct(dims, F32)


def call(body, outs, scratch, operands, flops, touched, far_in=(), far_out=False):
    return pl.pallas_call(
        body,
        out_shape=outs,
        in_specs=[ANY if i in far_in else VMEM for i in range(len(operands))],
        out_specs=jax.tree.map(lambda _: ANY if far_out else VMEM, outs),
        scratch_shapes=scratch,
        compiler_params=pltpu.CompilerParams(vmem_limit_bytes=LIMIT),
        cost_estimate=pl.CostEstimate(flops=flops, bytes_accessed=touched, transcendentals=0),
        name=body.__name__,
    )(*operands)


def lane_index(rows=8):
    return lax.broadcasted_iota(jnp.int32, (rows, LANES), 1)


def row_index():
    return lax.broadcasted_iota(jnp.int32, (8, LANES), 0)


def minors(inner, outer):
    theta = delta = jnp.ones_like(inner[0])
    inverse = []
    for i in range(len(inner)):
        delta = theta + outer[i] * delta
        theta_next = delta + inner[i] * theta
        inverse.append(theta / theta_next)
        theta = theta_next
    return inverse


def parity():
    return lax.rem(lax.axis_index("gy"), 2)


def child_factors(mix_ref, keep, a_ref, b_ref, c_ref):
    depth = mix_ref.shape[0]
    half = depth // 2
    zero = jnp.zeros_like(keep)
    top_inner = [mix_ref[i] for i in range(half)]
    top_outer = [zero] + top_inner[:-1]
    low_outer = [mix_ref[depth - 1 - i] for i in range(half)]
    low_inner = [mix_ref[depth - 2 - i] for i in range(half)]
    for levels, inner, outer in (
        (range(half), top_inner, top_outer),
        (range(depth - 1, half - 1, -1), low_inner, low_outer),
    ):
        inverse = minors(inner, outer)
        for i, k in enumerate(levels):
            a_ref[k] = inverse[i] * keep
            b_ref[k] = inverse[i] * outer[i]
            c_ref[k] = inverse[i] * inner[i]


def block_rows(source_ref, k, weights, sums_ref, i, place):
    vectors = source_ref.shape[1]
    for r in range(2):
        total = source_ref[k, :, 4 * r, :] * weights[4 * r]
        for j in range(4 * r + 1, 4 * r + 4):
            total = total + source_ref[k, :, j, :] * weights[j]
        column = (2 * place + r) * LANES
        sums_ref[pl.ds(i * vectors, vectors), column : column + LANES] = total


def block_columns(sums_ref):
    wide = sums_ref.shape[1]
    p = lax.broadcasted_iota(jnp.int32, (wide, LANES), 0)
    q = lax.broadcasted_iota(jnp.int32, (wide, LANES), 1)
    pick = jnp.where(p // 4 == q, F32(0.0625), F32(0.0))
    return jnp.dot(
        sums_ref[...], pick, precision=lax.Precision.HIGHEST, preferred_element_type=F32
    )


def child_middle(carry, c_ref, half):
    vectors = len(carry) // 2
    top, low = c_ref[half - 1], c_ref[half]
    scale = 1.0 / (1.0 - top * low)
    first = [(carry[v] + top * carry[vectors + v]) * scale for v in range(vectors)]
    second = [(carry[vectors + v] + low * carry[v]) * scale for v in range(vectors)]
    return first + second


def child_up(carry, c_ref, solved_ref, mate_rows, far_rows, cols_ref):
    depth, vectors = solved_ref.shape[0], solved_ref.shape[1]
    half = depth // 2
    lane = lane_index()
    pair = lane >> 1
    odd = parity()
    mate_row, far_row = 7 * (1 - odd), 7 * odd

    def emit(i, values, packed):
        k_low = depth - 1 - i
        packed = list(packed)
        inside = i % LEVELS if isinstance(i, int) else lax.rem(i, LEVELS)
        for side, k, base in ((0, i, inside * vectors), (1, k_low, (LEVELS - 1 - inside) * vectors)):
            for v in range(vectors):
                x = values[side * vectors + v]
                solved_ref[k, v] = x
                at = base + v
                packed[side] = jnp.where(pair == at, pltpu.roll(x, 2 * at + 1 & (LANES - 1), 1), packed[side])
            mate_rows[pl.ds(k * vectors, vectors), :] = solved_ref[k, :, mate_row, :]
            far_rows[pl.ds(k * vectors, vectors), :] = solved_ref[k, :, far_row, :]
        return packed

    def up(i, state):
        k_low = depth - 1 - i
        top, low = c_ref[i], c_ref[k_low]
        values = []
        for v in range(vectors):
            values.append(solved_ref[i, v] + top * state[v])
        for v in range(vectors):
            values.append(solved_ref[k_low, v] + low * state[vectors + v])
        return tuple(values) + tuple(emit(i, values, state[2 * vectors :]))

    def keep_columns(group, packed):
        for side, g in ((0, group), (1, depth // LEVELS - 1 - group)):
            cols_ref[LEVELS * g : LEVELS * g + 8, :] = packed[side]

    blank = jnp.zeros((8, LANES), F32)
    values = child_middle(carry, c_ref, half)
    state = tuple(values) + tuple(emit(half - 1, values, [blank] * 2))
    for group in range(half // LEVELS - 1, -1, -1):
        last = LEVELS * (group + 1) - 1
        if group == half // LEVELS - 1:
            last -= 1
        count = last - LEVELS * group + 1
        state = lax.fori_loop(0, count, lambda step, state, last=last: up(last - step, state), state)
        keep_columns(group, state[2 * vectors :])
        state = state[: 2 * vectors] + (blank,) * 2


def child_first(
    x_hbm, mix_hbm, relax_hbm,
    sums_out, solved_ref, mate_rows, far_rows, cols_ref, a_ref, b_ref, c_ref,
    x_ref, mix_ref, relax_ref, sums_ref, sems,
):
    depth, vectors = x_ref.shape[0], x_ref.shape[1]
    half = depth // 2
    small = [
        pltpu.make_async_copy(mix_hbm, mix_ref, sems.at[0]),
        pltpu.make_async_copy(relax_hbm, relax_ref, sems.at[1]),
    ]
    for copy in small:
        copy.start()
    size, large = 4, []
    for start in range(0, half, size):
        for first in (start, depth - size - start):
            part = pl.ds(first, size)
            large.append(pltpu.make_async_copy(x_hbm.at[part], x_ref.at[part], sems.at[len(large) + 2]))
            large[-1].start()
    for copy in small:
        copy.wait()
    child_factors(mix_ref, 1.0 - relax_ref[...], a_ref, b_ref, c_ref)
    weights = [relax_ref[j : j + 1, :] for j in range(8)]

    def down(i, carry):
        k_low = depth - 1 - i
        values = []
        for side, k in ((0, i), (1, k_low)):
            a, b = a_ref[k], b_ref[k]
            for v in range(vectors):
                y = a * x_ref[k, v] + b * carry[side * vectors + v]
                solved_ref[k, v] = y
                values.append(y)
            block_rows(x_ref, k, weights, sums_ref, i, side)
        return tuple(values)

    carry = (jnp.zeros((8, LANES), F32),) * (2 * vectors)
    for part, start in enumerate(range(0, half, size)):
        large[2 * part].wait()
        large[2 * part + 1].wait()
        carry = lax.fori_loop(start, start + size, down, carry)
    sums_out[...] = block_columns(sums_ref)
    child_up(carry, c_ref, solved_ref, mate_rows, far_rows, cols_ref)


def merge_edges(cols_ref, merged_ref, rows):
    count = lax.axis_size("gx")
    at = lax.axis_index("gx")
    east, west = lax.rem(at + 1, count), lax.rem(at + count - 1, count)
    even = (lane_index() & 1) == 0
    for g in range(rows // 8):
        part = pl.ds(8 * g, 8)
        merged_ref[part, :] = jnp.where(even, cols_ref[west, part, :], pltpu.roll(cols_ref[east, part, :], LANES - 2, 1))


def child_halos(mate_ref, far_ref, cols_ref, north_ref, south_ref, merged_ref):
    swap = jnp.broadcast_to(parity(), (8, LANES)) == 1

    def sort(i, _):
        part = pl.ds(pl.multiple_of(8 * i, 8), 8)
        mate, far = mate_ref[part, :], far_ref[part, :]
        north_ref[part, :] = jnp.where(swap, far, mate)
        south_ref[part, :] = jnp.where(swap, mate, far)
        return 0

    lax.fori_loop(0, north_ref.shape[0] // 8, sort, 0, unroll=8)
    merge_edges(cols_ref, merged_ref, merged_ref.shape[0])


def child_cell(solved_ref, k, v, base, edges, rates, north_ref, south_ref, lane, row):
    vectors = solved_ref.shape[1]
    s = solved_ref[k, v]
    line = k * vectors + v
    edge = pltpu.roll(edges, (LANES - 2 * (base + v)) & (LANES - 1), 1)
    north_edge = jnp.broadcast_to(north_ref[pl.ds(line, 1), :], (8, LANES))
    south_edge = jnp.broadcast_to(south_ref[pl.ds(line, 1), :], (8, LANES))
    east = jnp.where(lane == LANES - 1, edge, pltpu.roll(s, LANES - 1, 1))
    west = jnp.where(lane == 0, edge, pltpu.roll(s, 1, 1))
    north = jnp.where(row == 7, north_edge, pltpu.roll(s, 7, 0))
    south = jnp.where(row == 0, south_edge, pltpu.roll(s, 1, 0))
    return (rates[0] * s + rates[1] * east) + (rates[2] * west + rates[3] * north) + rates[4] * south


def child_second(
    solved_in, a_ref, b_ref, c_ref, rates_ref, relax_ref, mate_in, far_in, cols_in,
    parent_ref, pa_ref, pb_ref, pc_ref, feed_ref,
    sums_out, solved_ref, psolved_ref, mate_rows, far_rows, cols_ref,
    x_ref, sums_ref, north_ref, south_ref, merged_ref,
):
    depth, vectors = solved_in.shape[0], solved_in.shape[1]
    half = depth // 2
    groups = depth // LEVELS
    lane, row = lane_index(), row_index()
    weights = [relax_ref[j : j + 1, :] for j in range(8)]
    child_halos(mate_in, far_in, cols_in, north_ref, south_ref, merged_ref)

    def down(i, carry, edges):
        k_low = depth - 1 - i
        inside = lax.rem(i, LEVELS)
        values = []
        for side, k, base in ((0, i, inside * vectors), (1, k_low, (LEVELS - 1 - inside) * vectors)):
            a, b = a_ref[k], b_ref[k]
            rates = [rates_ref[d, k] for d in range(5)]
            for v in range(vectors):
                x = child_cell(solved_in, k, v, base, edges[side], rates, north_ref, south_ref, lane, row)
                x_ref[k, v] = x
                y = a * x + b * carry[side * vectors + v]
                solved_ref[k, v] = y
                values.append(y)
            block_rows(x_ref, k, weights, sums_ref, i, side)
        rhs = parent_ref[i] + feed_ref[pl.ds(i * 8, 8), :]
        psolved = pa_ref[pl.ds(i, 1), :] * rhs + pb_ref[pl.ds(i, 1), :] * carry[2 * vectors]
        psolved_ref[i] = psolved
        return tuple(values) + (psolved,)

    carry = (jnp.zeros((8, LANES), F32),) * (2 * vectors + 1)
    for group in range(half // LEVELS):
        edges = [merged_ref[8 * g : 8 * g + 8, :] for g in (group, groups - 1 - group)]
        carry = lax.fori_loop(
            LEVELS * group, LEVELS * (group + 1), lambda i, carry, edges=edges: down(i, carry, edges), carry
        )
    sums_out[...] = block_columns(sums_ref)
    parent_up(carry[-1], pc_ref, psolved_ref, mate_rows, far_rows, depth * vectors, cols_ref, 8 * groups)
    child_up(carry[:-1], c_ref, solved_ref, mate_rows, far_rows, cols_ref)


def child_last(
    solved_in, rates_ref, mate_in, far_in, cols_in, out_hbm, out_ref, north_ref, south_ref, merged_ref, sems
):
    depth, vectors = solved_in.shape[0], solved_in.shape[1]
    lane, row = lane_index(), row_index()
    child_halos(mate_in, far_in, cols_in, north_ref, south_ref, merged_ref)
    copies = []
    for group in range(depth // LEVELS):
        edges = merged_ref[8 * group : 8 * group + 8, :]

        def level(inside, _):
            k = LEVELS * group + inside
            rates = [rates_ref[d, k] for d in range(5)]
            for v in range(vectors):
                out_ref[k, v] = child_cell(
                    solved_in, k, v, inside * vectors, edges, rates, north_ref, south_ref, lane, row
                )
            return 0

        lax.fori_loop(0, LEVELS, level, 0)
        part = pl.ds(LEVELS * group, LEVELS)
        copies.append(pltpu.make_async_copy(out_ref.at[part], out_hbm.at[part], sems.at[group]))
        copies[-1].start()
    for copy in copies:
        copy.wait()


def prepare(
    parent_ref, rates_ref, mix_ref, land_ref, child_rates_ref, child_land_ref, after_ref,
    packed_ref, prates_ref, pa_ref, pb_ref, pc_ref, child_out_ref, mixed,
):
    depth = child_rates_ref.shape[1]
    vectors = packed_ref.shape[1]
    half = depth // 2
    places = [(h, r, 64 * h + 32 * r) for h in range(2) for r in range(2)]
    land = jnp.concatenate([land_ref[r : r + 1, :] for _ in range(2) for r in range(2)], axis=1).astype(F32)

    def level(i, _):
        for h, r, lo in places:
            k = depth - 1 - i if h else i
            packed_ref[i, :, lo : lo + 32] = parent_ref[pl.ds(2 * vectors * k + r, vectors, stride=2), :]
            mixed[pl.ds(i, 1), lo : lo + 32] = mix_ref[pl.ds(2 * k + r, 1), :]
            for d in range(4):
                prates_ref[d + 1, pl.ds(i, 1), lo : lo + 32] = rates_ref[pl.ds(2 * (d * depth + k) + r, 1), :]
        return 0

    lax.fori_loop(0, half, level, 0)
    land = jnp.broadcast_to(land, (half, LANES))
    sides = [prates_ref[d] for d in range(1, 5)]
    prates_ref[0] = land * (1.0 - (sides[0] + sides[1] + sides[2] + sides[3]))
    for d in range(4):
        prates_ref[d + 1] = land * sides[d]
    upper = lane_index(1) < 64
    rows = [mixed[i : i + 1, :] for i in range(half)]
    inner, outer = [], []
    for i in range(half):
        nearer = rows[i + 1] if i + 1 < half else pltpu.roll(rows[i], 64, 1)
        inner.append(jnp.where(upper, rows[i], nearer))
        outer.append(jnp.where(upper, rows[i - 1] if i else jnp.zeros_like(rows[0]), rows[i]))
    inverse = minors(inner, outer)
    for i in range(half):
        pa_ref[i : i + 1, :] = inverse[i]
        pb_ref[i : i + 1, :] = inverse[i] * outer[i]
        pc_ref[i : i + 1, :] = inverse[i] * inner[i]
    child_land = child_land_ref[...].astype(F32)

    def child_level(k, _):
        sides = [child_rates_ref[d, k] for d in range(4)]
        child_out_ref[0, k] = child_land * (1.0 - (sides[0] + sides[1] + sides[2] + sides[3]))
        for d in range(4):
            child_out_ref[d + 1, k] = child_land * sides[d]
        return 0

    lax.fori_loop(0, depth, child_level, 0, unroll=4)


def parent_up(carry, pc_ref, psolved_ref, mate_rows, far_rows, lines, cols_ref, cols_at):
    half = psolved_ref.shape[0]
    lane = lane_index()
    middle = pc_ref[half - 1 : half, :]
    scale = 1.0 / (1.0 - middle * pltpu.roll(middle, 64, 1))
    x = (carry + middle * pltpu.roll(carry, 64, 1)) * scale
    tiles = [None] * half
    tiles[half - 1] = x
    for i in range(half - 2, -1, -1):
        x = psolved_ref[i] + pc_ref[i : i + 1, :] * x
        tiles[i] = x
    packed = jnp.zeros((8, LANES), F32)
    for i in range(half):
        psolved_ref[i] = tiles[i]
        packed = jnp.where(((lane & 31) >> 1) == i, pltpu.roll(tiles[i], 2 * i + 1, 1), packed)
    cols_ref[cols_at : cols_at + 8, :] = packed
    first = (lane & 32) == 0
    swap = jnp.broadcast_to(parity(), (8, LANES)) == 1
    for j in range(half // 2):
        one, two = tiles[j], tiles[j + half // 2]
        lo = jnp.where(first, one, pltpu.roll(two, 32, 1))
        hi = jnp.where(first, pltpu.roll(one, 96, 1), two)
        part = slice(lines + 8 * j, lines + 8 * j + 8)
        mate_rows[part, :] = jnp.where(swap, lo, hi)
        far_rows[part, :] = jnp.where(swap, hi, lo)


def parent_edges(cols_ref, at):
    count = lax.axis_size("gx")
    here = lax.axis_index("gx")
    east, west = lax.rem(here + 1, count), lax.rem(here + count - 1, count)
    part = slice(at, at + 8)
    even = (lane_index() & 1) == 0
    return jnp.where(even, cols_ref[west, part, :], pltpu.roll(cols_ref[east, part, :], 62, 1))


def parent_transport(psolved_ref, prates_ref, mate_row, far_row, edges, i):
    half = psolved_ref.shape[0]
    lane = lane_index()
    swap = jnp.broadcast_to(parity(), (8, LANES)) == 1
    x = psolved_ref[i]
    mate, far = mate_row(i % (half // 2)), far_row(i % (half // 2))
    lo, hi = jnp.where(swap, far, mate), jnp.where(swap, mate, far)
    if i < half // 2:
        lo = pltpu.roll(lo, 32, 1)
    else:
        hi = pltpu.roll(hi, 96, 1)
    first = (lane & 32) == 0
    to_north = jnp.where(first, pltpu.roll(x, 96, 1), lo)
    to_south = jnp.where(first, hi, pltpu.roll(x, 32, 1))
    edge = pltpu.roll(edges, (LANES - 2 * i - 32) & (LANES - 1), 1)
    column = lane & 31
    to_east = jnp.where(column == 31, edge, pltpu.roll(x, 127, 1))
    to_west = jnp.where(column == 0, edge, pltpu.roll(x, 1, 1))
    parts = [prates_ref[d, i : i + 1, :] for d in range(5)]
    return (parts[0] * x + parts[1] * to_east) + (parts[2] * to_west + parts[3] * to_north) + parts[4] * to_south


def parent_second(
    psolved_in, prates_ref, pa_ref, pb_ref, pc_ref, mate_in, far_in, cols_in, feed_ref,
    psolved_ref, mate_rows, far_rows, cols_ref,
):
    half = psolved_in.shape[0]
    lines = mate_in.shape[0] - mate_rows.shape[0]
    edges = parent_edges(cols_in, cols_in.shape[1] - 8)
    mate = lambda j: mate_in[lines + 8 * j : lines + 8 * j + 8, :]
    far = lambda j: far_in[lines + 8 * j : lines + 8 * j + 8, :]
    y = jnp.zeros((8, LANES), F32)
    for i in range(half):
        rhs = parent_transport(psolved_in, prates_ref, mate, far, edges, i)
        rhs = rhs + feed_ref[8 * i : 8 * i + 8, :]
        y = pa_ref[i : i + 1, :] * rhs + pb_ref[i : i + 1, :] * y
        psolved_ref[i] = y
    parent_up(y, pc_ref, psolved_ref, mate_rows, far_rows, 0, cols_ref, 0)


def parent_last(psolved_in, prates_ref, mate_in, far_in, cols_in, out_ref):
    half, vectors = psolved_in.shape[0], psolved_in.shape[1]
    edges = parent_edges(cols_in, 0)
    odd = parity()
    mate = lambda j: mate_in[1 - odd, 8 * j : 8 * j + 8, :]
    far = lambda j: far_in[odd, 8 * j : 8 * j + 8, :]
    for i in range(half):
        x = parent_transport(psolved_in, prates_ref, mate, far, edges, i)
        for h in range(2):
            for r in range(2):
                lo = 64 * h + 32 * r
                k = 2 * half - 1 - i if h else i
                out_ref[pl.ds(2 * vectors * k + r, vectors, stride=2), :] = x[:, lo : lo + 32]


def passed_along(value, axis, steps):
    count = lax.axis_size(axis)
    return lax.ppermute(value, axis, [(i, (i + steps) % count) for i in range(count)])


def couples(count):
    mates = [[i, i + 1] for i in range(0, count, 2)]
    fars = [[i, (i + 1) % count] for i in range(1, count, 2)]
    return mates, fars


def swapped(value, groups):
    return lax.ppermute(value, "gy", [pair for a, b in groups for pair in ((a, b), (b, a))])


def local(
    child_adjoint,
    parent_adjoint,
    child_rates,
    child_mixing,
    child_land,
    parent_rates,
    parent_mixing,
    parent_land,
    relaxation,
):
    depth, vectors, lines, columns = child_adjoint.shape
    half = depth // 2
    quarter = lax.axis_size("gy") // 4
    mates, fars = couples(lax.axis_size("gy"))
    field = shape(depth, vectors, lines, columns)
    factor = shape(depth, lines, columns)
    tiles = shape(half, vectors, LANES)
    sums = shape(half * vectors, LANES)
    count = depth * vectors
    edge = depth // LEVELS * 8
    sum_scratch = pltpu.VMEM((half * vectors, 4 * LANES), F32)
    halo_scratch = [pltpu.VMEM((count, LANES), F32), pltpu.VMEM((count, LANES), F32), pltpu.VMEM((edge, LANES), F32)]
    narrow = parent_adjoint.shape[-1]

    sums1, solved, mate, far, cols, a, b, c = call(
        child_first,
        [sums, field, shape(count, LANES), shape(count, LANES), shape(edge, LANES), factor, factor, factor],
        [
            pltpu.VMEM(field.shape, F32),
            pltpu.VMEM(factor.shape, F32),
            pltpu.VMEM((lines, columns), F32),
            sum_scratch,
            pltpu.SemaphoreType.DMA((2 + half // 2,)),
        ],
        [child_adjoint, child_mixing, relaxation],
        4_000_000,
        3_000_000,
        far_in=(0, 1, 2),
    )
    all_cols = lax.all_gather(cols, "gx")
    mate_in, far_in = swapped(mate, mates), swapped(far, fars)
    feed = passed_along(sums1, "gy", quarter)
    packed, prates, pa, pb, pc, rates = call(
        prepare,
        [tiles, shape(5, half, LANES)] + [shape(half, LANES)] * 3 + [shape(5, depth, lines, columns)],
        [pltpu.VMEM((half, LANES), F32)],
        [
            parent_adjoint.reshape(-1, narrow),
            parent_rates.reshape(-1, narrow),
            parent_mixing.reshape(-1, narrow),
            parent_land,
            child_rates,
            child_land,
            cols,
        ],
        1_000_000,
        3_000_000,
    )
    rows = count + half // 2 * vectors
    sums2, solved, psolved, mate, far, cols = call(
        child_second,
        [sums, field, tiles, shape(rows, LANES), shape(rows, LANES), shape(edge + 8, LANES)],
        [pltpu.VMEM(field.shape, F32), sum_scratch] + halo_scratch,
        [solved, a, b, c, rates, relaxation, mate_in, far_in, all_cols, packed, pa, pb, pc, feed],
        8_000_000,
        3_000_000,
    )
    all_cols = lax.all_gather(cols, "gx")
    mate_in, far_in = swapped(mate, mates), swapped(far, fars)
    feed = passed_along(sums2, "gy", quarter)
    few = half // 2 * vectors
    psolved, mate, far, cols = call(
        parent_second,
        [tiles, shape(few, LANES), shape(few, LANES), shape(8, LANES)],
        [],
        [psolved, prates, pa, pb, pc, mate_in, far_in, all_cols, feed],
        1_000_000,
        500_000,
    )
    last_cols = lax.all_gather(cols, "gx")
    last_mate = lax.all_gather(mate, "gy", axis_index_groups=mates)
    last_far = lax.all_gather(far, "gy", axis_index_groups=fars)
    child_out = call(
        child_last,
        field,
        [pltpu.VMEM(field.shape, F32)] + halo_scratch + [pltpu.SemaphoreType.DMA((depth // LEVELS,))],
        [solved, rates, mate_in, far_in, all_cols],
        4_000_000,
        3_000_000,
        far_out=True,
    )
    parent_out = call(
        parent_last,
        shape(depth * vectors * 2, narrow),
        [],
        [psolved, prates, last_mate, last_far, last_cols],
        500_000,
        500_000,
    )
    return (child_out, parent_out.reshape(parent_adjoint.shape))


def solution(mesh):
    wide = P(None, None, "gy", "gx")
    level = P(None, "gy", "gx")
    flat = P("gy", "gx")
    in_specs = (wide, wide, wide, level, flat, wide, level, flat, flat)
    return jax.shard_map(local, mesh=mesh, in_specs=in_specs, out_specs=(wide, wide), check_vma=False)
```

time: 42.4 us -> 61.6 us (1.45)
  blocking collectives: 0 us -> 31.4 us
  starting transfers between devices: 16.2 us -> 9.23 us
  waiting for transfers between devices: 6.91 us -> 0.02 us
  Pallas kernels: 14.8 us -> 15.7 us
  local copies, waits for them, and re-layouts: 3.51 us -> 4.16 us
    all_gather x0 -> x5, blocking collectives: none -> 31.4 us  [the longest x2 16.6 us: local(): all_cols = lax.all_gather(cols, 'gx')]
    ppermute x14 -> x2, starting transfers between devices: 16.2 us -> 0.01 us  [passed_along(): lax.ppermute(value, axis, [(i, (i + steps) % count) for i in range(count)])]
    ppermute x0 -> x4, starting transfers between devices: none -> 9.22 us  [swapped(): lax.ppermute(value, 'gy', [pair for a, b in groups for pair in ((a, b), (...]
    ppermute x14 -> x2, waiting for transfers between devices: 6.91 us -> 0.01 us  [passed_along(): lax.ppermute(value, axis, [(i, (i + steps) % count) for i in range(count)])]
    pallas_call x6, Pallas kernels: 14.8 us -> 15.7 us  [call(): pl.pallas_call(body, out_shape=outs, in_specs=[ANY if i in far_in else VM...]
    unnamed x18 -> x20, local copies, waits for them, and re-layouts: 3.51 us -> 4.16 us
  transfers between devices with their start and end apart: 14 -> 6, of which waited for: 5 -> 0; matrix products, arithmetic and copies ran while one was open for 0% -> 0% of each run, Pallas kernels for 11% -> 3%
where the time goes in v2:
time: 61.6 us; the launch traced here: 61.3 us
  blocking collectives  31.4 us (51%)
  Pallas kernels  15.7 us (25%)
  starting transfers between devices  9.23 us (15%)
  local copies, waits for them, and re-layouts  4.16 us (7%)
  between operations  0.76 us (1%)
    all_gather x2, blocking collectives, local(): all_cols = lax.all_gather(cols, 'gx')  16.6 us
    pallas_call x6, Pallas kernels, call(): pl.pallas_call(body, out_shape=outs, in_specs=[ANY if i in far_in else VM...  15.7 us
    ppermute x4, starting transfers between devices, swapped(): lax.ppermute(value, 'gy', [pair for a, b in groups for pair in ((a, b), (...  9.22 us
    all_gather x1, blocking collectives, local(): last_cols = lax.all_gather(cols, 'gx')  7.19 us
    all_gather x1, blocking collectives, local(): last_far = lax.all_gather(far, 'gy', axis_index_groups=fars)  5.85 us
    unnamed x20, local copies, waits for them, and re-layouts  4.16 us
    all_gather x1, blocking collectives, local(): last_mate = lax.all_gather(mate, 'gy', axis_index_groups=mates)  1.84 us
  transfers between devices with their start and end apart: 6, of which 0 were waited for; matrix products, arithmetic and copies ran while one was open for 0% of the time, Pallas kernels for 3%

profile of v2, /device:TPU:0, one launch (start us, length us, event | category | flops | bytes accessed | tf_op | source)
XLA Modules:
  0.0 61.3 jit_solution(599909640865514317)
XLA Ops:
  0.6 1.2 %copy-done = f32[32,8,8,128]{3,2,1,0:T(8,128)S(1)} copy-done((f32[32,8,8,128]{3,2,1,0:T(8,128)S(1)}, f32[32,8,8,128]{3,2,1,0:T(8,128)}, u32[]{:S(2)}) %copy-start) | copy-done | bytes 1048600
  1.9 0.9 %copy-done.3 = f32[32,8,128]{2,1,0:T(8,128)S(1)} copy-done((f32[32,8,128]{2,1,0:T(8,128)S(1)}, f32[32,8,128]{2,1,0:T(8,128)}, u32[]{:S(2)}) %copy-start.3) | copy-done | bytes 131096
  2.8 0.7 %copy-done.6 = f32[8,128]{1,0:T(8,128)S(1)} copy-done((f32[8,128]{1,0:T(8,128)S(1)}, f32[8,128]{1,0:T(8,128)}, u32[]{:S(2)}) %copy-start.6) | copy-done | bytes 4120
  3.5 4.3 %child_first.1 = (f32[128,128]{1,0:T(8,128)S(1)}, f32[32,8,8,128]{3,2,1,0:T(8,128)S(1)}, f32[256,128]{1,0:T(8,128)S(1)}, f32[256,128]{1,0:T(8,128)S(1)}, f32[32,...) custom-call(f32[32,8,8,128]{3,2,1,0:T(8,128)S(1)} %copy-done, ...), custom_call_target="tpu_custom_call" | custom-call | flops 4000000 | bytes 3000000 | tf_op jit(solution)/shard_map/child_first/pallas_call | solution.py:21
  7.7 0.5 collective-permute-start
  8.2 4.7 %collective-permute-start.1 = (f32[256,128]{1,0:T(8,128)S(1)}, f32[256,128]{1,0:T(8,128)S(1)}, u32[]{:S(2)}, u32[]{:S(2)}) collective-permute-start(f32[256,128]{1,0:T(8,128)S(1)} %get-tuple-element.33), channel_id=1, source_target_pairs={{1,2},{2,1},{3,4},{4,3},{5,6},{6,5},{7,0},{0,7},{9,10},{10,9},{11,... | collective-permute-start | bytes 393224 | tf_op jit(solution)/shard_map/ppermute | solution.py:458
  13.0 0.0 collective-permute-start.2
  13.0 0.6 %copy-done.8 = s32[8,128]{1,0:T(8,128)S(1)} copy-done((s32[8,128]{1,0:T(8,128)S(1)}, s32[8,128]{1,0:T(8,128)}, u32[]{:S(2)}) %copy-start.8) | copy-done | bytes 4120
  13.6 0.0 copy-done.9
  13.7 1.7 %prepare.1 = (f32[16,8,128]{2,1,0:T(8,128)S(1)}, f32[5,16,128]{2,1,0:T(8,128)S(1)}, f32[16,128]{1,0:T(8,128)S(1)}, f32[16,128]{1,0:T(8,128)S(1)}, f32[16,128]{1,0:T(8,128)S(1)}, /*index=5*/f32[5,32,8,128]{3,2,1,0:T(8,128)S(1)}) custom-call(f32[512,32]{1,0:T(8,128)S(1)} %bitcast.11, f32[256,32]{1,0:T(8,128)S(1)} %bitcast.15, f32[64,32]{1,0:T(8,128)S(1)} %bitcast.17, ...), custom_call_target="tpu_custom_call" | custom-call | flops 1000000 | bytes 3000000 | tf_op jit(solution)/shard_map/prepare/pallas_call | solution.py:21
  15.3 8.2 %all-gather = f32[128,128]{1,0:T(8,128)S(1)} all-gather(f32[32,128]{1,0:T(8,128)S(1)} %get-tuple-element.30.after_ref), channel_id=2, replica_groups=mesh['gx'=4,'gy'=8] {'gx'}, dimensions={0}, use_global_device_ids=true | all-gather | bytes 81920 | tf_op jit(solution)/shard_map/all_gather | solution.py:501
  23.6 0.0 collective-permute-done.1.far_in
  23.6 0.0 copy-start.7
  23.6 0.7 %copy-done.7 = f32[8,128]{1,0:T(8,128)S(1)} copy-done((f32[8,128]{1,0:T(8,128)S(1)}, f32[8,128]{1,0:T(8,128)}, u32[]{:S(2)}) %copy-start.7) | copy-done | bytes 4120
  24.3 4.4 %child_second.1 = (f32[128,128]{1,0:T(8,128)S(1)}, f32[32,8,8,128]{3,2,1,0:T(8,128)S(1)}, f32[16,8,128]{2,1,0:T(8,128)S(1)}, f32[320,128]{1,0:T(8,128)S(1)}, f32...) custom-call(f32[32,8,8,128]{3,2,1,0:T(8,128)S(1)} %get-tuple-element.26.solved_in, f32[32,8,128]{2,1,0:T(8,128)S(1)} %get-tuple-element.27.a_ref, ...), custom_call_target="tpu_custom_call" | custom-call | flops 8000000 | bytes 3000000 | tf_op jit(solution)/shard_map/child_second/pallas_call | solution.py:21
  28.7 0.1 collective-permute-start.3
  28.8 3.9 %collective-permute-start.4 = (f32[320,128]{1,0:T(8,128)S(1)}, f32[320,128]{1,0:T(8,128)S(1)}, u32[]{:S(2)}, u32[]{:S(2)}) collective-permute-start(f32[320,128]{1,0:T(8,128)S(1)} %get-tuple-element.41), channel_id=1, source_target_pairs={{1,2},{2,1},{3,4},{4,3},{5,6},{6,5},{7,0},{0,7},{9,10},{10,9},{11,... | collective-permute-start | bytes 491528 | tf_op jit(solution)/shard_map/ppermute | solution.py:458
  32.7 8.3 %all-gather.1 = f32[160,128]{1,0:T(8,128)S(1)} all-gather(f32[40,128]{1,0:T(8,128)S(1)} %get-tuple-element.42), channel_id=3, replica_groups=mesh['gx'=4,'gy'=8] {'gx'}, dimensions={0}, use_global_device_ids=true | all-gather | bytes 102400 | tf_op jit(solution)/shard_map/all_gather | solution.py:529
  41.1 0.4 parent_second.1
  41.4 7.2 %all-gather.4 = f32[32,128]{1,0:T(8,128)S(1)} all-gather(f32[8,128]{1,0:T(8,128)S(1)} %get-tuple-element.49), channel_id=6, replica_groups=mesh['gx'=4,'gy'=8] {'gx'}, dimensions={0}, use_global_device_ids=true | all-gather | bytes 20480 | tf_op jit(solution)/shard_map/all_gather | solution.py:541
  48.6 1.8 %all-gather.2 = f32[128,128]{1,0:T(8,128)S(1)} all-gather(f32[64,128]{1,0:T(8,128)S(1)} %get-tuple-element.47), channel_id=4, replica_groups={{0,1},{2,3},{4,5},{6,7},{8,9},{10,11},{12,13},{14,15},{16,17},{18,19},{..., dimensions={0}, use_global_device_ids=true | all-gather | bytes 98304 | tf_op jit(solution)/shard_map/all_gather | solution.py:542
  50.5 5.9 %all-gather.3 = f32[128,128]{1,0:T(8,128)S(1)} all-gather(f32[64,128]{1,0:T(8,128)S(1)} %get-tuple-element.48), channel_id=5, replica_groups={{1,2},{3,4},{5,6},{7,0},{9,10},{11,12},{13,14},{15,8},{17,18},{19,20},{..., dimensions={0}, use_global_device_ids=true | all-gather | bytes 98304 | tf_op jit(solution)/shard_map/all_gather | solution.py:543
  56.3 1.0 %parent_last.1 = f32[512,32]{1,0:T(8,128)} custom-call(f32[16,8,128]{2,1,0:T(8,128)S(1)} %get-tuple-element.46.psolved_in, f32[5,16,128]{2,1,0:T(8,128)S(1)} %get-tuple-element.44.prates_ref, f32[2,64,128]{2,1,0:T(8,128)S(1)} %bitcast.13, f32[2,64,128]{2,1,0:T(8,128)S(1)} %bitcast.14, f32[4,8,128]{2,1,0:T(8,128)S(1)} %bitcast.16), custom_call_target="tpu_custom_call" | custom-call | flops 500000 | bytes 500000 | tf_op jit(solution)/shard_map/parent_last/pallas_call | solution.py:21
  57.3 3.9 %child_last.1 = f32[32,8,8,128]{3,2,1,0:T(8,128)} custom-call(f32[32,8,8,128]{3,2,1,0:T(8,128)S(1)} %get-tuple-element.39.solved_in, f32[5,32,8,128]{3,2,1,0:T(8,128)S(1)} %get-tuple-element.31.rates_ref, f32[320,128]{1,0:T(8,128)S(1)} %collective-permute-done.3.mate_in, f32[320,128]{1,0:T(8,128)S(1)} %collective-permute-done.4.far_in, ...), custom_call_target="tpu_custom_call" | custom-call | flops 4000000 | bytes 3000000 | tf_op jit(solution)/shard_map/child_last/pallas_call | solution.py:21
  (19 shorter events, 0.0 us)
Async XLA Ops:
  0.6 1.2 %copy-start = (f32[32,8,8,128]{3,2,1,0:T(8,128)S(1)}, f32[32,8,8,128]{3,2,1,0:T(8,128)}, u32[]{:S(2)}) copy-start(f32[32,8,8,128]{3,2,1,0:T(8,128)} %x_hbm.1) | copy-start | bytes 3145732
  1.9 0.9 %copy-start.3 = (f32[32,8,128]{2,1,0:T(8,128)S(1)}, f32[32,8,128]{2,1,0:T(8,128)}, u32[]{:S(2)}) copy-start(f32[32,8,128]{2,1,0:T(8,128)} %mix_hbm.1) | copy-start | bytes 393220
  2.8 0.7 %copy-start.6 = (f32[8,128]{1,0:T(8,128)S(1)}, f32[8,128]{1,0:T(8,128)}, u32[]{:S(2)}) copy-start(f32[8,128]{1,0:T(8,128)} %relax_ref.1) | copy-start | bytes 12292
  3.4 9.5 %copy-start.1 = (f32[4,32,8,128]{3,2,1,0:T(8,128)S(1)}, f32[4,32,8,128]{3,2,1,0:T(8,128)}, u32[]{:S(2)}) copy-start(f32[4,32,8,128]{3,2,1,0:T(8,128)} %child_rates_ref.1) | copy-start | bytes 1572868
  3.5 9.5 %copy-start.2 = (f32[32,8,2,32]{3,2,1,0:T(2,128)S(1)}, f32[32,8,2,32]{3,2,1,0:T(2,128)}, u32[]{:S(2)}) copy-start(f32[32,8,2,32]{3,2,1,0:T(2,128)} %param.10) | copy-start | bytes 196612
  3.5 9.5 %copy-start.4 = (f32[4,32,2,32]{3,2,1,0:T(2,128)S(1)}, f32[4,32,2,32]{3,2,1,0:T(2,128)}, u32[]{:S(2)}) copy-start(f32[4,32,2,32]{3,2,1,0:T(2,128)} %param.14) | copy-start | bytes 98308
  3.5 9.5 %copy-start.5 = (f32[32,2,32]{2,1,0:T(2,128)S(1)}, f32[32,2,32]{2,1,0:T(2,128)}, u32[]{:S(2)}) copy-start(f32[32,2,32]{2,1,0:T(2,128)} %param.15) | copy-start | bytes 24580
  7.7 15.9 %collective-permute-start = (f32[256,128]{1,0:T(8,128)S(1)}, f32[256,128]{1,0:T(8,128)S(1)}, u32[]{:S(2)}, u32[]{:S(2)}) collective-permute-start(f32[256,128]{1,0:T(8,128)S(1)} %get-tuple-element.32), channel_id=1, source_target_pairs={{0,1},{1,0},{2,3},{3,2},{4,5},{5,4},{6,7},{7,6},{8,9},{9,8},{10,11... | collective-permute-start | bytes 393224 | tf_op jit(solution)/shard_map/ppermute | solution.py:458
  8.2 15.3 %collective-permute-start.1 = (f32[256,128]{1,0:T(8,128)S(1)}, f32[256,128]{1,0:T(8,128)S(1)}, u32[]{:S(2)}, u32[]{:S(2)}) collective-permute-start(f32[256,128]{1,0:T(8,128)S(1)} %get-tuple-element.33), channel_id=1, source_target_pairs={{1,2},{2,1},{3,4},{4,3},{5,6},{6,5},{7,0},{0,7},{9,10},{10,9},{11,... | collective-permute-start | bytes 393224 | tf_op jit(solution)/shard_map/ppermute | solution.py:458
  13.0 0.7 %copy-start.8 = (s32[8,128]{1,0:T(8,128)S(1)}, s32[8,128]{1,0:T(8,128)}, u32[]{:S(2)}) copy-start(s32[8,128]{1,0:T(8,128)} %child_land_ref.1) | copy-start | bytes 12292
  13.0 10.6 %collective-permute-start.2 = (f32[128,128]{1,0:T(8,128)S(1)}, f32[128,128]{1,0:T(8,128)S(1)}, u32[]{:S(2)}, u32[]{:S(2)}) collective-permute-start(f32[128,128]{1,0:T(8,128)S(1)} %get-tuple-element.38), channel_id=1, source_target_pairs={{0,2},{1,3},{2,4},{3,5},{4,6},{5,7},{6,0},{7,1},{8,10},{9,11},{10,... | collective-permute-start | bytes 196616 | tf_op jit(solution)/shard_map/ppermute | solution.py:448
  13.0 0.7 %copy-start.9 = (s32[2,32]{1,0:T(2,128)S(1)}, s32[2,32]{1,0:T(2,128)}, u32[]{:S(2)}) copy-start(s32[2,32]{1,0:T(2,128)} %land_ref.1) | copy-start | bytes 772
  23.6 0.7 %copy-start.7 = (f32[8,128]{1,0:T(8,128)S(1)}, f32[8,128]{1,0:T(8,128)}, u32[]{:S(2)}) copy-start(f32[8,128]{1,0:T(8,128)} %relax_ref.1) | copy-start | bytes 12292
  28.7 12.3 %collective-permute-start.3 = (f32[320,128]{1,0:T(8,128)S(1)}, f32[320,128]{1,0:T(8,128)S(1)}, u32[]{:S(2)}, u32[]{:S(2)}) collective-permute-start(f32[320,128]{1,0:T(8,128)S(1)} %get-tuple-element.40), channel_id=1, source_target_pairs={{0,1},{1,0},{2,3},{3,2},{4,5},{5,4},{6,7},{7,6},{8,9},{9,8},{10,11... | collective-permute-start | bytes 491528 | tf_op jit(solution)/shard_map/ppermute | solution.py:458
  28.8 12.3 %collective-permute-start.4 = (f32[320,128]{1,0:T(8,128)S(1)}, f32[320,128]{1,0:T(8,128)S(1)}, u32[]{:S(2)}, u32[]{:S(2)}) collective-permute-start(f32[320,128]{1,0:T(8,128)S(1)} %get-tuple-element.41), channel_id=1, source_target_pairs={{1,2},{2,1},{3,4},{4,3},{5,6},{6,5},{7,0},{0,7},{9,10},{10,9},{11,... | collective-permute-start | bytes 491528 | tf_op jit(solution)/shard_map/ppermute | solution.py:458
  32.7 8.3 %collective-permute-start.5 = (f32[128,128]{1,0:T(8,128)S(1)}, f32[128,128]{1,0:T(8,128)S(1)}, u32[]{:S(2)}, u32[]{:S(2)}) collective-permute-start(f32[128,128]{1,0:T(8,128)S(1)} %get-tuple-element.45), channel_id=1, source_target_pairs={{0,2},{1,3},{2,4},{3,5},{4,6},{5,7},{6,0},{7,1},{8,10},{9,11},{10,... | collective-permute-start | bytes 196616 | tf_op jit(solution)/shard_map/ppermute | solution.py:448

commit v3 on v2

--- a/solution.py
+++ b/solution.py
@@ -7,7 +7,7 @@
 
 F32 = jnp.float32
 VMEM = pl.BlockSpec(memory_space=pltpu.VMEM)
-ANY = pl.BlockSpec(memory_space=pl.ANY)
+FAR = pl.BlockSpec(memory_space=pltpu.HBM)
 LIMIT = 40 * 1024 * 1024
 LANES = 128
 LEVELS = 8
@@ -21,8 +21,8 @@
     return pl.pallas_call(
         body,
         out_shape=outs,
-        in_specs=[ANY if i in far_in else VMEM for i in range(len(operands))],
-        out_specs=jax.tree.map(lambda _: ANY if far_out else VMEM, outs),
+        in_specs=[FAR if i in far_in else VMEM for i in range(len(operands))],
+        out_specs=jax.tree.map(lambda _: FAR if far_out else VMEM, outs),
         scratch_shapes=scratch,
         compiler_params=pltpu.CompilerParams(vmem_limit_bytes=LIMIT),
         cost_estimate=pl.CostEstimate(flops=flops, bytes_accessed=touched, transcendentals=0),
@@ -49,8 +49,8 @@
     return inverse
 
 
-def parity():
-    return lax.rem(lax.axis_index("gy"), 2)
+def parity(axis):
+    return lax.rem(lax.axis_index(axis), 2)
 
 
 def child_factors(mix_ref, keep, a_ref, b_ref, c_ref):
@@ -106,7 +106,7 @@
     half = depth // 2
     lane = lane_index()
     pair = lane >> 1
-    odd = parity()
+    odd = parity("gy")
     mate_row, far_row = 7 * (1 - odd), 7 * odd
 
     def emit(i, values, packed):
@@ -145,7 +145,7 @@
         if group == half // LEVELS - 1:
             last -= 1
         count = last - LEVELS * group + 1
-        state = lax.fori_loop(0, count, lambda step, state, last=last: up(last - step, state), state)
+        state = lax.fori_loop(0, count, lambda step, state, last=last: up(last - step, state), state, unroll=4 if count % 4 == 0 else count)
         keep_columns(group, state[2 * vectors :])
         state = state[: 2 * vectors] + (blank,) * 2
 
@@ -190,23 +190,19 @@
     for part, start in enumerate(range(0, half, size)):
         large[2 * part].wait()
         large[2 * part + 1].wait()
-        carry = lax.fori_loop(start, start + size, down, carry)
+        carry = lax.fori_loop(start, start + size, down, carry, unroll=size)
     sums_out[...] = block_columns(sums_ref)
     child_up(carry, c_ref, solved_ref, mate_rows, far_rows, cols_ref)
 
 
-def merge_edges(cols_ref, merged_ref, rows):
-    count = lax.axis_size("gx")
-    at = lax.axis_index("gx")
-    east, west = lax.rem(at + 1, count), lax.rem(at + count - 1, count)
-    even = (lane_index() & 1) == 0
-    for g in range(rows // 8):
-        part = pl.ds(8 * g, 8)
-        merged_ref[part, :] = jnp.where(even, cols_ref[west, part, :], pltpu.roll(cols_ref[east, part, :], LANES - 2, 1))
-
-
-def child_halos(mate_ref, far_ref, cols_ref, north_ref, south_ref, merged_ref):
-    swap = jnp.broadcast_to(parity(), (8, LANES)) == 1
+def merge_edges(mate, far, turn):
+    swap = jnp.broadcast_to(parity("gx"), (8, LANES)) == 1
+    east, west = jnp.where(swap, far, mate), jnp.where(swap, mate, far)
+    return jnp.where((lane_index() & 1) == 0, west, pltpu.roll(east, turn, 1))
+
+
+def child_halos(mate_ref, far_ref, north_ref, south_ref, mate_cols, far_cols, merged_ref):
+    swap = jnp.broadcast_to(parity("gy"), (8, LANES)) == 1
 
     def sort(i, _):
         part = pl.ds(pl.multiple_of(8 * i, 8), 8)
@@ -216,7 +212,9 @@
         return 0
 
     lax.fori_loop(0, north_ref.shape[0] // 8, sort, 0, unroll=8)
-    merge_edges(cols_ref, merged_ref, merged_ref.shape[0])
+    for g in range(merged_ref.shape[0] // 8):
+        part = slice(8 * g, 8 * g + 8)
+        merged_ref[part, :] = merge_edges(mate_cols[part, :], far_cols[part, :], LANES - 2)
 
 
 def child_cell(solved_ref, k, v, base, edges, rates, north_ref, south_ref, lane, row):
@@ -234,7 +232,7 @@
 
 
 def child_second(
-    solved_in, a_ref, b_ref, c_ref, rates_ref, relax_ref, mate_in, far_in, cols_in,
+    solved_in, a_ref, b_ref, c_ref, rates_ref, relax_ref, mate_in, far_in, mate_cols, far_cols,
     parent_ref, pa_ref, pb_ref, pc_ref, feed_ref,
     sums_out, solved_ref, psolved_ref, mate_rows, far_rows, cols_ref,
     x_ref, sums_ref, north_ref, south_ref, merged_ref,
@@ -244,7 +242,7 @@
     groups = depth // LEVELS
     lane, row = lane_index(), row_index()
     weights = [relax_ref[j : j + 1, :] for j in range(8)]
-    child_halos(mate_in, far_in, cols_in, north_ref, south_ref, merged_ref)
+    child_halos(mate_in, far_in, north_ref, south_ref, mate_cols, far_cols, merged_ref)
 
     def down(i, carry, edges):
         k_low = depth - 1 - i
@@ -269,7 +267,7 @@
     for group in range(half // LEVELS):
         edges = [merged_ref[8 * g : 8 * g + 8, :] for g in (group, groups - 1 - group)]
         carry = lax.fori_loop(
-            LEVELS * group, LEVELS * (group + 1), lambda i, carry, edges=edges: down(i, carry, edges), carry
+            LEVELS * group, LEVELS * (group + 1), lambda i, carry, edges=edges: down(i, carry, edges), carry, unroll=4
         )
     sums_out[...] = block_columns(sums_ref)
     parent_up(carry[-1], pc_ref, psolved_ref, mate_rows, far_rows, depth * vectors, cols_ref, 8 * groups)
@@ -277,11 +275,11 @@
 
 
 def child_last(
-    solved_in, rates_ref, mate_in, far_in, cols_in, out_hbm, out_ref, north_ref, south_ref, merged_ref, sems
+    solved_in, rates_ref, mate_in, far_in, mate_cols, far_cols, out_hbm, out_ref, north_ref, south_ref, merged_ref, sems
 ):
     depth, vectors = solved_in.shape[0], solved_in.shape[1]
     lane, row = lane_index(), row_index()
-    child_halos(mate_in, far_in, cols_in, north_ref, south_ref, merged_ref)
+    child_halos(mate_in, far_in, north_ref, south_ref, mate_cols, far_cols, merged_ref)
     copies = []
     for group in range(depth // LEVELS):
         edges = merged_ref[8 * group : 8 * group + 8, :]
@@ -295,7 +293,7 @@
                 )
             return 0
 
-        lax.fori_loop(0, LEVELS, level, 0)
+        lax.fori_loop(0, LEVELS, level, 0, unroll=4)
         part = pl.ds(LEVELS * group, LEVELS)
         copies.append(pltpu.make_async_copy(out_ref.at[part], out_hbm.at[part], sems.at[group]))
         copies[-1].start()
@@ -369,7 +367,7 @@
         packed = jnp.where(((lane & 31) >> 1) == i, pltpu.roll(tiles[i], 2 * i + 1, 1), packed)
     cols_ref[cols_at : cols_at + 8, :] = packed
     first = (lane & 32) == 0
-    swap = jnp.broadcast_to(parity(), (8, LANES)) == 1
+    swap = jnp.broadcast_to(parity("gy"), (8, LANES)) == 1
     for j in range(half // 2):
         one, two = tiles[j], tiles[j + half // 2]
         lo = jnp.where(first, one, pltpu.roll(two, 32, 1))
@@ -379,19 +377,14 @@
         far_rows[part, :] = jnp.where(swap, hi, lo)
 
 
-def parent_edges(cols_ref, at):
-    count = lax.axis_size("gx")
-    here = lax.axis_index("gx")
-    east, west = lax.rem(here + 1, count), lax.rem(here + count - 1, count)
-    part = slice(at, at + 8)
-    even = (lane_index() & 1) == 0
-    return jnp.where(even, cols_ref[west, part, :], pltpu.roll(cols_ref[east, part, :], 62, 1))
+def parent_edges(mate_cols, far_cols, at):
+    return merge_edges(mate_cols[at : at + 8, :], far_cols[at : at + 8, :], 62)
 
 
 def parent_transport(psolved_ref, prates_ref, mate_row, far_row, edges, i):
     half = psolved_ref.shape[0]
     lane = lane_index()
-    swap = jnp.broadcast_to(parity(), (8, LANES)) == 1
+    swap = jnp.broadcast_to(parity("gy"), (8, LANES)) == 1
     x = psolved_ref[i]
     mate, far = mate_row(i % (half // 2)), far_row(i % (half // 2))
     lo, hi = jnp.where(swap, far, mate), jnp.where(swap, mate, far)
@@ -411,12 +404,12 @@
 
 
 def parent_second(
-    psolved_in, prates_ref, pa_ref, pb_ref, pc_ref, mate_in, far_in, cols_in, feed_ref,
+    psolved_in, prates_ref, pa_ref, pb_ref, pc_ref, mate_in, far_in, mate_cols, far_cols, feed_ref,
     psolved_ref, mate_rows, far_rows, cols_ref,
 ):
     half = psolved_in.shape[0]
     lines = mate_in.shape[0] - mate_rows.shape[0]
-    edges = parent_edges(cols_in, cols_in.shape[1] - 8)
+    edges = parent_edges(mate_cols, far_cols, mate_cols.shape[0] - 8)
     mate = lambda j: mate_in[lines + 8 * j : lines + 8 * j + 8, :]
     far = lambda j: far_in[lines + 8 * j : lines + 8 * j + 8, :]
     y = jnp.zeros((8, LANES), F32)
@@ -428,12 +421,11 @@
     parent_up(y, pc_ref, psolved_ref, mate_rows, far_rows, 0, cols_ref, 0)
 
 
-def parent_last(psolved_in, prates_ref, mate_in, far_in, cols_in, out_ref):
+def parent_last(psolved_in, prates_ref, mate_in, far_in, mate_cols, far_cols, out_ref):
     half, vectors = psolved_in.shape[0], psolved_in.shape[1]
-    edges = parent_edges(cols_in, 0)
-    odd = parity()
-    mate = lambda j: mate_in[1 - odd, 8 * j : 8 * j + 8, :]
-    far = lambda j: far_in[odd, 8 * j : 8 * j + 8, :]
+    edges = parent_edges(mate_cols, far_cols, 0)
+    mate = lambda j: mate_in[8 * j : 8 * j + 8, :]
+    far = lambda j: far_in[8 * j : 8 * j + 8, :]
     for i in range(half):
         x = parent_transport(psolved_in, prates_ref, mate, far, edges, i)
         for h in range(2):
@@ -448,14 +440,17 @@
     return lax.ppermute(value, axis, [(i, (i + steps) % count) for i in range(count)])
 
 
-def couples(count):
-    mates = [[i, i + 1] for i in range(0, count, 2)]
-    fars = [[i, (i + 1) % count] for i in range(1, count, 2)]
-    return mates, fars
-
-
-def swapped(value, groups):
-    return lax.ppermute(value, "gy", [pair for a, b in groups for pair in ((a, b), (b, a))])
+def swapped(value, axis, offset):
+    count = lax.axis_size(axis)
+    pairs = []
+    for i in range(offset, count, 2):
+        j = (i + 1) % count
+        pairs += [(i, j), (j, i)]
+    return lax.ppermute(value, axis, pairs)
+
+
+def halos_of(mate, far, cols):
+    return [swapped(mate, "gy", 0), swapped(far, "gy", 1), swapped(cols, "gx", 0), swapped(cols, "gx", 1)]
 
 
 def local(
@@ -472,7 +467,6 @@
     depth, vectors, lines, columns = child_adjoint.shape
     half = depth // 2
     quarter = lax.axis_size("gy") // 4
-    mates, fars = couples(lax.axis_size("gy"))
     field = shape(depth, vectors, lines, columns)
     factor = shape(depth, lines, columns)
     tiles = shape(half, vectors, LANES)
@@ -498,8 +492,7 @@
         3_000_000,
         far_in=(0, 1, 2),
     )
-    all_cols = lax.all_gather(cols, "gx")
-    mate_in, far_in = swapped(mate, mates), swapped(far, fars)
+    halos = halos_of(mate, far, cols)
     feed = passed_along(sums1, "gy", quarter)
     packed, prates, pa, pb, pc, rates = call(
         prepare,
@@ -522,30 +515,27 @@
         child_second,
         [sums, field, tiles, shape(rows, LANES), shape(rows, LANES), shape(edge + 8, LANES)],
         [pltpu.VMEM(field.shape, F32), sum_scratch] + halo_scratch,
-        [solved, a, b, c, rates, relaxation, mate_in, far_in, all_cols, packed, pa, pb, pc, feed],
+        [solved, a, b, c, rates, relaxation, *halos, packed, pa, pb, pc, feed],
         8_000_000,
         3_000_000,
     )
-    all_cols = lax.all_gather(cols, "gx")
-    mate_in, far_in = swapped(mate, mates), swapped(far, fars)
+    halos = halos_of(mate, far, cols)
     feed = passed_along(sums2, "gy", quarter)
     few = half // 2 * vectors
     psolved, mate, far, cols = call(
         parent_second,
         [tiles, shape(few, LANES), shape(few, LANES), shape(8, LANES)],
         [],
-        [psolved, prates, pa, pb, pc, mate_in, far_in, all_cols, feed],
+        [psolved, prates, pa, pb, pc, *halos, feed],
         1_000_000,
         500_000,
     )
-    last_cols = lax.all_gather(cols, "gx")
-    last_mate = lax.all_gather(mate, "gy", axis_index_groups=mates)
-    last_far = lax.all_gather(far, "gy", axis_index_groups=fars)
+    last_halos = halos_of(mate, far, cols)
     child_out = call(
         child_last,
         field,
         [pltpu.VMEM(field.shape, F32)] + halo_scratch + [pltpu.SemaphoreType.DMA((depth // LEVELS,))],
-        [solved, rates, mate_in, far_in, all_cols],
+        [solved, rates, *halos],
         4_000_000,
         3_000_000,
         far_out=True,
@@ -554,7 +544,7 @@
         parent_last,
         shape(depth * vectors * 2, narrow),
         [],
-        [psolved, prates, last_mate, last_far, last_cols],
+        [psolved, prates, *last_halos],
         500_000,
         500_000,
     )

time: 61.6 us -> 41.8 us (0.68)
  blocking collectives: 31.4 us -> 0 us
  starting transfers between devices: 9.23 us -> 19.4 us
  waiting for transfers between devices: 0.02 us -> 5.72 us
  Pallas kernels: 15.7 us -> 11.5 us
    all_gather x5 -> x0, blocking collectives: 31.4 us -> none  [the longest x2 16.6 us: local(): all_cols = lax.all_gather(cols, 'gx')]
    ppermute x4 -> x12, starting transfers between devices: 9.22 us -> 19.4 us  [swapped(): return lax.ppermute(value, axis, pairs)]
    ppermute x4 -> x12, waiting for transfers between devices: 0.01 us -> 4.26 us  [swapped(): return lax.ppermute(value, axis, pairs)]
    pallas_call x6, Pallas kernels: 15.7 us -> 11.5 us  [call(): pl.pallas_call(body, out_shape=outs, in_specs=[FAR if i in far_in else VM...]
    ppermute x2, waiting for transfers between devices: 0.01 us -> 1.47 us  [passed_along(): lax.ppermute(value, axis, [(i, (i + steps) % count) for i in range(count)])]
  transfers between devices with their start and end apart: 6 -> 14, of which waited for: 0 -> 4; matrix products, arithmetic and copies ran while one was open for 0% -> 0% of each run, Pallas kernels for 3% -> 9%
where the time goes in v3:
time: 41.8 us; the launch traced here: 41.5 us
  starting transfers between devices  19.4 us (46%)
  Pallas kernels  11.5 us (28%)
  waiting for transfers between devices  5.72 us (14%)
  local copies, waits for them, and re-layouts  4.16 us (10%)
  between operations  0.76 us (2%)
    ppermute x12, starting transfers between devices, swapped(): return lax.ppermute(value, axis, pairs)  19.4 us
    pallas_call x6, Pallas kernels, call(): pl.pallas_call(body, out_shape=outs, in_specs=[FAR if i in far_in else VM...  11.5 us
    ppermute x12, waiting for transfers between devices, swapped(): return lax.ppermute(value, axis, pairs)  4.26 us
    unnamed x20, local copies, waits for them, and re-layouts  4.16 us
    ppermute x2, waiting for transfers between devices, passed_along(): lax.ppermute(value, axis, [(i, (i + steps) % count) for i in range(count)])  1.47 us
  transfers between devices with their start and end apart: 14, of which 4 were waited for; matrix products, arithmetic and copies ran while one was open for 0% of the time, Pallas kernels for 9%

profile of v3, /device:TPU:0, one launch (start us, length us, event | category | flops | bytes accessed | tf_op | source)
XLA Modules:
  0.0 41.5 jit_solution(4174931485799905866)
XLA Ops:
  0.6 1.2 %copy-done = f32[32,8,8,128]{3,2,1,0:T(8,128)S(1)} copy-done((f32[32,8,8,128]{3,2,1,0:T(8,128)S(1)}, f32[32,8,8,128]{3,2,1,0:T(8,128)}, u32[]{:S(2)}) %copy-start) | copy-done | bytes 1048600
  1.9 0.9 %copy-done.3 = f32[32,8,128]{2,1,0:T(8,128)S(1)} copy-done((f32[32,8,128]{2,1,0:T(8,128)S(1)}, f32[32,8,128]{2,1,0:T(8,128)}, u32[]{:S(2)}) %copy-start.3) | copy-done | bytes 131096
  2.8 0.7 %copy-done.6 = f32[8,128]{1,0:T(8,128)S(1)} copy-done((f32[8,128]{1,0:T(8,128)S(1)}, f32[8,128]{1,0:T(8,128)}, u32[]{:S(2)}) %copy-start.6) | copy-done | bytes 4120
  3.5 3.4 %child_first.1 = (f32[128,128]{1,0:T(8,128)S(1)}, f32[32,8,8,128]{3,2,1,0:T(8,128)S(1)}, f32[256,128]{1,0:T(8,128)S(1)}, f32[256,128]{1,0:T(8,128)S(1)}, f32[32,...) custom-call(f32[32,8,8,128]{3,2,1,0:T(8,128)S(1)} %copy-done, ...), custom_call_target="tpu_custom_call" | custom-call | flops 4000000 | bytes 3000000 | tf_op jit(solution)/shard_map/child_first/pallas_call | solution.py:21
  6.8 0.5 %collective-permute-start = (f32[256,128]{1,0:T(8,128)S(1)}, f32[256,128]{1,0:T(8,128)S(1)}, u32[]{:S(2)}, u32[]{:S(2)}) collective-permute-start(f32[256,128]{1,0:T(8,128)S(1)} %get-tuple-element.32), channel_id=1, source_target_pairs={{0,1},{1,0},{2,3},{3,2},{4,5},{5,4},{6,7},{7,6},{8,9},{9,8},{10,11... | collective-permute-start | bytes 393224 | tf_op jit(solution)/shard_map/ppermute | solution.py:449
  7.4 4.7 %collective-permute-start.1 = (f32[256,128]{1,0:T(8,128)S(1)}, f32[256,128]{1,0:T(8,128)S(1)}, u32[]{:S(2)}, u32[]{:S(2)}) collective-permute-start(f32[256,128]{1,0:T(8,128)S(1)} %get-tuple-element.33), channel_id=1, source_target_pairs={{1,2},{2,1},{3,4},{4,3},{5,6},{6,5},{7,0},{0,7},{9,10},{10,9},{11,... | collective-permute-start | bytes 393224 | tf_op jit(solution)/shard_map/ppermute | solution.py:449
  12.1 2.4 %collective-permute-start.3 = (f32[32,128]{1,0:T(8,128)S(1)}, f32[32,128]{1,0:T(8,128)S(1)}, u32[]{:S(2)}, u32[]{:S(2)}) collective-permute-start(f32[32,128]{1,0:T(8,128)S(1)} %get-tuple-element.30.after_ref), channel_id=1, source_target_pairs={{8,16},{16,8},{24,0},{0,24},{9,17},{17,9},{25,1},{1,25},{10,18},{1... | collective-permute-start | bytes 49160 | tf_op jit(solution)/shard_map/ppermute | solution.py:449
  14.5 0.5 %collective-permute-start.2 = (f32[32,128]{1,0:T(8,128)S(1)}, f32[32,128]{1,0:T(8,128)S(1)}, u32[]{:S(2)}, u32[]{:S(2)}) collective-permute-start(f32[32,128]{1,0:T(8,128)S(1)} %get-tuple-element.30.after_ref), channel_id=1, source_target_pairs={{0,8},{8,0},{16,24},{24,16},{1,9},{9,1},{17,25},{25,17},{2,10},{10... | collective-permute-start | bytes 49160 | tf_op jit(solution)/shard_map/ppermute | solution.py:449
  15.1 0.6 %copy-done.9 = s32[2,32]{1,0:T(2,128)S(1)} copy-done((s32[2,32]{1,0:T(2,128)S(1)}, s32[2,32]{1,0:T(2,128)}, u32[]{:S(2)}) %copy-start.9) | copy-done | bytes 280
  15.7 1.7 %prepare.1 = (f32[16,8,128]{2,1,0:T(8,128)S(1)}, f32[5,16,128]{2,1,0:T(8,128)S(1)}, f32[16,128]{1,0:T(8,128)S(1)}, f32[16,128]{1,0:T(8,128)S(1)}, f32[16,128]{1,0:T(8,128)S(1)}, /*index=5*/f32[5,32,8,128]{3,2,1,0:T(8,128)S(1)}) custom-call(f32[512,32]{1,0:T(8,128)S(1)} %bitcast.4, f32[256,32]{1,0:T(8,128)S(1)} %bitcast.5, f32[64,32]{1,0:T(8,128)S(1)} %bitcast.6, ...), custom_call_target="tpu_custom_call" | custom-call | flops 1000000 | bytes 3000000 | tf_op jit(solution)/shard_map/prepare/pallas_call | solution.py:21
  17.4 0.8 %collective-permute-done.2.mate_cols = f32[32,128]{1,0:T(8,128)S(1)} collective-permute-done((f32[32,128]{1,0:T(8,128)S(1)}, f32[32,128]{1,0:T(8,128)S(1)}, u32[]{:S(2)}, u32[]{:S(2)}) %collective-permute-start.2) | collective-permute-done | bytes 16416 | tf_op jit(solution)/shard_map/ppermute | solution.py:449
  18.3 0.7 %copy-done.7 = f32[8,128]{1,0:T(8,128)S(1)} copy-done((f32[8,128]{1,0:T(8,128)S(1)}, f32[8,128]{1,0:T(8,128)}, u32[]{:S(2)}) %copy-start.7) | copy-done | bytes 4120
  19.0 2.8 %child_second.1 = (f32[128,128]{1,0:T(8,128)S(1)}, f32[32,8,8,128]{3,2,1,0:T(8,128)S(1)}, f32[16,8,128]{2,1,0:T(8,128)S(1)}, f32[320,128]{1,0:T(8,128)S(1)}, f32...) custom-call(f32[32,8,8,128]{3,2,1,0:T(8,128)S(1)} %get-tuple-element.26.solved_in, f32[32,8,128]{2,1,0:T(8,128)S(1)} %get-tuple-element.27.a_ref, ...), custom_call_target="tpu_custom_call" | custom-call | flops 8000000 | bytes 3000000 | tf_op jit(solution)/shard_map/child_second/pallas_call | solution.py:21
  21.9 3.9 %collective-permute-start.6 = (f32[320,128]{1,0:T(8,128)S(1)}, f32[320,128]{1,0:T(8,128)S(1)}, u32[]{:S(2)}, u32[]{:S(2)}) collective-permute-start(f32[320,128]{1,0:T(8,128)S(1)} %get-tuple-element.41), channel_id=1, source_target_pairs={{1,2},{2,1},{3,4},{4,3},{5,6},{6,5},{7,0},{0,7},{9,10},{10,9},{11,... | collective-permute-start | bytes 491528 | tf_op jit(solution)/shard_map/ppermute | solution.py:449
  25.8 0.9 %collective-permute-start.8 = (f32[40,128]{1,0:T(8,128)S(1)}, f32[40,128]{1,0:T(8,128)S(1)}, u32[]{:S(2)}, u32[]{:S(2)}) collective-permute-start(f32[40,128]{1,0:T(8,128)S(1)} %get-tuple-element.42), channel_id=1, source_target_pairs={{8,16},{16,8},{24,0},{0,24},{9,17},{17,9},{25,1},{1,25},{10,18},{1... | collective-permute-start | bytes 61448 | tf_op jit(solution)/shard_map/ppermute | solution.py:449
  26.7 1.1 %collective-permute-start.7 = (f32[40,128]{1,0:T(8,128)S(1)}, f32[40,128]{1,0:T(8,128)S(1)}, u32[]{:S(2)}, u32[]{:S(2)}) collective-permute-start(f32[40,128]{1,0:T(8,128)S(1)} %get-tuple-element.42), channel_id=1, source_target_pairs={{0,8},{8,0},{16,24},{24,16},{1,9},{9,1},{17,25},{25,17},{2,10},{10... | collective-permute-start | bytes 61448 | tf_op jit(solution)/shard_map/ppermute | solution.py:449
  27.8 2.7 %collective-permute-done.8.far_cols = f32[40,128]{1,0:T(8,128)S(1)} collective-permute-done((f32[40,128]{1,0:T(8,128)S(1)}, f32[40,128]{1,0:T(8,128)S(1)}, u32[]{:S(2)}, u32[]{:S(2)}) %collective-permute-start.8) | collective-permute-done | bytes 20512 | tf_op jit(solution)/shard_map/ppermute | solution.py:449
  30.5 1.5 %collective-permute-done.9.feed_ref = f32[128,128]{1,0:T(8,128)S(1)} collective-permute-done((f32[128,128]{1,0:T(8,128)S(1)}, f32[128,128]{1,0:T(8,128)S(1)}, u32[]{:S(2)}, u32[]{:S(2)}) %collective-permute-start.9) | collective-permute-done | bytes 65568 | tf_op jit(solution)/shard_map/ppermute | solution.py:440
  32.5 2.5 %collective-permute-start.11 = (f32[64,128]{1,0:T(8,128)S(1)}, f32[64,128]{1,0:T(8,128)S(1)}, u32[]{:S(2)}, u32[]{:S(2)}) collective-permute-start(f32[64,128]{1,0:T(8,128)S(1)} %get-tuple-element.48), channel_id=1, source_target_pairs={{1,2},{2,1},{3,4},{4,3},{5,6},{6,5},{7,0},{0,7},{9,10},{10,9},{11,... | collective-permute-start | bytes 98312 | tf_op jit(solution)/shard_map/ppermute | solution.py:449
  34.9 2.0 %collective-permute-start.13 = (f32[8,128]{1,0:T(8,128)S(1)}, f32[8,128]{1,0:T(8,128)S(1)}, u32[]{:S(2)}, u32[]{:S(2)}) collective-permute-start(f32[8,128]{1,0:T(8,128)S(1)} %get-tuple-element.49), channel_id=1, source_target_pairs={{8,16},{16,8},{24,0},{0,24},{9,17},{17,9},{25,1},{1,25},{10,18},{1... | collective-permute-start | bytes 12296 | tf_op jit(solution)/shard_map/ppermute | solution.py:449
  36.9 0.7 %collective-permute-start.12 = (f32[8,128]{1,0:T(8,128)S(1)}, f32[8,128]{1,0:T(8,128)S(1)}, u32[]{:S(2)}, u32[]{:S(2)}) collective-permute-start(f32[8,128]{1,0:T(8,128)S(1)} %get-tuple-element.49), channel_id=1, source_target_pairs={{0,8},{8,0},{16,24},{24,16},{1,9},{9,1},{17,25},{25,17},{2,10},{10... | collective-permute-start | bytes 12296 | tf_op jit(solution)/shard_map/ppermute | solution.py:449
  37.6 2.2 %child_last.1 = f32[32,8,8,128]{3,2,1,0:T(8,128)} custom-call(f32[32,8,8,128]{3,2,1,0:T(8,128)S(1)} %get-tuple-element.39.solved_in, f32[5,32,8,128]{3,2,1,0:T(8,128)S(1)} %get-tuple-element.31.rates_ref, f32[320,128]{1,0:T(8,128)S(1)} %collective-permute-done.5.mate_in, f32[320,128]{1,0:T(8,128)S(1)} %collective-permute-done.6.far_in, ...), custom_call_target="tpu_custom_call" | custom-call | flops 4000000 | bytes 3000000 | tf_op jit(solution)/shard_map/child_last/pallas_call | solution.py:21
  39.9 0.7 %collective-permute-done.12.mate_cols = f32[8,128]{1,0:T(8,128)S(1)} collective-permute-done((f32[8,128]{1,0:T(8,128)S(1)}, f32[8,128]{1,0:T(8,128)S(1)}, u32[]{:S(2)}, u32[]{:S(2)}) %collective-permute-start.12) | collective-permute-done | bytes 4128 | tf_op jit(solution)/shard_map/ppermute | solution.py:449
  40.5 1.0 %parent_last.1 = f32[512,32]{1,0:T(8,128)} custom-call(f32[16,8,128]{2,1,0:T(8,128)S(1)} %get-tuple-element.46.psolved_in, f32[5,16,128]{2,1,0:T(8,128)S(1)} %get-tuple-element.44.prates_ref, f32[64,128]{1,0:T(8,128)S(1)} %collective-permute-done.10.mate_in, f32[64,128]{1,0:T(8,128)S(1)} %collective-permute-done.11.far_in, ...), custom_call_target="tpu_custom_call" | custom-call | flops 500000 | bytes 500000 | tf_op jit(solution)/shard_map/parent_last/pallas_call | solution.py:21
  (30 shorter events, 0.6 us)
Async XLA Ops:
  0.6 1.2 %copy-start = (f32[32,8,8,128]{3,2,1,0:T(8,128)S(1)}, f32[32,8,8,128]{3,2,1,0:T(8,128)}, u32[]{:S(2)}) copy-start(f32[32,8,8,128]{3,2,1,0:T(8,128)} %x_hbm.1) | copy-start | bytes 3145732
  1.9 0.9 %copy-start.3 = (f32[32,8,128]{2,1,0:T(8,128)S(1)}, f32[32,8,128]{2,1,0:T(8,128)}, u32[]{:S(2)}) copy-start(f32[32,8,128]{2,1,0:T(8,128)} %mix_hbm.1) | copy-start | bytes 393220
  2.8 0.7 %copy-start.6 = (f32[8,128]{1,0:T(8,128)S(1)}, f32[8,128]{1,0:T(8,128)}, u32[]{:S(2)}) copy-start(f32[8,128]{1,0:T(8,128)} %relax_ref.1) | copy-start | bytes 12292
  3.4 11.6 %copy-start.1 = (f32[4,32,8,128]{3,2,1,0:T(8,128)S(1)}, f32[4,32,8,128]{3,2,1,0:T(8,128)}, u32[]{:S(2)}) copy-start(f32[4,32,8,128]{3,2,1,0:T(8,128)} %child_rates_ref.1) | copy-start | bytes 1572868
  3.5 11.6 %copy-start.2 = (f32[32,8,2,32]{3,2,1,0:T(2,128)S(1)}, f32[32,8,2,32]{3,2,1,0:T(2,128)}, u32[]{:S(2)}) copy-start(f32[32,8,2,32]{3,2,1,0:T(2,128)} %param.10) | copy-start | bytes 196612
  3.5 11.6 %copy-start.4 = (f32[4,32,2,32]{3,2,1,0:T(2,128)S(1)}, f32[4,32,2,32]{3,2,1,0:T(2,128)}, u32[]{:S(2)}) copy-start(f32[4,32,2,32]{3,2,1,0:T(2,128)} %param.14) | copy-start | bytes 98308
  3.5 11.6 %copy-start.5 = (f32[32,2,32]{2,1,0:T(2,128)S(1)}, f32[32,2,32]{2,1,0:T(2,128)}, u32[]{:S(2)}) copy-start(f32[32,2,32]{2,1,0:T(2,128)} %param.15) | copy-start | bytes 24580
  6.8 11.4 %collective-permute-start = (f32[256,128]{1,0:T(8,128)S(1)}, f32[256,128]{1,0:T(8,128)S(1)}, u32[]{:S(2)}, u32[]{:S(2)}) collective-permute-start(f32[256,128]{1,0:T(8,128)S(1)} %get-tuple-element.32), channel_id=1, source_target_pairs={{0,1},{1,0},{2,3},{3,2},{4,5},{5,4},{6,7},{7,6},{8,9},{9,8},{10,11... | collective-permute-start | bytes 393224 | tf_op jit(solution)/shard_map/ppermute | solution.py:449
  7.4 10.9 %collective-permute-start.1 = (f32[256,128]{1,0:T(8,128)S(1)}, f32[256,128]{1,0:T(8,128)S(1)}, u32[]{:S(2)}, u32[]{:S(2)}) collective-permute-start(f32[256,128]{1,0:T(8,128)S(1)} %get-tuple-element.33), channel_id=1, source_target_pairs={{1,2},{2,1},{3,4},{4,3},{5,6},{6,5},{7,0},{0,7},{9,10},{10,9},{11,... | collective-permute-start | bytes 393224 | tf_op jit(solution)/shard_map/ppermute | solution.py:449
  12.1 3.0 %copy-start.8 = (s32[8,128]{1,0:T(8,128)S(1)}, s32[8,128]{1,0:T(8,128)}, u32[]{:S(2)}) copy-start(s32[8,128]{1,0:T(8,128)} %child_land_ref.1) | copy-start | bytes 12292
  12.1 6.2 %collective-permute-start.4 = (f32[128,128]{1,0:T(8,128)S(1)}, f32[128,128]{1,0:T(8,128)S(1)}, u32[]{:S(2)}, u32[]{:S(2)}) collective-permute-start(f32[128,128]{1,0:T(8,128)S(1)} %get-tuple-element.38), channel_id=1, source_target_pairs={{0,2},{1,3},{2,4},{3,5},{4,6},{5,7},{6,0},{7,1},{8,10},{9,11},{10,... | collective-permute-start | bytes 196616 | tf_op jit(solution)/shard_map/ppermute | solution.py:440
  12.1 5.3 %collective-permute-start.3 = (f32[32,128]{1,0:T(8,128)S(1)}, f32[32,128]{1,0:T(8,128)S(1)}, u32[]{:S(2)}, u32[]{:S(2)}) collective-permute-start(f32[32,128]{1,0:T(8,128)S(1)} %get-tuple-element.30.after_ref), channel_id=1, source_target_pairs={{8,16},{16,8},{24,0},{0,24},{9,17},{17,9},{25,1},{1,25},{10,18},{1... | collective-permute-start | bytes 49160 | tf_op jit(solution)/shard_map/ppermute | solution.py:449
  14.5 3.7 %collective-permute-start.2 = (f32[32,128]{1,0:T(8,128)S(1)}, f32[32,128]{1,0:T(8,128)S(1)}, u32[]{:S(2)}, u32[]{:S(2)}) collective-permute-start(f32[32,128]{1,0:T(8,128)S(1)} %get-tuple-element.30.after_ref), channel_id=1, source_target_pairs={{0,8},{8,0},{16,24},{24,16},{1,9},{9,1},{17,25},{25,17},{2,10},{10... | collective-permute-start | bytes 49160 | tf_op jit(solution)/shard_map/ppermute | solution.py:449
  15.1 0.7 %copy-start.9 = (s32[2,32]{1,0:T(2,128)S(1)}, s32[2,32]{1,0:T(2,128)}, u32[]{:S(2)}) copy-start(s32[2,32]{1,0:T(2,128)} %land_ref.1) | copy-start | bytes 772
  18.3 0.7 %copy-start.7 = (f32[8,128]{1,0:T(8,128)S(1)}, f32[8,128]{1,0:T(8,128)}, u32[]{:S(2)}) copy-start(f32[8,128]{1,0:T(8,128)} %relax_ref.1) | copy-start | bytes 12292
  21.8 10.2 %collective-permute-start.5 = (f32[320,128]{1,0:T(8,128)S(1)}, f32[320,128]{1,0:T(8,128)S(1)}, u32[]{:S(2)}, u32[]{:S(2)}) collective-permute-start(f32[320,128]{1,0:T(8,128)S(1)} %get-tuple-element.40), channel_id=1, source_target_pairs={{0,1},{1,0},{2,3},{3,2},{4,5},{5,4},{6,7},{7,6},{8,9},{9,8},{10,11... | collective-permute-start | bytes 491528 | tf_op jit(solution)/shard_map/ppermute | solution.py:449
  21.9 10.1 %collective-permute-start.6 = (f32[320,128]{1,0:T(8,128)S(1)}, f32[320,128]{1,0:T(8,128)S(1)}, u32[]{:S(2)}, u32[]{:S(2)}) collective-permute-start(f32[320,128]{1,0:T(8,128)S(1)} %get-tuple-element.41), channel_id=1, source_target_pairs={{1,2},{2,1},{3,4},{4,3},{5,6},{6,5},{7,0},{0,7},{9,10},{10,9},{11,... | collective-permute-start | bytes 491528 | tf_op jit(solution)/shard_map/ppermute | solution.py:449
  25.8 6.2 %collective-permute-start.9 = (f32[128,128]{1,0:T(8,128)S(1)}, f32[128,128]{1,0:T(8,128)S(1)}, u32[]{:S(2)}, u32[]{:S(2)}) collective-permute-start(f32[128,128]{1,0:T(8,128)S(1)} %get-tuple-element.45), channel_id=1, source_target_pairs={{0,2},{1,3},{2,4},{3,5},{4,6},{5,7},{6,0},{7,1},{8,10},{9,11},{10,... | collective-permute-start | bytes 196616 | tf_op jit(solution)/shard_map/ppermute | solution.py:440
  25.8 4.7 %collective-permute-start.8 = (f32[40,128]{1,0:T(8,128)S(1)}, f32[40,128]{1,0:T(8,128)S(1)}, u32[]{:S(2)}, u32[]{:S(2)}) collective-permute-start(f32[40,128]{1,0:T(8,128)S(1)} %get-tuple-element.42), channel_id=1, source_target_pairs={{8,16},{16,8},{24,0},{0,24},{9,17},{17,9},{25,1},{1,25},{10,18},{1... | collective-permute-start | bytes 61448 | tf_op jit(solution)/shard_map/ppermute | solution.py:449
  26.7 3.8 %collective-permute-start.7 = (f32[40,128]{1,0:T(8,128)S(1)}, f32[40,128]{1,0:T(8,128)S(1)}, u32[]{:S(2)}, u32[]{:S(2)}) collective-permute-start(f32[40,128]{1,0:T(8,128)S(1)} %get-tuple-element.42), channel_id=1, source_target_pairs={{0,8},{8,0},{16,24},{24,16},{1,9},{9,1},{17,25},{25,17},{2,10},{10... | collective-permute-start | bytes 61448 | tf_op jit(solution)/shard_map/ppermute | solution.py:449
  32.4 8.2 %collective-permute-start.10 = (f32[64,128]{1,0:T(8,128)S(1)}, f32[64,128]{1,0:T(8,128)S(1)}, u32[]{:S(2)}, u32[]{:S(2)}) collective-permute-start(f32[64,128]{1,0:T(8,128)S(1)} %get-tuple-element.47), channel_id=1, source_target_pairs={{0,1},{1,0},{2,3},{3,2},{4,5},{5,4},{6,7},{7,6},{8,9},{9,8},{10,11... | collective-permute-start | bytes 98312 | tf_op jit(solution)/shard_map/ppermute | solution.py:449
  32.5 8.1 %collective-permute-start.11 = (f32[64,128]{1,0:T(8,128)S(1)}, f32[64,128]{1,0:T(8,128)S(1)}, u32[]{:S(2)}, u32[]{:S(2)}) collective-permute-start(f32[64,128]{1,0:T(8,128)S(1)} %get-tuple-element.48), channel_id=1, source_target_pairs={{1,2},{2,1},{3,4},{4,3},{5,6},{6,5},{7,0},{0,7},{9,10},{10,9},{11,... | collective-permute-start | bytes 98312 | tf_op jit(solution)/shard_map/ppermute | solution.py:449
  34.9 4.9 %collective-permute-start.13 = (f32[8,128]{1,0:T(8,128)S(1)}, f32[8,128]{1,0:T(8,128)S(1)}, u32[]{:S(2)}, u32[]{:S(2)}) collective-permute-start(f32[8,128]{1,0:T(8,128)S(1)} %get-tuple-element.49), channel_id=1, source_target_pairs={{8,16},{16,8},{24,0},{0,24},{9,17},{17,9},{25,1},{1,25},{10,18},{1... | collective-permute-start | bytes 12296 | tf_op jit(solution)/shard_map/ppermute | solution.py:449
  36.9 3.6 %collective-permute-start.12 = (f32[8,128]{1,0:T(8,128)S(1)}, f32[8,128]{1,0:T(8,128)S(1)}, u32[]{:S(2)}, u32[]{:S(2)}) collective-permute-start(f32[8,128]{1,0:T(8,128)S(1)} %get-tuple-element.49), channel_id=1, source_target_pairs={{0,8},{8,0},{16,24},{24,16},{1,9},{9,1},{17,25},{25,17},{2,10},{10... | collective-permute-start | bytes 12296 | tf_op jit(solution)/shard_map/ppermute | solution.py:449

commit v4 on v3

--- a/solution.py
+++ b/solution.py
@@ -18,6 +18,7 @@
 
 
 def call(body, outs, scratch, operands, flops, touched, far_in=(), far_out=False):
+    operands = [pltpu.with_memory_space_constraint(x, pltpu.HBM) if i in far_in else x for i, x in enumerate(operands)]
     return pl.pallas_call(
         body,
         out_shape=outs,
@@ -150,49 +151,65 @@
         state = state[: 2 * vectors] + (blank,) * 2
 
 
-def child_first(
-    x_hbm, mix_hbm, relax_hbm,
-    sums_out, solved_ref, mate_rows, far_rows, cols_ref, a_ref, b_ref, c_ref,
-    x_ref, mix_ref, relax_ref, sums_ref, sems,
+def begin(
+    x_hbm, mix_hbm, relax_hbm, land_hbm, parent_land_hbm,
+    sums_out, x_ref, a_ref, b_ref, c_ref, relax_ref, land_ref, parent_land_ref,
+    mix_ref, land_in, parent_land_in, sums_ref, sems,
 ):
-    depth, vectors = x_ref.shape[0], x_ref.shape[1]
+    depth = x_ref.shape[0]
     half = depth // 2
-    small = [
-        pltpu.make_async_copy(mix_hbm, mix_ref, sems.at[0]),
-        pltpu.make_async_copy(relax_hbm, relax_ref, sems.at[1]),
-    ]
-    for copy in small:
-        copy.start()
+    small = []
+    for source, target in (
+        (mix_hbm, mix_ref), (relax_hbm, relax_ref), (land_hbm, land_in), (parent_land_hbm, parent_land_in),
+    ):
+        small.append(pltpu.make_async_copy(source, target, sems.at[len(small)]))
+        small[-1].start()
     size, large = 4, []
     for start in range(0, half, size):
         for first in (start, depth - size - start):
             part = pl.ds(first, size)
-            large.append(pltpu.make_async_copy(x_hbm.at[part], x_ref.at[part], sems.at[len(large) + 2]))
+            large.append(pltpu.make_async_copy(x_hbm.at[part], x_ref.at[part], sems.at[len(large) + len(small)]))
             large[-1].start()
     for copy in small:
         copy.wait()
+    land_ref[...] = land_in[...].astype(F32)
+    parent_land_ref[...] = parent_land_in[...].astype(F32)
     child_factors(mix_ref, 1.0 - relax_ref[...], a_ref, b_ref, c_ref)
     weights = [relax_ref[j : j + 1, :] for j in range(8)]
 
+    def level(i, _):
+        for side, k in ((0, i), (1, depth - 1 - i)):
+            block_rows(x_ref, k, weights, sums_ref, i, side)
+        return 0
+
+    for part, start in enumerate(range(0, half, size)):
+        large[2 * part].wait()
+        large[2 * part + 1].wait()
+        lax.fori_loop(start, start + size, level, 0, unroll=size)
+    sums_out[...] = block_columns(sums_ref)
+
+
+def child_first(x_ref, a_ref, b_ref, c_ref, solved_ref, mate_rows, far_rows, cols_ref):
+    depth, vectors = x_ref.shape[0], x_ref.shape[1]
+    half = depth // 2
+
     def down(i, carry):
-        k_low = depth - 1 - i
         values = []
-        for side, k in ((0, i), (1, k_low)):
+        for side, k in ((0, i), (1, depth - 1 - i)):
             a, b = a_ref[k], b_ref[k]
             for v in range(vectors):
                 y = a * x_ref[k, v] + b * carry[side * vectors + v]
                 solved_ref[k, v] = y
                 values.append(y)
-            block_rows(x_ref, k, weights, sums_ref, i, side)
         return tuple(values)
 
-    carry = (jnp.zeros((8, LANES), F32),) * (2 * vectors)
-    for part, start in enumerate(range(0, half, size)):
-        large[2 * part].wait()
-        large[2 * part + 1].wait()
-        carry = lax.fori_loop(start, start + size, down, carry, unroll=size)
-    sums_out[...] = block_columns(sums_ref)
+    carry = lax.fori_loop(0, half, down, (jnp.zeros((8, LANES), F32),) * (2 * vectors), unroll=4)
     child_up(carry, c_ref, solved_ref, mate_rows, far_rows, cols_ref)
+
+
+def combine(sides, land):
+    east, west, north, south = sides
+    return [land * part for part in (1.0 - (east + west + north + south), east, west, north, south)]
 
 
 def merge_edges(mate, far, turn):
@@ -232,7 +249,7 @@
 
 
 def child_second(
-    solved_in, a_ref, b_ref, c_ref, rates_ref, relax_ref, mate_in, far_in, mate_cols, far_cols,
+    solved_in, a_ref, b_ref, c_ref, rates_ref, land_ref, relax_ref, mate_in, far_in, mate_cols, far_cols,
     parent_ref, pa_ref, pb_ref, pc_ref, feed_ref,
     sums_out, solved_ref, psolved_ref, mate_rows, far_rows, cols_ref,
     x_ref, sums_ref, north_ref, south_ref, merged_ref,
@@ -242,6 +259,7 @@
     groups = depth // LEVELS
     lane, row = lane_index(), row_index()
     weights = [relax_ref[j : j + 1, :] for j in range(8)]
+    land = land_ref[...]
     child_halos(mate_in, far_in, north_ref, south_ref, mate_cols, far_cols, merged_ref)
 
     def down(i, carry, edges):
@@ -250,7 +268,7 @@
         values = []
         for side, k, base in ((0, i, inside * vectors), (1, k_low, (LEVELS - 1 - inside) * vectors)):
             a, b = a_ref[k], b_ref[k]
-            rates = [rates_ref[d, k] for d in range(5)]
+            rates = combine([rates_ref[d, k] for d in range(4)], land)
             for v in range(vectors):
                 x = child_cell(solved_in, k, v, base, edges[side], rates, north_ref, south_ref, lane, row)
                 x_ref[k, v] = x
@@ -275,10 +293,11 @@
 
 
 def child_last(
-    solved_in, rates_ref, mate_in, far_in, mate_cols, far_cols, out_hbm, out_ref, north_ref, south_ref, merged_ref, sems
+    solved_in, rates_ref, land_ref, mate_in, far_in, mate_cols, far_cols, out_hbm, out_ref, north_ref, south_ref, merged_ref, sems
 ):
     depth, vectors = solved_in.shape[0], solved_in.shape[1]
     lane, row = lane_index(), row_index()
+    land = land_ref[...]
     child_halos(mate_in, far_in, north_ref, south_ref, mate_cols, far_cols, merged_ref)
     copies = []
     for group in range(depth // LEVELS):
@@ -286,7 +305,7 @@
 
         def level(inside, _):
             k = LEVELS * group + inside
-            rates = [rates_ref[d, k] for d in range(5)]
+            rates = combine([rates_ref[d, k] for d in range(4)], land)
             for v in range(vectors):
                 out_ref[k, v] = child_cell(
                     solved_in, k, v, inside * vectors, edges, rates, north_ref, south_ref, lane, row
@@ -301,31 +320,16 @@
         copy.wait()
 
 
-def prepare(
-    parent_ref, rates_ref, mix_ref, land_ref, child_rates_ref, child_land_ref, after_ref,
-    packed_ref, prates_ref, pa_ref, pb_ref, pc_ref, child_out_ref, mixed,
-):
-    depth = child_rates_ref.shape[1]
-    vectors = packed_ref.shape[1]
-    half = depth // 2
-    places = [(h, r, 64 * h + 32 * r) for h in range(2) for r in range(2)]
-    land = jnp.concatenate([land_ref[r : r + 1, :] for _ in range(2) for r in range(2)], axis=1).astype(F32)
-
-    def level(i, _):
-        for h, r, lo in places:
+PLACES = [(h, r, 64 * h + 32 * r) for h in range(2) for r in range(2)]
+
+
+def parent_begin(parent_ref, mix_ref, after_ref, packed_ref, pa_ref, pb_ref, pc_ref, mixed):
+    half, vectors = packed_ref.shape[0], packed_ref.shape[1]
+    depth = 2 * half
+    for i in range(half):
+        for h, r, lo in PLACES:
             k = depth - 1 - i if h else i
-            packed_ref[i, :, lo : lo + 32] = parent_ref[pl.ds(2 * vectors * k + r, vectors, stride=2), :]
-            mixed[pl.ds(i, 1), lo : lo + 32] = mix_ref[pl.ds(2 * k + r, 1), :]
-            for d in range(4):
-                prates_ref[d + 1, pl.ds(i, 1), lo : lo + 32] = rates_ref[pl.ds(2 * (d * depth + k) + r, 1), :]
-        return 0
-
-    lax.fori_loop(0, half, level, 0)
-    land = jnp.broadcast_to(land, (half, LANES))
-    sides = [prates_ref[d] for d in range(1, 5)]
-    prates_ref[0] = land * (1.0 - (sides[0] + sides[1] + sides[2] + sides[3]))
-    for d in range(4):
-        prates_ref[d + 1] = land * sides[d]
+            mixed[i : i + 1, lo : lo + 32] = mix_ref[2 * k + r : 2 * k + r + 1, :]
     upper = lane_index(1) < 64
     rows = [mixed[i : i + 1, :] for i in range(half)]
     inner, outer = [], []
@@ -338,16 +342,24 @@
         pa_ref[i : i + 1, :] = inverse[i]
         pb_ref[i : i + 1, :] = inverse[i] * outer[i]
         pc_ref[i : i + 1, :] = inverse[i] * inner[i]
-    child_land = child_land_ref[...].astype(F32)
-
-    def child_level(k, _):
-        sides = [child_rates_ref[d, k] for d in range(4)]
-        child_out_ref[0, k] = child_land * (1.0 - (sides[0] + sides[1] + sides[2] + sides[3]))
-        for d in range(4):
-            child_out_ref[d + 1, k] = child_land * sides[d]
-        return 0
-
-    lax.fori_loop(0, depth, child_level, 0, unroll=4)
+        for h, r, lo in PLACES:
+            k = depth - 1 - i if h else i
+            packed_ref[i, :, lo : lo + 32] = parent_ref[pl.ds(2 * vectors * k + r, vectors, stride=2), :]
+
+
+def parent_rates_packed(rates_ref, land_ref, after_ref, prates_ref):
+    half = prates_ref.shape[1]
+    depth = 2 * half
+    for i in range(half):
+        for h, r, lo in PLACES:
+            k = depth - 1 - i if h else i
+            for d in range(4):
+                at = 2 * (d * depth + k) + r
+                prates_ref[d + 1, i : i + 1, lo : lo + 32] = rates_ref[at : at + 1, :]
+    land = jnp.concatenate([land_ref[r : r + 1, :] for _, r, _ in PLACES], axis=1)
+    land = jnp.broadcast_to(land, (half, LANES))
+    for d, part in enumerate(combine([prates_ref[d] for d in range(1, 5)], land)):
+        prates_ref[d] = part
 
 
 def parent_up(carry, pc_ref, psolved_ref, mate_rows, far_rows, lines, cols_ref, cols_at):
@@ -477,50 +489,58 @@
     halo_scratch = [pltpu.VMEM((count, LANES), F32), pltpu.VMEM((count, LANES), F32), pltpu.VMEM((edge, LANES), F32)]
     narrow = parent_adjoint.shape[-1]
 
-    sums1, solved, mate, far, cols, a, b, c = call(
-        child_first,
-        [sums, field, shape(count, LANES), shape(count, LANES), shape(edge, LANES), factor, factor, factor],
+    sums1, x, a, b, c, relax, land, parent_land = call(
+        begin,
+        [sums, field, factor, factor, factor, shape(lines, columns), shape(lines, columns), shape(*parent_land.shape)],
         [
-            pltpu.VMEM(field.shape, F32),
             pltpu.VMEM(factor.shape, F32),
-            pltpu.VMEM((lines, columns), F32),
+            pltpu.VMEM(child_land.shape, jnp.int32),
+            pltpu.VMEM(parent_land.shape, jnp.int32),
             sum_scratch,
-            pltpu.SemaphoreType.DMA((2 + half // 2,)),
+            pltpu.SemaphoreType.DMA((4 + half // 2,)),
         ],
-        [child_adjoint, child_mixing, relaxation],
+        [child_adjoint, child_mixing, relaxation, child_land, parent_land],
         4_000_000,
         3_000_000,
-        far_in=(0, 1, 2),
+        far_in=range(5),
+    )
+    feed = passed_along(sums1, "gy", quarter)
+    solved, mate, far, cols = call(
+        child_first,
+        [field, shape(count, LANES), shape(count, LANES), shape(edge, LANES)],
+        [],
+        [x, a, b, c],
+        4_000_000,
+        3_000_000,
     )
     halos = halos_of(mate, far, cols)
-    feed = passed_along(sums1, "gy", quarter)
-    packed, prates, pa, pb, pc, rates = call(
-        prepare,
-        [tiles, shape(5, half, LANES)] + [shape(half, LANES)] * 3 + [shape(5, depth, lines, columns)],
+    packed, pa, pb, pc = call(
+        parent_begin,
+        [tiles] + [shape(half, LANES)] * 3,
         [pltpu.VMEM((half, LANES), F32)],
-        [
-            parent_adjoint.reshape(-1, narrow),
-            parent_rates.reshape(-1, narrow),
-            parent_mixing.reshape(-1, narrow),
-            parent_land,
-            child_rates,
-            child_land,
-            cols,
-        ],
+        [parent_adjoint.reshape(-1, narrow), parent_mixing.reshape(-1, narrow), cols],
+        500_000,
         1_000_000,
-        3_000_000,
     )
     rows = count + half // 2 * vectors
     sums2, solved, psolved, mate, far, cols = call(
         child_second,
         [sums, field, tiles, shape(rows, LANES), shape(rows, LANES), shape(edge + 8, LANES)],
         [pltpu.VMEM(field.shape, F32), sum_scratch] + halo_scratch,
-        [solved, a, b, c, rates, relaxation, *halos, packed, pa, pb, pc, feed],
+        [solved, a, b, c, child_rates, land, relax, *halos, packed, pa, pb, pc, feed],
         8_000_000,
         3_000_000,
     )
     halos = halos_of(mate, far, cols)
     feed = passed_along(sums2, "gy", quarter)
+    prates = call(
+        parent_rates_packed,
+        shape(5, half, LANES),
+        [],
+        [parent_rates.reshape(-1, narrow), parent_land, cols],
+        500_000,
+        1_000_000,
+    )
     few = half // 2 * vectors
     psolved, mate, far, cols = call(
         parent_second,
@@ -535,7 +555,7 @@
         child_last,
         field,
         [pltpu.VMEM(field.shape, F32)] + halo_scratch + [pltpu.SemaphoreType.DMA((depth // LEVELS,))],
-        [solved, rates, *halos],
+        [solved, child_rates, land, *halos],
         4_000_000,
         3_000_000,
         far_out=True,

time: 41.8 us -> 37.9 us (0.907)
  local copies, waits for them, and re-layouts: 4.16 us -> 0.03 us
  waiting for transfers between devices: 5.72 us -> 7.74 us
  Pallas kernels: 11.5 us -> 10 us
    unnamed x20 -> x8, local copies, waits for them, and re-layouts: 4.16 us -> 0.03 us
    ppermute x12, waiting for transfers between devices: 4.26 us -> 6.27 us  [swapped(): return lax.ppermute(value, axis, pairs)]
    pallas_call x6 -> x8, Pallas kernels: 11.5 us -> 10 us  [call(): pl.pallas_call(body, out_shape=outs, in_specs=[FAR if i in far_in else VM...]
  transfers between devices with their start and end apart: 14 -> 14, of which waited for: 4 -> 5; matrix products, arithmetic and copies ran while one was open for 0% -> 0% of each run, Pallas kernels for 9% -> 7%
where the time goes in v4:
time: 37.9 us; the launch traced here: 37.8 us
  starting transfers between devices  19.3 us (51%)
  Pallas kernels  10 us (26%)
  waiting for transfers between devices  7.74 us (20%)
  between operations  0.76 us (2%)
    ppermute x12, starting transfers between devices, swapped(): return lax.ppermute(value, axis, pairs)  19.3 us
    pallas_call x8, Pallas kernels, call(): pl.pallas_call(body, out_shape=outs, in_specs=[FAR if i in far_in else VM...  10 us
    ppermute x12, waiting for transfers between devices, swapped(): return lax.ppermute(value, axis, pairs)  6.27 us
    ppermute x2, waiting for transfers between devices, passed_along(): lax.ppermute(value, axis, [(i, (i + steps) % count) for i in range(count)])  1.47 us
  transfers between devices with their start and end apart: 14, of which 5 were waited for; matrix products, arithmetic and copies ran while one was open for 0% of the time, Pallas kernels for 7%

profile of v4, /device:TPU:0, one launch (start us, length us, event | category | flops | bytes accessed | tf_op | source)
XLA Modules:
  0.0 37.8 jit_solution(12489836324380109297)
XLA Ops:
  0.6 2.2 %begin.1 = (f32[128,128]{1,0:T(8,128)S(1)}, f32[32,8,8,128]{3,2,1,0:T(8,128)S(1)}, f32[32,8,128]{2,1,0:T(8,128)S(1)}, f32[32,8,128]{2,1,0:T(8,128)S(1)}, f32[32,...) custom-call(f32[32,8,8,128]{3,2,1,0:T(8,128)} %x_hbm.1, ...), custom_call_target="tpu_custom_call" | custom-call | flops 4000000 | bytes 3000000 | tf_op jit(solution)/shard_map/begin/pallas_call | solution.py:22
  2.9 0.8 %child_first.1 = (f32[32,8,8,128]{3,2,1,0:T(8,128)S(1)}, f32[256,128]{1,0:T(8,128)S(1)}, f32[256,128]{1,0:T(8,128)S(1)}, f32[32,128]{1,0:T(8,128)S(1)}) custom-call(f32[32,8,8,128]{3,2,1,0:T(8,128)S(1)} %get-tuple-element.28.x_ref, f32[32,8,128]{2,1,0:T(8,128)S(1)} %get-tuple-element.29.a_ref, f32[32,8,128]{2,1,0:T(8,128)S(1)} %get-tuple-element.30.b_ref, ...), custom_call_target="tpu_custom_call" | custom-call | flops 4000000 | bytes 3000000 | tf_op jit(solution)/shard_map/child_first/pallas_call | solution.py:22
  3.7 0.5 %collective-permute-start = (f32[256,128]{1,0:T(8,128)S(1)}, f32[256,128]{1,0:T(8,128)S(1)}, u32[]{:S(2)}, u32[]{:S(2)}) collective-permute-start(f32[256,128]{1,0:T(8,128)S(1)} %get-tuple-element.35), channel_id=1, source_target_pairs={{0,1},{1,0},{2,3},{3,2},{4,5},{5,4},{6,7},{7,6},{8,9},{9,8},{10,11... | collective-permute-start | bytes 393224 | tf_op jit(solution)/shard_map/ppermute | solution.py:461
  4.2 4.7 %collective-permute-start.1 = (f32[256,128]{1,0:T(8,128)S(1)}, f32[256,128]{1,0:T(8,128)S(1)}, u32[]{:S(2)}, u32[]{:S(2)}) collective-permute-start(f32[256,128]{1,0:T(8,128)S(1)} %get-tuple-element.36), channel_id=1, source_target_pairs={{1,2},{2,1},{3,4},{4,3},{5,6},{6,5},{7,0},{0,7},{9,10},{10,9},{11,... | collective-permute-start | bytes 393224 | tf_op jit(solution)/shard_map/ppermute | solution.py:461
  9.0 2.4 %collective-permute-start.3 = (f32[32,128]{1,0:T(8,128)S(1)}, f32[32,128]{1,0:T(8,128)S(1)}, u32[]{:S(2)}, u32[]{:S(2)}) collective-permute-start(f32[32,128]{1,0:T(8,128)S(1)} %get-tuple-element.37.after_ref), channel_id=1, source_target_pairs={{8,16},{16,8},{24,0},{0,24},{9,17},{17,9},{25,1},{1,25},{10,18},{1... | collective-permute-start | bytes 49160 | tf_op jit(solution)/shard_map/ppermute | solution.py:461
  11.4 0.5 %collective-permute-start.2 = (f32[32,128]{1,0:T(8,128)S(1)}, f32[32,128]{1,0:T(8,128)S(1)}, u32[]{:S(2)}, u32[]{:S(2)}) collective-permute-start(f32[32,128]{1,0:T(8,128)S(1)} %get-tuple-element.37.after_ref), channel_id=1, source_target_pairs={{0,8},{8,0},{16,24},{24,16},{1,9},{9,1},{17,25},{25,17},{2,10},{10... | collective-permute-start | bytes 49160 | tf_op jit(solution)/shard_map/ppermute | solution.py:461
  11.9 0.2 parent_begin.1
  12.1 1.4 %collective-permute-done.3.far_cols = f32[32,128]{1,0:T(8,128)S(1)} collective-permute-done((f32[32,128]{1,0:T(8,128)S(1)}, f32[32,128]{1,0:T(8,128)S(1)}, u32[]{:S(2)}, u32[]{:S(2)}) %collective-permute-start.3) | collective-permute-done | bytes 16416 | tf_op jit(solution)/shard_map/ppermute | solution.py:461
  13.6 1.5 %collective-permute-done.2.mate_cols = f32[32,128]{1,0:T(8,128)S(1)} collective-permute-done((f32[32,128]{1,0:T(8,128)S(1)}, f32[32,128]{1,0:T(8,128)S(1)}, u32[]{:S(2)}, u32[]{:S(2)}) %collective-permute-start.2) | collective-permute-done | bytes 16416 | tf_op jit(solution)/shard_map/ppermute | solution.py:461
  15.2 2.9 %child_second.1 = (f32[128,128]{1,0:T(8,128)S(1)}, f32[32,8,8,128]{3,2,1,0:T(8,128)S(1)}, f32[16,8,128]{2,1,0:T(8,128)S(1)}, f32[320,128]{1,0:T(8,128)S(1)}, f32...) custom-call(f32[32,8,8,128]{3,2,1,0:T(8,128)S(1)} %get-tuple-element.32.solved_in, f32[32,8,128]{2,1,0:T(8,128)S(1)} %get-tuple-element.29.a_ref, ...), custom_call_target="tpu_custom_call" | custom-call | flops 8000000 | bytes 3000000 | tf_op jit(solution)/shard_map/child_second/pallas_call | solution.py:22
  18.1 0.1 collective-permute-start.5
  18.2 3.9 %collective-permute-start.6 = (f32[320,128]{1,0:T(8,128)S(1)}, f32[320,128]{1,0:T(8,128)S(1)}, u32[]{:S(2)}, u32[]{:S(2)}) collective-permute-start(f32[320,128]{1,0:T(8,128)S(1)} %get-tuple-element.45), channel_id=1, source_target_pairs={{1,2},{2,1},{3,4},{4,3},{5,6},{6,5},{7,0},{0,7},{9,10},{10,9},{11,... | collective-permute-start | bytes 491528 | tf_op jit(solution)/shard_map/ppermute | solution.py:461
  22.1 0.9 %collective-permute-start.8 = (f32[40,128]{1,0:T(8,128)S(1)}, f32[40,128]{1,0:T(8,128)S(1)}, u32[]{:S(2)}, u32[]{:S(2)}) collective-permute-start(f32[40,128]{1,0:T(8,128)S(1)} %get-tuple-element.46.after_ref), channel_id=1, source_target_pairs={{8,16},{16,8},{24,0},{0,24},{9,17},{17,9},{25,1},{1,25},{10,18},{1... | collective-permute-start | bytes 61448 | tf_op jit(solution)/shard_map/ppermute | solution.py:461
  23.0 1.1 %collective-permute-start.7 = (f32[40,128]{1,0:T(8,128)S(1)}, f32[40,128]{1,0:T(8,128)S(1)}, u32[]{:S(2)}, u32[]{:S(2)}) collective-permute-start(f32[40,128]{1,0:T(8,128)S(1)} %get-tuple-element.46.after_ref), channel_id=1, source_target_pairs={{0,8},{8,0},{16,24},{24,16},{1,9},{9,1},{17,25},{25,17},{2,10},{10... | collective-permute-start | bytes 61448 | tf_op jit(solution)/shard_map/ppermute | solution.py:461
  24.1 0.3 parent_rates_packed.1.prates_ref
  24.3 2.4 %collective-permute-done.8.far_cols = f32[40,128]{1,0:T(8,128)S(1)} collective-permute-done((f32[40,128]{1,0:T(8,128)S(1)}, f32[40,128]{1,0:T(8,128)S(1)}, u32[]{:S(2)}, u32[]{:S(2)}) %collective-permute-start.8) | collective-permute-done | bytes 20512 | tf_op jit(solution)/shard_map/ppermute | solution.py:461
  26.8 1.5 %collective-permute-done.9.feed_ref = f32[128,128]{1,0:T(8,128)S(1)} collective-permute-done((f32[128,128]{1,0:T(8,128)S(1)}, f32[128,128]{1,0:T(8,128)S(1)}, u32[]{:S(2)}, u32[]{:S(2)}) %collective-permute-start.9) | collective-permute-done | bytes 65568 | tf_op jit(solution)/shard_map/ppermute | solution.py:452
  28.2 0.4 %parent_second.1 = (f32[16,8,128]{2,1,0:T(8,128)S(1)}, f32[64,128]{1,0:T(8,128)S(1)}, f32[64,128]{1,0:T(8,128)S(1)}, f32[8,128]{1,0:T(8,128)S(1)}) custom-call(f32[16,8,128]{2,1,0:T(8,128)S(1)} %get-tuple-element.47.psolved_in, f32[5,16,128]{2,1,0:T(8,128)S(1)} %parent_rates_packed.1.prates_ref, f32[16,128]{1,0:T(8,128)S(1)} %get-tuple-element.39.pa_ref, ...), custom_call_target="tpu_custom_call" | custom-call | flops 1000000 | bytes 500000 | tf_op jit(solution)/shard_map/parent_second/pallas_call | solution.py:22
  28.7 2.5 %collective-permute-start.11 = (f32[64,128]{1,0:T(8,128)S(1)}, f32[64,128]{1,0:T(8,128)S(1)}, u32[]{:S(2)}, u32[]{:S(2)}) collective-permute-start(f32[64,128]{1,0:T(8,128)S(1)} %get-tuple-element.52), channel_id=1, source_target_pairs={{1,2},{2,1},{3,4},{4,3},{5,6},{6,5},{7,0},{0,7},{9,10},{10,9},{11,... | collective-permute-start | bytes 98312 | tf_op jit(solution)/shard_map/ppermute | solution.py:461
  31.2 2.0 %collective-permute-start.13 = (f32[8,128]{1,0:T(8,128)S(1)}, f32[8,128]{1,0:T(8,128)S(1)}, u32[]{:S(2)}, u32[]{:S(2)}) collective-permute-start(f32[8,128]{1,0:T(8,128)S(1)} %get-tuple-element.53), channel_id=1, source_target_pairs={{8,16},{16,8},{24,0},{0,24},{9,17},{17,9},{25,1},{1,25},{10,18},{1... | collective-permute-start | bytes 12296 | tf_op jit(solution)/shard_map/ppermute | solution.py:461
  33.2 0.5 %collective-permute-start.12 = (f32[8,128]{1,0:T(8,128)S(1)}, f32[8,128]{1,0:T(8,128)S(1)}, u32[]{:S(2)}, u32[]{:S(2)}) collective-permute-start(f32[8,128]{1,0:T(8,128)S(1)} %get-tuple-element.53), channel_id=1, source_target_pairs={{0,8},{8,0},{16,24},{24,16},{1,9},{9,1},{17,25},{25,17},{2,10},{10... | collective-permute-start | bytes 12296 | tf_op jit(solution)/shard_map/ppermute | solution.py:461
  33.7 2.2 %child_last.1 = f32[32,8,8,128]{3,2,1,0:T(8,128)} custom-call(f32[32,8,8,128]{3,2,1,0:T(8,128)S(1)} %get-tuple-element.43.solved_in, f32[4,32,8,128]{3,2,1,0:T(8,128)S(1)} %copy-done, f32[8,128]{1,0:T(8,128)S(1)} %get-tuple-element.33.land_ref, f32[320,128]{1,0:T(8,128)S(1)} %collective-permute-done.5.mate_in, f32[320,128]{1,0:T(8,128)S(1)} %collective-permute-done.6.far_in, ...), custom_call_target="tpu_custom_call" | custom-call | flops 4000000 | bytes 3000000 | tf_op jit(solution)/shard_map/child_last/pallas_call | solution.py:22
  36.0 0.8 %collective-permute-done.12.mate_cols = f32[8,128]{1,0:T(8,128)S(1)} collective-permute-done((f32[8,128]{1,0:T(8,128)S(1)}, f32[8,128]{1,0:T(8,128)S(1)}, u32[]{:S(2)}, u32[]{:S(2)}) %collective-permute-start.12) | collective-permute-done | bytes 4128 | tf_op jit(solution)/shard_map/ppermute | solution.py:461
  36.8 1.0 %parent_last.1 = f32[512,32]{1,0:T(8,128)} custom-call(f32[16,8,128]{2,1,0:T(8,128)S(1)} %get-tuple-element.50.psolved_in, f32[5,16,128]{2,1,0:T(8,128)S(1)} %parent_rates_packed.1.prates_ref, f32[64,128]{1,0:T(8,128)S(1)} %collective-permute-done.10.mate_in, f32[64,128]{1,0:T(8,128)S(1)} %collective-permute-done.11.far_in, ...), custom_call_target="tpu_custom_call" | custom-call | flops 500000 | bytes 500000 | tf_op jit(solution)/shard_map/parent_last/pallas_call | solution.py:22
  (20 shorter events, 0.1 us)
Async XLA Ops:
  2.9 9.1 %copy-start.1 = (f32[32,8,2,32]{3,2,1,0:T(2,128)S(1)}, f32[32,8,2,32]{3,2,1,0:T(2,128)}, u32[]{:S(2)}) copy-start(f32[32,8,2,32]{3,2,1,0:T(2,128)} %param.10) | copy-start | bytes 196612
  2.9 9.1 %copy-start.3 = (f32[32,2,32]{2,1,0:T(2,128)S(1)}, f32[32,2,32]{2,1,0:T(2,128)}, u32[]{:S(2)}) copy-start(f32[32,2,32]{2,1,0:T(2,128)} %param.15) | copy-start | bytes 24580
  2.9 12.3 %copy-start = (f32[4,32,8,128]{3,2,1,0:T(8,128)S(1)}, f32[4,32,8,128]{3,2,1,0:T(8,128)}, u32[]{:S(2)}) copy-start(f32[4,32,8,128]{3,2,1,0:T(8,128)} %rates_ref.3) | copy-start | bytes 1572868
  3.7 11.4 %collective-permute-start = (f32[256,128]{1,0:T(8,128)S(1)}, f32[256,128]{1,0:T(8,128)S(1)}, u32[]{:S(2)}, u32[]{:S(2)}) collective-permute-start(f32[256,128]{1,0:T(8,128)S(1)} %get-tuple-element.35), channel_id=1, source_target_pairs={{0,1},{1,0},{2,3},{3,2},{4,5},{5,4},{6,7},{7,6},{8,9},{9,8},{10,11... | collective-permute-start | bytes 393224 | tf_op jit(solution)/shard_map/ppermute | solution.py:461
  4.2 10.9 %collective-permute-start.1 = (f32[256,128]{1,0:T(8,128)S(1)}, f32[256,128]{1,0:T(8,128)S(1)}, u32[]{:S(2)}, u32[]{:S(2)}) collective-permute-start(f32[256,128]{1,0:T(8,128)S(1)} %get-tuple-element.36), channel_id=1, source_target_pairs={{1,2},{2,1},{3,4},{4,3},{5,6},{6,5},{7,0},{0,7},{9,10},{10,9},{11,... | collective-permute-start | bytes 393224 | tf_op jit(solution)/shard_map/ppermute | solution.py:461
  9.0 6.2 %collective-permute-start.4 = (f32[128,128]{1,0:T(8,128)S(1)}, f32[128,128]{1,0:T(8,128)S(1)}, u32[]{:S(2)}, u32[]{:S(2)}) collective-permute-start(f32[128,128]{1,0:T(8,128)S(1)} %get-tuple-element.42), channel_id=1, source_target_pairs={{0,2},{1,3},{2,4},{3,5},{4,6},{5,7},{6,0},{7,1},{8,10},{9,11},{10,... | collective-permute-start | bytes 196616 | tf_op jit(solution)/shard_map/ppermute | solution.py:452
  9.0 4.6 %collective-permute-start.3 = (f32[32,128]{1,0:T(8,128)S(1)}, f32[32,128]{1,0:T(8,128)S(1)}, u32[]{:S(2)}, u32[]{:S(2)}) collective-permute-start(f32[32,128]{1,0:T(8,128)S(1)} %get-tuple-element.37.after_ref), channel_id=1, source_target_pairs={{8,16},{16,8},{24,0},{0,24},{9,17},{17,9},{25,1},{1,25},{10,18},{1... | collective-permute-start | bytes 49160 | tf_op jit(solution)/shard_map/ppermute | solution.py:461
  11.4 3.7 %collective-permute-start.2 = (f32[32,128]{1,0:T(8,128)S(1)}, f32[32,128]{1,0:T(8,128)S(1)}, u32[]{:S(2)}, u32[]{:S(2)}) collective-permute-start(f32[32,128]{1,0:T(8,128)S(1)} %get-tuple-element.37.after_ref), channel_id=1, source_target_pairs={{0,8},{8,0},{16,24},{24,16},{1,9},{9,1},{17,25},{25,17},{2,10},{10... | collective-permute-start | bytes 49160 | tf_op jit(solution)/shard_map/ppermute | solution.py:461
  15.2 8.9 %copy-start.2 = (f32[4,32,2,32]{3,2,1,0:T(2,128)S(1)}, f32[4,32,2,32]{3,2,1,0:T(2,128)}, u32[]{:S(2)}) copy-start(f32[4,32,2,32]{3,2,1,0:T(2,128)} %param.14) | copy-start | bytes 98308
  18.1 10.2 %collective-permute-start.5 = (f32[320,128]{1,0:T(8,128)S(1)}, f32[320,128]{1,0:T(8,128)S(1)}, u32[]{:S(2)}, u32[]{:S(2)}) collective-permute-start(f32[320,128]{1,0:T(8,128)S(1)} %get-tuple-element.44), channel_id=1, source_target_pairs={{0,1},{1,0},{2,3},{3,2},{4,5},{5,4},{6,7},{7,6},{8,9},{9,8},{10,11... | collective-permute-start | bytes 491528 | tf_op jit(solution)/shard_map/ppermute | solution.py:461
  18.2 10.1 %collective-permute-start.6 = (f32[320,128]{1,0:T(8,128)S(1)}, f32[320,128]{1,0:T(8,128)S(1)}, u32[]{:S(2)}, u32[]{:S(2)}) collective-permute-start(f32[320,128]{1,0:T(8,128)S(1)} %get-tuple-element.45), channel_id=1, source_target_pairs={{1,2},{2,1},{3,4},{4,3},{5,6},{6,5},{7,0},{0,7},{9,10},{10,9},{11,... | collective-permute-start | bytes 491528 | tf_op jit(solution)/shard_map/ppermute | solution.py:461
  22.1 6.2 %collective-permute-start.9 = (f32[128,128]{1,0:T(8,128)S(1)}, f32[128,128]{1,0:T(8,128)S(1)}, u32[]{:S(2)}, u32[]{:S(2)}) collective-permute-start(f32[128,128]{1,0:T(8,128)S(1)} %get-tuple-element.49), channel_id=1, source_target_pairs={{0,2},{1,3},{2,4},{3,5},{4,6},{5,7},{6,0},{7,1},{8,10},{9,11},{10,... | collective-permute-start | bytes 196616 | tf_op jit(solution)/shard_map/ppermute | solution.py:452
  22.1 4.7 %collective-permute-start.8 = (f32[40,128]{1,0:T(8,128)S(1)}, f32[40,128]{1,0:T(8,128)S(1)}, u32[]{:S(2)}, u32[]{:S(2)}) collective-permute-start(f32[40,128]{1,0:T(8,128)S(1)} %get-tuple-element.46.after_ref), channel_id=1, source_target_pairs={{8,16},{16,8},{24,0},{0,24},{9,17},{17,9},{25,1},{1,25},{10,18},{1... | collective-permute-start | bytes 61448 | tf_op jit(solution)/shard_map/ppermute | solution.py:461
  23.0 3.8 %collective-permute-start.7 = (f32[40,128]{1,0:T(8,128)S(1)}, f32[40,128]{1,0:T(8,128)S(1)}, u32[]{:S(2)}, u32[]{:S(2)}) collective-permute-start(f32[40,128]{1,0:T(8,128)S(1)} %get-tuple-element.46.after_ref), channel_id=1, source_target_pairs={{0,8},{8,0},{16,24},{24,16},{1,9},{9,1},{17,25},{25,17},{2,10},{10... | collective-permute-start | bytes 61448 | tf_op jit(solution)/shard_map/ppermute | solution.py:461
  28.6 8.2 %collective-permute-start.10 = (f32[64,128]{1,0:T(8,128)S(1)}, f32[64,128]{1,0:T(8,128)S(1)}, u32[]{:S(2)}, u32[]{:S(2)}) collective-permute-start(f32[64,128]{1,0:T(8,128)S(1)} %get-tuple-element.51), channel_id=1, source_target_pairs={{0,1},{1,0},{2,3},{3,2},{4,5},{5,4},{6,7},{7,6},{8,9},{9,8},{10,11... | collective-permute-start | bytes 98312 | tf_op jit(solution)/shard_map/ppermute | solution.py:461
  28.7 8.1 %collective-permute-start.11 = (f32[64,128]{1,0:T(8,128)S(1)}, f32[64,128]{1,0:T(8,128)S(1)}, u32[]{:S(2)}, u32[]{:S(2)}) collective-permute-start(f32[64,128]{1,0:T(8,128)S(1)} %get-tuple-element.52), channel_id=1, source_target_pairs={{1,2},{2,1},{3,4},{4,3},{5,6},{6,5},{7,0},{0,7},{9,10},{10,9},{11,... | collective-permute-start | bytes 98312 | tf_op jit(solution)/shard_map/ppermute | solution.py:461
  31.2 4.8 %collective-permute-start.13 = (f32[8,128]{1,0:T(8,128)S(1)}, f32[8,128]{1,0:T(8,128)S(1)}, u32[]{:S(2)}, u32[]{:S(2)}) collective-permute-start(f32[8,128]{1,0:T(8,128)S(1)} %get-tuple-element.53), channel_id=1, source_target_pairs={{8,16},{16,8},{24,0},{0,24},{9,17},{17,9},{25,1},{1,25},{10,18},{1... | collective-permute-start | bytes 12296 | tf_op jit(solution)/shard_map/ppermute | solution.py:461
  33.2 3.6 %collective-permute-start.12 = (f32[8,128]{1,0:T(8,128)S(1)}, f32[8,128]{1,0:T(8,128)S(1)}, u32[]{:S(2)}, u32[]{:S(2)}) collective-permute-start(f32[8,128]{1,0:T(8,128)S(1)} %get-tuple-element.53), channel_id=1, source_target_pairs={{0,8},{8,0},{16,24},{24,16},{1,9},{9,1},{17,25},{25,17},{2,10},{10... | collective-permute-start | bytes 12296 | tf_op jit(solution)/shard_map/ppermute | solution.py:461

commit v5 on v4

--- a/solution.py
+++ b/solution.py
@@ -10,6 +10,7 @@
 FAR = pl.BlockSpec(memory_space=pltpu.HBM)
 LIMIT = 40 * 1024 * 1024
 LANES = 128
+LONG = 1_000_000_000
 LEVELS = 8
 
 
@@ -152,8 +153,8 @@
 
 
 def begin(
-    x_hbm, mix_hbm, relax_hbm, land_hbm, parent_land_hbm,
-    sums_out, x_ref, a_ref, b_ref, c_ref, relax_ref, land_ref, parent_land_ref,
+    x_hbm, mix_hbm, relax_hbm, land_hbm, parent_land_hbm, rates_hbm,
+    sums_out, x_ref, a_ref, b_ref, c_ref, relax_ref, land_ref, parent_land_ref, rates_ref,
     mix_ref, land_in, parent_land_in, sums_ref, sems,
 ):
     depth = x_ref.shape[0]
@@ -170,6 +171,8 @@
             part = pl.ds(first, size)
             large.append(pltpu.make_async_copy(x_hbm.at[part], x_ref.at[part], sems.at[len(large) + len(small)]))
             large[-1].start()
+    rates_copy = pltpu.make_async_copy(rates_hbm, rates_ref, sems.at[len(large) + len(small)])
+    rates_copy.start()
     for copy in small:
         copy.wait()
     land_ref[...] = land_in[...].astype(F32)
@@ -187,6 +190,7 @@
         large[2 * part + 1].wait()
         lax.fori_loop(start, start + size, level, 0, unroll=size)
     sums_out[...] = block_columns(sums_ref)
+    rates_copy.wait()
 
 
 def child_first(x_ref, a_ref, b_ref, c_ref, solved_ref, mate_rows, far_rows, cols_ref):
@@ -248,48 +252,49 @@
     return (rates[0] * s + rates[1] * east) + (rates[2] * west + rates[3] * north) + rates[4] * south
 
 
-def child_second(
-    solved_in, a_ref, b_ref, c_ref, rates_ref, land_ref, relax_ref, mate_in, far_in, mate_cols, far_cols,
-    parent_ref, pa_ref, pb_ref, pc_ref, feed_ref,
-    sums_out, solved_ref, psolved_ref, mate_rows, far_rows, cols_ref,
-    x_ref, sums_ref, north_ref, south_ref, merged_ref,
+def child_between(
+    solved_in, rates_ref, land_ref, relax_ref, after_ref, mate_in, far_in, mate_cols, far_cols,
+    sums_out, x_ref,
+    sums_ref, north_ref, south_ref, merged_ref,
 ):
     depth, vectors = solved_in.shape[0], solved_in.shape[1]
-    half = depth // 2
-    groups = depth // LEVELS
     lane, row = lane_index(), row_index()
     weights = [relax_ref[j : j + 1, :] for j in range(8)]
     land = land_ref[...]
     child_halos(mate_in, far_in, north_ref, south_ref, mate_cols, far_cols, merged_ref)
-
-    def down(i, carry, edges):
-        k_low = depth - 1 - i
+    half, groups = depth // 2, depth // LEVELS
+
+    def level(i, _, edges):
         inside = lax.rem(i, LEVELS)
-        values = []
-        for side, k, base in ((0, i, inside * vectors), (1, k_low, (LEVELS - 1 - inside) * vectors)):
-            a, b = a_ref[k], b_ref[k]
+        for side, k, base in ((0, i, inside * vectors), (1, depth - 1 - i, (LEVELS - 1 - inside) * vectors)):
             rates = combine([rates_ref[d, k] for d in range(4)], land)
             for v in range(vectors):
-                x = child_cell(solved_in, k, v, base, edges[side], rates, north_ref, south_ref, lane, row)
-                x_ref[k, v] = x
-                y = a * x + b * carry[side * vectors + v]
-                solved_ref[k, v] = y
-                values.append(y)
+                x_ref[k, v] = child_cell(
+                    solved_in, k, v, base, edges[side], rates, north_ref, south_ref, lane, row
+                )
             block_rows(x_ref, k, weights, sums_ref, i, side)
-        rhs = parent_ref[i] + feed_ref[pl.ds(i * 8, 8), :]
-        psolved = pa_ref[pl.ds(i, 1), :] * rhs + pb_ref[pl.ds(i, 1), :] * carry[2 * vectors]
-        psolved_ref[i] = psolved
-        return tuple(values) + (psolved,)
-
-    carry = (jnp.zeros((8, LANES), F32),) * (2 * vectors + 1)
+        return 0
+
     for group in range(half // LEVELS):
         edges = [merged_ref[8 * g : 8 * g + 8, :] for g in (group, groups - 1 - group)]
-        carry = lax.fori_loop(
-            LEVELS * group, LEVELS * (group + 1), lambda i, carry, edges=edges: down(i, carry, edges), carry, unroll=4
+        lax.fori_loop(
+            LEVELS * group, LEVELS * (group + 1), lambda i, _, edges=edges: level(i, _, edges), 0, unroll=4
         )
     sums_out[...] = block_columns(sums_ref)
-    parent_up(carry[-1], pc_ref, psolved_ref, mate_rows, far_rows, depth * vectors, cols_ref, 8 * groups)
-    child_up(carry[:-1], c_ref, solved_ref, mate_rows, far_rows, cols_ref)
+
+
+def child_second(
+    x_ref, a_ref, b_ref, c_ref, parent_ref, pa_ref, pb_ref, pc_ref,
+    solved_ref, psolved_ref, mate_rows, far_rows, cols_ref,
+):
+    depth, vectors = x_ref.shape[0], x_ref.shape[1]
+    y = jnp.zeros((8, LANES), F32)
+    for i in range(depth // 2):
+        y = pa_ref[i : i + 1, :] * parent_ref[i] + pb_ref[i : i + 1, :] * y
+        psolved_ref[i] = y
+    lines, at = depth * vectors, depth // LEVELS * 8
+    parent_up(y, pc_ref, psolved_ref, mate_rows, far_rows, lines, cols_ref, at)
+    child_first(x_ref, a_ref, b_ref, c_ref, solved_ref, mate_rows, far_rows, cols_ref)
 
 
 def child_last(
@@ -323,12 +328,20 @@
 PLACES = [(h, r, 64 * h + 32 * r) for h in range(2) for r in range(2)]
 
 
-def parent_begin(parent_ref, mix_ref, after_ref, packed_ref, pa_ref, pb_ref, pc_ref, mixed):
+def parent_fed(parent_ref, feed_ref, after_ref, packed_ref):
     half, vectors = packed_ref.shape[0], packed_ref.shape[1]
-    depth = 2 * half
     for i in range(half):
         for h, r, lo in PLACES:
-            k = depth - 1 - i if h else i
+            k = 2 * half - 1 - i if h else i
+            packed_ref[i, :, lo : lo + 32] = parent_ref[pl.ds(2 * vectors * k + r, vectors, stride=2), :]
+        packed_ref[i] = packed_ref[i] + feed_ref[vectors * i : vectors * (i + 1), :]
+
+
+def parent_factors(mix_ref, fed_ref, far_ref, mate_cols, far_cols, pa_ref, pb_ref, pc_ref, mixed):
+    half = pa_ref.shape[0]
+    for i in range(half):
+        for h, r, lo in PLACES:
+            k = 2 * half - 1 - i if h else i
             mixed[i : i + 1, lo : lo + 32] = mix_ref[2 * k + r : 2 * k + r + 1, :]
     upper = lane_index(1) < 64
     rows = [mixed[i : i + 1, :] for i in range(half)]
@@ -342,23 +355,24 @@
         pa_ref[i : i + 1, :] = inverse[i]
         pb_ref[i : i + 1, :] = inverse[i] * outer[i]
         pc_ref[i : i + 1, :] = inverse[i] * inner[i]
-        for h, r, lo in PLACES:
-            k = depth - 1 - i if h else i
-            packed_ref[i, :, lo : lo + 32] = parent_ref[pl.ds(2 * vectors * k + r, vectors, stride=2), :]
-
-
-def parent_rates_packed(rates_ref, land_ref, after_ref, prates_ref):
-    half = prates_ref.shape[1]
+
+
+def parent_rates_packed(rates_ref, feed_ref, after_ref, packed_ref):
+    half = packed_ref.shape[1]
     depth = 2 * half
     for i in range(half):
         for h, r, lo in PLACES:
             k = depth - 1 - i if h else i
             for d in range(4):
                 at = 2 * (d * depth + k) + r
-                prates_ref[d + 1, i : i + 1, lo : lo + 32] = rates_ref[at : at + 1, :]
+                packed_ref[d, i : i + 1, lo : lo + 32] = rates_ref[at : at + 1, :]
+
+
+def parent_rates_masked(packed_ref, land_ref, far_ref, mate_cols, far_cols, prates_ref):
+    half = packed_ref.shape[1]
     land = jnp.concatenate([land_ref[r : r + 1, :] for _, r, _ in PLACES], axis=1)
     land = jnp.broadcast_to(land, (half, LANES))
-    for d, part in enumerate(combine([prates_ref[d] for d in range(1, 5)], land)):
+    for d, part in enumerate(combine([packed_ref[d] for d in range(4)], land)):
         prates_ref[d] = part
 
 
@@ -489,20 +503,21 @@
     halo_scratch = [pltpu.VMEM((count, LANES), F32), pltpu.VMEM((count, LANES), F32), pltpu.VMEM((edge, LANES), F32)]
     narrow = parent_adjoint.shape[-1]
 
-    sums1, x, a, b, c, relax, land, parent_land = call(
+    sums1, x, a, b, c, relax, land, parent_land, rates = call(
         begin,
-        [sums, field, factor, factor, factor, shape(lines, columns), shape(lines, columns), shape(*parent_land.shape)],
+        [sums, field, factor, factor, factor, shape(lines, columns), shape(lines, columns), shape(*parent_land.shape)]
+        + [shape(*child_rates.shape)],
         [
             pltpu.VMEM(factor.shape, F32),
             pltpu.VMEM(child_land.shape, jnp.int32),
             pltpu.VMEM(parent_land.shape, jnp.int32),
             sum_scratch,
-            pltpu.SemaphoreType.DMA((4 + half // 2,)),
+            pltpu.SemaphoreType.DMA((5 + half // 2,)),
         ],
-        [child_adjoint, child_mixing, relaxation, child_land, parent_land],
+        [child_adjoint, child_mixing, relaxation, child_land, parent_land, child_rates],
         4_000_000,
         3_000_000,
-        far_in=range(5),
+        far_in=range(6),
     )
     feed = passed_along(sums1, "gy", quarter)
     solved, mate, far, cols = call(
@@ -514,31 +529,55 @@
         3_000_000,
     )
     halos = halos_of(mate, far, cols)
-    packed, pa, pb, pc = call(
-        parent_begin,
-        [tiles] + [shape(half, LANES)] * 3,
+    fed = call(
+        parent_fed,
+        tiles,
+        [],
+        [parent_adjoint.reshape(-1, narrow), feed, cols],
+        LONG,
+        1_000_000,
+    )
+    pa, pb, pc = call(
+        parent_factors,
+        [shape(half, LANES)] * 3,
         [pltpu.VMEM((half, LANES), F32)],
-        [parent_adjoint.reshape(-1, narrow), parent_mixing.reshape(-1, narrow), cols],
-        500_000,
+        [parent_mixing.reshape(-1, narrow), fed, *halos[1:]],
+        LONG,
         1_000_000,
     )
-    rows = count + half // 2 * vectors
-    sums2, solved, psolved, mate, far, cols = call(
-        child_second,
-        [sums, field, tiles, shape(rows, LANES), shape(rows, LANES), shape(edge + 8, LANES)],
-        [pltpu.VMEM(field.shape, F32), sum_scratch] + halo_scratch,
-        [solved, a, b, c, child_rates, land, relax, *halos, packed, pa, pb, pc, feed],
+    sums2, x = call(
+        child_between,
+        [sums, field],
+        [sum_scratch] + halo_scratch,
+        [solved, rates, land, relax, pa, *halos],
         8_000_000,
         3_000_000,
     )
+    feed = passed_along(sums2, "gy", quarter)
+    rows = count + half // 2 * vectors
+    solved, psolved, mate, far, cols = call(
+        child_second,
+        [field, tiles, shape(rows, LANES), shape(rows, LANES), shape(edge + 8, LANES)],
+        [],
+        [x, a, b, c, fed, pa, pb, pc],
+        8_000_000,
+        3_000_000,
+    )
     halos = halos_of(mate, far, cols)
-    feed = passed_along(sums2, "gy", quarter)
+    packed_rates = call(
+        parent_rates_packed,
+        shape(4, half, LANES),
+        [],
+        [parent_rates.reshape(-1, narrow), feed, cols],
+        1_450_000_000,
+        1_000_000,
+    )
     prates = call(
-        parent_rates_packed,
+        parent_rates_masked,
         shape(5, half, LANES),
         [],
-        [parent_rates.reshape(-1, narrow), parent_land, cols],
-        500_000,
+        [packed_rates, parent_land, *halos[1:]],
+        LONG,
         1_000_000,
     )
     few = half // 2 * vectors
@@ -555,7 +594,7 @@
         child_last,
         field,
         [pltpu.VMEM(field.shape, F32)] + halo_scratch + [pltpu.SemaphoreType.DMA((depth // LEVELS,))],
-        [solved, child_rates, land, *halos],
+        [solved, rates, land, *halos],
         4_000_000,
         3_000_000,
         far_out=True,

time: 37.9 us -> 35.9 us (0.947)
  starting transfers between devices: 19.3 us -> 17.1 us
  Pallas kernels: 10 us -> 10.5 us
    ppermute x12, starting transfers between devices: 19.3 us -> 13.8 us  [swapped(): return lax.ppermute(value, axis, pairs)]
    ppermute x2, starting transfers between devices: 0.01 us -> 3.29 us  [passed_along(): lax.ppermute(value, axis, [(i, (i + steps) % count) for i in range(count)])]
    ppermute x2, waiting for transfers between devices: 1.47 us -> 0.91 us  [passed_along(): lax.ppermute(value, axis, [(i, (i + steps) % count) for i in range(count)])]
    pallas_call x8 -> x11, Pallas kernels: 10 us -> 10.5 us  [call(): pl.pallas_call(body, out_shape=outs, in_specs=[FAR if i in far_in else VM...]
  transfers between devices with their start and end apart: 14 -> 14, of which waited for: 5 -> 7; matrix products, arithmetic and copies ran while one was open for 0% -> 0% of each run, Pallas kernels for 7% -> 13%
where the time goes in v5:
time: 35.9 us; the launch traced here: 35.8 us
  starting transfers between devices  17.1 us (48%)
  Pallas kernels  10.5 us (29%)
  waiting for transfers between devices  7.5 us (21%)
  between operations  0.75 us (2%)
    ppermute x12, starting transfers between devices, swapped(): return lax.ppermute(value, axis, pairs)  13.8 us
    pallas_call x11, Pallas kernels, call(): pl.pallas_call(body, out_shape=outs, in_specs=[FAR if i in far_in else VM...  10.5 us
    ppermute x12, waiting for transfers between devices, swapped(): return lax.ppermute(value, axis, pairs)  6.58 us
    ppermute x2, starting transfers between devices, passed_along(): lax.ppermute(value, axis, [(i, (i + steps) % count) for i in range(count)])  3.29 us
    ppermute x2, waiting for transfers between devices, passed_along(): lax.ppermute(value, axis, [(i, (i + steps) % count) for i in range(count)])  0.91 us
  transfers between devices with their start and end apart: 14, of which 7 were waited for; matrix products, arithmetic and copies ran while one was open for 0% of the time, Pallas kernels for 13%

profile of v5, /device:TPU:0, one launch (start us, length us, event | category | flops | bytes accessed | tf_op | source)
XLA Modules:
  0.0 35.8 jit_solution(5250617214163039621)
XLA Ops:
  0.6 2.2 %begin.1 = (f32[128,128]{1,0:T(8,128)S(1)}, f32[32,8,8,128]{3,2,1,0:T(8,128)S(1)}, f32[32,8,128]{2,1,0:T(8,128)S(1)}, f32[32,8,128]{2,1,0:T(8,128)S(1)}, f32[32,...) custom-call(f32[32,8,8,128]{3,2,1,0:T(8,128)} %x_hbm.1, ...), custom_call_target="tpu_custom_call" | custom-call | flops 4000000 | bytes 3000000 | tf_op jit(solution)/shard_map/begin/pallas_call | solution.py:23
  2.9 3.1 %collective-permute-start = (f32[128,128]{1,0:T(8,128)S(1)}, f32[128,128]{1,0:T(8,128)S(1)}, u32[]{:S(2)}, u32[]{:S(2)}) collective-permute-start(f32[128,128]{1,0:T(8,128)S(1)} %get-tuple-element.37), channel_id=1, source_target_pairs={{0,2},{1,3},{2,4},{3,5},{4,6},{5,7},{6,0},{7,1},{8,10},{9,11},{10,... | collective-permute-start | bytes 196616 | tf_op jit(solution)/shard_map/ppermute | solution.py:466
  5.9 0.8 %child_first.1 = (f32[32,8,8,128]{3,2,1,0:T(8,128)S(1)}, f32[256,128]{1,0:T(8,128)S(1)}, f32[256,128]{1,0:T(8,128)S(1)}, f32[32,128]{1,0:T(8,128)S(1)}) custom-call(f32[32,8,8,128]{3,2,1,0:T(8,128)S(1)} %get-tuple-element.29.x_ref, f32[32,8,128]{2,1,0:T(8,128)S(1)} %get-tuple-element.30.a_ref, f32[32,8,128]{2,1,0:T(8,128)S(1)} %get-tuple-element.31.b_ref, ...), custom_call_target="tpu_custom_call" | custom-call | flops 4000000 | bytes 3000000 | tf_op jit(solution)/shard_map/child_first/pallas_call | solution.py:23
  6.8 1.6 %collective-permute-start.1 = (f32[256,128]{1,0:T(8,128)S(1)}, f32[256,128]{1,0:T(8,128)S(1)}, u32[]{:S(2)}, u32[]{:S(2)}) collective-permute-start(f32[256,128]{1,0:T(8,128)S(1)} %get-tuple-element.39), channel_id=1, source_target_pairs={{1,2},{2,1},{3,4},{4,3},{5,6},{6,5},{7,0},{0,7},{9,10},{10,9},{11,... | collective-permute-start | bytes 393224 | tf_op jit(solution)/shard_map/ppermute | solution.py:475
  8.3 2.4 %collective-permute-start.3 = (f32[32,128]{1,0:T(8,128)S(1)}, f32[32,128]{1,0:T(8,128)S(1)}, u32[]{:S(2)}, u32[]{:S(2)}) collective-permute-start(f32[32,128]{1,0:T(8,128)S(1)} %get-tuple-element.38.after_ref), channel_id=1, source_target_pairs={{8,16},{16,8},{24,0},{0,24},{9,17},{17,9},{25,1},{1,25},{10,18},{1... | collective-permute-start | bytes 49160 | tf_op jit(solution)/shard_map/ppermute | solution.py:475
  10.8 0.5 %collective-permute-start.2 = (f32[32,128]{1,0:T(8,128)S(1)}, f32[32,128]{1,0:T(8,128)S(1)}, u32[]{:S(2)}, u32[]{:S(2)}) collective-permute-start(f32[32,128]{1,0:T(8,128)S(1)} %get-tuple-element.38.after_ref), channel_id=1, source_target_pairs={{0,8},{8,0},{16,24},{24,16},{1,9},{9,1},{17,25},{25,17},{2,10},{10... | collective-permute-start | bytes 49160 | tf_op jit(solution)/shard_map/ppermute | solution.py:475
  11.5 1.5 %collective-permute-done.3.far_cols = f32[32,128]{1,0:T(8,128)S(1)} collective-permute-done((f32[32,128]{1,0:T(8,128)S(1)}, f32[32,128]{1,0:T(8,128)S(1)}, u32[]{:S(2)}, u32[]{:S(2)}) %collective-permute-start.3) | collective-permute-done | bytes 16416 | tf_op jit(solution)/shard_map/ppermute | solution.py:475
  13.0 1.5 %collective-permute-done.2.mate_cols = f32[32,128]{1,0:T(8,128)S(1)} collective-permute-done((f32[32,128]{1,0:T(8,128)S(1)}, f32[32,128]{1,0:T(8,128)S(1)}, u32[]{:S(2)}, u32[]{:S(2)}) %collective-permute-start.2) | collective-permute-done | bytes 16416 | tf_op jit(solution)/shard_map/ppermute | solution.py:475
  14.7 2.2 %child_between.1 = (f32[128,128]{1,0:T(8,128)S(1)}, f32[32,8,8,128]{3,2,1,0:T(8,128)S(1)}) custom-call(f32[32,8,8,128]{3,2,1,0:T(8,128)S(1)} %get-tuple-element.33.solved_in, f32[4,32,8,128]{3,2,1,0:T(8,128)S(1)} %get-tuple-element.34.rates_ref, f32[8,128]{1,0:T(8,128)S(1)} %get-tuple-element.35.land_ref, f32[8,128]{1,0:T(8,128)S(1)} %get-tuple-element.36.relax_ref, ...), custom_call_target="tpu_custom_call" | custom-call | flops 8000000 | bytes 3000000 | tf_op jit(solution)/shard_map/child_between/pallas_call | solution.py:23
  17.1 1.0 %child_second.1 = (f32[32,8,8,128]{3,2,1,0:T(8,128)S(1)}, f32[16,8,128]{2,1,0:T(8,128)S(1)}, f32[320,128]{1,0:T(8,128)S(1)}, f32[320,128]{1,0:T(8,128)S(1)}, f32[40,128]{1,0:T(8,128)S(1)}) custom-call(f32[32,8,8,128]{3,2,1,0:T(8,128)S(1)} %get-tuple-element.42.x_ref, f32[32,8,128]{2,1,0:T(8,128)S(1)} %get-tuple-element.30.a_ref, ...), custom_call_target="tpu_custom_call" | custom-call | flops 8000000 | bytes 3000000 | tf_op jit(solution)/shard_map/child_second/pallas_call | solution.py:23
  18.1 2.1 %collective-permute-start.6 = (f32[320,128]{1,0:T(8,128)S(1)}, f32[320,128]{1,0:T(8,128)S(1)}, u32[]{:S(2)}, u32[]{:S(2)}) collective-permute-start(f32[320,128]{1,0:T(8,128)S(1)} %get-tuple-element.47), channel_id=1, source_target_pairs={{1,2},{2,1},{3,4},{4,3},{5,6},{6,5},{7,0},{0,7},{9,10},{10,9},{11,... | collective-permute-start | bytes 491528 | tf_op jit(solution)/shard_map/ppermute | solution.py:475
  20.2 1.3 %collective-permute-start.8 = (f32[40,128]{1,0:T(8,128)S(1)}, f32[40,128]{1,0:T(8,128)S(1)}, u32[]{:S(2)}, u32[]{:S(2)}) collective-permute-start(f32[40,128]{1,0:T(8,128)S(1)} %get-tuple-element.48.after_ref), channel_id=1, source_target_pairs={{8,16},{16,8},{24,0},{0,24},{9,17},{17,9},{25,1},{1,25},{10,18},{1... | collective-permute-start | bytes 61448 | tf_op jit(solution)/shard_map/ppermute | solution.py:475
  21.5 0.7 %collective-permute-start.7 = (f32[40,128]{1,0:T(8,128)S(1)}, f32[40,128]{1,0:T(8,128)S(1)}, u32[]{:S(2)}, u32[]{:S(2)}) collective-permute-start(f32[40,128]{1,0:T(8,128)S(1)} %get-tuple-element.48.after_ref), channel_id=1, source_target_pairs={{0,8},{8,0},{16,24},{24,16},{1,9},{9,1},{17,25},{25,17},{2,10},{10... | collective-permute-start | bytes 61448 | tf_op jit(solution)/shard_map/ppermute | solution.py:475
  22.2 0.9 %collective-permute-done.9.feed_ref = f32[128,128]{1,0:T(8,128)S(1)} collective-permute-done((f32[128,128]{1,0:T(8,128)S(1)}, f32[128,128]{1,0:T(8,128)S(1)}, u32[]{:S(2)}, u32[]{:S(2)}) %collective-permute-start.9) | collective-permute-done | bytes 65568 | tf_op jit(solution)/shard_map/ppermute | solution.py:466
  23.4 1.5 %collective-permute-done.8.far_cols = f32[40,128]{1,0:T(8,128)S(1)} collective-permute-done((f32[40,128]{1,0:T(8,128)S(1)}, f32[40,128]{1,0:T(8,128)S(1)}, u32[]{:S(2)}, u32[]{:S(2)}) %collective-permute-start.8) | collective-permute-done | bytes 20512 | tf_op jit(solution)/shard_map/ppermute | solution.py:475
  24.9 0.4 %collective-permute-done.7.mate_cols = f32[40,128]{1,0:T(8,128)S(1)} collective-permute-done((f32[40,128]{1,0:T(8,128)S(1)}, f32[40,128]{1,0:T(8,128)S(1)}, u32[]{:S(2)}, u32[]{:S(2)}) %collective-permute-start.7) | collective-permute-done | bytes 20512 | tf_op jit(solution)/shard_map/ppermute | solution.py:475
  25.3 1.0 %collective-permute-done.6.far_in.far_ref = f32[320,128]{1,0:T(8,128)S(1)} collective-permute-done((f32[320,128]{1,0:T(8,128)S(1)}, f32[320,128]{1,0:T(8,128)S(1)}, u32[]{:S(2)}, u32[]{:S(2)}) %collective-permute-start.6) | collective-permute-done | bytes 163872 | tf_op jit(solution)/shard_map/ppermute | solution.py:475
  26.3 0.4 %parent_second.1 = (f32[16,8,128]{2,1,0:T(8,128)S(1)}, f32[64,128]{1,0:T(8,128)S(1)}, f32[64,128]{1,0:T(8,128)S(1)}, f32[8,128]{1,0:T(8,128)S(1)}) custom-call(f32[16,8,128]{2,1,0:T(8,128)S(1)} %get-tuple-element.49.psolved_in, f32[5,16,128]{2,1,0:T(8,128)S(1)} %parent_rates_masked.1.prates_ref, f32[16,128]{1,0:T(8,128)S(1)} %get-tuple-element.40.after_ref.pa_ref, ...), custom_call_target="tpu_custom_call" | custom-call | flops 1000000 | bytes 500000 | tf_op jit(solution)/shard_map/parent_second/pallas_call | solution.py:23
  26.8 2.2 %collective-permute-start.11 = (f32[64,128]{1,0:T(8,128)S(1)}, f32[64,128]{1,0:T(8,128)S(1)}, u32[]{:S(2)}, u32[]{:S(2)}) collective-permute-start(f32[64,128]{1,0:T(8,128)S(1)} %get-tuple-element.54), channel_id=1, source_target_pairs={{1,2},{2,1},{3,4},{4,3},{5,6},{6,5},{7,0},{0,7},{9,10},{10,9},{11,... | collective-permute-start | bytes 98312 | tf_op jit(solution)/shard_map/ppermute | solution.py:475
  29.0 2.2 %collective-permute-start.13 = (f32[8,128]{1,0:T(8,128)S(1)}, f32[8,128]{1,0:T(8,128)S(1)}, u32[]{:S(2)}, u32[]{:S(2)}) collective-permute-start(f32[8,128]{1,0:T(8,128)S(1)} %get-tuple-element.55), channel_id=1, source_target_pairs={{8,16},{16,8},{24,0},{0,24},{9,17},{17,9},{25,1},{1,25},{10,18},{1... | collective-permute-start | bytes 12296 | tf_op jit(solution)/shard_map/ppermute | solution.py:475
  31.2 0.7 %collective-permute-start.12 = (f32[8,128]{1,0:T(8,128)S(1)}, f32[8,128]{1,0:T(8,128)S(1)}, u32[]{:S(2)}, u32[]{:S(2)}) collective-permute-start(f32[8,128]{1,0:T(8,128)S(1)} %get-tuple-element.55), channel_id=1, source_target_pairs={{0,8},{8,0},{16,24},{24,16},{1,9},{9,1},{17,25},{25,17},{2,10},{10... | collective-permute-start | bytes 12296 | tf_op jit(solution)/shard_map/ppermute | solution.py:475
  31.9 2.2 %child_last.1 = f32[32,8,8,128]{3,2,1,0:T(8,128)} custom-call(f32[32,8,8,128]{3,2,1,0:T(8,128)S(1)} %get-tuple-element.45.solved_in, f32[4,32,8,128]{3,2,1,0:T(8,128)S(1)} %get-tuple-element.34.rates_ref, f32[8,128]{1,0:T(8,128)S(1)} %get-tuple-element.35.land_ref, f32[320,128]{1,0:T(8,128)S(1)} %collective-permute-done.5.mate_in, ...), custom_call_target="tpu_custom_call" | custom-call | flops 4000000 | bytes 3000000 | tf_op jit(solution)/shard_map/child_last/pallas_call | solution.py:23
  34.1 0.7 %collective-permute-done.12.mate_cols = f32[8,128]{1,0:T(8,128)S(1)} collective-permute-done((f32[8,128]{1,0:T(8,128)S(1)}, f32[8,128]{1,0:T(8,128)S(1)}, u32[]{:S(2)}, u32[]{:S(2)}) %collective-permute-start.12) | collective-permute-done | bytes 4128 | tf_op jit(solution)/shard_map/ppermute | solution.py:475
  34.8 1.0 %parent_last.1 = f32[512,32]{1,0:T(8,128)} custom-call(f32[16,8,128]{2,1,0:T(8,128)S(1)} %get-tuple-element.52.psolved_in, f32[5,16,128]{2,1,0:T(8,128)S(1)} %parent_rates_masked.1.prates_ref, f32[64,128]{1,0:T(8,128)S(1)} %collective-permute-done.10.mate_in, f32[64,128]{1,0:T(8,128)S(1)} %collective-permute-done.11.far_in, ...), custom_call_target="tpu_custom_call" | custom-call | flops 500000 | bytes 500000 | tf_op jit(solution)/shard_map/parent_last/pallas_call | solution.py:23
  (21 shorter events, 0.9 us)
Async XLA Ops:
  2.9 8.4 %collective-permute-start = (f32[128,128]{1,0:T(8,128)S(1)}, f32[128,128]{1,0:T(8,128)S(1)}, u32[]{:S(2)}, u32[]{:S(2)}) collective-permute-start(f32[128,128]{1,0:T(8,128)S(1)} %get-tuple-element.37), channel_id=1, source_target_pairs={{0,2},{1,3},{2,4},{3,5},{4,6},{5,7},{6,0},{7,1},{8,10},{9,11},{10,... | collective-permute-start | bytes 196616 | tf_op jit(solution)/shard_map/ppermute | solution.py:466
  5.9 5.4 %copy-start = (f32[32,8,2,32]{3,2,1,0:T(2,128)S(1)}, f32[32,8,2,32]{3,2,1,0:T(2,128)}, u32[]{:S(2)}) copy-start(f32[32,8,2,32]{3,2,1,0:T(2,128)} %param.10) | copy-start | bytes 196612
  6.8 7.7 %collective-permute-start.1 = (f32[256,128]{1,0:T(8,128)S(1)}, f32[256,128]{1,0:T(8,128)S(1)}, u32[]{:S(2)}, u32[]{:S(2)}) collective-permute-start(f32[256,128]{1,0:T(8,128)S(1)} %get-tuple-element.39), channel_id=1, source_target_pairs={{1,2},{2,1},{3,4},{4,3},{5,6},{6,5},{7,0},{0,7},{9,10},{10,9},{11,... | collective-permute-start | bytes 393224 | tf_op jit(solution)/shard_map/ppermute | solution.py:475
  8.3 4.6 %collective-permute-start.3 = (f32[32,128]{1,0:T(8,128)S(1)}, f32[32,128]{1,0:T(8,128)S(1)}, u32[]{:S(2)}, u32[]{:S(2)}) collective-permute-start(f32[32,128]{1,0:T(8,128)S(1)} %get-tuple-element.38.after_ref), channel_id=1, source_target_pairs={{8,16},{16,8},{24,0},{0,24},{9,17},{17,9},{25,1},{1,25},{10,18},{1... | collective-permute-start | bytes 49160 | tf_op jit(solution)/shard_map/ppermute | solution.py:475
  10.8 3.7 %collective-permute-start.2 = (f32[32,128]{1,0:T(8,128)S(1)}, f32[32,128]{1,0:T(8,128)S(1)}, u32[]{:S(2)}, u32[]{:S(2)}) collective-permute-start(f32[32,128]{1,0:T(8,128)S(1)} %get-tuple-element.38.after_ref), channel_id=1, source_target_pairs={{0,8},{8,0},{16,24},{24,16},{1,9},{9,1},{17,25},{25,17},{2,10},{10... | collective-permute-start | bytes 49160 | tf_op jit(solution)/shard_map/ppermute | solution.py:475
  11.3 3.4 %collective-permute-start.4 = (f32[256,128]{1,0:T(8,128)S(1)}, f32[256,128]{1,0:T(8,128)S(1)}, u32[]{:S(2)}, u32[]{:S(2)}) collective-permute-start(f32[256,128]{1,0:T(8,128)S(1)} %get-tuple-element.41), channel_id=1, source_target_pairs={{0,1},{1,0},{2,3},{3,2},{4,5},{5,4},{6,7},{7,6},{8,9},{9,8},{10,11... | collective-permute-start | bytes 393224 | tf_op jit(solution)/shard_map/ppermute | solution.py:475
  11.3 3.2 %copy-start.2 = (f32[32,2,32]{2,1,0:T(2,128)S(1)}, f32[32,2,32]{2,1,0:T(2,128)}, u32[]{:S(2)}) copy-start(f32[32,2,32]{2,1,0:T(2,128)} %param.15) | copy-start | bytes 24580
  16.9 6.3 %collective-permute-start.9 = (f32[128,128]{1,0:T(8,128)S(1)}, f32[128,128]{1,0:T(8,128)S(1)}, u32[]{:S(2)}, u32[]{:S(2)}) collective-permute-start(f32[128,128]{1,0:T(8,128)S(1)} %get-tuple-element.50), channel_id=1, source_target_pairs={{0,2},{1,3},{2,4},{3,5},{4,6},{5,7},{6,0},{7,1},{8,10},{9,11},{10,... | collective-permute-start | bytes 196616 | tf_op jit(solution)/shard_map/ppermute | solution.py:466
  17.1 6.1 %copy-start.1 = (f32[4,32,2,32]{3,2,1,0:T(2,128)S(1)}, f32[4,32,2,32]{3,2,1,0:T(2,128)}, u32[]{:S(2)}) copy-start(f32[4,32,2,32]{3,2,1,0:T(2,128)} %param.14) | copy-start | bytes 98308
  18.1 8.1 %collective-permute-start.6 = (f32[320,128]{1,0:T(8,128)S(1)}, f32[320,128]{1,0:T(8,128)S(1)}, u32[]{:S(2)}, u32[]{:S(2)}) collective-permute-start(f32[320,128]{1,0:T(8,128)S(1)} %get-tuple-element.47), channel_id=1, source_target_pairs={{1,2},{2,1},{3,4},{4,3},{5,6},{6,5},{7,0},{0,7},{9,10},{10,9},{11,... | collective-permute-start | bytes 491528 | tf_op jit(solution)/shard_map/ppermute | solution.py:475
  20.2 4.7 %collective-permute-start.8 = (f32[40,128]{1,0:T(8,128)S(1)}, f32[40,128]{1,0:T(8,128)S(1)}, u32[]{:S(2)}, u32[]{:S(2)}) collective-permute-start(f32[40,128]{1,0:T(8,128)S(1)} %get-tuple-element.48.after_ref), channel_id=1, source_target_pairs={{8,16},{16,8},{24,0},{0,24},{9,17},{17,9},{25,1},{1,25},{10,18},{1... | collective-permute-start | bytes 61448 | tf_op jit(solution)/shard_map/ppermute | solution.py:475
  21.5 3.8 %collective-permute-start.7 = (f32[40,128]{1,0:T(8,128)S(1)}, f32[40,128]{1,0:T(8,128)S(1)}, u32[]{:S(2)}, u32[]{:S(2)}) collective-permute-start(f32[40,128]{1,0:T(8,128)S(1)} %get-tuple-element.48.after_ref), channel_id=1, source_target_pairs={{0,8},{8,0},{16,24},{24,16},{1,9},{9,1},{17,25},{25,17},{2,10},{10... | collective-permute-start | bytes 61448 | tf_op jit(solution)/shard_map/ppermute | solution.py:475
  22.2 4.1 %collective-permute-start.5 = (f32[320,128]{1,0:T(8,128)S(1)}, f32[320,128]{1,0:T(8,128)S(1)}, u32[]{:S(2)}, u32[]{:S(2)}) collective-permute-start(f32[320,128]{1,0:T(8,128)S(1)} %get-tuple-element.46), channel_id=1, source_target_pairs={{0,1},{1,0},{2,3},{3,2},{4,5},{5,4},{6,7},{7,6},{8,9},{9,8},{10,11... | collective-permute-start | bytes 491528 | tf_op jit(solution)/shard_map/ppermute | solution.py:475
  26.7 8.1 %collective-permute-start.10 = (f32[64,128]{1,0:T(8,128)S(1)}, f32[64,128]{1,0:T(8,128)S(1)}, u32[]{:S(2)}, u32[]{:S(2)}) collective-permute-start(f32[64,128]{1,0:T(8,128)S(1)} %get-tuple-element.53), channel_id=1, source_target_pairs={{0,1},{1,0},{2,3},{3,2},{4,5},{5,4},{6,7},{7,6},{8,9},{9,8},{10,11... | collective-permute-start | bytes 98312 | tf_op jit(solution)/shard_map/ppermute | solution.py:475
  26.8 8.0 %collective-permute-start.11 = (f32[64,128]{1,0:T(8,128)S(1)}, f32[64,128]{1,0:T(8,128)S(1)}, u32[]{:S(2)}, u32[]{:S(2)}) collective-permute-start(f32[64,128]{1,0:T(8,128)S(1)} %get-tuple-element.54), channel_id=1, source_target_pairs={{1,2},{2,1},{3,4},{4,3},{5,6},{6,5},{7,0},{0,7},{9,10},{10,9},{11,... | collective-permute-start | bytes 98312 | tf_op jit(solution)/shard_map/ppermute | solution.py:475
  29.0 5.1 %collective-permute-start.13 = (f32[8,128]{1,0:T(8,128)S(1)}, f32[8,128]{1,0:T(8,128)S(1)}, u32[]{:S(2)}, u32[]{:S(2)}) collective-permute-start(f32[8,128]{1,0:T(8,128)S(1)} %get-tuple-element.55), channel_id=1, source_target_pairs={{8,16},{16,8},{24,0},{0,24},{9,17},{17,9},{25,1},{1,25},{10,18},{1... | collective-permute-start | bytes 12296 | tf_op jit(solution)/shard_map/ppermute | solution.py:475
  31.2 3.6 %collective-permute-start.12 = (f32[8,128]{1,0:T(8,128)S(1)}, f32[8,128]{1,0:T(8,128)S(1)}, u32[]{:S(2)}, u32[]{:S(2)}) collective-permute-start(f32[8,128]{1,0:T(8,128)S(1)} %get-tuple-element.55), channel_id=1, source_target_pairs={{0,8},{8,0},{16,24},{24,16},{1,9},{9,1},{17,25},{25,17},{2,10},{10... | collective-permute-start | bytes 12296 | tf_op jit(solution)/shard_map/ppermute | solution.py:475

commit v6 on v5

--- a/solution.py
+++ b/solution.py
@@ -11,6 +11,7 @@
 LIMIT = 40 * 1024 * 1024
 LANES = 128
 LONG = 1_000_000_000
+INNER = 10_000_000
 LEVELS = 8
 
 
@@ -222,55 +223,63 @@
     return jnp.where((lane_index() & 1) == 0, west, pltpu.roll(east, turn, 1))
 
 
-def child_halos(mate_ref, far_ref, north_ref, south_ref, mate_cols, far_cols, merged_ref):
-    swap = jnp.broadcast_to(parity("gy"), (8, LANES)) == 1
-
-    def sort(i, _):
-        part = pl.ds(pl.multiple_of(8 * i, 8), 8)
-        mate, far = mate_ref[part, :], far_ref[part, :]
-        north_ref[part, :] = jnp.where(swap, far, mate)
-        south_ref[part, :] = jnp.where(swap, mate, far)
+def child_inner(solved_ref, rates_ref, land_ref, after_ref, inner_ref, row_ref, column_ref):
+    depth, vectors = solved_ref.shape[0], solved_ref.shape[1]
+    lane, row = lane_index(), row_index()
+    land = land_ref[...]
+
+    def level(k, _):
+        centre, east, west, north, south = combine([rates_ref[d, k] for d in range(4)], land)
+        column_ref[k] = jnp.where(lane == 0, west, jnp.where(lane == LANES - 1, east, 0.0))
+        row_ref[k] = jnp.where(row == 0, south, jnp.where(row == 7, north, 0.0))
+        east, west = jnp.where(lane == LANES - 1, 0.0, east), jnp.where(lane == 0, 0.0, west)
+        north, south = jnp.where(row == 7, 0.0, north), jnp.where(row == 0, 0.0, south)
+        for v in range(vectors):
+            s = solved_ref[k, v]
+            across = east * pltpu.roll(s, LANES - 1, 1) + west * pltpu.roll(s, 1, 1)
+            along = north * pltpu.roll(s, 7, 0) + south * pltpu.roll(s, 1, 0)
+            inner_ref[k, v] = centre * s + across + along
         return 0
 
-    lax.fori_loop(0, north_ref.shape[0] // 8, sort, 0, unroll=8)
+    lax.fori_loop(0, depth, level, 0, unroll=4)
+
+
+def edge_merger(mate_cols, far_cols, merged_ref):
     for g in range(merged_ref.shape[0] // 8):
         part = slice(8 * g, 8 * g + 8)
         merged_ref[part, :] = merge_edges(mate_cols[part, :], far_cols[part, :], LANES - 2)
 
 
-def child_cell(solved_ref, k, v, base, edges, rates, north_ref, south_ref, lane, row):
-    vectors = solved_ref.shape[1]
-    s = solved_ref[k, v]
-    line = k * vectors + v
-    edge = pltpu.roll(edges, (LANES - 2 * (base + v)) & (LANES - 1), 1)
-    north_edge = jnp.broadcast_to(north_ref[pl.ds(line, 1), :], (8, LANES))
-    south_edge = jnp.broadcast_to(south_ref[pl.ds(line, 1), :], (8, LANES))
-    east = jnp.where(lane == LANES - 1, edge, pltpu.roll(s, LANES - 1, 1))
-    west = jnp.where(lane == 0, edge, pltpu.roll(s, 1, 1))
-    north = jnp.where(row == 7, north_edge, pltpu.roll(s, 7, 0))
-    south = jnp.where(row == 0, south_edge, pltpu.roll(s, 1, 0))
-    return (rates[0] * s + rates[1] * east) + (rates[2] * west + rates[3] * north) + rates[4] * south
+def edged(inner_ref, row_rates, column_rates, mate_ref, far_ref, edges, k, v, at, mates):
+    line = pl.ds(k * inner_ref.shape[1] + v, 1)
+    mate = jnp.broadcast_to(mate_ref[line, :], (8, LANES))
+    far = jnp.broadcast_to(far_ref[line, :], (8, LANES))
+    edge = pltpu.roll(edges, (LANES - 2 * at) & (LANES - 1), 1)
+    return inner_ref[k, v] + row_rates * jnp.where(mates, mate, far) + column_rates * edge
+
+
+def mate_rows_mask():
+    return row_index() == 7 * (1 - parity("gy"))
 
 
 def child_between(
-    solved_in, rates_ref, land_ref, relax_ref, after_ref, mate_in, far_in, mate_cols, far_cols,
+    inner_ref, row_ref, column_ref, relax_ref, after_ref, mate_in, far_in, mate_cols, far_cols,
     sums_out, x_ref,
-    sums_ref, north_ref, south_ref, merged_ref,
+    sums_ref, merged_ref,
 ):
-    depth, vectors = solved_in.shape[0], solved_in.shape[1]
-    lane, row = lane_index(), row_index()
+    depth, vectors = inner_ref.shape[0], inner_ref.shape[1]
+    half, groups = depth // 2, depth // LEVELS
+    mates = mate_rows_mask()
     weights = [relax_ref[j : j + 1, :] for j in range(8)]
-    land = land_ref[...]
-    child_halos(mate_in, far_in, north_ref, south_ref, mate_cols, far_cols, merged_ref)
-    half, groups = depth // 2, depth // LEVELS
+    edge_merger(mate_cols, far_cols, merged_ref)
 
     def level(i, _, edges):
         inside = lax.rem(i, LEVELS)
         for side, k, base in ((0, i, inside * vectors), (1, depth - 1 - i, (LEVELS - 1 - inside) * vectors)):
-            rates = combine([rates_ref[d, k] for d in range(4)], land)
+            row_rates, column_rates = row_ref[k], column_ref[k]
             for v in range(vectors):
-                x_ref[k, v] = child_cell(
-                    solved_in, k, v, base, edges[side], rates, north_ref, south_ref, lane, row
+                x_ref[k, v] = edged(
+                    inner_ref, row_rates, column_rates, mate_in, far_in, edges[side], k, v, base + v, mates
                 )
             block_rows(x_ref, k, weights, sums_ref, i, side)
         return 0
@@ -298,22 +307,21 @@
 
 
 def child_last(
-    solved_in, rates_ref, land_ref, mate_in, far_in, mate_cols, far_cols, out_hbm, out_ref, north_ref, south_ref, merged_ref, sems
+    inner_ref, row_ref, column_ref, mate_in, far_in, mate_cols, far_cols, out_hbm, out_ref, merged_ref, sems
 ):
-    depth, vectors = solved_in.shape[0], solved_in.shape[1]
-    lane, row = lane_index(), row_index()
-    land = land_ref[...]
-    child_halos(mate_in, far_in, north_ref, south_ref, mate_cols, far_cols, merged_ref)
+    depth, vectors = inner_ref.shape[0], inner_ref.shape[1]
+    mates = mate_rows_mask()
+    edge_merger(mate_cols, far_cols, merged_ref)
     copies = []
     for group in range(depth // LEVELS):
         edges = merged_ref[8 * group : 8 * group + 8, :]
 
         def level(inside, _):
             k = LEVELS * group + inside
-            rates = combine([rates_ref[d, k] for d in range(4)], land)
+            row_rates, column_rates = row_ref[k], column_ref[k]
             for v in range(vectors):
-                out_ref[k, v] = child_cell(
-                    solved_in, k, v, inside * vectors, edges, rates, north_ref, south_ref, lane, row
+                out_ref[k, v] = edged(
+                    inner_ref, row_rates, column_rates, mate_in, far_in, edges, k, v, inside * vectors + v, mates
                 )
             return 0
 
@@ -500,7 +508,7 @@
     count = depth * vectors
     edge = depth // LEVELS * 8
     sum_scratch = pltpu.VMEM((half * vectors, 4 * LANES), F32)
-    halo_scratch = [pltpu.VMEM((count, LANES), F32), pltpu.VMEM((count, LANES), F32), pltpu.VMEM((edge, LANES), F32)]
+    edge_scratch = [pltpu.VMEM((edge, LANES), F32)]
     narrow = parent_adjoint.shape[-1]
 
     sums1, x, a, b, c, relax, land, parent_land, rates = call(
@@ -529,11 +537,19 @@
         3_000_000,
     )
     halos = halos_of(mate, far, cols)
+    inner, row_rates, column_rates = call(
+        child_inner,
+        [field, factor, factor],
+        [],
+        [solved, rates, land, cols],
+        INNER,
+        4_000_000,
+    )
     fed = call(
         parent_fed,
         tiles,
         [],
-        [parent_adjoint.reshape(-1, narrow), feed, cols],
+        [parent_adjoint.reshape(-1, narrow), feed, inner],
         LONG,
         1_000_000,
     )
@@ -548,8 +564,8 @@
     sums2, x = call(
         child_between,
         [sums, field],
-        [sum_scratch] + halo_scratch,
-        [solved, rates, land, relax, pa, *halos],
+        [sum_scratch] + edge_scratch,
+        [inner, row_rates, column_rates, relax, pa, *halos],
         8_000_000,
         3_000_000,
     )
@@ -564,11 +580,19 @@
         3_000_000,
     )
     halos = halos_of(mate, far, cols)
+    inner, row_rates, column_rates = call(
+        child_inner,
+        [field, factor, factor],
+        [],
+        [solved, rates, land, cols],
+        INNER,
+        4_000_000,
+    )
     packed_rates = call(
         parent_rates_packed,
         shape(4, half, LANES),
         [],
-        [parent_rates.reshape(-1, narrow), feed, cols],
+        [parent_rates.reshape(-1, narrow), feed, inner],
         1_450_000_000,
         1_000_000,
     )
@@ -593,8 +617,8 @@
     child_out = call(
         child_last,
         field,
-        [pltpu.VMEM(field.shape, F32)] + halo_scratch + [pltpu.SemaphoreType.DMA((depth // LEVELS,))],
-        [solved, rates, land, *halos],
+        [pltpu.VMEM(field.shape, F32)] + edge_scratch + [pltpu.SemaphoreType.DMA((depth // LEVELS,))],
+        [inner, row_rates, column_rates, *halos],
         4_000_000,
         3_000_000,
         far_out=True,

time: 35.9 us -> 35.6 us (level)
  waiting for transfers between devices: 7.5 us -> 5.84 us
  Pallas kernels: 10.5 us -> 11.6 us
    pallas_call x11 -> x13, Pallas kernels: 10.5 us -> 11.6 us  [call(): pl.pallas_call(body, out_shape=outs, in_specs=[FAR if i in far_in else VM...]
    ppermute x2, waiting for transfers between devices: 0.91 us -> 0.01 us  [passed_along(): lax.ppermute(value, axis, [(i, (i + steps) % count) for i in range(count)])]
    ppermute x12, waiting for transfers between devices: 6.58 us -> 5.83 us  [swapped(): return lax.ppermute(value, axis, pairs)]
  transfers between devices with their start and end apart: 14 -> 14, of which waited for: 7 -> 6; matrix products, arithmetic and copies ran while one was open for 0% -> 0% of each run, Pallas kernels for 13% -> 18%
where the time goes in v6:
time: 35.6 us; the launch traced here: 35.5 us
  starting transfers between devices  17.2 us (48%)
  Pallas kernels  11.6 us (33%)
  waiting for transfers between devices  5.84 us (16%)
  between operations  0.78 us (2%)
    ppermute x12, starting transfers between devices, swapped(): return lax.ppermute(value, axis, pairs)  13.9 us
    pallas_call x13, Pallas kernels, call(): pl.pallas_call(body, out_shape=outs, in_specs=[FAR if i in far_in else VM...  11.6 us
    ppermute x12, waiting for transfers between devices, swapped(): return lax.ppermute(value, axis, pairs)  5.83 us
    ppermute x2, starting transfers between devices, passed_along(): lax.ppermute(value, axis, [(i, (i + steps) % count) for i in range(count)])  3.3 us
  transfers between devices with their start and end apart: 14, of which 6 were waited for; matrix products, arithmetic and copies ran while one was open for 0% of the time, Pallas kernels for 18%

profile of v6, /device:TPU:0, one launch (start us, length us, event | category | flops | bytes accessed | tf_op | source)
XLA Modules:
  0.0 35.5 jit_solution(6162519269383522732)
XLA Ops:
  0.6 2.3 %begin.1 = (f32[128,128]{1,0:T(8,128)S(1)}, f32[32,8,8,128]{3,2,1,0:T(8,128)S(1)}, f32[32,8,128]{2,1,0:T(8,128)S(1)}, f32[32,8,128]{2,1,0:T(8,128)S(1)}, f32[32,...) custom-call(f32[32,8,8,128]{3,2,1,0:T(8,128)} %x_hbm.1, ...), custom_call_target="tpu_custom_call" | custom-call | flops 4000000 | bytes 3000000 | tf_op jit(solution)/shard_map/begin/pallas_call | solution.py:24
  2.9 3.1 %collective-permute-start = (f32[128,128]{1,0:T(8,128)S(1)}, f32[128,128]{1,0:T(8,128)S(1)}, u32[]{:S(2)}, u32[]{:S(2)}) collective-permute-start(f32[128,128]{1,0:T(8,128)S(1)} %get-tuple-element.47), channel_id=1, source_target_pairs={{0,2},{1,3},{2,4},{3,5},{4,6},{5,7},{6,0},{7,1},{8,10},{9,11},{10,... | collective-permute-start | bytes 196616 | tf_op jit(solution)/shard_map/ppermute | solution.py:474
  6.0 0.8 %child_first.1 = (f32[32,8,8,128]{3,2,1,0:T(8,128)S(1)}, f32[256,128]{1,0:T(8,128)S(1)}, f32[256,128]{1,0:T(8,128)S(1)}, f32[32,128]{1,0:T(8,128)S(1)}) custom-call(f32[32,8,8,128]{3,2,1,0:T(8,128)S(1)} %get-tuple-element.35.x_ref, f32[32,8,128]{2,1,0:T(8,128)S(1)} %get-tuple-element.36.a_ref, f32[32,8,128]{2,1,0:T(8,128)S(1)} %get-tuple-element.37.b_ref, ...), custom_call_target="tpu_custom_call" | custom-call | flops 4000000 | bytes 3000000 | tf_op jit(solution)/shard_map/child_first/pallas_call | solution.py:24
  6.8 1.5 %collective-permute-start.1 = (f32[256,128]{1,0:T(8,128)S(1)}, f32[256,128]{1,0:T(8,128)S(1)}, u32[]{:S(2)}, u32[]{:S(2)}) collective-permute-start(f32[256,128]{1,0:T(8,128)S(1)} %get-tuple-element.48), channel_id=1, source_target_pairs={{1,2},{2,1},{3,4},{4,3},{5,6},{6,5},{7,0},{0,7},{9,10},{10,9},{11,... | collective-permute-start | bytes 393224 | tf_op jit(solution)/shard_map/ppermute | solution.py:483
  8.3 2.4 %collective-permute-start.3 = (f32[32,128]{1,0:T(8,128)S(1)}, f32[32,128]{1,0:T(8,128)S(1)}, u32[]{:S(2)}, u32[]{:S(2)}) collective-permute-start(f32[32,128]{1,0:T(8,128)S(1)} %get-tuple-element.42.after_ref), channel_id=1, source_target_pairs={{8,16},{16,8},{24,0},{0,24},{9,17},{17,9},{25,1},{1,25},{10,18},{1... | collective-permute-start | bytes 49160 | tf_op jit(solution)/shard_map/ppermute | solution.py:483
  10.8 0.5 %collective-permute-start.2 = (f32[32,128]{1,0:T(8,128)S(1)}, f32[32,128]{1,0:T(8,128)S(1)}, u32[]{:S(2)}, u32[]{:S(2)}) collective-permute-start(f32[32,128]{1,0:T(8,128)S(1)} %get-tuple-element.42.after_ref), channel_id=1, source_target_pairs={{0,8},{8,0},{16,24},{24,16},{1,9},{9,1},{17,25},{25,17},{2,10},{10... | collective-permute-start | bytes 49160 | tf_op jit(solution)/shard_map/ppermute | solution.py:483
  11.3 1.1 %child_inner.2 = (f32[32,8,8,128]{3,2,1,0:T(8,128)S(1)}, f32[32,8,128]{2,1,0:T(8,128)S(1)}, f32[32,8,128]{2,1,0:T(8,128)S(1)}) custom-call(f32[32,8,8,128]{3,2,1,0:T(8,128)S(1)} %get-tuple-element.39.solved_ref, f32[4,32,8,128]{3,2,1,0:T(8,128)S(1)} %get-tuple-element.40.rates_ref, f32[8,128]{1,0:T(8,128)S(1)} %get-tuple-element.41.land_ref, ...), custom_call_target="tpu_custom_call" | custom-call | flops 10000000 | bytes 4000000 | tf_op jit(solution)/shard_map/child_inner/pallas_call | solution.py:24
  13.0 1.5 %collective-permute-done.2.mate_cols = f32[32,128]{1,0:T(8,128)S(1)} collective-permute-done((f32[32,128]{1,0:T(8,128)S(1)}, f32[32,128]{1,0:T(8,128)S(1)}, u32[]{:S(2)}, u32[]{:S(2)}) %collective-permute-start.2) | collective-permute-done | bytes 16416 | tf_op jit(solution)/shard_map/ppermute | solution.py:483
  14.7 1.7 %child_between.1 = (f32[128,128]{1,0:T(8,128)S(1)}, f32[32,8,8,128]{3,2,1,0:T(8,128)S(1)}) custom-call(f32[32,8,8,128]{3,2,1,0:T(8,128)S(1)} %get-tuple-element.43.after_ref.inner_ref, f32[32,8,128]{2,1,0:T(8,128)S(1)} %get-tuple-element.44.row_ref, f32[32,8,128]{2,1,0:T(8,128)S(1)} %get-tuple-element.45.column_ref, ...), custom_call_target="tpu_custom_call" | custom-call | flops 8000000 | bytes 3000000 | tf_op jit(solution)/shard_map/child_between/pallas_call | solution.py:24
  16.6 1.0 %child_second.1 = (f32[32,8,8,128]{3,2,1,0:T(8,128)S(1)}, f32[16,8,128]{2,1,0:T(8,128)S(1)}, f32[320,128]{1,0:T(8,128)S(1)}, f32[320,128]{1,0:T(8,128)S(1)}, f32[40,128]{1,0:T(8,128)S(1)}) custom-call(f32[32,8,8,128]{3,2,1,0:T(8,128)S(1)} %get-tuple-element.51.x_ref, f32[32,8,128]{2,1,0:T(8,128)S(1)} %get-tuple-element.36.a_ref, ...), custom_call_target="tpu_custom_call" | custom-call | flops 8000000 | bytes 3000000 | tf_op jit(solution)/shard_map/child_second/pallas_call | solution.py:24
  17.7 2.2 %collective-permute-start.6 = (f32[320,128]{1,0:T(8,128)S(1)}, f32[320,128]{1,0:T(8,128)S(1)}, u32[]{:S(2)}, u32[]{:S(2)}) collective-permute-start(f32[320,128]{1,0:T(8,128)S(1)} %get-tuple-element.60), channel_id=1, source_target_pairs={{1,2},{2,1},{3,4},{4,3},{5,6},{6,5},{7,0},{0,7},{9,10},{10,9},{11,... | collective-permute-start | bytes 491528 | tf_op jit(solution)/shard_map/ppermute | solution.py:483
  19.9 1.4 %collective-permute-start.8 = (f32[40,128]{1,0:T(8,128)S(1)}, f32[40,128]{1,0:T(8,128)S(1)}, u32[]{:S(2)}, u32[]{:S(2)}) collective-permute-start(f32[40,128]{1,0:T(8,128)S(1)} %get-tuple-element.55.after_ref), channel_id=1, source_target_pairs={{8,16},{16,8},{24,0},{0,24},{9,17},{17,9},{25,1},{1,25},{10,18},{1... | collective-permute-start | bytes 61448 | tf_op jit(solution)/shard_map/ppermute | solution.py:483
  21.3 0.5 %collective-permute-start.7 = (f32[40,128]{1,0:T(8,128)S(1)}, f32[40,128]{1,0:T(8,128)S(1)}, u32[]{:S(2)}, u32[]{:S(2)}) collective-permute-start(f32[40,128]{1,0:T(8,128)S(1)} %get-tuple-element.55.after_ref), channel_id=1, source_target_pairs={{0,8},{8,0},{16,24},{24,16},{1,9},{9,1},{17,25},{25,17},{2,10},{10... | collective-permute-start | bytes 61448 | tf_op jit(solution)/shard_map/ppermute | solution.py:483
  21.9 1.1 %child_inner.3 = (f32[32,8,8,128]{3,2,1,0:T(8,128)S(1)}, f32[32,8,128]{2,1,0:T(8,128)S(1)}, f32[32,8,128]{2,1,0:T(8,128)S(1)}) custom-call(f32[32,8,8,128]{3,2,1,0:T(8,128)S(1)} %get-tuple-element.54.solved_ref, f32[4,32,8,128]{3,2,1,0:T(8,128)S(1)} %get-tuple-element.40.rates_ref, f32[8,128]{1,0:T(8,128)S(1)} %get-tuple-element.41.land_ref, ...), custom_call_target="tpu_custom_call" | custom-call | flops 10000000 | bytes 4000000 | tf_op jit(solution)/shard_map/child_inner/pallas_call | solution.py:24
  23.3 1.3 %collective-permute-done.8.far_cols = f32[40,128]{1,0:T(8,128)S(1)} collective-permute-done((f32[40,128]{1,0:T(8,128)S(1)}, f32[40,128]{1,0:T(8,128)S(1)}, u32[]{:S(2)}, u32[]{:S(2)}) %collective-permute-start.8) | collective-permute-done | bytes 20512 | tf_op jit(solution)/shard_map/ppermute | solution.py:483
  24.6 0.5 %collective-permute-done.7.mate_cols = f32[40,128]{1,0:T(8,128)S(1)} collective-permute-done((f32[40,128]{1,0:T(8,128)S(1)}, f32[40,128]{1,0:T(8,128)S(1)}, u32[]{:S(2)}, u32[]{:S(2)}) %collective-permute-start.7) | collective-permute-done | bytes 20512 | tf_op jit(solution)/shard_map/ppermute | solution.py:483
  25.1 0.6 %collective-permute-done.6.far_in.far_ref = f32[320,128]{1,0:T(8,128)S(1)} collective-permute-done((f32[320,128]{1,0:T(8,128)S(1)}, f32[320,128]{1,0:T(8,128)S(1)}, u32[]{:S(2)}, u32[]{:S(2)}) %collective-permute-start.6) | collective-permute-done | bytes 163872 | tf_op jit(solution)/shard_map/ppermute | solution.py:483
  25.9 0.4 %parent_second.1 = (f32[16,8,128]{2,1,0:T(8,128)S(1)}, f32[64,128]{1,0:T(8,128)S(1)}, f32[64,128]{1,0:T(8,128)S(1)}, f32[8,128]{1,0:T(8,128)S(1)}) custom-call(f32[16,8,128]{2,1,0:T(8,128)S(1)} %get-tuple-element.61.psolved_in, f32[5,16,128]{2,1,0:T(8,128)S(1)} %parent_rates_masked.1.prates_ref, f32[16,128]{1,0:T(8,128)S(1)} %get-tuple-element.49.after_ref.pa_ref, ...), custom_call_target="tpu_custom_call" | custom-call | flops 1000000 | bytes 500000 | tf_op jit(solution)/shard_map/parent_second/pallas_call | solution.py:24
  26.3 2.2 %collective-permute-start.11 = (f32[64,128]{1,0:T(8,128)S(1)}, f32[64,128]{1,0:T(8,128)S(1)}, u32[]{:S(2)}, u32[]{:S(2)}) collective-permute-start(f32[64,128]{1,0:T(8,128)S(1)} %get-tuple-element.66), channel_id=1, source_target_pairs={{1,2},{2,1},{3,4},{4,3},{5,6},{6,5},{7,0},{0,7},{9,10},{10,9},{11,... | collective-permute-start | bytes 98312 | tf_op jit(solution)/shard_map/ppermute | solution.py:483
  28.5 2.3 %collective-permute-start.13 = (f32[8,128]{1,0:T(8,128)S(1)}, f32[8,128]{1,0:T(8,128)S(1)}, u32[]{:S(2)}, u32[]{:S(2)}) collective-permute-start(f32[8,128]{1,0:T(8,128)S(1)} %get-tuple-element.67), channel_id=1, source_target_pairs={{8,16},{16,8},{24,0},{0,24},{9,17},{17,9},{25,1},{1,25},{10,18},{1... | collective-permute-start | bytes 12296 | tf_op jit(solution)/shard_map/ppermute | solution.py:483
  30.9 0.5 %collective-permute-start.12 = (f32[8,128]{1,0:T(8,128)S(1)}, f32[8,128]{1,0:T(8,128)S(1)}, u32[]{:S(2)}, u32[]{:S(2)}) collective-permute-start(f32[8,128]{1,0:T(8,128)S(1)} %get-tuple-element.67), channel_id=1, source_target_pairs={{0,8},{8,0},{16,24},{24,16},{1,9},{9,1},{17,25},{25,17},{2,10},{10... | collective-permute-start | bytes 12296 | tf_op jit(solution)/shard_map/ppermute | solution.py:483
  31.4 1.6 %child_last.1 = f32[32,8,8,128]{3,2,1,0:T(8,128)} custom-call(f32[32,8,8,128]{3,2,1,0:T(8,128)S(1)} %get-tuple-element.56.inner_ref.after_ref, f32[32,8,128]{2,1,0:T(8,128)S(1)} %get-tuple-element.57.row_ref, f32[32,8,128]{2,1,0:T(8,128)S(1)} %get-tuple-element.58.column_ref, f32[320,128]{1,0:T(8,128)S(1)} %collective-permute-done.5.mate_in, ...), custom_call_target="tpu_custom_call" | custom-call | flops 4000000 | bytes 3000000 | tf_op jit(solution)/shard_map/child_last/pallas_call | solution.py:24
  33.1 1.4 %collective-permute-done.12.mate_cols = f32[8,128]{1,0:T(8,128)S(1)} collective-permute-done((f32[8,128]{1,0:T(8,128)S(1)}, f32[8,128]{1,0:T(8,128)S(1)}, u32[]{:S(2)}, u32[]{:S(2)}) %collective-permute-start.12) | collective-permute-done | bytes 4128 | tf_op jit(solution)/shard_map/ppermute | solution.py:483
  34.5 1.0 %parent_last.1 = f32[512,32]{1,0:T(8,128)} custom-call(f32[16,8,128]{2,1,0:T(8,128)S(1)} %get-tuple-element.64.psolved_in, f32[5,16,128]{2,1,0:T(8,128)S(1)} %parent_rates_masked.1.prates_ref, f32[64,128]{1,0:T(8,128)S(1)} %collective-permute-done.10.mate_in, f32[64,128]{1,0:T(8,128)S(1)} %collective-permute-done.11.far_in, ...), custom_call_target="tpu_custom_call" | custom-call | flops 500000 | bytes 500000 | tf_op jit(solution)/shard_map/parent_last/pallas_call | solution.py:24
  (23 shorter events, 1.3 us)
Async XLA Ops:
  2.9 9.6 %collective-permute-start = (f32[128,128]{1,0:T(8,128)S(1)}, f32[128,128]{1,0:T(8,128)S(1)}, u32[]{:S(2)}, u32[]{:S(2)}) collective-permute-start(f32[128,128]{1,0:T(8,128)S(1)} %get-tuple-element.47), channel_id=1, source_target_pairs={{0,2},{1,3},{2,4},{3,5},{4,6},{5,7},{6,0},{7,1},{8,10},{9,11},{10,... | collective-permute-start | bytes 196616 | tf_op jit(solution)/shard_map/ppermute | solution.py:474
  6.8 7.7 %collective-permute-start.1 = (f32[256,128]{1,0:T(8,128)S(1)}, f32[256,128]{1,0:T(8,128)S(1)}, u32[]{:S(2)}, u32[]{:S(2)}) collective-permute-start(f32[256,128]{1,0:T(8,128)S(1)} %get-tuple-element.48), channel_id=1, source_target_pairs={{1,2},{2,1},{3,4},{4,3},{5,6},{6,5},{7,0},{0,7},{9,10},{10,9},{11,... | collective-permute-start | bytes 393224 | tf_op jit(solution)/shard_map/ppermute | solution.py:483
  8.3 4.6 %collective-permute-start.3 = (f32[32,128]{1,0:T(8,128)S(1)}, f32[32,128]{1,0:T(8,128)S(1)}, u32[]{:S(2)}, u32[]{:S(2)}) collective-permute-start(f32[32,128]{1,0:T(8,128)S(1)} %get-tuple-element.42.after_ref), channel_id=1, source_target_pairs={{8,16},{16,8},{24,0},{0,24},{9,17},{17,9},{25,1},{1,25},{10,18},{1... | collective-permute-start | bytes 49160 | tf_op jit(solution)/shard_map/ppermute | solution.py:483
  10.8 3.7 %collective-permute-start.2 = (f32[32,128]{1,0:T(8,128)S(1)}, f32[32,128]{1,0:T(8,128)S(1)}, u32[]{:S(2)}, u32[]{:S(2)}) collective-permute-start(f32[32,128]{1,0:T(8,128)S(1)} %get-tuple-element.42.after_ref), channel_id=1, source_target_pairs={{0,8},{8,0},{16,24},{24,16},{1,9},{9,1},{17,25},{25,17},{2,10},{10... | collective-permute-start | bytes 49160 | tf_op jit(solution)/shard_map/ppermute | solution.py:483
  11.3 3.4 %collective-permute-start.4 = (f32[256,128]{1,0:T(8,128)S(1)}, f32[256,128]{1,0:T(8,128)S(1)}, u32[]{:S(2)}, u32[]{:S(2)}) collective-permute-start(f32[256,128]{1,0:T(8,128)S(1)} %get-tuple-element.50), channel_id=1, source_target_pairs={{0,1},{1,0},{2,3},{3,2},{4,5},{5,4},{6,7},{7,6},{8,9},{9,8},{10,11... | collective-permute-start | bytes 393224 | tf_op jit(solution)/shard_map/ppermute | solution.py:483
  11.3 1.1 %copy-start = (f32[32,8,2,32]{3,2,1,0:T(2,128)S(1)}, f32[32,8,2,32]{3,2,1,0:T(2,128)}, u32[]{:S(2)}) copy-start(f32[32,8,2,32]{3,2,1,0:T(2,128)} %param.10) | copy-start | bytes 196612
  12.5 2.1 %copy-start.2 = (f32[32,2,32]{2,1,0:T(2,128)S(1)}, f32[32,2,32]{2,1,0:T(2,128)}, u32[]{:S(2)}) copy-start(f32[32,2,32]{2,1,0:T(2,128)} %param.15) | copy-start | bytes 24580
  16.4 6.6 %collective-permute-start.9 = (f32[128,128]{1,0:T(8,128)S(1)}, f32[128,128]{1,0:T(8,128)S(1)}, u32[]{:S(2)}, u32[]{:S(2)}) collective-permute-start(f32[128,128]{1,0:T(8,128)S(1)} %get-tuple-element.62), channel_id=1, source_target_pairs={{0,2},{1,3},{2,4},{3,5},{4,6},{5,7},{6,0},{7,1},{8,10},{9,11},{10,... | collective-permute-start | bytes 196616 | tf_op jit(solution)/shard_map/ppermute | solution.py:474
  17.7 8.1 %collective-permute-start.6 = (f32[320,128]{1,0:T(8,128)S(1)}, f32[320,128]{1,0:T(8,128)S(1)}, u32[]{:S(2)}, u32[]{:S(2)}) collective-permute-start(f32[320,128]{1,0:T(8,128)S(1)} %get-tuple-element.60), channel_id=1, source_target_pairs={{1,2},{2,1},{3,4},{4,3},{5,6},{6,5},{7,0},{0,7},{9,10},{10,9},{11,... | collective-permute-start | bytes 491528 | tf_op jit(solution)/shard_map/ppermute | solution.py:483
  19.9 4.7 %collective-permute-start.8 = (f32[40,128]{1,0:T(8,128)S(1)}, f32[40,128]{1,0:T(8,128)S(1)}, u32[]{:S(2)}, u32[]{:S(2)}) collective-permute-start(f32[40,128]{1,0:T(8,128)S(1)} %get-tuple-element.55.after_ref), channel_id=1, source_target_pairs={{8,16},{16,8},{24,0},{0,24},{9,17},{17,9},{25,1},{1,25},{10,18},{1... | collective-permute-start | bytes 61448 | tf_op jit(solution)/shard_map/ppermute | solution.py:483
  21.3 3.8 %collective-permute-start.7 = (f32[40,128]{1,0:T(8,128)S(1)}, f32[40,128]{1,0:T(8,128)S(1)}, u32[]{:S(2)}, u32[]{:S(2)}) collective-permute-start(f32[40,128]{1,0:T(8,128)S(1)} %get-tuple-element.55.after_ref), channel_id=1, source_target_pairs={{0,8},{8,0},{16,24},{24,16},{1,9},{9,1},{17,25},{25,17},{2,10},{10... | collective-permute-start | bytes 61448 | tf_op jit(solution)/shard_map/ppermute | solution.py:483
  21.9 4.0 %collective-permute-start.5 = (f32[320,128]{1,0:T(8,128)S(1)}, f32[320,128]{1,0:T(8,128)S(1)}, u32[]{:S(2)}, u32[]{:S(2)}) collective-permute-start(f32[320,128]{1,0:T(8,128)S(1)} %get-tuple-element.59), channel_id=1, source_target_pairs={{0,1},{1,0},{2,3},{3,2},{4,5},{5,4},{6,7},{7,6},{8,9},{9,8},{10,11... | collective-permute-start | bytes 491528 | tf_op jit(solution)/shard_map/ppermute | solution.py:483
  21.9 1.1 %copy-start.1 = (f32[4,32,2,32]{3,2,1,0:T(2,128)S(1)}, f32[4,32,2,32]{3,2,1,0:T(2,128)}, u32[]{:S(2)}) copy-start(f32[4,32,2,32]{3,2,1,0:T(2,128)} %param.14) | copy-start | bytes 98308
  26.2 8.2 %collective-permute-start.10 = (f32[64,128]{1,0:T(8,128)S(1)}, f32[64,128]{1,0:T(8,128)S(1)}, u32[]{:S(2)}, u32[]{:S(2)}) collective-permute-start(f32[64,128]{1,0:T(8,128)S(1)} %get-tuple-element.65), channel_id=1, source_target_pairs={{0,1},{1,0},{2,3},{3,2},{4,5},{5,4},{6,7},{7,6},{8,9},{9,8},{10,11... | collective-permute-start | bytes 98312 | tf_op jit(solution)/shard_map/ppermute | solution.py:483
  26.3 8.2 %collective-permute-start.11 = (f32[64,128]{1,0:T(8,128)S(1)}, f32[64,128]{1,0:T(8,128)S(1)}, u32[]{:S(2)}, u32[]{:S(2)}) collective-permute-start(f32[64,128]{1,0:T(8,128)S(1)} %get-tuple-element.66), channel_id=1, source_target_pairs={{1,2},{2,1},{3,4},{4,3},{5,6},{6,5},{7,0},{0,7},{9,10},{10,9},{11,... | collective-permute-start | bytes 98312 | tf_op jit(solution)/shard_map/ppermute | solution.py:483
  28.5 4.5 %collective-permute-start.13 = (f32[8,128]{1,0:T(8,128)S(1)}, f32[8,128]{1,0:T(8,128)S(1)}, u32[]{:S(2)}, u32[]{:S(2)}) collective-permute-start(f32[8,128]{1,0:T(8,128)S(1)} %get-tuple-element.67), channel_id=1, source_target_pairs={{8,16},{16,8},{24,0},{0,24},{9,17},{17,9},{25,1},{1,25},{10,18},{1... | collective-permute-start | bytes 12296 | tf_op jit(solution)/shard_map/ppermute | solution.py:483
  30.9 3.6 %collective-permute-start.12 = (f32[8,128]{1,0:T(8,128)S(1)}, f32[8,128]{1,0:T(8,128)S(1)}, u32[]{:S(2)}, u32[]{:S(2)}) collective-permute-start(f32[8,128]{1,0:T(8,128)S(1)} %get-tuple-element.67), channel_id=1, source_target_pairs={{0,8},{8,0},{16,24},{24,16},{1,9},{9,1},{17,25},{25,17},{2,10},{10... | collective-permute-start | bytes 12296 | tf_op jit(solution)/shard_map/ppermute | solution.py:483

commit v7 on v6

--- a/solution.py
+++ b/solution.py
@@ -89,10 +89,14 @@
     wide = sums_ref.shape[1]
     p = lax.broadcasted_iota(jnp.int32, (wide, LANES), 0)
     q = lax.broadcasted_iota(jnp.int32, (wide, LANES), 1)
-    pick = jnp.where(p // 4 == q, F32(0.0625), F32(0.0))
-    return jnp.dot(
-        sums_ref[...], pick, precision=lax.Precision.HIGHEST, preferred_element_type=F32
-    )
+    pick = jnp.where(p // 4 == q, F32(0.0625), F32(0.0)).astype(jnp.bfloat16)
+    rest, total = sums_ref[...], None
+    for _ in range(3):
+        part = rest.astype(jnp.bfloat16)
+        rest = rest - part.astype(F32)
+        product = jnp.dot(part, pick, preferred_element_type=F32)
+        total = product if total is None else total + product
+    return total
 
 
 def child_middle(carry, c_ref, half):
@@ -154,8 +158,8 @@
 
 
 def begin(
-    x_hbm, mix_hbm, relax_hbm, land_hbm, parent_land_hbm, rates_hbm,
-    sums_out, x_ref, a_ref, b_ref, c_ref, relax_ref, land_ref, parent_land_ref, rates_ref,
+    x_hbm, mix_hbm, relax_hbm, land_hbm, parent_land_hbm,
+    sums_out, x_ref, a_ref, b_ref, c_ref, relax_ref, land_ref, parent_land_ref,
     mix_ref, land_in, parent_land_in, sums_ref, sems,
 ):
     depth = x_ref.shape[0]
@@ -172,8 +176,6 @@
             part = pl.ds(first, size)
             large.append(pltpu.make_async_copy(x_hbm.at[part], x_ref.at[part], sems.at[len(large) + len(small)]))
             large[-1].start()
-    rates_copy = pltpu.make_async_copy(rates_hbm, rates_ref, sems.at[len(large) + len(small)])
-    rates_copy.start()
     for copy in small:
         copy.wait()
     land_ref[...] = land_in[...].astype(F32)
@@ -191,10 +193,18 @@
         large[2 * part + 1].wait()
         lax.fori_loop(start, start + size, level, 0, unroll=size)
     sums_out[...] = block_columns(sums_ref)
-    rates_copy.wait()
-
-
-def child_first(x_ref, a_ref, b_ref, c_ref, solved_ref, mate_rows, far_rows, cols_ref):
+
+
+def child_first(
+    x_ref, a_ref, b_ref, c_ref, rates_hbm, solved_ref, mate_rows, far_rows, cols_ref, rates_ref, sem
+):
+    copy = pltpu.make_async_copy(rates_hbm, rates_ref, sem)
+    copy.start()
+    child_solve(x_ref, a_ref, b_ref, c_ref, solved_ref, mate_rows, far_rows, cols_ref)
+    copy.wait()
+
+
+def child_solve(x_ref, a_ref, b_ref, c_ref, solved_ref, mate_rows, far_rows, cols_ref):
     depth, vectors = x_ref.shape[0], x_ref.shape[1]
     half = depth // 2
 
@@ -250,16 +260,19 @@
         merged_ref[part, :] = merge_edges(mate_cols[part, :], far_cols[part, :], LANES - 2)
 
 
-def edged(inner_ref, row_rates, column_rates, mate_ref, far_ref, edges, k, v, at, mates):
-    line = pl.ds(k * inner_ref.shape[1] + v, 1)
-    mate = jnp.broadcast_to(mate_ref[line, :], (8, LANES))
-    far = jnp.broadcast_to(far_ref[line, :], (8, LANES))
-    edge = pltpu.roll(edges, (LANES - 2 * at) & (LANES - 1), 1)
-    return inner_ref[k, v] + row_rates * jnp.where(mates, mate, far) + column_rates * edge
-
-
-def mate_rows_mask():
-    return row_index() == 7 * (1 - parity("gy"))
+def column_edges(target_ref, inner_ref, column_ref, edges, k, base):
+    rates = column_ref[k]
+    for v in range(inner_ref.shape[1]):
+        edge = pltpu.roll(edges, (LANES - 2 * (base + v)) & (LANES - 1), 1)
+        target_ref[k, v] = inner_ref[k, v] + rates * edge
+
+
+def row_edges(target_ref, row_ref, mate_ref, far_ref, k):
+    vectors = target_ref.shape[1]
+    odd = parity("gy")
+    for halo_ref, at in ((mate_ref, 7 * (1 - odd)), (far_ref, 7 * odd)):
+        part = row_ref[k, pl.ds(at, 1), :] * halo_ref[pl.ds(pl.multiple_of(k * vectors, vectors), vectors), :]
+        target_ref[k, :, at, :] = target_ref[k, :, at, :] + part
 
 
 def child_between(
@@ -268,27 +281,31 @@
     sums_ref, merged_ref,
 ):
     depth, vectors = inner_ref.shape[0], inner_ref.shape[1]
-    half, groups = depth // 2, depth // LEVELS
-    mates = mate_rows_mask()
+    half = depth // 2
     weights = [relax_ref[j : j + 1, :] for j in range(8)]
     edge_merger(mate_cols, far_cols, merged_ref)
-
-    def level(i, _, edges):
-        inside = lax.rem(i, LEVELS)
-        for side, k, base in ((0, i, inside * vectors), (1, depth - 1 - i, (LEVELS - 1 - inside) * vectors)):
-            row_rates, column_rates = row_ref[k], column_ref[k]
-            for v in range(vectors):
-                x_ref[k, v] = edged(
-                    inner_ref, row_rates, column_rates, mate_in, far_in, edges[side], k, v, base + v, mates
-                )
+    for group in range(depth // LEVELS):
+        edges = merged_ref[8 * group : 8 * group + 8, :]
+        first = LEVELS * group
+
+        def columns(inside, _):
+            column_edges(x_ref, inner_ref, column_ref, edges, first + inside, inside * vectors)
+            return 0
+
+        lax.fori_loop(0, LEVELS, columns, 0, unroll=4)
+
+    def rows(k, _):
+        row_edges(x_ref, row_ref, mate_in, far_in, k)
+        return 0
+
+    lax.fori_loop(0, depth, rows, 0, unroll=8)
+
+    def level(i, _):
+        for side, k in ((0, i), (1, depth - 1 - i)):
             block_rows(x_ref, k, weights, sums_ref, i, side)
         return 0
 
-    for group in range(half // LEVELS):
-        edges = [merged_ref[8 * g : 8 * g + 8, :] for g in (group, groups - 1 - group)]
-        lax.fori_loop(
-            LEVELS * group, LEVELS * (group + 1), lambda i, _, edges=edges: level(i, _, edges), 0, unroll=4
-        )
+    lax.fori_loop(0, half, level, 0, unroll=4)
     sums_out[...] = block_columns(sums_ref)
 
 
@@ -303,30 +320,30 @@
         psolved_ref[i] = y
     lines, at = depth * vectors, depth // LEVELS * 8
     parent_up(y, pc_ref, psolved_ref, mate_rows, far_rows, lines, cols_ref, at)
-    child_first(x_ref, a_ref, b_ref, c_ref, solved_ref, mate_rows, far_rows, cols_ref)
+    child_solve(x_ref, a_ref, b_ref, c_ref, solved_ref, mate_rows, far_rows, cols_ref)
 
 
 def child_last(
     inner_ref, row_ref, column_ref, mate_in, far_in, mate_cols, far_cols, out_hbm, out_ref, merged_ref, sems
 ):
     depth, vectors = inner_ref.shape[0], inner_ref.shape[1]
-    mates = mate_rows_mask()
     edge_merger(mate_cols, far_cols, merged_ref)
     copies = []
     for group in range(depth // LEVELS):
         edges = merged_ref[8 * group : 8 * group + 8, :]
-
-        def level(inside, _):
-            k = LEVELS * group + inside
-            row_rates, column_rates = row_ref[k], column_ref[k]
-            for v in range(vectors):
-                out_ref[k, v] = edged(
-                    inner_ref, row_rates, column_rates, mate_in, far_in, edges, k, v, inside * vectors + v, mates
-                )
+        first = LEVELS * group
+
+        def columns(inside, _):
+            column_edges(out_ref, inner_ref, column_ref, edges, first + inside, inside * vectors)
             return 0
 
-        lax.fori_loop(0, LEVELS, level, 0, unroll=4)
-        part = pl.ds(LEVELS * group, LEVELS)
+        def rows(inside, _):
+            row_edges(out_ref, row_ref, mate_in, far_in, first + inside)
+            return 0
+
+        lax.fori_loop(0, LEVELS, columns, 0, unroll=4)
+        lax.fori_loop(0, LEVELS, rows, 0, unroll=LEVELS)
+        part = pl.ds(first, LEVELS)
         copies.append(pltpu.make_async_copy(out_ref.at[part], out_hbm.at[part], sems.at[group]))
         copies[-1].start()
     for copy in copies:
@@ -511,30 +528,30 @@
     edge_scratch = [pltpu.VMEM((edge, LANES), F32)]
     narrow = parent_adjoint.shape[-1]
 
-    sums1, x, a, b, c, relax, land, parent_land, rates = call(
+    sums1, x, a, b, c, relax, land, parent_land = call(
         begin,
-        [sums, field, factor, factor, factor, shape(lines, columns), shape(lines, columns), shape(*parent_land.shape)]
-        + [shape(*child_rates.shape)],
+        [sums, field, factor, factor, factor, shape(lines, columns), shape(lines, columns), shape(*parent_land.shape)],
         [
             pltpu.VMEM(factor.shape, F32),
             pltpu.VMEM(child_land.shape, jnp.int32),
             pltpu.VMEM(parent_land.shape, jnp.int32),
             sum_scratch,
-            pltpu.SemaphoreType.DMA((5 + half // 2,)),
+            pltpu.SemaphoreType.DMA((4 + half // 2,)),
         ],
-        [child_adjoint, child_mixing, relaxation, child_land, parent_land, child_rates],
+        [child_adjoint, child_mixing, relaxation, child_land, parent_land],
         4_000_000,
         3_000_000,
-        far_in=range(6),
+        far_in=range(5),
     )
     feed = passed_along(sums1, "gy", quarter)
-    solved, mate, far, cols = call(
+    solved, mate, far, cols, rates = call(
         child_first,
-        [field, shape(count, LANES), shape(count, LANES), shape(edge, LANES)],
-        [],
-        [x, a, b, c],
+        [field, shape(count, LANES), shape(count, LANES), shape(edge, LANES), shape(*child_rates.shape)],
+        [pltpu.SemaphoreType.DMA],
+        [x, a, b, c, child_rates],
         4_000_000,
         3_000_000,
+        far_in=(4,),
     )
     halos = halos_of(mate, far, cols)
     inner, row_rates, column_rates = call(

time: 35.6 us -> 36.7 us (1.031)
  Pallas kernels: 11.6 us -> 13.2 us
  waiting for transfers between devices: 5.84 us -> 5.26 us
    pallas_call x13, Pallas kernels: 11.6 us -> 13.2 us  [call(): pl.pallas_call(body, out_shape=outs, in_specs=[FAR if i in far_in else VM...]
    ppermute x12, waiting for transfers between devices: 5.83 us -> 5.26 us  [swapped(): return lax.ppermute(value, axis, pairs)]
  transfers between devices with their start and end apart: 14 -> 14, of which waited for: 6 -> 6; matrix products, arithmetic and copies ran while one was open for 0% -> 0% of each run, Pallas kernels for 18% -> 20%
where the time goes in v7:
time: 36.7 us; the launch traced here: 36.4 us
  starting transfers between devices  17.2 us (47%)
  Pallas kernels  13.2 us (36%)
  waiting for transfers between devices  5.26 us (14%)
  between operations  0.78 us (2%)
    ppermute x12, starting transfers between devices, swapped(): return lax.ppermute(value, axis, pairs)  13.9 us
    pallas_call x13, Pallas kernels, call(): pl.pallas_call(body, out_shape=outs, in_specs=[FAR if i in far_in else VM...  13.2 us
    ppermute x12, waiting for transfers between devices, swapped(): return lax.ppermute(value, axis, pairs)  5.26 us
    ppermute x2, starting transfers between devices, passed_along(): lax.ppermute(value, axis, [(i, (i + steps) % count) for i in range(count)])  3.3 us
  transfers between devices with their start and end apart: 14, of which 6 were waited for; matrix products, arithmetic and copies ran while one was open for 0% of the time, Pallas kernels for 20%

profile of v7, /device:TPU:0, one launch (start us, length us, event | category | flops | bytes accessed | tf_op | source)
XLA Modules:
  0.0 36.4 jit_solution(3514639521452525431)
XLA Ops:
  0.6 2.1 %begin.1 = (f32[128,128]{1,0:T(8,128)S(1)}, f32[32,8,8,128]{3,2,1,0:T(8,128)S(1)}, f32[32,8,128]{2,1,0:T(8,128)S(1)}, f32[32,8,128]{2,1,0:T(8,128)S(1)}, f32[32,...) custom-call(f32[32,8,8,128]{3,2,1,0:T(8,128)} %x_hbm.1, ...), custom_call_target="tpu_custom_call" | custom-call | flops 4000000 | bytes 3000000 | tf_op jit(solution)/shard_map/begin/pallas_call | solution.py:24
  2.7 3.1 %collective-permute-start = (f32[128,128]{1,0:T(8,128)S(1)}, f32[128,128]{1,0:T(8,128)S(1)}, u32[]{:S(2)}, u32[]{:S(2)}) collective-permute-start(f32[128,128]{1,0:T(8,128)S(1)} %get-tuple-element.47), channel_id=1, source_target_pairs={{0,2},{1,3},{2,4},{3,5},{4,6},{5,7},{6,0},{7,1},{8,10},{9,11},{10,... | collective-permute-start | bytes 196616 | tf_op jit(solution)/shard_map/ppermute | solution.py:491
  5.8 1.1 %child_first.1 = (f32[32,8,8,128]{3,2,1,0:T(8,128)S(1)}, f32[256,128]{1,0:T(8,128)S(1)}, f32[256,128]{1,0:T(8,128)S(1)}, f32[32,128]{1,0:T(8,128)S(1)}, f32[4,32,8,128]{3,2,1,0:T(8,128)S(1)}) custom-call(f32[32,8,8,128]{3,2,1,0:T(8,128)S(1)} %get-tuple-element.35.x_ref, f32[32,8,128]{2,1,0:T(8,128)S(1)} %get-tuple-element.36.a_ref, ...), custom_call_target="tpu_custom_call" | custom-call | flops 4000000 | bytes 3000000 | tf_op jit(solution)/shard_map/child_first/pallas_call | solution.py:24
  6.9 1.6 %collective-permute-start.1 = (f32[256,128]{1,0:T(8,128)S(1)}, f32[256,128]{1,0:T(8,128)S(1)}, u32[]{:S(2)}, u32[]{:S(2)}) collective-permute-start(f32[256,128]{1,0:T(8,128)S(1)} %get-tuple-element.48), channel_id=1, source_target_pairs={{1,2},{2,1},{3,4},{4,3},{5,6},{6,5},{7,0},{0,7},{9,10},{10,9},{11,... | collective-permute-start | bytes 393224 | tf_op jit(solution)/shard_map/ppermute | solution.py:500
  8.4 2.4 %collective-permute-start.3 = (f32[32,128]{1,0:T(8,128)S(1)}, f32[32,128]{1,0:T(8,128)S(1)}, u32[]{:S(2)}, u32[]{:S(2)}) collective-permute-start(f32[32,128]{1,0:T(8,128)S(1)} %get-tuple-element.42.after_ref), channel_id=1, source_target_pairs={{8,16},{16,8},{24,0},{0,24},{9,17},{17,9},{25,1},{1,25},{10,18},{1... | collective-permute-start | bytes 49160 | tf_op jit(solution)/shard_map/ppermute | solution.py:500
  10.9 0.5 %collective-permute-start.2 = (f32[32,128]{1,0:T(8,128)S(1)}, f32[32,128]{1,0:T(8,128)S(1)}, u32[]{:S(2)}, u32[]{:S(2)}) collective-permute-start(f32[32,128]{1,0:T(8,128)S(1)} %get-tuple-element.42.after_ref), channel_id=1, source_target_pairs={{0,8},{8,0},{16,24},{24,16},{1,9},{9,1},{17,25},{25,17},{2,10},{10... | collective-permute-start | bytes 49160 | tf_op jit(solution)/shard_map/ppermute | solution.py:500
  11.4 1.1 %child_inner.2 = (f32[32,8,8,128]{3,2,1,0:T(8,128)S(1)}, f32[32,8,128]{2,1,0:T(8,128)S(1)}, f32[32,8,128]{2,1,0:T(8,128)S(1)}) custom-call(f32[32,8,8,128]{3,2,1,0:T(8,128)S(1)} %get-tuple-element.39.solved_ref, f32[4,32,8,128]{3,2,1,0:T(8,128)S(1)} %get-tuple-element.40.rates_ref, f32[8,128]{1,0:T(8,128)S(1)} %get-tuple-element.41.land_ref, ...), custom_call_target="tpu_custom_call" | custom-call | flops 10000000 | bytes 4000000 | tf_op jit(solution)/shard_map/child_inner/pallas_call | solution.py:24
  13.1 1.5 %collective-permute-done.2.mate_cols = f32[32,128]{1,0:T(8,128)S(1)} collective-permute-done((f32[32,128]{1,0:T(8,128)S(1)}, f32[32,128]{1,0:T(8,128)S(1)}, u32[]{:S(2)}, u32[]{:S(2)}) %collective-permute-start.2) | collective-permute-done | bytes 16416 | tf_op jit(solution)/shard_map/ppermute | solution.py:500
  14.8 2.6 %child_between.1 = (f32[128,128]{1,0:T(8,128)S(1)}, f32[32,8,8,128]{3,2,1,0:T(8,128)S(1)}) custom-call(f32[32,8,8,128]{3,2,1,0:T(8,128)S(1)} %get-tuple-element.43.after_ref.inner_ref, f32[32,8,128]{2,1,0:T(8,128)S(1)} %get-tuple-element.44.row_ref, f32[32,8,128]{2,1,0:T(8,128)S(1)} %get-tuple-element.45.column_ref, ...), custom_call_target="tpu_custom_call" | custom-call | flops 8000000 | bytes 3000000 | tf_op jit(solution)/shard_map/child_between/pallas_call | solution.py:24
  17.6 1.0 %child_second.1 = (f32[32,8,8,128]{3,2,1,0:T(8,128)S(1)}, f32[16,8,128]{2,1,0:T(8,128)S(1)}, f32[320,128]{1,0:T(8,128)S(1)}, f32[320,128]{1,0:T(8,128)S(1)}, f32[40,128]{1,0:T(8,128)S(1)}) custom-call(f32[32,8,8,128]{3,2,1,0:T(8,128)S(1)} %get-tuple-element.51.x_ref, f32[32,8,128]{2,1,0:T(8,128)S(1)} %get-tuple-element.36.a_ref, ...), custom_call_target="tpu_custom_call" | custom-call | flops 8000000 | bytes 3000000 | tf_op jit(solution)/shard_map/child_second/pallas_call | solution.py:24
  18.6 2.2 %collective-permute-start.6 = (f32[320,128]{1,0:T(8,128)S(1)}, f32[320,128]{1,0:T(8,128)S(1)}, u32[]{:S(2)}, u32[]{:S(2)}) collective-permute-start(f32[320,128]{1,0:T(8,128)S(1)} %get-tuple-element.60), channel_id=1, source_target_pairs={{1,2},{2,1},{3,4},{4,3},{5,6},{6,5},{7,0},{0,7},{9,10},{10,9},{11,... | collective-permute-start | bytes 491528 | tf_op jit(solution)/shard_map/ppermute | solution.py:500
  20.9 1.4 %collective-permute-start.8 = (f32[40,128]{1,0:T(8,128)S(1)}, f32[40,128]{1,0:T(8,128)S(1)}, u32[]{:S(2)}, u32[]{:S(2)}) collective-permute-start(f32[40,128]{1,0:T(8,128)S(1)} %get-tuple-element.55.after_ref), channel_id=1, source_target_pairs={{8,16},{16,8},{24,0},{0,24},{9,17},{17,9},{25,1},{1,25},{10,18},{1... | collective-permute-start | bytes 61448 | tf_op jit(solution)/shard_map/ppermute | solution.py:500
  22.3 0.5 %collective-permute-start.7 = (f32[40,128]{1,0:T(8,128)S(1)}, f32[40,128]{1,0:T(8,128)S(1)}, u32[]{:S(2)}, u32[]{:S(2)}) collective-permute-start(f32[40,128]{1,0:T(8,128)S(1)} %get-tuple-element.55.after_ref), channel_id=1, source_target_pairs={{0,8},{8,0},{16,24},{24,16},{1,9},{9,1},{17,25},{25,17},{2,10},{10... | collective-permute-start | bytes 61448 | tf_op jit(solution)/shard_map/ppermute | solution.py:500
  22.9 1.1 %child_inner.3 = (f32[32,8,8,128]{3,2,1,0:T(8,128)S(1)}, f32[32,8,128]{2,1,0:T(8,128)S(1)}, f32[32,8,128]{2,1,0:T(8,128)S(1)}) custom-call(f32[32,8,8,128]{3,2,1,0:T(8,128)S(1)} %get-tuple-element.54.solved_ref, f32[4,32,8,128]{3,2,1,0:T(8,128)S(1)} %get-tuple-element.40.rates_ref, f32[8,128]{1,0:T(8,128)S(1)} %get-tuple-element.41.land_ref, ...), custom_call_target="tpu_custom_call" | custom-call | flops 10000000 | bytes 4000000 | tf_op jit(solution)/shard_map/child_inner/pallas_call | solution.py:24
  24.3 1.3 %collective-permute-done.8.far_cols = f32[40,128]{1,0:T(8,128)S(1)} collective-permute-done((f32[40,128]{1,0:T(8,128)S(1)}, f32[40,128]{1,0:T(8,128)S(1)}, u32[]{:S(2)}, u32[]{:S(2)}) %collective-permute-start.8) | collective-permute-done | bytes 20512 | tf_op jit(solution)/shard_map/ppermute | solution.py:500
  25.6 0.5 %collective-permute-done.7.mate_cols = f32[40,128]{1,0:T(8,128)S(1)} collective-permute-done((f32[40,128]{1,0:T(8,128)S(1)}, f32[40,128]{1,0:T(8,128)S(1)}, u32[]{:S(2)}, u32[]{:S(2)}) %collective-permute-start.7) | collective-permute-done | bytes 20512 | tf_op jit(solution)/shard_map/ppermute | solution.py:500
  26.1 0.6 %collective-permute-done.6.far_in.far_ref = f32[320,128]{1,0:T(8,128)S(1)} collective-permute-done((f32[320,128]{1,0:T(8,128)S(1)}, f32[320,128]{1,0:T(8,128)S(1)}, u32[]{:S(2)}, u32[]{:S(2)}) %collective-permute-start.6) | collective-permute-done | bytes 163872 | tf_op jit(solution)/shard_map/ppermute | solution.py:500
  26.8 0.4 %parent_second.1 = (f32[16,8,128]{2,1,0:T(8,128)S(1)}, f32[64,128]{1,0:T(8,128)S(1)}, f32[64,128]{1,0:T(8,128)S(1)}, f32[8,128]{1,0:T(8,128)S(1)}) custom-call(f32[16,8,128]{2,1,0:T(8,128)S(1)} %get-tuple-element.61.psolved_in, f32[5,16,128]{2,1,0:T(8,128)S(1)} %parent_rates_masked.1.prates_ref, f32[16,128]{1,0:T(8,128)S(1)} %get-tuple-element.49.after_ref.pa_ref, ...), custom_call_target="tpu_custom_call" | custom-call | flops 1000000 | bytes 500000 | tf_op jit(solution)/shard_map/parent_second/pallas_call | solution.py:24
  27.3 2.2 %collective-permute-start.11 = (f32[64,128]{1,0:T(8,128)S(1)}, f32[64,128]{1,0:T(8,128)S(1)}, u32[]{:S(2)}, u32[]{:S(2)}) collective-permute-start(f32[64,128]{1,0:T(8,128)S(1)} %get-tuple-element.66), channel_id=1, source_target_pairs={{1,2},{2,1},{3,4},{4,3},{5,6},{6,5},{7,0},{0,7},{9,10},{10,9},{11,... | collective-permute-start | bytes 98312 | tf_op jit(solution)/shard_map/ppermute | solution.py:500
  29.5 2.3 %collective-permute-start.13 = (f32[8,128]{1,0:T(8,128)S(1)}, f32[8,128]{1,0:T(8,128)S(1)}, u32[]{:S(2)}, u32[]{:S(2)}) collective-permute-start(f32[8,128]{1,0:T(8,128)S(1)} %get-tuple-element.67), channel_id=1, source_target_pairs={{8,16},{16,8},{24,0},{0,24},{9,17},{17,9},{25,1},{1,25},{10,18},{1... | collective-permute-start | bytes 12296 | tf_op jit(solution)/shard_map/ppermute | solution.py:500
  31.8 0.5 %collective-permute-start.12 = (f32[8,128]{1,0:T(8,128)S(1)}, f32[8,128]{1,0:T(8,128)S(1)}, u32[]{:S(2)}, u32[]{:S(2)}) collective-permute-start(f32[8,128]{1,0:T(8,128)S(1)} %get-tuple-element.67), channel_id=1, source_target_pairs={{0,8},{8,0},{16,24},{24,16},{1,9},{9,1},{17,25},{25,17},{2,10},{10... | collective-permute-start | bytes 12296 | tf_op jit(solution)/shard_map/ppermute | solution.py:500
  32.4 2.2 %child_last.1 = f32[32,8,8,128]{3,2,1,0:T(8,128)} custom-call(f32[32,8,8,128]{3,2,1,0:T(8,128)S(1)} %get-tuple-element.56.inner_ref.after_ref, f32[32,8,128]{2,1,0:T(8,128)S(1)} %get-tuple-element.57.row_ref, f32[32,8,128]{2,1,0:T(8,128)S(1)} %get-tuple-element.58.column_ref, f32[320,128]{1,0:T(8,128)S(1)} %collective-permute-done.5.mate_in, ...), custom_call_target="tpu_custom_call" | custom-call | flops 4000000 | bytes 3000000 | tf_op jit(solution)/shard_map/child_last/pallas_call | solution.py:24
  34.6 0.9 %collective-permute-done.12.mate_cols = f32[8,128]{1,0:T(8,128)S(1)} collective-permute-done((f32[8,128]{1,0:T(8,128)S(1)}, f32[8,128]{1,0:T(8,128)S(1)}, u32[]{:S(2)}, u32[]{:S(2)}) %collective-permute-start.12) | collective-permute-done | bytes 4128 | tf_op jit(solution)/shard_map/ppermute | solution.py:500
  35.5 1.0 %parent_last.1 = f32[512,32]{1,0:T(8,128)} custom-call(f32[16,8,128]{2,1,0:T(8,128)S(1)} %get-tuple-element.64.psolved_in, f32[5,16,128]{2,1,0:T(8,128)S(1)} %parent_rates_masked.1.prates_ref, f32[64,128]{1,0:T(8,128)S(1)} %collective-permute-done.10.mate_in, f32[64,128]{1,0:T(8,128)S(1)} %collective-permute-done.11.far_in, ...), custom_call_target="tpu_custom_call" | custom-call | flops 500000 | bytes 500000 | tf_op jit(solution)/shard_map/parent_last/pallas_call | solution.py:24
  (23 shorter events, 1.3 us)
Async XLA Ops:
  2.7 9.8 %collective-permute-start = (f32[128,128]{1,0:T(8,128)S(1)}, f32[128,128]{1,0:T(8,128)S(1)}, u32[]{:S(2)}, u32[]{:S(2)}) collective-permute-start(f32[128,128]{1,0:T(8,128)S(1)} %get-tuple-element.47), channel_id=1, source_target_pairs={{0,2},{1,3},{2,4},{3,5},{4,6},{5,7},{6,0},{7,1},{8,10},{9,11},{10,... | collective-permute-start | bytes 196616 | tf_op jit(solution)/shard_map/ppermute | solution.py:491
  6.9 7.7 %collective-permute-start.1 = (f32[256,128]{1,0:T(8,128)S(1)}, f32[256,128]{1,0:T(8,128)S(1)}, u32[]{:S(2)}, u32[]{:S(2)}) collective-permute-start(f32[256,128]{1,0:T(8,128)S(1)} %get-tuple-element.48), channel_id=1, source_target_pairs={{1,2},{2,1},{3,4},{4,3},{5,6},{6,5},{7,0},{0,7},{9,10},{10,9},{11,... | collective-permute-start | bytes 393224 | tf_op jit(solution)/shard_map/ppermute | solution.py:500
  8.4 4.6 %collective-permute-start.3 = (f32[32,128]{1,0:T(8,128)S(1)}, f32[32,128]{1,0:T(8,128)S(1)}, u32[]{:S(2)}, u32[]{:S(2)}) collective-permute-start(f32[32,128]{1,0:T(8,128)S(1)} %get-tuple-element.42.after_ref), channel_id=1, source_target_pairs={{8,16},{16,8},{24,0},{0,24},{9,17},{17,9},{25,1},{1,25},{10,18},{1... | collective-permute-start | bytes 49160 | tf_op jit(solution)/shard_map/ppermute | solution.py:500
  10.9 3.7 %collective-permute-start.2 = (f32[32,128]{1,0:T(8,128)S(1)}, f32[32,128]{1,0:T(8,128)S(1)}, u32[]{:S(2)}, u32[]{:S(2)}) collective-permute-start(f32[32,128]{1,0:T(8,128)S(1)} %get-tuple-element.42.after_ref), channel_id=1, source_target_pairs={{0,8},{8,0},{16,24},{24,16},{1,9},{9,1},{17,25},{25,17},{2,10},{10... | collective-permute-start | bytes 49160 | tf_op jit(solution)/shard_map/ppermute | solution.py:500
  11.4 3.4 %collective-permute-start.4 = (f32[256,128]{1,0:T(8,128)S(1)}, f32[256,128]{1,0:T(8,128)S(1)}, u32[]{:S(2)}, u32[]{:S(2)}) collective-permute-start(f32[256,128]{1,0:T(8,128)S(1)} %get-tuple-element.50), channel_id=1, source_target_pairs={{0,1},{1,0},{2,3},{3,2},{4,5},{5,4},{6,7},{7,6},{8,9},{9,8},{10,11... | collective-permute-start | bytes 393224 | tf_op jit(solution)/shard_map/ppermute | solution.py:500
  11.4 1.1 %copy-start = (f32[32,8,2,32]{3,2,1,0:T(2,128)S(1)}, f32[32,8,2,32]{3,2,1,0:T(2,128)}, u32[]{:S(2)}) copy-start(f32[32,8,2,32]{3,2,1,0:T(2,128)} %param.10) | copy-start | bytes 196612
  12.5 2.1 %copy-start.2 = (f32[32,2,32]{2,1,0:T(2,128)S(1)}, f32[32,2,32]{2,1,0:T(2,128)}, u32[]{:S(2)}) copy-start(f32[32,2,32]{2,1,0:T(2,128)} %param.15) | copy-start | bytes 24580
  17.4 6.6 %collective-permute-start.9 = (f32[128,128]{1,0:T(8,128)S(1)}, f32[128,128]{1,0:T(8,128)S(1)}, u32[]{:S(2)}, u32[]{:S(2)}) collective-permute-start(f32[128,128]{1,0:T(8,128)S(1)} %get-tuple-element.62), channel_id=1, source_target_pairs={{0,2},{1,3},{2,4},{3,5},{4,6},{5,7},{6,0},{7,1},{8,10},{9,11},{10,... | collective-permute-start | bytes 196616 | tf_op jit(solution)/shard_map/ppermute | solution.py:491
  18.6 8.1 %collective-permute-start.6 = (f32[320,128]{1,0:T(8,128)S(1)}, f32[320,128]{1,0:T(8,128)S(1)}, u32[]{:S(2)}, u32[]{:S(2)}) collective-permute-start(f32[320,128]{1,0:T(8,128)S(1)} %get-tuple-element.60), channel_id=1, source_target_pairs={{1,2},{2,1},{3,4},{4,3},{5,6},{6,5},{7,0},{0,7},{9,10},{10,9},{11,... | collective-permute-start | bytes 491528 | tf_op jit(solution)/shard_map/ppermute | solution.py:500
  20.9 4.7 %collective-permute-start.8 = (f32[40,128]{1,0:T(8,128)S(1)}, f32[40,128]{1,0:T(8,128)S(1)}, u32[]{:S(2)}, u32[]{:S(2)}) collective-permute-start(f32[40,128]{1,0:T(8,128)S(1)} %get-tuple-element.55.after_ref), channel_id=1, source_target_pairs={{8,16},{16,8},{24,0},{0,24},{9,17},{17,9},{25,1},{1,25},{10,18},{1... | collective-permute-start | bytes 61448 | tf_op jit(solution)/shard_map/ppermute | solution.py:500
  22.3 3.8 %collective-permute-start.7 = (f32[40,128]{1,0:T(8,128)S(1)}, f32[40,128]{1,0:T(8,128)S(1)}, u32[]{:S(2)}, u32[]{:S(2)}) collective-permute-start(f32[40,128]{1,0:T(8,128)S(1)} %get-tuple-element.55.after_ref), channel_id=1, source_target_pairs={{0,8},{8,0},{16,24},{24,16},{1,9},{9,1},{17,25},{25,17},{2,10},{10... | collective-permute-start | bytes 61448 | tf_op jit(solution)/shard_map/ppermute | solution.py:500
  22.9 4.0 %collective-permute-start.5 = (f32[320,128]{1,0:T(8,128)S(1)}, f32[320,128]{1,0:T(8,128)S(1)}, u32[]{:S(2)}, u32[]{:S(2)}) collective-permute-start(f32[320,128]{1,0:T(8,128)S(1)} %get-tuple-element.59), channel_id=1, source_target_pairs={{0,1},{1,0},{2,3},{3,2},{4,5},{5,4},{6,7},{7,6},{8,9},{9,8},{10,11... | collective-permute-start | bytes 491528 | tf_op jit(solution)/shard_map/ppermute | solution.py:500
  22.9 1.1 %copy-start.1 = (f32[4,32,2,32]{3,2,1,0:T(2,128)S(1)}, f32[4,32,2,32]{3,2,1,0:T(2,128)}, u32[]{:S(2)}) copy-start(f32[4,32,2,32]{3,2,1,0:T(2,128)} %param.14) | copy-start | bytes 98308
  27.2 8.2 %collective-permute-start.10 = (f32[64,128]{1,0:T(8,128)S(1)}, f32[64,128]{1,0:T(8,128)S(1)}, u32[]{:S(2)}, u32[]{:S(2)}) collective-permute-start(f32[64,128]{1,0:T(8,128)S(1)} %get-tuple-element.65), channel_id=1, source_target_pairs={{0,1},{1,0},{2,3},{3,2},{4,5},{5,4},{6,7},{7,6},{8,9},{9,8},{10,11... | collective-permute-start | bytes 98312 | tf_op jit(solution)/shard_map/ppermute | solution.py:500
  27.3 8.2 %collective-permute-start.11 = (f32[64,128]{1,0:T(8,128)S(1)}, f32[64,128]{1,0:T(8,128)S(1)}, u32[]{:S(2)}, u32[]{:S(2)}) collective-permute-start(f32[64,128]{1,0:T(8,128)S(1)} %get-tuple-element.66), channel_id=1, source_target_pairs={{1,2},{2,1},{3,4},{4,3},{5,6},{6,5},{7,0},{0,7},{9,10},{10,9},{11,... | collective-permute-start | bytes 98312 | tf_op jit(solution)/shard_map/ppermute | solution.py:500
  29.5 5.1 %collective-permute-start.13 = (f32[8,128]{1,0:T(8,128)S(1)}, f32[8,128]{1,0:T(8,128)S(1)}, u32[]{:S(2)}, u32[]{:S(2)}) collective-permute-start(f32[8,128]{1,0:T(8,128)S(1)} %get-tuple-element.67), channel_id=1, source_target_pairs={{8,16},{16,8},{24,0},{0,24},{9,17},{17,9},{25,1},{1,25},{10,18},{1... | collective-permute-start | bytes 12296 | tf_op jit(solution)/shard_map/ppermute | solution.py:500
  31.8 3.6 %collective-permute-start.12 = (f32[8,128]{1,0:T(8,128)S(1)}, f32[8,128]{1,0:T(8,128)S(1)}, u32[]{:S(2)}, u32[]{:S(2)}) collective-permute-start(f32[8,128]{1,0:T(8,128)S(1)} %get-tuple-element.67), channel_id=1, source_target_pairs={{0,8},{8,0},{16,24},{24,16},{1,9},{9,1},{17,25},{25,17},{2,10},{10... | collective-permute-start | bytes 12296 | tf_op jit(solution)/shard_map/ppermute | solution.py:500

commit v8 on v6

--- a/solution.py
+++ b/solution.py
@@ -89,10 +89,14 @@
     wide = sums_ref.shape[1]
     p = lax.broadcasted_iota(jnp.int32, (wide, LANES), 0)
     q = lax.broadcasted_iota(jnp.int32, (wide, LANES), 1)
-    pick = jnp.where(p // 4 == q, F32(0.0625), F32(0.0))
-    return jnp.dot(
-        sums_ref[...], pick, precision=lax.Precision.HIGHEST, preferred_element_type=F32
-    )
+    pick = jnp.where(p // 4 == q, F32(0.0625), F32(0.0)).astype(jnp.bfloat16)
+    rest, total = sums_ref[...], None
+    for _ in range(3):
+        part = rest.astype(jnp.bfloat16)
+        rest = rest - part.astype(F32)
+        product = jnp.dot(part, pick, preferred_element_type=F32)
+        total = product if total is None else total + product
+    return total
 
 
 def child_middle(carry, c_ref, half):
@@ -109,8 +113,7 @@
     half = depth // 2
     lane = lane_index()
     pair = lane >> 1
-    odd = parity("gy")
-    mate_row, far_row = 7 * (1 - odd), 7 * odd
+    swap = jnp.broadcast_to(parity("gy"), (8, LANES)) == 1
 
     def emit(i, values, packed):
         k_low = depth - 1 - i
@@ -122,8 +125,9 @@
                 solved_ref[k, v] = x
                 at = base + v
                 packed[side] = jnp.where(pair == at, pltpu.roll(x, 2 * at + 1 & (LANES - 1), 1), packed[side])
-            mate_rows[pl.ds(k * vectors, vectors), :] = solved_ref[k, :, mate_row, :]
-            far_rows[pl.ds(k * vectors, vectors), :] = solved_ref[k, :, far_row, :]
+            lo, hi = solved_ref[k, :, 0, :], solved_ref[k, :, 7, :]
+            mate_rows[pl.ds(k * vectors, vectors), :] = jnp.where(swap, lo, hi)
+            far_rows[pl.ds(k * vectors, vectors), :] = jnp.where(swap, hi, lo)
         return packed
 
     def up(i, state):

time: 35.6 us -> 35.2 us (0.989)
  Pallas kernels: 11.6 us -> 11.2 us
    pallas_call x13, Pallas kernels: 11.6 us -> 11.2 us  [call(): pl.pallas_call(body, out_shape=outs, in_specs=[FAR if i in far_in else VM...]
  transfers between devices with their start and end apart: 14 -> 14, of which waited for: 6 -> 6; matrix products, arithmetic and copies ran while one was open for 0% -> 0% of each run, Pallas kernels for 18% -> 17%
where the time goes in v8:
time: 35.2 us; the launch traced here: 35 us
  starting transfers between devices  17.1 us (49%)
  Pallas kernels  11.2 us (32%)
  waiting for transfers between devices  5.97 us (17%)
  between operations  0.78 us (2%)
    ppermute x12, starting transfers between devices, swapped(): return lax.ppermute(value, axis, pairs)  13.8 us
    pallas_call x13, Pallas kernels, call(): pl.pallas_call(body, out_shape=outs, in_specs=[FAR if i in far_in else VM...  11.2 us
    ppermute x12, waiting for transfers between devices, swapped(): return lax.ppermute(value, axis, pairs)  5.97 us
    ppermute x2, starting transfers between devices, passed_along(): lax.ppermute(value, axis, [(i, (i + steps) % count) for i in range(count)])  3.3 us
  transfers between devices with their start and end apart: 14, of which 6 were waited for; matrix products, arithmetic and copies ran while one was open for 0% of the time, Pallas kernels for 17%

profile of v8, /device:TPU:0, one launch (start us, length us, event | category | flops | bytes accessed | tf_op | source)
XLA Modules:
  0.0 35.0 jit_solution(5779452528342361693)
XLA Ops:
  0.6 2.1 %begin.1 = (f32[128,128]{1,0:T(8,128)S(1)}, f32[32,8,8,128]{3,2,1,0:T(8,128)S(1)}, f32[32,8,128]{2,1,0:T(8,128)S(1)}, f32[32,8,128]{2,1,0:T(8,128)S(1)}, f32[32,...) custom-call(f32[32,8,8,128]{3,2,1,0:T(8,128)} %x_hbm.1, ...), custom_call_target="tpu_custom_call" | custom-call | flops 4000000 | bytes 3000000 | tf_op jit(solution)/shard_map/begin/pallas_call | solution.py:24
  2.7 3.1 %collective-permute-start = (f32[128,128]{1,0:T(8,128)S(1)}, f32[128,128]{1,0:T(8,128)S(1)}, u32[]{:S(2)}, u32[]{:S(2)}) collective-permute-start(f32[128,128]{1,0:T(8,128)S(1)} %get-tuple-element.47), channel_id=1, source_target_pairs={{0,2},{1,3},{2,4},{3,5},{4,6},{5,7},{6,0},{7,1},{8,10},{9,11},{10,... | collective-permute-start | bytes 196616 | tf_op jit(solution)/shard_map/ppermute | solution.py:478
  5.8 0.7 %child_first.1 = (f32[32,8,8,128]{3,2,1,0:T(8,128)S(1)}, f32[256,128]{1,0:T(8,128)S(1)}, f32[256,128]{1,0:T(8,128)S(1)}, f32[32,128]{1,0:T(8,128)S(1)}) custom-call(f32[32,8,8,128]{3,2,1,0:T(8,128)S(1)} %get-tuple-element.35.x_ref, f32[32,8,128]{2,1,0:T(8,128)S(1)} %get-tuple-element.36.a_ref, f32[32,8,128]{2,1,0:T(8,128)S(1)} %get-tuple-element.37.b_ref, ...), custom_call_target="tpu_custom_call" | custom-call | flops 4000000 | bytes 3000000 | tf_op jit(solution)/shard_map/child_first/pallas_call | solution.py:24
  6.5 1.6 %collective-permute-start.1 = (f32[256,128]{1,0:T(8,128)S(1)}, f32[256,128]{1,0:T(8,128)S(1)}, u32[]{:S(2)}, u32[]{:S(2)}) collective-permute-start(f32[256,128]{1,0:T(8,128)S(1)} %get-tuple-element.48), channel_id=1, source_target_pairs={{1,2},{2,1},{3,4},{4,3},{5,6},{6,5},{7,0},{0,7},{9,10},{10,9},{11,... | collective-permute-start | bytes 393224 | tf_op jit(solution)/shard_map/ppermute | solution.py:487
  8.1 2.4 %collective-permute-start.3 = (f32[32,128]{1,0:T(8,128)S(1)}, f32[32,128]{1,0:T(8,128)S(1)}, u32[]{:S(2)}, u32[]{:S(2)}) collective-permute-start(f32[32,128]{1,0:T(8,128)S(1)} %get-tuple-element.42.after_ref), channel_id=1, source_target_pairs={{8,16},{16,8},{24,0},{0,24},{9,17},{17,9},{25,1},{1,25},{10,18},{1... | collective-permute-start | bytes 49160 | tf_op jit(solution)/shard_map/ppermute | solution.py:487
  10.5 0.5 %collective-permute-start.2 = (f32[32,128]{1,0:T(8,128)S(1)}, f32[32,128]{1,0:T(8,128)S(1)}, u32[]{:S(2)}, u32[]{:S(2)}) collective-permute-start(f32[32,128]{1,0:T(8,128)S(1)} %get-tuple-element.42.after_ref), channel_id=1, source_target_pairs={{0,8},{8,0},{16,24},{24,16},{1,9},{9,1},{17,25},{25,17},{2,10},{10... | collective-permute-start | bytes 49160 | tf_op jit(solution)/shard_map/ppermute | solution.py:487
  11.1 1.1 %child_inner.2 = (f32[32,8,8,128]{3,2,1,0:T(8,128)S(1)}, f32[32,8,128]{2,1,0:T(8,128)S(1)}, f32[32,8,128]{2,1,0:T(8,128)S(1)}) custom-call(f32[32,8,8,128]{3,2,1,0:T(8,128)S(1)} %get-tuple-element.39.solved_ref, f32[4,32,8,128]{3,2,1,0:T(8,128)S(1)} %get-tuple-element.40.rates_ref, f32[8,128]{1,0:T(8,128)S(1)} %get-tuple-element.41.land_ref, ...), custom_call_target="tpu_custom_call" | custom-call | flops 10000000 | bytes 4000000 | tf_op jit(solution)/shard_map/child_inner/pallas_call | solution.py:24
  12.7 1.5 %collective-permute-done.2.mate_cols = f32[32,128]{1,0:T(8,128)S(1)} collective-permute-done((f32[32,128]{1,0:T(8,128)S(1)}, f32[32,128]{1,0:T(8,128)S(1)}, u32[]{:S(2)}, u32[]{:S(2)}) %collective-permute-start.2) | collective-permute-done | bytes 16416 | tf_op jit(solution)/shard_map/ppermute | solution.py:487
  14.4 1.6 %child_between.1 = (f32[128,128]{1,0:T(8,128)S(1)}, f32[32,8,8,128]{3,2,1,0:T(8,128)S(1)}) custom-call(f32[32,8,8,128]{3,2,1,0:T(8,128)S(1)} %get-tuple-element.43.after_ref.inner_ref, f32[32,8,128]{2,1,0:T(8,128)S(1)} %get-tuple-element.44.row_ref, f32[32,8,128]{2,1,0:T(8,128)S(1)} %get-tuple-element.45.column_ref, ...), custom_call_target="tpu_custom_call" | custom-call | flops 8000000 | bytes 3000000 | tf_op jit(solution)/shard_map/child_between/pallas_call | solution.py:24
  16.3 0.9 %child_second.1 = (f32[32,8,8,128]{3,2,1,0:T(8,128)S(1)}, f32[16,8,128]{2,1,0:T(8,128)S(1)}, f32[320,128]{1,0:T(8,128)S(1)}, f32[320,128]{1,0:T(8,128)S(1)}, f32[40,128]{1,0:T(8,128)S(1)}) custom-call(f32[32,8,8,128]{3,2,1,0:T(8,128)S(1)} %get-tuple-element.51.x_ref, f32[32,8,128]{2,1,0:T(8,128)S(1)} %get-tuple-element.36.a_ref, ...), custom_call_target="tpu_custom_call" | custom-call | flops 8000000 | bytes 3000000 | tf_op jit(solution)/shard_map/child_second/pallas_call | solution.py:24
  17.2 2.2 %collective-permute-start.6 = (f32[320,128]{1,0:T(8,128)S(1)}, f32[320,128]{1,0:T(8,128)S(1)}, u32[]{:S(2)}, u32[]{:S(2)}) collective-permute-start(f32[320,128]{1,0:T(8,128)S(1)} %get-tuple-element.60), channel_id=1, source_target_pairs={{1,2},{2,1},{3,4},{4,3},{5,6},{6,5},{7,0},{0,7},{9,10},{10,9},{11,... | collective-permute-start | bytes 491528 | tf_op jit(solution)/shard_map/ppermute | solution.py:487
  19.4 1.4 %collective-permute-start.8 = (f32[40,128]{1,0:T(8,128)S(1)}, f32[40,128]{1,0:T(8,128)S(1)}, u32[]{:S(2)}, u32[]{:S(2)}) collective-permute-start(f32[40,128]{1,0:T(8,128)S(1)} %get-tuple-element.55.after_ref), channel_id=1, source_target_pairs={{8,16},{16,8},{24,0},{0,24},{9,17},{17,9},{25,1},{1,25},{10,18},{1... | collective-permute-start | bytes 61448 | tf_op jit(solution)/shard_map/ppermute | solution.py:487
  20.9 0.5 %collective-permute-start.7 = (f32[40,128]{1,0:T(8,128)S(1)}, f32[40,128]{1,0:T(8,128)S(1)}, u32[]{:S(2)}, u32[]{:S(2)}) collective-permute-start(f32[40,128]{1,0:T(8,128)S(1)} %get-tuple-element.55.after_ref), channel_id=1, source_target_pairs={{0,8},{8,0},{16,24},{24,16},{1,9},{9,1},{17,25},{25,17},{2,10},{10... | collective-permute-start | bytes 61448 | tf_op jit(solution)/shard_map/ppermute | solution.py:487
  21.4 1.1 %child_inner.3 = (f32[32,8,8,128]{3,2,1,0:T(8,128)S(1)}, f32[32,8,128]{2,1,0:T(8,128)S(1)}, f32[32,8,128]{2,1,0:T(8,128)S(1)}) custom-call(f32[32,8,8,128]{3,2,1,0:T(8,128)S(1)} %get-tuple-element.54.solved_ref, f32[4,32,8,128]{3,2,1,0:T(8,128)S(1)} %get-tuple-element.40.rates_ref, f32[8,128]{1,0:T(8,128)S(1)} %get-tuple-element.41.land_ref, ...), custom_call_target="tpu_custom_call" | custom-call | flops 10000000 | bytes 4000000 | tf_op jit(solution)/shard_map/child_inner/pallas_call | solution.py:24
  22.8 1.3 %collective-permute-done.8.far_cols = f32[40,128]{1,0:T(8,128)S(1)} collective-permute-done((f32[40,128]{1,0:T(8,128)S(1)}, f32[40,128]{1,0:T(8,128)S(1)}, u32[]{:S(2)}, u32[]{:S(2)}) %collective-permute-start.8) | collective-permute-done | bytes 20512 | tf_op jit(solution)/shard_map/ppermute | solution.py:487
  24.1 0.5 %collective-permute-done.7.mate_cols = f32[40,128]{1,0:T(8,128)S(1)} collective-permute-done((f32[40,128]{1,0:T(8,128)S(1)}, f32[40,128]{1,0:T(8,128)S(1)}, u32[]{:S(2)}, u32[]{:S(2)}) %collective-permute-start.7) | collective-permute-done | bytes 20512 | tf_op jit(solution)/shard_map/ppermute | solution.py:487
  24.7 0.8 %collective-permute-done.6.far_in.far_ref = f32[320,128]{1,0:T(8,128)S(1)} collective-permute-done((f32[320,128]{1,0:T(8,128)S(1)}, f32[320,128]{1,0:T(8,128)S(1)}, u32[]{:S(2)}, u32[]{:S(2)}) %collective-permute-start.6) | collective-permute-done | bytes 163872 | tf_op jit(solution)/shard_map/ppermute | solution.py:487
  25.5 0.4 %parent_second.1 = (f32[16,8,128]{2,1,0:T(8,128)S(1)}, f32[64,128]{1,0:T(8,128)S(1)}, f32[64,128]{1,0:T(8,128)S(1)}, f32[8,128]{1,0:T(8,128)S(1)}) custom-call(f32[16,8,128]{2,1,0:T(8,128)S(1)} %get-tuple-element.61.psolved_in, f32[5,16,128]{2,1,0:T(8,128)S(1)} %parent_rates_masked.1.prates_ref, f32[16,128]{1,0:T(8,128)S(1)} %get-tuple-element.49.after_ref.pa_ref, ...), custom_call_target="tpu_custom_call" | custom-call | flops 1000000 | bytes 500000 | tf_op jit(solution)/shard_map/parent_second/pallas_call | solution.py:24
  26.0 2.1 %collective-permute-start.11 = (f32[64,128]{1,0:T(8,128)S(1)}, f32[64,128]{1,0:T(8,128)S(1)}, u32[]{:S(2)}, u32[]{:S(2)}) collective-permute-start(f32[64,128]{1,0:T(8,128)S(1)} %get-tuple-element.66), channel_id=1, source_target_pairs={{1,2},{2,1},{3,4},{4,3},{5,6},{6,5},{7,0},{0,7},{9,10},{10,9},{11,... | collective-permute-start | bytes 98312 | tf_op jit(solution)/shard_map/ppermute | solution.py:487
  28.1 2.3 %collective-permute-start.13 = (f32[8,128]{1,0:T(8,128)S(1)}, f32[8,128]{1,0:T(8,128)S(1)}, u32[]{:S(2)}, u32[]{:S(2)}) collective-permute-start(f32[8,128]{1,0:T(8,128)S(1)} %get-tuple-element.67), channel_id=1, source_target_pairs={{8,16},{16,8},{24,0},{0,24},{9,17},{17,9},{25,1},{1,25},{10,18},{1... | collective-permute-start | bytes 12296 | tf_op jit(solution)/shard_map/ppermute | solution.py:487
  30.4 0.5 %collective-permute-start.12 = (f32[8,128]{1,0:T(8,128)S(1)}, f32[8,128]{1,0:T(8,128)S(1)}, u32[]{:S(2)}, u32[]{:S(2)}) collective-permute-start(f32[8,128]{1,0:T(8,128)S(1)} %get-tuple-element.67), channel_id=1, source_target_pairs={{0,8},{8,0},{16,24},{24,16},{1,9},{9,1},{17,25},{25,17},{2,10},{10... | collective-permute-start | bytes 12296 | tf_op jit(solution)/shard_map/ppermute | solution.py:487
  30.9 1.6 %child_last.1 = f32[32,8,8,128]{3,2,1,0:T(8,128)} custom-call(f32[32,8,8,128]{3,2,1,0:T(8,128)S(1)} %get-tuple-element.56.inner_ref.after_ref, f32[32,8,128]{2,1,0:T(8,128)S(1)} %get-tuple-element.57.row_ref, f32[32,8,128]{2,1,0:T(8,128)S(1)} %get-tuple-element.58.column_ref, f32[320,128]{1,0:T(8,128)S(1)} %collective-permute-done.5.mate_in, ...), custom_call_target="tpu_custom_call" | custom-call | flops 4000000 | bytes 3000000 | tf_op jit(solution)/shard_map/child_last/pallas_call | solution.py:24
  32.6 1.4 %collective-permute-done.12.mate_cols = f32[8,128]{1,0:T(8,128)S(1)} collective-permute-done((f32[8,128]{1,0:T(8,128)S(1)}, f32[8,128]{1,0:T(8,128)S(1)}, u32[]{:S(2)}, u32[]{:S(2)}) %collective-permute-start.12) | collective-permute-done | bytes 4128 | tf_op jit(solution)/shard_map/ppermute | solution.py:487
  34.0 1.0 %parent_last.1 = f32[512,32]{1,0:T(8,128)} custom-call(f32[16,8,128]{2,1,0:T(8,128)S(1)} %get-tuple-element.64.psolved_in, f32[5,16,128]{2,1,0:T(8,128)S(1)} %parent_rates_masked.1.prates_ref, f32[64,128]{1,0:T(8,128)S(1)} %collective-permute-done.10.mate_in, f32[64,128]{1,0:T(8,128)S(1)} %collective-permute-done.11.far_in, ...), custom_call_target="tpu_custom_call" | custom-call | flops 500000 | bytes 500000 | tf_op jit(solution)/shard_map/parent_last/pallas_call | solution.py:24
  (23 shorter events, 1.3 us)
Async XLA Ops:
  2.7 9.4 %collective-permute-start = (f32[128,128]{1,0:T(8,128)S(1)}, f32[128,128]{1,0:T(8,128)S(1)}, u32[]{:S(2)}, u32[]{:S(2)}) collective-permute-start(f32[128,128]{1,0:T(8,128)S(1)} %get-tuple-element.47), channel_id=1, source_target_pairs={{0,2},{1,3},{2,4},{3,5},{4,6},{5,7},{6,0},{7,1},{8,10},{9,11},{10,... | collective-permute-start | bytes 196616 | tf_op jit(solution)/shard_map/ppermute | solution.py:478
  6.5 7.7 %collective-permute-start.1 = (f32[256,128]{1,0:T(8,128)S(1)}, f32[256,128]{1,0:T(8,128)S(1)}, u32[]{:S(2)}, u32[]{:S(2)}) collective-permute-start(f32[256,128]{1,0:T(8,128)S(1)} %get-tuple-element.48), channel_id=1, source_target_pairs={{1,2},{2,1},{3,4},{4,3},{5,6},{6,5},{7,0},{0,7},{9,10},{10,9},{11,... | collective-permute-start | bytes 393224 | tf_op jit(solution)/shard_map/ppermute | solution.py:487
  8.1 4.6 %collective-permute-start.3 = (f32[32,128]{1,0:T(8,128)S(1)}, f32[32,128]{1,0:T(8,128)S(1)}, u32[]{:S(2)}, u32[]{:S(2)}) collective-permute-start(f32[32,128]{1,0:T(8,128)S(1)} %get-tuple-element.42.after_ref), channel_id=1, source_target_pairs={{8,16},{16,8},{24,0},{0,24},{9,17},{17,9},{25,1},{1,25},{10,18},{1... | collective-permute-start | bytes 49160 | tf_op jit(solution)/shard_map/ppermute | solution.py:487
  10.5 3.7 %collective-permute-start.2 = (f32[32,128]{1,0:T(8,128)S(1)}, f32[32,128]{1,0:T(8,128)S(1)}, u32[]{:S(2)}, u32[]{:S(2)}) collective-permute-start(f32[32,128]{1,0:T(8,128)S(1)} %get-tuple-element.42.after_ref), channel_id=1, source_target_pairs={{0,8},{8,0},{16,24},{24,16},{1,9},{9,1},{17,25},{25,17},{2,10},{10... | collective-permute-start | bytes 49160 | tf_op jit(solution)/shard_map/ppermute | solution.py:487
  11.1 3.4 %collective-permute-start.4 = (f32[256,128]{1,0:T(8,128)S(1)}, f32[256,128]{1,0:T(8,128)S(1)}, u32[]{:S(2)}, u32[]{:S(2)}) collective-permute-start(f32[256,128]{1,0:T(8,128)S(1)} %get-tuple-element.50), channel_id=1, source_target_pairs={{0,1},{1,0},{2,3},{3,2},{4,5},{5,4},{6,7},{7,6},{8,9},{9,8},{10,11... | collective-permute-start | bytes 393224 | tf_op jit(solution)/shard_map/ppermute | solution.py:487
  11.1 1.1 %copy-start = (f32[32,8,2,32]{3,2,1,0:T(2,128)S(1)}, f32[32,8,2,32]{3,2,1,0:T(2,128)}, u32[]{:S(2)}) copy-start(f32[32,8,2,32]{3,2,1,0:T(2,128)} %param.10) | copy-start | bytes 196612
  12.2 2.1 %copy-start.2 = (f32[32,2,32]{2,1,0:T(2,128)S(1)}, f32[32,2,32]{2,1,0:T(2,128)}, u32[]{:S(2)}) copy-start(f32[32,2,32]{2,1,0:T(2,128)} %param.15) | copy-start | bytes 24580
  16.0 6.5 %collective-permute-start.9 = (f32[128,128]{1,0:T(8,128)S(1)}, f32[128,128]{1,0:T(8,128)S(1)}, u32[]{:S(2)}, u32[]{:S(2)}) collective-permute-start(f32[128,128]{1,0:T(8,128)S(1)} %get-tuple-element.62), channel_id=1, source_target_pairs={{0,2},{1,3},{2,4},{3,5},{4,6},{5,7},{6,0},{7,1},{8,10},{9,11},{10,... | collective-permute-start | bytes 196616 | tf_op jit(solution)/shard_map/ppermute | solution.py:478
  17.2 8.2 %collective-permute-start.6 = (f32[320,128]{1,0:T(8,128)S(1)}, f32[320,128]{1,0:T(8,128)S(1)}, u32[]{:S(2)}, u32[]{:S(2)}) collective-permute-start(f32[320,128]{1,0:T(8,128)S(1)} %get-tuple-element.60), channel_id=1, source_target_pairs={{1,2},{2,1},{3,4},{4,3},{5,6},{6,5},{7,0},{0,7},{9,10},{10,9},{11,... | collective-permute-start | bytes 491528 | tf_op jit(solution)/shard_map/ppermute | solution.py:487
  19.4 4.7 %collective-permute-start.8 = (f32[40,128]{1,0:T(8,128)S(1)}, f32[40,128]{1,0:T(8,128)S(1)}, u32[]{:S(2)}, u32[]{:S(2)}) collective-permute-start(f32[40,128]{1,0:T(8,128)S(1)} %get-tuple-element.55.after_ref), channel_id=1, source_target_pairs={{8,16},{16,8},{24,0},{0,24},{9,17},{17,9},{25,1},{1,25},{10,18},{1... | collective-permute-start | bytes 61448 | tf_op jit(solution)/shard_map/ppermute | solution.py:487
  20.9 3.8 %collective-permute-start.7 = (f32[40,128]{1,0:T(8,128)S(1)}, f32[40,128]{1,0:T(8,128)S(1)}, u32[]{:S(2)}, u32[]{:S(2)}) collective-permute-start(f32[40,128]{1,0:T(8,128)S(1)} %get-tuple-element.55.after_ref), channel_id=1, source_target_pairs={{0,8},{8,0},{16,24},{24,16},{1,9},{9,1},{17,25},{25,17},{2,10},{10... | collective-permute-start | bytes 61448 | tf_op jit(solution)/shard_map/ppermute | solution.py:487
  21.4 4.1 %collective-permute-start.5 = (f32[320,128]{1,0:T(8,128)S(1)}, f32[320,128]{1,0:T(8,128)S(1)}, u32[]{:S(2)}, u32[]{:S(2)}) collective-permute-start(f32[320,128]{1,0:T(8,128)S(1)} %get-tuple-element.59), channel_id=1, source_target_pairs={{0,1},{1,0},{2,3},{3,2},{4,5},{5,4},{6,7},{7,6},{8,9},{9,8},{10,11... | collective-permute-start | bytes 491528 | tf_op jit(solution)/shard_map/ppermute | solution.py:487
  21.4 1.1 %copy-start.1 = (f32[4,32,2,32]{3,2,1,0:T(2,128)S(1)}, f32[4,32,2,32]{3,2,1,0:T(2,128)}, u32[]{:S(2)}) copy-start(f32[4,32,2,32]{3,2,1,0:T(2,128)} %param.14) | copy-start | bytes 98308
  25.9 8.1 %collective-permute-start.10 = (f32[64,128]{1,0:T(8,128)S(1)}, f32[64,128]{1,0:T(8,128)S(1)}, u32[]{:S(2)}, u32[]{:S(2)}) collective-permute-start(f32[64,128]{1,0:T(8,128)S(1)} %get-tuple-element.65), channel_id=1, source_target_pairs={{0,1},{1,0},{2,3},{3,2},{4,5},{5,4},{6,7},{7,6},{8,9},{9,8},{10,11... | collective-permute-start | bytes 98312 | tf_op jit(solution)/shard_map/ppermute | solution.py:487
  26.0 8.0 %collective-permute-start.11 = (f32[64,128]{1,0:T(8,128)S(1)}, f32[64,128]{1,0:T(8,128)S(1)}, u32[]{:S(2)}, u32[]{:S(2)}) collective-permute-start(f32[64,128]{1,0:T(8,128)S(1)} %get-tuple-element.66), channel_id=1, source_target_pairs={{1,2},{2,1},{3,4},{4,3},{5,6},{6,5},{7,0},{0,7},{9,10},{10,9},{11,... | collective-permute-start | bytes 98312 | tf_op jit(solution)/shard_map/ppermute | solution.py:487
  28.1 4.5 %collective-permute-start.13 = (f32[8,128]{1,0:T(8,128)S(1)}, f32[8,128]{1,0:T(8,128)S(1)}, u32[]{:S(2)}, u32[]{:S(2)}) collective-permute-start(f32[8,128]{1,0:T(8,128)S(1)} %get-tuple-element.67), channel_id=1, source_target_pairs={{8,16},{16,8},{24,0},{0,24},{9,17},{17,9},{25,1},{1,25},{10,18},{1... | collective-permute-start | bytes 12296 | tf_op jit(solution)/shard_map/ppermute | solution.py:487
  30.4 3.6 %collective-permute-start.12 = (f32[8,128]{1,0:T(8,128)S(1)}, f32[8,128]{1,0:T(8,128)S(1)}, u32[]{:S(2)}, u32[]{:S(2)}) collective-permute-start(f32[8,128]{1,0:T(8,128)S(1)} %get-tuple-element.67), channel_id=1, source_target_pairs={{0,8},{8,0},{16,24},{24,16},{1,9},{9,1},{17,25},{25,17},{2,10},{10... | collective-permute-start | bytes 12296 | tf_op jit(solution)/shard_map/ppermute | solution.py:487

commit v9 on v8

--- a/solution.py
+++ b/solution.py
@@ -142,7 +142,8 @@
 
     def keep_columns(group, packed):
         for side, g in ((0, group), (1, depth // LEVELS - 1 - group)):
-            cols_ref[LEVELS * g : LEVELS * g + 8, :] = packed[side]
+            for slot in range(cols_ref.shape[0]):
+                cols_ref[slot, LEVELS * g : LEVELS * g + 8, :] = packed[side]
 
     blank = jnp.zeros((8, LANES), F32)
     values = child_middle(carry, c_ref, half)
@@ -221,9 +222,10 @@
     return [land * part for part in (1.0 - (east + west + north + south), east, west, north, south)]
 
 
-def merge_edges(mate, far, turn):
-    swap = jnp.broadcast_to(parity("gx"), (8, LANES)) == 1
-    east, west = jnp.where(swap, far, mate), jnp.where(swap, mate, far)
+def merge_edges(cols_ref, part, turn):
+    count, here = lax.axis_size("gx"), lax.axis_index("gx")
+    east = cols_ref[lax.rem(here + 1, count), part, :]
+    west = cols_ref[lax.rem(here + count - 1, count), part, :]
     return jnp.where((lane_index() & 1) == 0, west, pltpu.roll(east, turn, 1))
 
 
@@ -248,10 +250,10 @@
     lax.fori_loop(0, depth, level, 0, unroll=4)
 
 
-def edge_merger(mate_cols, far_cols, merged_ref):
+def edge_merger(cols_ref, merged_ref):
     for g in range(merged_ref.shape[0] // 8):
         part = slice(8 * g, 8 * g + 8)
-        merged_ref[part, :] = merge_edges(mate_cols[part, :], far_cols[part, :], LANES - 2)
+        merged_ref[part, :] = merge_edges(cols_ref, part, LANES - 2)
 
 
 def edged(inner_ref, row_rates, column_rates, mate_ref, far_ref, edges, k, v, at, mates):
@@ -267,7 +269,7 @@
 
 
 def child_between(
-    inner_ref, row_ref, column_ref, relax_ref, after_ref, mate_in, far_in, mate_cols, far_cols,
+    inner_ref, row_ref, column_ref, relax_ref, after_ref, mate_in, far_in, cols_in,
     sums_out, x_ref,
     sums_ref, merged_ref,
 ):
@@ -275,7 +277,7 @@
     half, groups = depth // 2, depth // LEVELS
     mates = mate_rows_mask()
     weights = [relax_ref[j : j + 1, :] for j in range(8)]
-    edge_merger(mate_cols, far_cols, merged_ref)
+    edge_merger(cols_in, merged_ref)
 
     def level(i, _, edges):
         inside = lax.rem(i, LEVELS)
@@ -311,11 +313,11 @@
 
 
 def child_last(
-    inner_ref, row_ref, column_ref, mate_in, far_in, mate_cols, far_cols, out_hbm, out_ref, merged_ref, sems
+    inner_ref, row_ref, column_ref, mate_in, far_in, cols_in, out_hbm, out_ref, merged_ref, sems
 ):
     depth, vectors = inner_ref.shape[0], inner_ref.shape[1]
     mates = mate_rows_mask()
-    edge_merger(mate_cols, far_cols, merged_ref)
+    edge_merger(cols_in, merged_ref)
     copies = []
     for group in range(depth // LEVELS):
         edges = merged_ref[8 * group : 8 * group + 8, :]
@@ -349,7 +351,7 @@
         packed_ref[i] = packed_ref[i] + feed_ref[vectors * i : vectors * (i + 1), :]
 
 
-def parent_factors(mix_ref, fed_ref, far_ref, mate_cols, far_cols, pa_ref, pb_ref, pc_ref, mixed):
+def parent_factors(mix_ref, fed_ref, far_ref, cols_in, pa_ref, pb_ref, pc_ref, mixed):
     half = pa_ref.shape[0]
     for i in range(half):
         for h, r, lo in PLACES:
@@ -380,7 +382,7 @@
                 packed_ref[d, i : i + 1, lo : lo + 32] = rates_ref[at : at + 1, :]
 
 
-def parent_rates_masked(packed_ref, land_ref, far_ref, mate_cols, far_cols, prates_ref):
+def parent_rates_masked(packed_ref, land_ref, far_ref, cols_in, prates_ref):
     half = packed_ref.shape[1]
     land = jnp.concatenate([land_ref[r : r + 1, :] for _, r, _ in PLACES], axis=1)
     land = jnp.broadcast_to(land, (half, LANES))
@@ -403,7 +405,8 @@
     for i in range(half):
         psolved_ref[i] = tiles[i]
         packed = jnp.where(((lane & 31) >> 1) == i, pltpu.roll(tiles[i], 2 * i + 1, 1), packed)
-    cols_ref[cols_at : cols_at + 8, :] = packed
+    for slot in range(cols_ref.shape[0]):
+        cols_ref[slot, cols_at : cols_at + 8, :] = packed
     first = (lane & 32) == 0
     swap = jnp.broadcast_to(parity("gy"), (8, LANES)) == 1
     for j in range(half // 2):
@@ -413,10 +416,6 @@
         part = slice(lines + 8 * j, lines + 8 * j + 8)
         mate_rows[part, :] = jnp.where(swap, lo, hi)
         far_rows[part, :] = jnp.where(swap, hi, lo)
-
-
-def parent_edges(mate_cols, far_cols, at):
-    return merge_edges(mate_cols[at : at + 8, :], far_cols[at : at + 8, :], 62)
 
 
 def parent_transport(psolved_ref, prates_ref, mate_row, far_row, edges, i):
@@ -442,12 +441,12 @@
 
 
 def parent_second(
-    psolved_in, prates_ref, pa_ref, pb_ref, pc_ref, mate_in, far_in, mate_cols, far_cols, feed_ref,
+    psolved_in, prates_ref, pa_ref, pb_ref, pc_ref, mate_in, far_in, cols_in, feed_ref,
     psolved_ref, mate_rows, far_rows, cols_ref,
 ):
     half = psolved_in.shape[0]
     lines = mate_in.shape[0] - mate_rows.shape[0]
-    edges = parent_edges(mate_cols, far_cols, mate_cols.shape[0] - 8)
+    edges = merge_edges(cols_in, slice(cols_in.shape[1] - 8, cols_in.shape[1]), 62)
     mate = lambda j: mate_in[lines + 8 * j : lines + 8 * j + 8, :]
     far = lambda j: far_in[lines + 8 * j : lines + 8 * j + 8, :]
     y = jnp.zeros((8, LANES), F32)
@@ -459,9 +458,9 @@
     parent_up(y, pc_ref, psolved_ref, mate_rows, far_rows, 0, cols_ref, 0)
 
 
-def parent_last(psolved_in, prates_ref, mate_in, far_in, mate_cols, far_cols, out_ref):
+def parent_last(psolved_in, prates_ref, mate_in, far_in, cols_in, out_ref):
     half, vectors = psolved_in.shape[0], psolved_in.shape[1]
-    edges = parent_edges(mate_cols, far_cols, 0)
+    edges = merge_edges(cols_in, slice(0, 8), 62)
     mate = lambda j: mate_in[8 * j : 8 * j + 8, :]
     far = lambda j: far_in[8 * j : 8 * j + 8, :]
     for i in range(half):
@@ -488,7 +487,8 @@
 
 
 def halos_of(mate, far, cols):
-    return [swapped(mate, "gy", 0), swapped(far, "gy", 1), swapped(cols, "gx", 0), swapped(cols, "gx", 1)]
+    columns = lax.all_to_all(cols, "gx", 0, 0, tiled=True)
+    return [swapped(mate, "gy", 0), swapped(far, "gy", 1), columns]
 
 
 def local(
@@ -505,6 +505,7 @@
     depth, vectors, lines, columns = child_adjoint.shape
     half = depth // 2
     quarter = lax.axis_size("gy") // 4
+    slots = lax.axis_size("gx")
     field = shape(depth, vectors, lines, columns)
     factor = shape(depth, lines, columns)
     tiles = shape(half, vectors, LANES)
@@ -534,7 +535,7 @@
     feed = passed_along(sums1, "gy", quarter)
     solved, mate, far, cols = call(
         child_first,
-        [field, shape(count, LANES), shape(count, LANES), shape(edge, LANES)],
+        [field, shape(count, LANES), shape(count, LANES), shape(slots, edge, LANES)],
         [],
         [x, a, b, c],
         4_000_000,
@@ -577,7 +578,7 @@
     rows = count + half // 2 * vectors
     solved, psolved, mate, far, cols = call(
         child_second,
-        [field, tiles, shape(rows, LANES), shape(rows, LANES), shape(edge + 8, LANES)],
+        [field, tiles, shape(rows, LANES), shape(rows, LANES), shape(slots, edge + 8, LANES)],
         [],
         [x, a, b, c, fed, pa, pb, pc],
         8_000_000,
@@ -611,7 +612,7 @@
     few = half // 2 * vectors
     psolved, mate, far, cols = call(
         parent_second,
-        [tiles, shape(few, LANES), shape(few, LANES), shape(8, LANES)],
+        [tiles, shape(few, LANES), shape(few, LANES), shape(slots, 8, LANES)],
         [],
         [psolved, prates, pa, pb, pc, *halos, feed],
         1_000_000,

time: 35.2 us -> 46.5 us (1.32)
  Pallas kernels: 11.2 us -> 16.4 us
  local copies, waits for them, and re-layouts: 0.01 us -> 2.57 us
  starting transfers between devices: 17.1 us -> 19.4 us
  waiting for transfers between devices: 5.97 us -> 6.76 us
    all_to_all x0 -> x3, starting transfers between devices: none -> 11.3 us  [halos_of(): columns = lax.all_to_all(cols, 'gx', 0, 0, tiled=True)]
    ppermute x12 -> x6, starting transfers between devices: 13.8 us -> 5.06 us  [swapped(): return lax.ppermute(value, axis, pairs)]
    all_to_all x0 -> x3, waiting for transfers between devices: none -> 6.74 us  [halos_of(): columns = lax.all_to_all(cols, 'gx', 0, 0, tiled=True)]
    ppermute x12 -> x6, waiting for transfers between devices: 5.97 us -> 0.02 us  [swapped(): return lax.ppermute(value, axis, pairs)]
    pallas_call x13, Pallas kernels: 11.2 us -> 16.4 us  [call(): pl.pallas_call(body, out_shape=outs, in_specs=[FAR if i in far_in else VM...]
    unnamed x6 -> x26, local copies, waits for them, and re-layouts: 0.01 us -> 2.57 us
  transfers between devices with their start and end apart: 14 -> 11, of which waited for: 6 -> 3; matrix products, arithmetic and copies ran while one was open for 0% -> 0% of each run, Pallas kernels for 17% -> 22%
where the time goes in v9:
time: 46.5 us; the launch traced here: 45.9 us
  starting transfers between devices  19.4 us (42%)
  Pallas kernels  16.4 us (35%)
  waiting for transfers between devices  6.76 us (15%)
  local copies, waits for them, and re-layouts  2.57 us (6%)
  between operations  0.8 us (2%)
    pallas_call x13, Pallas kernels, call(): pl.pallas_call(body, out_shape=outs, in_specs=[FAR if i in far_in else VM...  16.4 us
    all_to_all x3, starting transfers between devices, halos_of(): columns = lax.all_to_all(cols, 'gx', 0, 0, tiled=True)  11.3 us
    all_to_all x3, waiting for transfers between devices, halos_of(): columns = lax.all_to_all(cols, 'gx', 0, 0, tiled=True)  6.74 us
    ppermute x6, starting transfers between devices, swapped(): return lax.ppermute(value, axis, pairs)  5.06 us
    ppermute x2, starting transfers between devices, passed_along(): lax.ppermute(value, axis, [(i, (i + steps) % count) for i in range(count)])  3.02 us
    unnamed x26, local copies, waits for them, and re-layouts  2.57 us
  transfers between devices with their start and end apart: 11, of which 3 were waited for; matrix products, arithmetic and copies ran while one was open for 0% of the time, Pallas kernels for 22%

profile of v9, /device:TPU:0, one launch (start us, length us, event | category | flops | bytes accessed | tf_op | source)
XLA Modules:
  0.0 45.9 jit_solution(4842092291231523610)
XLA Ops:
  0.6 2.1 %begin.1 = (f32[128,128]{1,0:T(8,128)S(1)}, f32[32,8,8,128]{3,2,1,0:T(8,128)S(1)}, f32[32,8,128]{2,1,0:T(8,128)S(1)}, f32[32,8,128]{2,1,0:T(8,128)S(1)}, f32[32,...) custom-call(f32[32,8,8,128]{3,2,1,0:T(8,128)} %x_hbm.1, ...), custom_call_target="tpu_custom_call" | custom-call | flops 4000000 | bytes 3000000 | tf_op jit(solution)/shard_map/begin/pallas_call | solution.py:24
  2.8 0.6 %copy-done.11 = f32[2,32]{1,0:T(2,128)} copy-done((f32[2,32]{1,0:T(2,128)}, f32[2,32]{1,0:T(2,128)S(1)}, u32[]{:S(2)}) %copy-start.11) | copy-done | bytes 280
  3.3 3.0 %collective-permute-start = (f32[128,128]{1,0:T(8,128)S(1)}, f32[128,128]{1,0:T(8,128)}, u32[]{:S(2)}, u32[]{:S(2)}) collective-permute-start(f32[128,128]{1,0:T(8,128)S(1)} %get-tuple-element.47), channel_id=1, source_target_pairs={{0,2},{1,3},{2,4},{3,5},{4,6},{5,7},{6,0},{7,1},{8,10},{9,11},{10,... | collective-permute-start | bytes 196616 | tf_op jit(solution)/shard_map/ppermute | solution.py:477
  6.3 1.4 %child_first.1 = (f32[32,8,8,128]{3,2,1,0:T(8,128)S(1)}, f32[256,128]{1,0:T(8,128)}, f32[256,128]{1,0:T(8,128)}, f32[4,32,128]{2,1,0:T(8,128)}) custom-call(f32[32,8,8,128]{3,2,1,0:T(8,128)S(1)} %get-tuple-element.35.x_ref, f32[32,8,128]{2,1,0:T(8,128)S(1)} %get-tuple-element.36.a_ref, f32[32,8,128]{2,1,0:T(8,128)S(1)} %get-tuple-element.37.b_ref, ...), custom_call_target="tpu_custom_call" | custom-call | flops 4000000 | bytes 3000000 | tf_op jit(solution)/shard_map/child_first/pallas_call | solution.py:24
  7.7 2.0 %collective-permute-start.1 = (f32[256,128]{1,0:T(8,128)}, f32[256,128]{1,0:T(8,128)S(1)}, u32[]{:S(2)}, u32[]{:S(2)}) collective-permute-start(f32[256,128]{1,0:T(8,128)} %get-tuple-element.48), channel_id=1, source_target_pairs={{1,2},{2,1},{3,4},{4,3},{5,6},{6,5},{7,0},{0,7},{9,10},{10,9},{11,... | collective-permute-start | bytes 393224 | tf_op jit(solution)/shard_map/ppermute | solution.py:486
  9.8 3.7 %all-to-all-start = ((f32[4,32,128]{2,1,0:T(8,128)}), f32[4,32,128]{2,1,0:T(8,128)S(1)}, u32[]{:S(2)}, u32[]{:S(2)}) async-start(f32[4,32,128]{2,1,0:T(8,128)} %get-tuple-element.42.after_ref), calls=%async_computation | async-start | bytes 131072 | tf_op jit(solution)/shard_map/all_to_all | solution.py:490
  13.5 2.0 %child_inner.2 = (f32[32,8,8,128]{3,2,1,0:T(8,128)S(1)}, f32[32,8,128]{2,1,0:T(8,128)S(1)}, f32[32,8,128]{2,1,0:T(8,128)S(1)}) custom-call(f32[32,8,8,128]{3,2,1,0:T(8,128)S(1)} %get-tuple-element.39.solved_ref, f32[4,32,8,128]{3,2,1,0:T(8,128)S(1)} %get-tuple-element.40.rates_ref, f32[8,128]{1,0:T(8,128)S(1)} %get-tuple-element.41.land_ref, ...), custom_call_target="tpu_custom_call" | custom-call | flops 10000000 | bytes 4000000 | tf_op jit(solution)/shard_map/child_inner/pallas_call | solution.py:24
  15.5 0.6 %copy-done = f32[32,8,128]{2,1,0:T(8,128)} copy-done((f32[32,8,128]{2,1,0:T(8,128)}, f32[32,8,128]{2,1,0:T(8,128)S(1)}, u32[]{:S(2)}) %copy-start) | copy-done | bytes 131096
  16.2 1.0 %parent_fed.1.fed_ref.parent_ref = f32[16,8,128]{2,1,0:T(8,128)S(1)} custom-call(f32[512,32]{1,0:T(8,128)S(1)} %bitcast.4, f32[128,128]{1,0:T(8,128)} %collective-permute-done.feed_ref, f32[32,8,8,128]{3,2,1,0:T(8,128)S(1)} %get-tuple-element.43.after_ref.inner_ref), custom_call_target="tpu_custom_call" | custom-call | flops 1000000000 | bytes 1000000 | tf_op jit(solution)/shard_map/parent_fed/pallas_call | solution.py:24
  17.1 1.2 %all-to-all-done.cols_in = f32[4,32,128]{2,1,0:T(8,128)S(1)} async-done(((f32[4,32,128]{2,1,0:T(8,128)}), f32[4,32,128]{2,1,0:T(8,128)S(1)}, u32[]{:S(2)}, u32[]{:S(2)}) %all-to-all-start) | async-done | bytes 65568 | tf_op jit(solution)/shard_map/all_to_all | solution.py:490
  18.5 0.7 %copy-done.1 = f32[32,8,128]{2,1,0:T(8,128)S(1)} copy-done((f32[32,8,128]{2,1,0:T(8,128)S(1)}, f32[32,8,128]{2,1,0:T(8,128)}, u32[]{:S(2)}) %copy-start.1) | copy-done | bytes 131096
  19.2 2.2 %child_between.1 = (f32[128,128]{1,0:T(8,128)}, f32[32,8,8,128]{3,2,1,0:T(8,128)S(1)}) custom-call(f32[32,8,8,128]{3,2,1,0:T(8,128)S(1)} %get-tuple-element.43.after_ref.inner_ref, f32[32,8,128]{2,1,0:T(8,128)S(1)} %get-tuple-element.44.row_ref, f32[32,8,128]{2,1,0:T(8,128)S(1)} %copy-done.1, f32[8,128]{1,0:T(8,128)S(1)} %copy-done.7, ...), custom_call_target="tpu_custom_call" | custom-call | flops 8000000 | bytes 3000000 | tf_op jit(solution)/shard_map/child_between/pallas_call | solution.py:24
  21.4 1.6 %child_second.1 = (f32[32,8,8,128]{3,2,1,0:T(8,128)S(1)}, f32[16,8,128]{2,1,0:T(8,128)S(1)}, f32[320,128]{1,0:T(8,128)}, f32[320,128]{1,0:T(8,128)}, f32[4,40,128]{2,1,0:T(8,128)}) custom-call(f32[32,8,8,128]{3,2,1,0:T(8,128)S(1)} %get-tuple-element.51.x_ref, f32[32,8,128]{2,1,0:T(8,128)S(1)} %get-tuple-element.36.a_ref, ...), custom_call_target="tpu_custom_call" | custom-call | flops 8000000 | bytes 3000000 | tf_op jit(solution)/shard_map/child_second/pallas_call | solution.py:24
  23.1 2.5 %collective-permute-start.4 = (f32[320,128]{1,0:T(8,128)}, f32[320,128]{1,0:T(8,128)S(1)}, u32[]{:S(2)}, u32[]{:S(2)}) collective-permute-start(f32[320,128]{1,0:T(8,128)} %get-tuple-element.60), channel_id=1, source_target_pairs={{1,2},{2,1},{3,4},{4,3},{5,6},{6,5},{7,0},{0,7},{9,10},{10,9},{11,... | collective-permute-start | bytes 491528 | tf_op jit(solution)/shard_map/ppermute | solution.py:486
  25.5 4.3 %all-to-all-start.1 = ((f32[4,40,128]{2,1,0:T(8,128)}), f32[4,40,128]{2,1,0:T(8,128)S(1)}, u32[]{:S(2)}, u32[]{:S(2)}) async-start(f32[4,40,128]{2,1,0:T(8,128)} %get-tuple-element.55.after_ref), calls=%async_computation.1 | async-start | bytes 163840 | tf_op jit(solution)/shard_map/all_to_all | solution.py:490
  29.9 2.0 %child_inner.3 = (f32[32,8,8,128]{3,2,1,0:T(8,128)S(1)}, f32[32,8,128]{2,1,0:T(8,128)S(1)}, f32[32,8,128]{2,1,0:T(8,128)S(1)}) custom-call(f32[32,8,8,128]{3,2,1,0:T(8,128)S(1)} %get-tuple-element.54.solved_ref, f32[4,32,8,128]{3,2,1,0:T(8,128)S(1)} %get-tuple-element.40.rates_ref, f32[8,128]{1,0:T(8,128)S(1)} %copy-done.5, ...), custom_call_target="tpu_custom_call" | custom-call | flops 10000000 | bytes 4000000 | tf_op jit(solution)/shard_map/child_inner/pallas_call | solution.py:24
  32.2 2.5 %all-to-all-done.1.cols_in = f32[4,40,128]{2,1,0:T(8,128)S(1)} async-done(((f32[4,40,128]{2,1,0:T(8,128)}), f32[4,40,128]{2,1,0:T(8,128)S(1)}, u32[]{:S(2)}, u32[]{:S(2)}) %all-to-all-start.1) | async-done | bytes 81952 | tf_op jit(solution)/shard_map/all_to_all | solution.py:490
  34.8 0.6 %copy-done.3 = f32[16,128]{1,0:T(8,128)S(1)} copy-done((f32[16,128]{1,0:T(8,128)S(1)}, f32[16,128]{1,0:T(8,128)}, u32[]{:S(2)}) %copy-start.3) | copy-done | bytes 8216
  35.5 1.0 %parent_second.1 = (f32[16,8,128]{2,1,0:T(8,128)S(1)}, f32[64,128]{1,0:T(8,128)S(1)}, f32[64,128]{1,0:T(8,128)S(1)}, f32[4,8,128]{2,1,0:T(8,128)}) custom-call(f32[16,8,128]{2,1,0:T(8,128)S(1)} %get-tuple-element.61.psolved_in, f32[5,16,128]{2,1,0:T(8,128)S(1)} %parent_rates_masked.1.prates_ref, f32[16,128]{1,0:T(8,128)S(1)} %get-tuple-element.49.after_ref.pa_ref, ...), custom_call_target="tpu_custom_call" | custom-call | flops 1000000 | bytes 500000 | tf_op jit(solution)/shard_map/parent_second/pallas_call | solution.py:24
  36.4 0.5 %collective-permute-start.7 = (f32[64,128]{1,0:T(8,128)S(1)}, f32[64,128]{1,0:T(8,128)S(1)}, u32[]{:S(2)}, u32[]{:S(2)}) collective-permute-start(f32[64,128]{1,0:T(8,128)S(1)} %get-tuple-element.66), channel_id=1, source_target_pairs={{1,2},{2,1},{3,4},{4,3},{5,6},{6,5},{7,0},{0,7},{9,10},{10,9},{11,... | collective-permute-start | bytes 98312 | tf_op jit(solution)/shard_map/ppermute | solution.py:486
  37.0 3.3 %all-to-all-start.2 = ((f32[4,8,128]{2,1,0:T(8,128)}), f32[4,8,128]{2,1,0:T(8,128)S(1)}, u32[]{:S(2)}, u32[]{:S(2)}) async-start(f32[4,8,128]{2,1,0:T(8,128)} %get-tuple-element.67), calls=%async_computation.2 | async-start | bytes 32768 | tf_op jit(solution)/shard_map/all_to_all | solution.py:490
  40.2 1.6 %child_last.1 = f32[32,8,8,128]{3,2,1,0:T(8,128)} custom-call(f32[32,8,8,128]{3,2,1,0:T(8,128)S(1)} %get-tuple-element.56.inner_ref.after_ref, f32[32,8,128]{2,1,0:T(8,128)S(1)} %get-tuple-element.57.row_ref, f32[32,8,128]{2,1,0:T(8,128)S(1)} %get-tuple-element.58.column_ref, f32[320,128]{1,0:T(8,128)S(1)} %collective-permute-done.3.mate_in, ...), custom_call_target="tpu_custom_call" | custom-call | flops 4000000 | bytes 3000000 | tf_op jit(solution)/shard_map/child_last/pallas_call | solution.py:24
  41.9 3.0 %all-to-all-done.2.cols_in = f32[4,8,128]{2,1,0:T(8,128)S(1)} async-done(((f32[4,8,128]{2,1,0:T(8,128)}), f32[4,8,128]{2,1,0:T(8,128)S(1)}, u32[]{:S(2)}, u32[]{:S(2)}) %all-to-all-start.2) | async-done | bytes 16416 | tf_op jit(solution)/shard_map/all_to_all | solution.py:490
  44.9 1.0 %parent_last.1 = f32[512,32]{1,0:T(8,128)} custom-call(f32[16,8,128]{2,1,0:T(8,128)S(1)} %get-tuple-element.64.psolved_in, f32[5,16,128]{2,1,0:T(8,128)S(1)} %parent_rates_masked.1.prates_ref, f32[64,128]{1,0:T(8,128)S(1)} %collective-permute-done.6.mate_in, f32[64,128]{1,0:T(8,128)S(1)} %collective-permute-done.7.far_in, ...), custom_call_target="tpu_custom_call" | custom-call | flops 500000 | bytes 500000 | tf_op jit(solution)/shard_map/parent_last/pallas_call | solution.py:24
  (37 shorter events, 0.6 us)
Async XLA Ops:
  2.7 0.6 %copy-start.11 = (f32[2,32]{1,0:T(2,128)}, f32[2,32]{1,0:T(2,128)S(1)}, u32[]{:S(2)}) copy-start(f32[2,32]{1,0:T(2,128)S(1)} %get-tuple-element.63.land_ref) | copy-start | bytes 772
  3.3 3.0 %copy-start.6 = (f32[8,128]{1,0:T(8,128)}, f32[8,128]{1,0:T(8,128)S(1)}, u32[]{:S(2)}) copy-start(f32[8,128]{1,0:T(8,128)S(1)} %get-tuple-element.46.relax_ref) | copy-start | bytes 12292
  3.3 10.2 %copy-start.4 = (f32[8,128]{1,0:T(8,128)}, f32[8,128]{1,0:T(8,128)S(1)}, u32[]{:S(2)}) copy-start(f32[8,128]{1,0:T(8,128)S(1)} %get-tuple-element.41.land_ref) | copy-start | bytes 12292
  3.3 12.8 %collective-permute-start = (f32[128,128]{1,0:T(8,128)S(1)}, f32[128,128]{1,0:T(8,128)}, u32[]{:S(2)}, u32[]{:S(2)}) collective-permute-start(f32[128,128]{1,0:T(8,128)S(1)} %get-tuple-element.47), channel_id=1, source_target_pairs={{0,2},{1,3},{2,4},{3,5},{4,6},{5,7},{6,0},{7,1},{8,10},{9,11},{10,... | collective-permute-start | bytes 196616 | tf_op jit(solution)/shard_map/ppermute | solution.py:477
  7.7 10.6 %collective-permute-start.1 = (f32[256,128]{1,0:T(8,128)}, f32[256,128]{1,0:T(8,128)S(1)}, u32[]{:S(2)}, u32[]{:S(2)}) collective-permute-start(f32[256,128]{1,0:T(8,128)} %get-tuple-element.48), channel_id=1, source_target_pairs={{1,2},{2,1},{3,4},{4,3},{5,6},{6,5},{7,0},{0,7},{9,10},{10,9},{11,... | collective-permute-start | bytes 393224 | tf_op jit(solution)/shard_map/ppermute | solution.py:486
  9.8 8.6 %all-to-all-start = ((f32[4,32,128]{2,1,0:T(8,128)}), f32[4,32,128]{2,1,0:T(8,128)S(1)}, u32[]{:S(2)}, u32[]{:S(2)}) async-start(f32[4,32,128]{2,1,0:T(8,128)} %get-tuple-element.42.after_ref), calls=%async_computation | async-start | bytes 131072 | tf_op jit(solution)/shard_map/all_to_all | solution.py:490
  13.5 5.0 %collective-permute-start.2 = (f32[256,128]{1,0:T(8,128)}, f32[256,128]{1,0:T(8,128)S(1)}, u32[]{:S(2)}, u32[]{:S(2)}) collective-permute-start(f32[256,128]{1,0:T(8,128)} %get-tuple-element.50), channel_id=1, source_target_pairs={{0,1},{1,0},{2,3},{3,2},{4,5},{5,4},{6,7},{7,6},{8,9},{9,8},{10,11... | collective-permute-start | bytes 393224 | tf_op jit(solution)/shard_map/ppermute | solution.py:486
  13.5 2.7 %copy-start.8 = (f32[32,8,2,32]{3,2,1,0:T(2,128)S(1)}, f32[32,8,2,32]{3,2,1,0:T(2,128)}, u32[]{:S(2)}) copy-start(f32[32,8,2,32]{3,2,1,0:T(2,128)} %param.10) | copy-start | bytes 196612
  15.5 0.6 %copy-start = (f32[32,8,128]{2,1,0:T(8,128)}, f32[32,8,128]{2,1,0:T(8,128)S(1)}, u32[]{:S(2)}) copy-start(f32[32,8,128]{2,1,0:T(8,128)S(1)} %get-tuple-element.45.column_ref) | copy-start | bytes 393220
  16.2 2.2 %copy-start.10 = (f32[32,2,32]{2,1,0:T(2,128)S(1)}, f32[32,2,32]{2,1,0:T(2,128)}, u32[]{:S(2)}) copy-start(f32[32,2,32]{2,1,0:T(2,128)} %param.15) | copy-start | bytes 24580
  18.3 0.9 %copy-start.1 = (f32[32,8,128]{2,1,0:T(8,128)S(1)}, f32[32,8,128]{2,1,0:T(8,128)}, u32[]{:S(2)}) copy-start(f32[32,8,128]{2,1,0:T(8,128)} %copy-done) | copy-start | bytes 393220
  18.5 2.9 %copy-start.2 = (f32[16,128]{1,0:T(8,128)}, f32[16,128]{1,0:T(8,128)S(1)}, u32[]{:S(2)}) copy-start(f32[16,128]{1,0:T(8,128)S(1)} %get-tuple-element.53.pc_ref) | copy-start | bytes 24580
  18.5 0.7 %copy-start.7 = (f32[8,128]{1,0:T(8,128)S(1)}, f32[8,128]{1,0:T(8,128)}, u32[]{:S(2)}) copy-start(f32[8,128]{1,0:T(8,128)} %copy-done.6) | copy-start | bytes 12292
  21.4 10.5 %collective-permute-start.5 = (f32[128,128]{1,0:T(8,128)}, f32[128,128]{1,0:T(8,128)S(1)}, u32[]{:S(2)}, u32[]{:S(2)}) collective-permute-start(f32[128,128]{1,0:T(8,128)} %get-tuple-element.62), channel_id=1, source_target_pairs={{0,2},{1,3},{2,4},{3,5},{4,6},{5,7},{6,0},{7,1},{8,10},{9,11},{10,... | collective-permute-start | bytes 196616 | tf_op jit(solution)/shard_map/ppermute | solution.py:477
  23.1 11.7 %collective-permute-start.4 = (f32[320,128]{1,0:T(8,128)}, f32[320,128]{1,0:T(8,128)S(1)}, u32[]{:S(2)}, u32[]{:S(2)}) collective-permute-start(f32[320,128]{1,0:T(8,128)} %get-tuple-element.60), channel_id=1, source_target_pairs={{1,2},{2,1},{3,4},{4,3},{5,6},{6,5},{7,0},{0,7},{9,10},{10,9},{11,... | collective-permute-start | bytes 491528 | tf_op jit(solution)/shard_map/ppermute | solution.py:486
  25.5 4.3 %copy-start.5 = (f32[8,128]{1,0:T(8,128)S(1)}, f32[8,128]{1,0:T(8,128)}, u32[]{:S(2)}) copy-start(f32[8,128]{1,0:T(8,128)} %copy-done.4) | copy-start | bytes 12292
  25.5 9.2 %all-to-all-start.1 = ((f32[4,40,128]{2,1,0:T(8,128)}), f32[4,40,128]{2,1,0:T(8,128)S(1)}, u32[]{:S(2)}, u32[]{:S(2)}) async-start(f32[4,40,128]{2,1,0:T(8,128)} %get-tuple-element.55.after_ref), calls=%async_computation.1 | async-start | bytes 163840 | tf_op jit(solution)/shard_map/all_to_all | solution.py:490
  29.9 5.0 %collective-permute-start.3 = (f32[320,128]{1,0:T(8,128)}, f32[320,128]{1,0:T(8,128)S(1)}, u32[]{:S(2)}, u32[]{:S(2)}) collective-permute-start(f32[320,128]{1,0:T(8,128)} %get-tuple-element.59), channel_id=1, source_target_pairs={{0,1},{1,0},{2,3},{3,2},{4,5},{5,4},{6,7},{7,6},{8,9},{9,8},{10,11... | collective-permute-start | bytes 491528 | tf_op jit(solution)/shard_map/ppermute | solution.py:486
  29.9 2.1 %copy-start.9 = (f32[4,32,2,32]{3,2,1,0:T(2,128)S(1)}, f32[4,32,2,32]{3,2,1,0:T(2,128)}, u32[]{:S(2)}) copy-start(f32[4,32,2,32]{3,2,1,0:T(2,128)} %param.14) | copy-start | bytes 98308
  32.2 2.5 %copy-start.12 = (f32[2,32]{1,0:T(2,128)S(1)}, f32[2,32]{1,0:T(2,128)}, u32[]{:S(2)}) copy-start(f32[2,32]{1,0:T(2,128)} %copy-done.11) | copy-start | bytes 772
  34.8 0.7 %copy-start.3 = (f32[16,128]{1,0:T(8,128)S(1)}, f32[16,128]{1,0:T(8,128)}, u32[]{:S(2)}) copy-start(f32[16,128]{1,0:T(8,128)} %copy-done.2) | copy-start | bytes 24580
  36.4 8.5 %collective-permute-start.6 = (f32[64,128]{1,0:T(8,128)S(1)}, f32[64,128]{1,0:T(8,128)S(1)}, u32[]{:S(2)}, u32[]{:S(2)}) collective-permute-start(f32[64,128]{1,0:T(8,128)S(1)} %get-tuple-element.65), channel_id=1, source_target_pairs={{0,1},{1,0},{2,3},{3,2},{4,5},{5,4},{6,7},{7,6},{8,9},{9,8},{10,11... | collective-permute-start | bytes 98312 | tf_op jit(solution)/shard_map/ppermute | solution.py:486
  36.4 8.5 %collective-permute-start.7 = (f32[64,128]{1,0:T(8,128)S(1)}, f32[64,128]{1,0:T(8,128)S(1)}, u32[]{:S(2)}, u32[]{:S(2)}) collective-permute-start(f32[64,128]{1,0:T(8,128)S(1)} %get-tuple-element.66), channel_id=1, source_target_pairs={{1,2},{2,1},{3,4},{4,3},{5,6},{6,5},{7,0},{0,7},{9,10},{10,9},{11,... | collective-permute-start | bytes 98312 | tf_op jit(solution)/shard_map/ppermute | solution.py:486
  37.0 7.9 %all-to-all-start.2 = ((f32[4,8,128]{2,1,0:T(8,128)}), f32[4,8,128]{2,1,0:T(8,128)S(1)}, u32[]{:S(2)}, u32[]{:S(2)}) async-start(f32[4,8,128]{2,1,0:T(8,128)} %get-tuple-element.67), calls=%async_computation.2 | async-start | bytes 32768 | tf_op jit(solution)/shard_map/all_to_all | solution.py:490

commit v10 on v8

--- a/solution.py
+++ b/solution.py
@@ -199,6 +199,10 @@
 
 
 def child_first(x_ref, a_ref, b_ref, c_ref, solved_ref, mate_rows, far_rows, cols_ref):
+    child_solve(x_ref, a_ref, b_ref, c_ref, solved_ref, mate_rows, far_rows, cols_ref, lambda k, v, _: x_ref[k, v])
+
+
+def child_solve(x_ref, a_ref, b_ref, c_ref, solved_ref, mate_rows, far_rows, cols_ref, load, row_ref=None):
     depth, vectors = x_ref.shape[0], x_ref.shape[1]
     half = depth // 2
 
@@ -206,8 +210,9 @@
         values = []
         for side, k in ((0, i), (1, depth - 1 - i)):
             a, b = a_ref[k], b_ref[k]
+            row_rates = None if row_ref is None else row_ref[k]
             for v in range(vectors):
-                y = a * x_ref[k, v] + b * carry[side * vectors + v]
+                y = a * load(k, v, row_rates) + b * carry[side * vectors + v]
                 solved_ref[k, v] = y
                 values.append(y)
         return tuple(values)
@@ -254,37 +259,33 @@
         merged_ref[part, :] = merge_edges(mate_cols[part, :], far_cols[part, :], LANES - 2)
 
 
-def edged(inner_ref, row_rates, column_rates, mate_ref, far_ref, edges, k, v, at, mates):
-    line = pl.ds(k * inner_ref.shape[1] + v, 1)
+def column_edged(inner_ref, column_rates, edges, k, v, at):
+    return inner_ref[k, v] + column_rates * pltpu.roll(edges, (LANES - 2 * at) & (LANES - 1), 1)
+
+
+def row_halo(mate_ref, far_ref, k, v, vectors, mates):
+    line = pl.ds(k * vectors + v, 1)
     mate = jnp.broadcast_to(mate_ref[line, :], (8, LANES))
     far = jnp.broadcast_to(far_ref[line, :], (8, LANES))
-    edge = pltpu.roll(edges, (LANES - 2 * at) & (LANES - 1), 1)
-    return inner_ref[k, v] + row_rates * jnp.where(mates, mate, far) + column_rates * edge
+    return jnp.where(mates, mate, far)
 
 
 def mate_rows_mask():
     return row_index() == 7 * (1 - parity("gy"))
 
 
-def child_between(
-    inner_ref, row_ref, column_ref, relax_ref, after_ref, mate_in, far_in, mate_cols, far_cols,
-    sums_out, x_ref,
-    sums_ref, merged_ref,
-):
+def child_columns(inner_ref, column_ref, relax_ref, mate_cols, far_cols, sums_ref, x_ref, merged_ref):
     depth, vectors = inner_ref.shape[0], inner_ref.shape[1]
     half, groups = depth // 2, depth // LEVELS
-    mates = mate_rows_mask()
     weights = [relax_ref[j : j + 1, :] for j in range(8)]
     edge_merger(mate_cols, far_cols, merged_ref)
 
     def level(i, _, edges):
         inside = lax.rem(i, LEVELS)
         for side, k, base in ((0, i, inside * vectors), (1, depth - 1 - i, (LEVELS - 1 - inside) * vectors)):
-            row_rates, column_rates = row_ref[k], column_ref[k]
+            column_rates = column_ref[k]
             for v in range(vectors):
-                x_ref[k, v] = edged(
-                    inner_ref, row_rates, column_rates, mate_in, far_in, edges[side], k, v, base + v, mates
-                )
+                x_ref[k, v] = column_edged(inner_ref, column_rates, edges[side], k, v, base + v)
             block_rows(x_ref, k, weights, sums_ref, i, side)
         return 0
 
@@ -293,11 +294,25 @@
         lax.fori_loop(
             LEVELS * group, LEVELS * (group + 1), lambda i, _, edges=edges: level(i, _, edges), 0, unroll=4
         )
+
+
+def child_rows(sums_in, row_ref, relax_ref, after_ref, mate_in, far_in, sums_out, sums_ref):
+    depth = row_ref.shape[0]
+    vectors = 2 * sums_in.shape[0] // depth
+    swap = jnp.broadcast_to(parity("gy"), (vectors, LANES)) == 1
+    for k in range(depth):
+        place, i = (0, k) if k < depth // 2 else (1, depth - 1 - k)
+        lines = slice(k * vectors, (k + 1) * vectors)
+        mate, far = mate_in[lines, :], far_in[lines, :]
+        for r, at, halo in ((0, 0, jnp.where(swap, mate, far)), (1, 7, jnp.where(swap, far, mate))):
+            share = (row_ref[k, at : at + 1, :] * relax_ref[at : at + 1, :]) * halo
+            part = slice(i * vectors, (i + 1) * vectors), slice((2 * place + r) * LANES, (2 * place + r + 1) * LANES)
+            sums_ref[part] = sums_in[part] + share
     sums_out[...] = block_columns(sums_ref)
 
 
 def child_second(
-    x_ref, a_ref, b_ref, c_ref, parent_ref, pa_ref, pb_ref, pc_ref,
+    x_ref, row_ref, mate_in, far_in, a_ref, b_ref, c_ref, parent_ref, pa_ref, pb_ref, pc_ref,
     solved_ref, psolved_ref, mate_rows, far_rows, cols_ref,
 ):
     depth, vectors = x_ref.shape[0], x_ref.shape[1]
@@ -307,7 +322,12 @@
         psolved_ref[i] = y
     lines, at = depth * vectors, depth // LEVELS * 8
     parent_up(y, pc_ref, psolved_ref, mate_rows, far_rows, lines, cols_ref, at)
-    child_first(x_ref, a_ref, b_ref, c_ref, solved_ref, mate_rows, far_rows, cols_ref)
+    mates = mate_rows_mask()
+
+    def load(k, v, row_rates):
+        return x_ref[k, v] + row_rates * row_halo(mate_in, far_in, k, v, vectors, mates)
+
+    child_solve(x_ref, a_ref, b_ref, c_ref, solved_ref, mate_rows, far_rows, cols_ref, load, row_ref)
 
 
 def child_last(
@@ -324,9 +344,9 @@
             k = LEVELS * group + inside
             row_rates, column_rates = row_ref[k], column_ref[k]
             for v in range(vectors):
-                out_ref[k, v] = edged(
-                    inner_ref, row_rates, column_rates, mate_in, far_in, edges, k, v, inside * vectors + v, mates
-                )
+                out_ref[k, v] = column_edged(
+                    inner_ref, column_rates, edges, k, v, inside * vectors + v
+                ) + row_rates * row_halo(mate_in, far_in, k, v, vectors, mates)
             return 0
 
         lax.fori_loop(0, LEVELS, level, 0, unroll=4)
@@ -349,7 +369,7 @@
         packed_ref[i] = packed_ref[i] + feed_ref[vectors * i : vectors * (i + 1), :]
 
 
-def parent_factors(mix_ref, fed_ref, far_ref, mate_cols, far_cols, pa_ref, pb_ref, pc_ref, mixed):
+def parent_factors(mix_ref, fed_ref, far_ref, x_ref, sums_ref, pa_ref, pb_ref, pc_ref, mixed):
     half = pa_ref.shape[0]
     for i in range(half):
         for h, r, lo in PLACES:
@@ -557,21 +577,29 @@
         LONG,
         1_000_000,
     )
+    raw_sums, x = call(
+        child_columns,
+        [shape(half * vectors, 4 * LANES), field],
+        edge_scratch,
+        [inner, column_rates, relax, *halos[2:]],
+        INNER,
+        3_000_000,
+    )
     pa, pb, pc = call(
         parent_factors,
         [shape(half, LANES)] * 3,
         [pltpu.VMEM((half, LANES), F32)],
-        [parent_mixing.reshape(-1, narrow), fed, *halos[1:]],
+        [parent_mixing.reshape(-1, narrow), fed, halos[1], x, raw_sums],
         LONG,
         1_000_000,
     )
-    sums2, x = call(
-        child_between,
-        [sums, field],
-        [sum_scratch] + edge_scratch,
-        [inner, row_rates, column_rates, relax, pa, *halos],
-        8_000_000,
-        3_000_000,
+    sums2 = call(
+        child_rows,
+        sums,
+        [sum_scratch],
+        [raw_sums, row_rates, relax, pa, *halos[:2]],
+        INNER,
+        1_000_000,
     )
     feed = passed_along(sums2, "gy", quarter)
     rows = count + half // 2 * vectors
@@ -579,7 +607,7 @@
         child_second,
         [field, tiles, shape(rows, LANES), shape(rows, LANES), shape(edge + 8, LANES)],
         [],
-        [x, a, b, c, fed, pa, pb, pc],
+        [x, row_rates, *halos[:2], a, b, c, fed, pa, pb, pc],
         8_000_000,
         3_000_000,
     )

time: 35.2 us -> 34.7 us (0.986)
  starting transfers between devices: 17.1 us -> 16.2 us
  local copies, waits for them, and re-layouts: 0.01 us -> 0.62 us
  waiting for transfers between devices: 5.97 us -> 5.54 us
    ppermute x12, starting transfers between devices: 13.8 us -> 12.9 us  [swapped(): return lax.ppermute(value, axis, pairs)]
    unnamed x6, local copies, waits for them, and re-layouts: 0.01 us -> 0.62 us
    ppermute x12, waiting for transfers between devices: 5.97 us -> 5.53 us  [swapped(): return lax.ppermute(value, axis, pairs)]
    pallas_call x13 -> x14, Pallas kernels: 11.2 us -> 11.3 us  [call(): pl.pallas_call(body, out_shape=outs, in_specs=[FAR if i in far_in else VM...]
  transfers between devices with their start and end apart: 14 -> 14, of which waited for: 6 -> 6; matrix products, arithmetic and copies ran while one was open for 0% -> 0% of each run, Pallas kernels for 17% -> 22%
where the time goes in v10:
time: 34.7 us; the launch traced here: 34.4 us
  starting transfers between devices  16.2 us (47%)
  Pallas kernels  11.3 us (33%)
  waiting for transfers between devices  5.54 us (16%)
  between operations  0.78 us (2%)
  local copies, waits for them, and re-layouts  0.62 us (2%)
    ppermute x12, starting transfers between devices, swapped(): return lax.ppermute(value, axis, pairs)  12.9 us
    pallas_call x14, Pallas kernels, call(): pl.pallas_call(body, out_shape=outs, in_specs=[FAR if i in far_in else VM...  11.3 us
    ppermute x12, waiting for transfers between devices, swapped(): return lax.ppermute(value, axis, pairs)  5.53 us
    ppermute x2, starting transfers between devices, passed_along(): lax.ppermute(value, axis, [(i, (i + steps) % count) for i in range(count)])  3.3 us
  transfers between devices with their start and end apart: 14, of which 6 were waited for; matrix products, arithmetic and copies ran while one was open for 0% of the time, Pallas kernels for 22%

profile of v10, /device:TPU:0, one launch (start us, length us, event | category | flops | bytes accessed | tf_op | source)
XLA Modules:
  0.0 34.4 jit_solution(15459847727860090712)
XLA Ops:
  0.6 2.1 %begin.1 = (f32[128,128]{1,0:T(8,128)S(1)}, f32[32,8,8,128]{3,2,1,0:T(8,128)S(1)}, f32[32,8,128]{2,1,0:T(8,128)S(1)}, f32[32,8,128]{2,1,0:T(8,128)S(1)}, f32[32,...) custom-call(f32[32,8,8,128]{3,2,1,0:T(8,128)} %x_hbm.1, ...), custom_call_target="tpu_custom_call" | custom-call | flops 4000000 | bytes 3000000 | tf_op jit(solution)/shard_map/begin/pallas_call | solution.py:24
  2.7 3.1 %collective-permute-start.4 = (f32[128,128]{1,0:T(8,128)S(1)}, f32[128,128]{1,0:T(8,128)S(1)}, u32[]{:S(2)}, u32[]{:S(2)}) collective-permute-start(f32[128,128]{1,0:T(8,128)S(1)} %get-tuple-element.50), channel_id=1, source_target_pairs={{0,2},{1,3},{2,4},{3,5},{4,6},{5,7},{6,0},{7,1},{8,10},{9,11},{10,... | collective-permute-start | bytes 196616 | tf_op jit(solution)/shard_map/ppermute | solution.py:498
  5.8 0.7 %child_first.1 = (f32[32,8,8,128]{3,2,1,0:T(8,128)S(1)}, f32[256,128]{1,0:T(8,128)S(1)}, f32[256,128]{1,0:T(8,128)S(1)}, f32[32,128]{1,0:T(8,128)S(1)}) custom-call(f32[32,8,8,128]{3,2,1,0:T(8,128)S(1)} %get-tuple-element.35.x_ref, f32[32,8,128]{2,1,0:T(8,128)S(1)} %get-tuple-element.36.a_ref, f32[32,8,128]{2,1,0:T(8,128)S(1)} %get-tuple-element.37.b_ref, ...), custom_call_target="tpu_custom_call" | custom-call | flops 4000000 | bytes 3000000 | tf_op jit(solution)/shard_map/child_first/pallas_call | solution.py:24
  6.5 1.6 %collective-permute-start.3 = (f32[256,128]{1,0:T(8,128)S(1)}, f32[256,128]{1,0:T(8,128)S(1)}, u32[]{:S(2)}, u32[]{:S(2)}) collective-permute-start(f32[256,128]{1,0:T(8,128)S(1)} %get-tuple-element.49), channel_id=1, source_target_pairs={{1,2},{2,1},{3,4},{4,3},{5,6},{6,5},{7,0},{0,7},{9,10},{10,9},{11,... | collective-permute-start | bytes 393224 | tf_op jit(solution)/shard_map/ppermute | solution.py:507
  8.1 2.4 %collective-permute-start.1 = (f32[32,128]{1,0:T(8,128)S(1)}, f32[32,128]{1,0:T(8,128)S(1)}, u32[]{:S(2)}, u32[]{:S(2)}) collective-permute-start(f32[32,128]{1,0:T(8,128)S(1)} %get-tuple-element.42.after_ref), channel_id=1, source_target_pairs={{8,16},{16,8},{24,0},{0,24},{9,17},{17,9},{25,1},{1,25},{10,18},{1... | collective-permute-start | bytes 49160 | tf_op jit(solution)/shard_map/ppermute | solution.py:507
  10.5 0.5 %collective-permute-start = (f32[32,128]{1,0:T(8,128)S(1)}, f32[32,128]{1,0:T(8,128)S(1)}, u32[]{:S(2)}, u32[]{:S(2)}) collective-permute-start(f32[32,128]{1,0:T(8,128)S(1)} %get-tuple-element.42.after_ref), channel_id=1, source_target_pairs={{0,8},{8,0},{16,24},{24,16},{1,9},{9,1},{17,25},{25,17},{2,10},{10... | collective-permute-start | bytes 49160 | tf_op jit(solution)/shard_map/ppermute | solution.py:507
  11.1 1.1 %child_inner.2 = (f32[32,8,8,128]{3,2,1,0:T(8,128)S(1)}, f32[32,8,128]{2,1,0:T(8,128)S(1)}, f32[32,8,128]{2,1,0:T(8,128)S(1)}) custom-call(f32[32,8,8,128]{3,2,1,0:T(8,128)S(1)} %get-tuple-element.39.solved_ref, f32[4,32,8,128]{3,2,1,0:T(8,128)S(1)} %get-tuple-element.40.rates_ref, f32[8,128]{1,0:T(8,128)S(1)} %get-tuple-element.41.land_ref, ...), custom_call_target="tpu_custom_call" | custom-call | flops 10000000 | bytes 4000000 | tf_op jit(solution)/shard_map/child_inner/pallas_call | solution.py:24
  12.2 0.5 %collective-permute-done.1.far_cols = f32[32,128]{1,0:T(8,128)S(1)} collective-permute-done((f32[32,128]{1,0:T(8,128)S(1)}, f32[32,128]{1,0:T(8,128)S(1)}, u32[]{:S(2)}, u32[]{:S(2)}) %collective-permute-start.1) | collective-permute-done | bytes 16416 | tf_op jit(solution)/shard_map/ppermute | solution.py:507
  12.7 1.5 %collective-permute-done.mate_cols = f32[32,128]{1,0:T(8,128)S(1)} collective-permute-done((f32[32,128]{1,0:T(8,128)S(1)}, f32[32,128]{1,0:T(8,128)S(1)}, u32[]{:S(2)}, u32[]{:S(2)}) %collective-permute-start) | collective-permute-done | bytes 16416 | tf_op jit(solution)/shard_map/ppermute | solution.py:507
  14.3 1.2 %child_columns.1 = (f32[128,512]{1,0:T(8,128)S(1)}, f32[32,8,8,128]{3,2,1,0:T(8,128)S(1)}) custom-call(f32[32,8,8,128]{3,2,1,0:T(8,128)S(1)} %get-tuple-element.43.inner_ref.after_ref, f32[32,8,128]{2,1,0:T(8,128)S(1)} %get-tuple-element.44.column_ref, f32[8,128]{1,0:T(8,128)S(1)} %get-tuple-element.45.relax_ref, ...), custom_call_target="tpu_custom_call" | custom-call | flops 10000000 | bytes 3000000 | tf_op jit(solution)/shard_map/child_columns/pallas_call | solution.py:24
  15.7 0.6 %copy-done.2 = f32[32,2,32]{2,1,0:T(2,128)S(1)} copy-done((f32[32,2,32]{2,1,0:T(2,128)S(1)}, f32[32,2,32]{2,1,0:T(2,128)}, u32[]{:S(2)}) %copy-start.2) | copy-done | bytes 8216
  17.0 1.1 %child_second.1 = (f32[32,8,8,128]{3,2,1,0:T(8,128)S(1)}, f32[16,8,128]{2,1,0:T(8,128)S(1)}, f32[320,128]{1,0:T(8,128)S(1)}, f32[320,128]{1,0:T(8,128)S(1)}, f32[40,128]{1,0:T(8,128)S(1)}) custom-call(f32[32,8,8,128]{3,2,1,0:T(8,128)S(1)} %get-tuple-element.46.x_ref, f32[32,8,128]{2,1,0:T(8,128)S(1)} %get-tuple-element.47.row_ref, ...), custom_call_target="tpu_custom_call" | custom-call | flops 8000000 | bytes 3000000 | tf_op jit(solution)/shard_map/child_second/pallas_call | solution.py:24
  18.1 2.1 %collective-permute-start.6 = (f32[320,128]{1,0:T(8,128)S(1)}, f32[320,128]{1,0:T(8,128)S(1)}, u32[]{:S(2)}, u32[]{:S(2)}) collective-permute-start(f32[320,128]{1,0:T(8,128)S(1)} %get-tuple-element.61), channel_id=1, source_target_pairs={{1,2},{2,1},{3,4},{4,3},{5,6},{6,5},{7,0},{0,7},{9,10},{10,9},{11,... | collective-permute-start | bytes 491528 | tf_op jit(solution)/shard_map/ppermute | solution.py:507
  20.2 1.2 %collective-permute-start.8 = (f32[40,128]{1,0:T(8,128)S(1)}, f32[40,128]{1,0:T(8,128)S(1)}, u32[]{:S(2)}, u32[]{:S(2)}) collective-permute-start(f32[40,128]{1,0:T(8,128)S(1)} %get-tuple-element.56.after_ref), channel_id=1, source_target_pairs={{8,16},{16,8},{24,0},{0,24},{9,17},{17,9},{25,1},{1,25},{10,18},{1... | collective-permute-start | bytes 61448 | tf_op jit(solution)/shard_map/ppermute | solution.py:507
  21.4 0.8 %collective-permute-start.7 = (f32[40,128]{1,0:T(8,128)S(1)}, f32[40,128]{1,0:T(8,128)S(1)}, u32[]{:S(2)}, u32[]{:S(2)}) collective-permute-start(f32[40,128]{1,0:T(8,128)S(1)} %get-tuple-element.56.after_ref), channel_id=1, source_target_pairs={{0,8},{8,0},{16,24},{24,16},{1,9},{9,1},{17,25},{25,17},{2,10},{10... | collective-permute-start | bytes 61448 | tf_op jit(solution)/shard_map/ppermute | solution.py:507
  22.2 1.1 %child_inner.3 = (f32[32,8,8,128]{3,2,1,0:T(8,128)S(1)}, f32[32,8,128]{2,1,0:T(8,128)S(1)}, f32[32,8,128]{2,1,0:T(8,128)S(1)}) custom-call(f32[32,8,8,128]{3,2,1,0:T(8,128)S(1)} %get-tuple-element.55.solved_ref, f32[4,32,8,128]{3,2,1,0:T(8,128)S(1)} %get-tuple-element.40.rates_ref, f32[8,128]{1,0:T(8,128)S(1)} %get-tuple-element.41.land_ref, ...), custom_call_target="tpu_custom_call" | custom-call | flops 10000000 | bytes 4000000 | tf_op jit(solution)/shard_map/child_inner/pallas_call | solution.py:24
  23.6 1.3 %collective-permute-done.8.far_cols = f32[40,128]{1,0:T(8,128)S(1)} collective-permute-done((f32[40,128]{1,0:T(8,128)S(1)}, f32[40,128]{1,0:T(8,128)S(1)}, u32[]{:S(2)}, u32[]{:S(2)}) %collective-permute-start.8) | collective-permute-done | bytes 20512 | tf_op jit(solution)/shard_map/ppermute | solution.py:507
  25.2 1.0 %collective-permute-done.6.far_in.far_ref = f32[320,128]{1,0:T(8,128)S(1)} collective-permute-done((f32[320,128]{1,0:T(8,128)S(1)}, f32[320,128]{1,0:T(8,128)S(1)}, u32[]{:S(2)}, u32[]{:S(2)}) %collective-permute-start.6) | collective-permute-done | bytes 163872 | tf_op jit(solution)/shard_map/ppermute | solution.py:507
  26.7 2.3 %collective-permute-start.11 = (f32[64,128]{1,0:T(8,128)S(1)}, f32[64,128]{1,0:T(8,128)S(1)}, u32[]{:S(2)}, u32[]{:S(2)}) collective-permute-start(f32[64,128]{1,0:T(8,128)S(1)} %get-tuple-element.66), channel_id=1, source_target_pairs={{1,2},{2,1},{3,4},{4,3},{5,6},{6,5},{7,0},{0,7},{9,10},{10,9},{11,... | collective-permute-start | bytes 98312 | tf_op jit(solution)/shard_map/ppermute | solution.py:507
  28.9 0.9 %collective-permute-start.13 = (f32[8,128]{1,0:T(8,128)S(1)}, f32[8,128]{1,0:T(8,128)S(1)}, u32[]{:S(2)}, u32[]{:S(2)}) collective-permute-start(f32[8,128]{1,0:T(8,128)S(1)} %get-tuple-element.67), channel_id=1, source_target_pairs={{8,16},{16,8},{24,0},{0,24},{9,17},{17,9},{25,1},{1,25},{10,18},{1... | collective-permute-start | bytes 12296 | tf_op jit(solution)/shard_map/ppermute | solution.py:507
  29.8 1.1 %collective-permute-start.12 = (f32[8,128]{1,0:T(8,128)S(1)}, f32[8,128]{1,0:T(8,128)S(1)}, u32[]{:S(2)}, u32[]{:S(2)}) collective-permute-start(f32[8,128]{1,0:T(8,128)S(1)} %get-tuple-element.67), channel_id=1, source_target_pairs={{0,8},{8,0},{16,24},{24,16},{1,9},{9,1},{17,25},{25,17},{2,10},{10... | collective-permute-start | bytes 12296 | tf_op jit(solution)/shard_map/ppermute | solution.py:507
  30.9 1.6 %child_last.1 = f32[32,8,8,128]{3,2,1,0:T(8,128)} custom-call(f32[32,8,8,128]{3,2,1,0:T(8,128)S(1)} %get-tuple-element.57.inner_ref.after_ref, f32[32,8,128]{2,1,0:T(8,128)S(1)} %get-tuple-element.58.row_ref, f32[32,8,128]{2,1,0:T(8,128)S(1)} %get-tuple-element.59.column_ref, f32[320,128]{1,0:T(8,128)S(1)} %collective-permute-done.5.mate_in, ...), custom_call_target="tpu_custom_call" | custom-call | flops 4000000 | bytes 3000000 | tf_op jit(solution)/shard_map/child_last/pallas_call | solution.py:24
  32.6 0.9 %collective-permute-done.13.far_cols = f32[8,128]{1,0:T(8,128)S(1)} collective-permute-done((f32[8,128]{1,0:T(8,128)S(1)}, f32[8,128]{1,0:T(8,128)S(1)}, u32[]{:S(2)}, u32[]{:S(2)}) %collective-permute-start.13) | collective-permute-done | bytes 4128 | tf_op jit(solution)/shard_map/ppermute | solution.py:507
  33.5 1.0 %parent_last.1 = f32[512,32]{1,0:T(8,128)} custom-call(f32[16,8,128]{2,1,0:T(8,128)S(1)} %get-tuple-element.64.psolved_in, f32[5,16,128]{2,1,0:T(8,128)S(1)} %parent_rates_masked.1.prates_ref, f32[64,128]{1,0:T(8,128)S(1)} %collective-permute-done.10.mate_in, f32[64,128]{1,0:T(8,128)S(1)} %collective-permute-done.11.far_in, ...), custom_call_target="tpu_custom_call" | custom-call | flops 500000 | bytes 500000 | tf_op jit(solution)/shard_map/parent_last/pallas_call | solution.py:24
  (24 shorter events, 1.9 us)
Async XLA Ops:
  2.7 12.7 %collective-permute-start.4 = (f32[128,128]{1,0:T(8,128)S(1)}, f32[128,128]{1,0:T(8,128)S(1)}, u32[]{:S(2)}, u32[]{:S(2)}) collective-permute-start(f32[128,128]{1,0:T(8,128)S(1)} %get-tuple-element.50), channel_id=1, source_target_pairs={{0,2},{1,3},{2,4},{3,5},{4,6},{5,7},{6,0},{7,1},{8,10},{9,11},{10,... | collective-permute-start | bytes 196616 | tf_op jit(solution)/shard_map/ppermute | solution.py:498
  6.5 9.1 %collective-permute-start.3 = (f32[256,128]{1,0:T(8,128)S(1)}, f32[256,128]{1,0:T(8,128)S(1)}, u32[]{:S(2)}, u32[]{:S(2)}) collective-permute-start(f32[256,128]{1,0:T(8,128)S(1)} %get-tuple-element.49), channel_id=1, source_target_pairs={{1,2},{2,1},{3,4},{4,3},{5,6},{6,5},{7,0},{0,7},{9,10},{10,9},{11,... | collective-permute-start | bytes 393224 | tf_op jit(solution)/shard_map/ppermute | solution.py:507
  8.1 4.6 %collective-permute-start.1 = (f32[32,128]{1,0:T(8,128)S(1)}, f32[32,128]{1,0:T(8,128)S(1)}, u32[]{:S(2)}, u32[]{:S(2)}) collective-permute-start(f32[32,128]{1,0:T(8,128)S(1)} %get-tuple-element.42.after_ref), channel_id=1, source_target_pairs={{8,16},{16,8},{24,0},{0,24},{9,17},{17,9},{25,1},{1,25},{10,18},{1... | collective-permute-start | bytes 49160 | tf_op jit(solution)/shard_map/ppermute | solution.py:507
  10.5 3.7 %collective-permute-start = (f32[32,128]{1,0:T(8,128)S(1)}, f32[32,128]{1,0:T(8,128)S(1)}, u32[]{:S(2)}, u32[]{:S(2)}) collective-permute-start(f32[32,128]{1,0:T(8,128)S(1)} %get-tuple-element.42.after_ref), channel_id=1, source_target_pairs={{0,8},{8,0},{16,24},{24,16},{1,9},{9,1},{17,25},{25,17},{2,10},{10... | collective-permute-start | bytes 49160 | tf_op jit(solution)/shard_map/ppermute | solution.py:507
  11.1 5.4 %collective-permute-start.2 = (f32[256,128]{1,0:T(8,128)S(1)}, f32[256,128]{1,0:T(8,128)S(1)}, u32[]{:S(2)}, u32[]{:S(2)}) collective-permute-start(f32[256,128]{1,0:T(8,128)S(1)} %get-tuple-element.48), channel_id=1, source_target_pairs={{0,1},{1,0},{2,3},{3,2},{4,5},{5,4},{6,7},{7,6},{8,9},{9,8},{10,11... | collective-permute-start | bytes 393224 | tf_op jit(solution)/shard_map/ppermute | solution.py:507
  14.3 1.2 %copy-start = (f32[32,8,2,32]{3,2,1,0:T(2,128)S(1)}, f32[32,8,2,32]{3,2,1,0:T(2,128)}, u32[]{:S(2)}) copy-start(f32[32,8,2,32]{3,2,1,0:T(2,128)} %param.10) | copy-start | bytes 196612
  15.5 0.8 %copy-start.2 = (f32[32,2,32]{2,1,0:T(2,128)S(1)}, f32[32,2,32]{2,1,0:T(2,128)}, u32[]{:S(2)}) copy-start(f32[32,2,32]{2,1,0:T(2,128)} %param.15) | copy-start | bytes 24580
  16.8 6.5 %collective-permute-start.9 = (f32[128,128]{1,0:T(8,128)S(1)}, f32[128,128]{1,0:T(8,128)S(1)}, u32[]{:S(2)}, u32[]{:S(2)}) collective-permute-start(f32[128,128]{1,0:T(8,128)S(1)} %child_rows.1), channel_id=1, source_target_pairs={{0,2},{1,3},{2,4},{3,5},{4,6},{5,7},{6,0},{7,1},{8,10},{9,11},{10,... | collective-permute-start | bytes 196616 | tf_op jit(solution)/shard_map/ppermute | solution.py:498
  18.1 8.0 %collective-permute-start.6 = (f32[320,128]{1,0:T(8,128)S(1)}, f32[320,128]{1,0:T(8,128)S(1)}, u32[]{:S(2)}, u32[]{:S(2)}) collective-permute-start(f32[320,128]{1,0:T(8,128)S(1)} %get-tuple-element.61), channel_id=1, source_target_pairs={{1,2},{2,1},{3,4},{4,3},{5,6},{6,5},{7,0},{0,7},{9,10},{10,9},{11,... | collective-permute-start | bytes 491528 | tf_op jit(solution)/shard_map/ppermute | solution.py:507
  20.2 4.7 %collective-permute-start.8 = (f32[40,128]{1,0:T(8,128)S(1)}, f32[40,128]{1,0:T(8,128)S(1)}, u32[]{:S(2)}, u32[]{:S(2)}) collective-permute-start(f32[40,128]{1,0:T(8,128)S(1)} %get-tuple-element.56.after_ref), channel_id=1, source_target_pairs={{8,16},{16,8},{24,0},{0,24},{9,17},{17,9},{25,1},{1,25},{10,18},{1... | collective-permute-start | bytes 61448 | tf_op jit(solution)/shard_map/ppermute | solution.py:507
  21.4 3.8 %collective-permute-start.7 = (f32[40,128]{1,0:T(8,128)S(1)}, f32[40,128]{1,0:T(8,128)S(1)}, u32[]{:S(2)}, u32[]{:S(2)}) collective-permute-start(f32[40,128]{1,0:T(8,128)S(1)} %get-tuple-element.56.after_ref), channel_id=1, source_target_pairs={{0,8},{8,0},{16,24},{24,16},{1,9},{9,1},{17,25},{25,17},{2,10},{10... | collective-permute-start | bytes 61448 | tf_op jit(solution)/shard_map/ppermute | solution.py:507
  22.2 4.0 %collective-permute-start.5 = (f32[320,128]{1,0:T(8,128)S(1)}, f32[320,128]{1,0:T(8,128)S(1)}, u32[]{:S(2)}, u32[]{:S(2)}) collective-permute-start(f32[320,128]{1,0:T(8,128)S(1)} %get-tuple-element.60), channel_id=1, source_target_pairs={{0,1},{1,0},{2,3},{3,2},{4,5},{5,4},{6,7},{7,6},{8,9},{9,8},{10,11... | collective-permute-start | bytes 491528 | tf_op jit(solution)/shard_map/ppermute | solution.py:507
  22.2 1.1 %copy-start.1 = (f32[4,32,2,32]{3,2,1,0:T(2,128)S(1)}, f32[4,32,2,32]{3,2,1,0:T(2,128)}, u32[]{:S(2)}) copy-start(f32[4,32,2,32]{3,2,1,0:T(2,128)} %param.14) | copy-start | bytes 98308
  26.6 6.9 %collective-permute-start.10 = (f32[64,128]{1,0:T(8,128)S(1)}, f32[64,128]{1,0:T(8,128)S(1)}, u32[]{:S(2)}, u32[]{:S(2)}) collective-permute-start(f32[64,128]{1,0:T(8,128)S(1)} %get-tuple-element.65), channel_id=1, source_target_pairs={{0,1},{1,0},{2,3},{3,2},{4,5},{5,4},{6,7},{7,6},{8,9},{9,8},{10,11... | collective-permute-start | bytes 98312 | tf_op jit(solution)/shard_map/ppermute | solution.py:507
  26.7 6.8 %collective-permute-start.11 = (f32[64,128]{1,0:T(8,128)S(1)}, f32[64,128]{1,0:T(8,128)S(1)}, u32[]{:S(2)}, u32[]{:S(2)}) collective-permute-start(f32[64,128]{1,0:T(8,128)S(1)} %get-tuple-element.66), channel_id=1, source_target_pairs={{1,2},{2,1},{3,4},{4,3},{5,6},{6,5},{7,0},{0,7},{9,10},{10,9},{11,... | collective-permute-start | bytes 98312 | tf_op jit(solution)/shard_map/ppermute | solution.py:507
  28.9 4.5 %collective-permute-start.13 = (f32[8,128]{1,0:T(8,128)S(1)}, f32[8,128]{1,0:T(8,128)S(1)}, u32[]{:S(2)}, u32[]{:S(2)}) collective-permute-start(f32[8,128]{1,0:T(8,128)S(1)} %get-tuple-element.67), channel_id=1, source_target_pairs={{8,16},{16,8},{24,0},{0,24},{9,17},{17,9},{25,1},{1,25},{10,18},{1... | collective-permute-start | bytes 12296 | tf_op jit(solution)/shard_map/ppermute | solution.py:507
  29.8 3.6 %collective-permute-start.12 = (f32[8,128]{1,0:T(8,128)S(1)}, f32[8,128]{1,0:T(8,128)S(1)}, u32[]{:S(2)}, u32[]{:S(2)}) collective-permute-start(f32[8,128]{1,0:T(8,128)S(1)} %get-tuple-element.67), channel_id=1, source_target_pairs={{0,8},{8,0},{16,24},{24,16},{1,9},{9,1},{17,25},{25,17},{2,10},{10... | collective-permute-start | bytes 12296 | tf_op jit(solution)/shard_map/ppermute | solution.py:507

commit v11 on v10

--- a/solution.py
+++ b/solution.py
@@ -274,7 +274,7 @@
     return row_index() == 7 * (1 - parity("gy"))
 
 
-def child_columns(inner_ref, column_ref, relax_ref, mate_cols, far_cols, sums_ref, x_ref, merged_ref):
+def child_columns(inner_ref, column_ref, relax_ref, after_ref, mate_cols, far_cols, sums_ref, x_ref, merged_ref):
     depth, vectors = inner_ref.shape[0], inner_ref.shape[1]
     half, groups = depth // 2, depth // LEVELS
     weights = [relax_ref[j : j + 1, :] for j in range(8)]
@@ -360,21 +360,18 @@
 PLACES = [(h, r, 64 * h + 32 * r) for h in range(2) for r in range(2)]
 
 
-def parent_fed(parent_ref, feed_ref, after_ref, packed_ref):
+def parent_fed(parent_ref, mix_ref, feed_ref, after_ref, packed_ref, mixed):
     half, vectors = packed_ref.shape[0], packed_ref.shape[1]
     for i in range(half):
         for h, r, lo in PLACES:
             k = 2 * half - 1 - i if h else i
             packed_ref[i, :, lo : lo + 32] = parent_ref[pl.ds(2 * vectors * k + r, vectors, stride=2), :]
+            mixed[i : i + 1, lo : lo + 32] = mix_ref[2 * k + r : 2 * k + r + 1, :]
         packed_ref[i] = packed_ref[i] + feed_ref[vectors * i : vectors * (i + 1), :]
 
 
-def parent_factors(mix_ref, fed_ref, far_ref, x_ref, sums_ref, pa_ref, pb_ref, pc_ref, mixed):
+def parent_factors(mixed, far_ref, x_ref, sums_ref, pa_ref, pb_ref, pc_ref):
     half = pa_ref.shape[0]
-    for i in range(half):
-        for h, r, lo in PLACES:
-            k = 2 * half - 1 - i if h else i
-            mixed[i : i + 1, lo : lo + 32] = mix_ref[2 * k + r : 2 * k + r + 1, :]
     upper = lane_index(1) < 64
     rows = [mixed[i : i + 1, :] for i in range(half)]
     inner, outer = [], []
@@ -569,11 +566,11 @@
         INNER,
         4_000_000,
     )
-    fed = call(
+    fed, mixed = call(
         parent_fed,
-        tiles,
-        [],
-        [parent_adjoint.reshape(-1, narrow), feed, inner],
+        [tiles, shape(half, LANES)],
+        [],
+        [parent_adjoint.reshape(-1, narrow), parent_mixing.reshape(-1, narrow), feed, inner],
         LONG,
         1_000_000,
     )
@@ -581,15 +578,15 @@
         child_columns,
         [shape(half * vectors, 4 * LANES), field],
         edge_scratch,
-        [inner, column_rates, relax, *halos[2:]],
+        [inner, column_rates, relax, mixed, *halos[2:]],
         INNER,
         3_000_000,
     )
     pa, pb, pc = call(
         parent_factors,
         [shape(half, LANES)] * 3,
-        [pltpu.VMEM((half, LANES), F32)],
-        [parent_mixing.reshape(-1, narrow), fed, halos[1], x, raw_sums],
+        [],
+        [mixed, halos[1], x, raw_sums],
         LONG,
         1_000_000,
     )

time: 34.7 us -> 33.9 us (0.977)
  local copies, waits for them, and re-layouts: 0.62 us -> 0.01 us
    unnamed x6, local copies, waits for them, and re-layouts: 0.62 us -> 0.01 us
  transfers between devices with their start and end apart: 14 -> 14, of which waited for: 6 -> 7; matrix products, arithmetic and copies ran while one was open for 0% -> 0% of each run, Pallas kernels for 22% -> 22%
where the time goes in v11:
time: 33.9 us; the launch traced here: 33.8 us
  starting transfers between devices  16.2 us (48%)
  Pallas kernels  11.3 us (33%)
  waiting for transfers between devices  5.52 us (16%)
  between operations  0.77 us (2%)
    ppermute x12, starting transfers between devices, swapped(): return lax.ppermute(value, axis, pairs)  12.9 us
    pallas_call x14, Pallas kernels, call(): pl.pallas_call(body, out_shape=outs, in_specs=[FAR if i in far_in else VM...  11.3 us
    ppermute x12, waiting for transfers between devices, swapped(): return lax.ppermute(value, axis, pairs)  5.51 us
    ppermute x2, starting transfers between devices, passed_along(): lax.ppermute(value, axis, [(i, (i + steps) % count) for i in range(count)])  3.3 us
  transfers between devices with their start and end apart: 14, of which 7 were waited for; matrix products, arithmetic and copies ran while one was open for 0% of the time, Pallas kernels for 22%

profile of v11, /device:TPU:0, one launch (start us, length us, event | category | flops | bytes accessed | tf_op | source)
XLA Modules:
  0.0 33.8 jit_solution(3119580228920140409)
XLA Ops:
  0.6 2.1 %begin.1 = (f32[128,128]{1,0:T(8,128)S(1)}, f32[32,8,8,128]{3,2,1,0:T(8,128)S(1)}, f32[32,8,128]{2,1,0:T(8,128)S(1)}, f32[32,8,128]{2,1,0:T(8,128)S(1)}, f32[32,...) custom-call(f32[32,8,8,128]{3,2,1,0:T(8,128)} %x_hbm.1, ...), custom_call_target="tpu_custom_call" | custom-call | flops 4000000 | bytes 3000000 | tf_op jit(solution)/shard_map/begin/pallas_call | solution.py:24
  2.7 3.1 %collective-permute-start = (f32[128,128]{1,0:T(8,128)S(1)}, f32[128,128]{1,0:T(8,128)S(1)}, u32[]{:S(2)}, u32[]{:S(2)}) collective-permute-start(f32[128,128]{1,0:T(8,128)S(1)} %get-tuple-element.48), channel_id=1, source_target_pairs={{0,2},{1,3},{2,4},{3,5},{4,6},{5,7},{6,0},{7,1},{8,10},{9,11},{10,... | collective-permute-start | bytes 196616 | tf_op jit(solution)/shard_map/ppermute | solution.py:495
  5.8 0.7 %child_first.1 = (f32[32,8,8,128]{3,2,1,0:T(8,128)S(1)}, f32[256,128]{1,0:T(8,128)S(1)}, f32[256,128]{1,0:T(8,128)S(1)}, f32[32,128]{1,0:T(8,128)S(1)}) custom-call(f32[32,8,8,128]{3,2,1,0:T(8,128)S(1)} %get-tuple-element.37.x_ref, f32[32,8,128]{2,1,0:T(8,128)S(1)} %get-tuple-element.38.a_ref, f32[32,8,128]{2,1,0:T(8,128)S(1)} %get-tuple-element.39.b_ref, ...), custom_call_target="tpu_custom_call" | custom-call | flops 4000000 | bytes 3000000 | tf_op jit(solution)/shard_map/child_first/pallas_call | solution.py:24
  6.5 1.6 %collective-permute-start.4 = (f32[256,128]{1,0:T(8,128)S(1)}, f32[256,128]{1,0:T(8,128)S(1)}, u32[]{:S(2)}, u32[]{:S(2)}) collective-permute-start(f32[256,128]{1,0:T(8,128)S(1)} %get-tuple-element.53), channel_id=1, source_target_pairs={{1,2},{2,1},{3,4},{4,3},{5,6},{6,5},{7,0},{0,7},{9,10},{10,9},{11,... | collective-permute-start | bytes 393224 | tf_op jit(solution)/shard_map/ppermute | solution.py:504
  8.1 2.4 %collective-permute-start.2 = (f32[32,128]{1,0:T(8,128)S(1)}, f32[32,128]{1,0:T(8,128)S(1)}, u32[]{:S(2)}, u32[]{:S(2)}) collective-permute-start(f32[32,128]{1,0:T(8,128)S(1)} %get-tuple-element.44.after_ref), channel_id=1, source_target_pairs={{8,16},{16,8},{24,0},{0,24},{9,17},{17,9},{25,1},{1,25},{10,18},{1... | collective-permute-start | bytes 49160 | tf_op jit(solution)/shard_map/ppermute | solution.py:504
  10.5 0.5 %collective-permute-start.1 = (f32[32,128]{1,0:T(8,128)S(1)}, f32[32,128]{1,0:T(8,128)S(1)}, u32[]{:S(2)}, u32[]{:S(2)}) collective-permute-start(f32[32,128]{1,0:T(8,128)S(1)} %get-tuple-element.44.after_ref), channel_id=1, source_target_pairs={{0,8},{8,0},{16,24},{24,16},{1,9},{9,1},{17,25},{25,17},{2,10},{10... | collective-permute-start | bytes 49160 | tf_op jit(solution)/shard_map/ppermute | solution.py:504
  11.1 1.1 %child_inner.2 = (f32[32,8,8,128]{3,2,1,0:T(8,128)S(1)}, f32[32,8,128]{2,1,0:T(8,128)S(1)}, f32[32,8,128]{2,1,0:T(8,128)S(1)}) custom-call(f32[32,8,8,128]{3,2,1,0:T(8,128)S(1)} %get-tuple-element.41.solved_ref, f32[4,32,8,128]{3,2,1,0:T(8,128)S(1)} %get-tuple-element.42.rates_ref, f32[8,128]{1,0:T(8,128)S(1)} %get-tuple-element.43.land_ref, ...), custom_call_target="tpu_custom_call" | custom-call | flops 10000000 | bytes 4000000 | tf_op jit(solution)/shard_map/child_inner/pallas_call | solution.py:24
  12.4 0.3 collective-permute-done.2.far_cols
  12.7 1.5 %collective-permute-done.1.mate_cols = f32[32,128]{1,0:T(8,128)S(1)} collective-permute-done((f32[32,128]{1,0:T(8,128)S(1)}, f32[32,128]{1,0:T(8,128)S(1)}, u32[]{:S(2)}, u32[]{:S(2)}) %collective-permute-start.1) | collective-permute-done | bytes 16416 | tf_op jit(solution)/shard_map/ppermute | solution.py:504
  14.3 1.2 %child_columns.1 = (f32[128,512]{1,0:T(8,128)S(1)}, f32[32,8,8,128]{3,2,1,0:T(8,128)S(1)}) custom-call(f32[32,8,8,128]{3,2,1,0:T(8,128)S(1)} %get-tuple-element.45.after_ref.inner_ref, f32[32,8,128]{2,1,0:T(8,128)S(1)} %get-tuple-element.46.column_ref, f32[8,128]{1,0:T(8,128)S(1)} %get-tuple-element.47.relax_ref, ...), custom_call_target="tpu_custom_call" | custom-call | flops 10000000 | bytes 3000000 | tf_op jit(solution)/shard_map/child_columns/pallas_call | solution.py:24
  16.1 1.1 %child_second.1 = (f32[32,8,8,128]{3,2,1,0:T(8,128)S(1)}, f32[16,8,128]{2,1,0:T(8,128)S(1)}, f32[320,128]{1,0:T(8,128)S(1)}, f32[320,128]{1,0:T(8,128)S(1)}, f32[40,128]{1,0:T(8,128)S(1)}) custom-call(f32[32,8,8,128]{3,2,1,0:T(8,128)S(1)} %get-tuple-element.50.x_ref, f32[32,8,128]{2,1,0:T(8,128)S(1)} %get-tuple-element.51.row_ref, ...), custom_call_target="tpu_custom_call" | custom-call | flops 8000000 | bytes 3000000 | tf_op jit(solution)/shard_map/child_second/pallas_call | solution.py:24
  17.2 2.1 %collective-permute-start.6 = (f32[320,128]{1,0:T(8,128)S(1)}, f32[320,128]{1,0:T(8,128)S(1)}, u32[]{:S(2)}, u32[]{:S(2)}) collective-permute-start(f32[320,128]{1,0:T(8,128)S(1)} %get-tuple-element.65), channel_id=1, source_target_pairs={{1,2},{2,1},{3,4},{4,3},{5,6},{6,5},{7,0},{0,7},{9,10},{10,9},{11,... | collective-permute-start | bytes 491528 | tf_op jit(solution)/shard_map/ppermute | solution.py:504
  19.3 1.2 %collective-permute-start.8 = (f32[40,128]{1,0:T(8,128)S(1)}, f32[40,128]{1,0:T(8,128)S(1)}, u32[]{:S(2)}, u32[]{:S(2)}) collective-permute-start(f32[40,128]{1,0:T(8,128)S(1)} %get-tuple-element.60.after_ref), channel_id=1, source_target_pairs={{8,16},{16,8},{24,0},{0,24},{9,17},{17,9},{25,1},{1,25},{10,18},{1... | collective-permute-start | bytes 61448 | tf_op jit(solution)/shard_map/ppermute | solution.py:504
  20.5 0.8 %collective-permute-start.7 = (f32[40,128]{1,0:T(8,128)S(1)}, f32[40,128]{1,0:T(8,128)S(1)}, u32[]{:S(2)}, u32[]{:S(2)}) collective-permute-start(f32[40,128]{1,0:T(8,128)S(1)} %get-tuple-element.60.after_ref), channel_id=1, source_target_pairs={{0,8},{8,0},{16,24},{24,16},{1,9},{9,1},{17,25},{25,17},{2,10},{10... | collective-permute-start | bytes 61448 | tf_op jit(solution)/shard_map/ppermute | solution.py:504
  21.3 1.1 %child_inner.3 = (f32[32,8,8,128]{3,2,1,0:T(8,128)S(1)}, f32[32,8,128]{2,1,0:T(8,128)S(1)}, f32[32,8,128]{2,1,0:T(8,128)S(1)}) custom-call(f32[32,8,8,128]{3,2,1,0:T(8,128)S(1)} %get-tuple-element.59.solved_ref, f32[4,32,8,128]{3,2,1,0:T(8,128)S(1)} %get-tuple-element.42.rates_ref, f32[8,128]{1,0:T(8,128)S(1)} %get-tuple-element.43.land_ref, ...), custom_call_target="tpu_custom_call" | custom-call | flops 10000000 | bytes 4000000 | tf_op jit(solution)/shard_map/child_inner/pallas_call | solution.py:24
  22.7 1.3 %collective-permute-done.8.far_cols = f32[40,128]{1,0:T(8,128)S(1)} collective-permute-done((f32[40,128]{1,0:T(8,128)S(1)}, f32[40,128]{1,0:T(8,128)S(1)}, u32[]{:S(2)}, u32[]{:S(2)}) %collective-permute-start.8) | collective-permute-done | bytes 20512 | tf_op jit(solution)/shard_map/ppermute | solution.py:504
  24.3 1.0 %collective-permute-done.6.far_in.far_ref = f32[320,128]{1,0:T(8,128)S(1)} collective-permute-done((f32[320,128]{1,0:T(8,128)S(1)}, f32[320,128]{1,0:T(8,128)S(1)}, u32[]{:S(2)}, u32[]{:S(2)}) %collective-permute-start.6) | collective-permute-done | bytes 163872 | tf_op jit(solution)/shard_map/ppermute | solution.py:504
  25.3 0.4 %parent_second.1 = (f32[16,8,128]{2,1,0:T(8,128)S(1)}, f32[64,128]{1,0:T(8,128)S(1)}, f32[64,128]{1,0:T(8,128)S(1)}, f32[8,128]{1,0:T(8,128)S(1)}) custom-call(f32[16,8,128]{2,1,0:T(8,128)S(1)} %get-tuple-element.66.psolved_in, f32[5,16,128]{2,1,0:T(8,128)S(1)} %parent_rates_masked.1.prates_ref, f32[16,128]{1,0:T(8,128)S(1)} %get-tuple-element.56.pa_ref.after_ref, ...), custom_call_target="tpu_custom_call" | custom-call | flops 1000000 | bytes 500000 | tf_op jit(solution)/shard_map/parent_second/pallas_call | solution.py:24
  25.8 2.3 %collective-permute-start.11 = (f32[64,128]{1,0:T(8,128)S(1)}, f32[64,128]{1,0:T(8,128)S(1)}, u32[]{:S(2)}, u32[]{:S(2)}) collective-permute-start(f32[64,128]{1,0:T(8,128)S(1)} %get-tuple-element.70), channel_id=1, source_target_pairs={{1,2},{2,1},{3,4},{4,3},{5,6},{6,5},{7,0},{0,7},{9,10},{10,9},{11,... | collective-permute-start | bytes 98312 | tf_op jit(solution)/shard_map/ppermute | solution.py:504
  28.1 1.1 %collective-permute-start.13 = (f32[8,128]{1,0:T(8,128)S(1)}, f32[8,128]{1,0:T(8,128)S(1)}, u32[]{:S(2)}, u32[]{:S(2)}) collective-permute-start(f32[8,128]{1,0:T(8,128)S(1)} %get-tuple-element.71), channel_id=1, source_target_pairs={{8,16},{16,8},{24,0},{0,24},{9,17},{17,9},{25,1},{1,25},{10,18},{1... | collective-permute-start | bytes 12296 | tf_op jit(solution)/shard_map/ppermute | solution.py:504
  29.2 0.9 %collective-permute-start.12 = (f32[8,128]{1,0:T(8,128)S(1)}, f32[8,128]{1,0:T(8,128)S(1)}, u32[]{:S(2)}, u32[]{:S(2)}) collective-permute-start(f32[8,128]{1,0:T(8,128)S(1)} %get-tuple-element.71), channel_id=1, source_target_pairs={{0,8},{8,0},{16,24},{24,16},{1,9},{9,1},{17,25},{25,17},{2,10},{10... | collective-permute-start | bytes 12296 | tf_op jit(solution)/shard_map/ppermute | solution.py:504
  30.1 1.6 %child_last.1 = f32[32,8,8,128]{3,2,1,0:T(8,128)} custom-call(f32[32,8,8,128]{3,2,1,0:T(8,128)S(1)} %get-tuple-element.61.inner_ref.after_ref, f32[32,8,128]{2,1,0:T(8,128)S(1)} %get-tuple-element.62.row_ref, f32[32,8,128]{2,1,0:T(8,128)S(1)} %get-tuple-element.63.column_ref, f32[320,128]{1,0:T(8,128)S(1)} %collective-permute-done.5.mate_in, ...), custom_call_target="tpu_custom_call" | custom-call | flops 4000000 | bytes 3000000 | tf_op jit(solution)/shard_map/child_last/pallas_call | solution.py:24
  31.7 0.9 %collective-permute-done.13.far_cols = f32[8,128]{1,0:T(8,128)S(1)} collective-permute-done((f32[8,128]{1,0:T(8,128)S(1)}, f32[8,128]{1,0:T(8,128)S(1)}, u32[]{:S(2)}, u32[]{:S(2)}) %collective-permute-start.13) | collective-permute-done | bytes 4128 | tf_op jit(solution)/shard_map/ppermute | solution.py:504
  32.8 1.0 %parent_last.1 = f32[512,32]{1,0:T(8,128)} custom-call(f32[16,8,128]{2,1,0:T(8,128)S(1)} %get-tuple-element.68.psolved_in, f32[5,16,128]{2,1,0:T(8,128)S(1)} %parent_rates_masked.1.prates_ref, f32[64,128]{1,0:T(8,128)S(1)} %collective-permute-done.10.mate_in, f32[64,128]{1,0:T(8,128)S(1)} %collective-permute-done.11.far_in, ...), custom_call_target="tpu_custom_call" | custom-call | flops 500000 | bytes 500000 | tf_op jit(solution)/shard_map/parent_last/pallas_call | solution.py:24
  (24 shorter events, 1.7 us)
Async XLA Ops:
  2.7 9.4 %collective-permute-start = (f32[128,128]{1,0:T(8,128)S(1)}, f32[128,128]{1,0:T(8,128)S(1)}, u32[]{:S(2)}, u32[]{:S(2)}) collective-permute-start(f32[128,128]{1,0:T(8,128)S(1)} %get-tuple-element.48), channel_id=1, source_target_pairs={{0,2},{1,3},{2,4},{3,5},{4,6},{5,7},{6,0},{7,1},{8,10},{9,11},{10,... | collective-permute-start | bytes 196616 | tf_op jit(solution)/shard_map/ppermute | solution.py:495
  6.5 9.0 %collective-permute-start.4 = (f32[256,128]{1,0:T(8,128)S(1)}, f32[256,128]{1,0:T(8,128)S(1)}, u32[]{:S(2)}, u32[]{:S(2)}) collective-permute-start(f32[256,128]{1,0:T(8,128)S(1)} %get-tuple-element.53), channel_id=1, source_target_pairs={{1,2},{2,1},{3,4},{4,3},{5,6},{6,5},{7,0},{0,7},{9,10},{10,9},{11,... | collective-permute-start | bytes 393224 | tf_op jit(solution)/shard_map/ppermute | solution.py:504
  8.1 4.6 %collective-permute-start.2 = (f32[32,128]{1,0:T(8,128)S(1)}, f32[32,128]{1,0:T(8,128)S(1)}, u32[]{:S(2)}, u32[]{:S(2)}) collective-permute-start(f32[32,128]{1,0:T(8,128)S(1)} %get-tuple-element.44.after_ref), channel_id=1, source_target_pairs={{8,16},{16,8},{24,0},{0,24},{9,17},{17,9},{25,1},{1,25},{10,18},{1... | collective-permute-start | bytes 49160 | tf_op jit(solution)/shard_map/ppermute | solution.py:504
  10.5 3.7 %collective-permute-start.1 = (f32[32,128]{1,0:T(8,128)S(1)}, f32[32,128]{1,0:T(8,128)S(1)}, u32[]{:S(2)}, u32[]{:S(2)}) collective-permute-start(f32[32,128]{1,0:T(8,128)S(1)} %get-tuple-element.44.after_ref), channel_id=1, source_target_pairs={{0,8},{8,0},{16,24},{24,16},{1,9},{9,1},{17,25},{25,17},{2,10},{10... | collective-permute-start | bytes 49160 | tf_op jit(solution)/shard_map/ppermute | solution.py:504
  11.1 4.5 %collective-permute-start.3 = (f32[256,128]{1,0:T(8,128)S(1)}, f32[256,128]{1,0:T(8,128)S(1)}, u32[]{:S(2)}, u32[]{:S(2)}) collective-permute-start(f32[256,128]{1,0:T(8,128)S(1)} %get-tuple-element.52), channel_id=1, source_target_pairs={{0,1},{1,0},{2,3},{3,2},{4,5},{5,4},{6,7},{7,6},{8,9},{9,8},{10,11... | collective-permute-start | bytes 393224 | tf_op jit(solution)/shard_map/ppermute | solution.py:504
  11.1 1.1 %copy-start = (f32[32,8,2,32]{3,2,1,0:T(2,128)S(1)}, f32[32,8,2,32]{3,2,1,0:T(2,128)}, u32[]{:S(2)}) copy-start(f32[32,8,2,32]{3,2,1,0:T(2,128)} %param.10) | copy-start | bytes 196612
  11.1 1.1 %copy-start.2 = (f32[32,2,32]{2,1,0:T(2,128)S(1)}, f32[32,2,32]{2,1,0:T(2,128)}, u32[]{:S(2)}) copy-start(f32[32,2,32]{2,1,0:T(2,128)} %param.15) | copy-start | bytes 24580
  15.9 6.5 %collective-permute-start.9 = (f32[128,128]{1,0:T(8,128)S(1)}, f32[128,128]{1,0:T(8,128)S(1)}, u32[]{:S(2)}, u32[]{:S(2)}) collective-permute-start(f32[128,128]{1,0:T(8,128)S(1)} %child_rows.1), channel_id=1, source_target_pairs={{0,2},{1,3},{2,4},{3,5},{4,6},{5,7},{6,0},{7,1},{8,10},{9,11},{10,... | collective-permute-start | bytes 196616 | tf_op jit(solution)/shard_map/ppermute | solution.py:495
  17.2 8.0 %collective-permute-start.6 = (f32[320,128]{1,0:T(8,128)S(1)}, f32[320,128]{1,0:T(8,128)S(1)}, u32[]{:S(2)}, u32[]{:S(2)}) collective-permute-start(f32[320,128]{1,0:T(8,128)S(1)} %get-tuple-element.65), channel_id=1, source_target_pairs={{1,2},{2,1},{3,4},{4,3},{5,6},{6,5},{7,0},{0,7},{9,10},{10,9},{11,... | collective-permute-start | bytes 491528 | tf_op jit(solution)/shard_map/ppermute | solution.py:504
  19.3 4.7 %collective-permute-start.8 = (f32[40,128]{1,0:T(8,128)S(1)}, f32[40,128]{1,0:T(8,128)S(1)}, u32[]{:S(2)}, u32[]{:S(2)}) collective-permute-start(f32[40,128]{1,0:T(8,128)S(1)} %get-tuple-element.60.after_ref), channel_id=1, source_target_pairs={{8,16},{16,8},{24,0},{0,24},{9,17},{17,9},{25,1},{1,25},{10,18},{1... | collective-permute-start | bytes 61448 | tf_op jit(solution)/shard_map/ppermute | solution.py:504
  20.5 3.8 %collective-permute-start.7 = (f32[40,128]{1,0:T(8,128)S(1)}, f32[40,128]{1,0:T(8,128)S(1)}, u32[]{:S(2)}, u32[]{:S(2)}) collective-permute-start(f32[40,128]{1,0:T(8,128)S(1)} %get-tuple-element.60.after_ref), channel_id=1, source_target_pairs={{0,8},{8,0},{16,24},{24,16},{1,9},{9,1},{17,25},{25,17},{2,10},{10... | collective-permute-start | bytes 61448 | tf_op jit(solution)/shard_map/ppermute | solution.py:504
  21.3 4.0 %collective-permute-start.5 = (f32[320,128]{1,0:T(8,128)S(1)}, f32[320,128]{1,0:T(8,128)S(1)}, u32[]{:S(2)}, u32[]{:S(2)}) collective-permute-start(f32[320,128]{1,0:T(8,128)S(1)} %get-tuple-element.64), channel_id=1, source_target_pairs={{0,1},{1,0},{2,3},{3,2},{4,5},{5,4},{6,7},{7,6},{8,9},{9,8},{10,11... | collective-permute-start | bytes 491528 | tf_op jit(solution)/shard_map/ppermute | solution.py:504
  21.3 1.1 %copy-start.1 = (f32[4,32,2,32]{3,2,1,0:T(2,128)S(1)}, f32[4,32,2,32]{3,2,1,0:T(2,128)}, u32[]{:S(2)}) copy-start(f32[4,32,2,32]{3,2,1,0:T(2,128)} %param.14) | copy-start | bytes 98308
  25.7 7.1 %collective-permute-start.10 = (f32[64,128]{1,0:T(8,128)S(1)}, f32[64,128]{1,0:T(8,128)S(1)}, u32[]{:S(2)}, u32[]{:S(2)}) collective-permute-start(f32[64,128]{1,0:T(8,128)S(1)} %get-tuple-element.69), channel_id=1, source_target_pairs={{0,1},{1,0},{2,3},{3,2},{4,5},{5,4},{6,7},{7,6},{8,9},{9,8},{10,11... | collective-permute-start | bytes 98312 | tf_op jit(solution)/shard_map/ppermute | solution.py:504
  25.8 7.0 %collective-permute-start.11 = (f32[64,128]{1,0:T(8,128)S(1)}, f32[64,128]{1,0:T(8,128)S(1)}, u32[]{:S(2)}, u32[]{:S(2)}) collective-permute-start(f32[64,128]{1,0:T(8,128)S(1)} %get-tuple-element.70), channel_id=1, source_target_pairs={{1,2},{2,1},{3,4},{4,3},{5,6},{6,5},{7,0},{0,7},{9,10},{10,9},{11,... | collective-permute-start | bytes 98312 | tf_op jit(solution)/shard_map/ppermute | solution.py:504
  28.1 4.5 %collective-permute-start.13 = (f32[8,128]{1,0:T(8,128)S(1)}, f32[8,128]{1,0:T(8,128)S(1)}, u32[]{:S(2)}, u32[]{:S(2)}) collective-permute-start(f32[8,128]{1,0:T(8,128)S(1)} %get-tuple-element.71), channel_id=1, source_target_pairs={{8,16},{16,8},{24,0},{0,24},{9,17},{17,9},{25,1},{1,25},{10,18},{1... | collective-permute-start | bytes 12296 | tf_op jit(solution)/shard_map/ppermute | solution.py:504
  29.2 3.6 %collective-permute-start.12 = (f32[8,128]{1,0:T(8,128)S(1)}, f32[8,128]{1,0:T(8,128)S(1)}, u32[]{:S(2)}, u32[]{:S(2)}) collective-permute-start(f32[8,128]{1,0:T(8,128)S(1)} %get-tuple-element.71), channel_id=1, source_target_pairs={{0,8},{8,0},{16,24},{24,16},{1,9},{9,1},{17,25},{25,17},{2,10},{10... | collective-permute-start | bytes 12296 | tf_op jit(solution)/shard_map/ppermute | solution.py:504

commit v12 on v11

--- a/solution.py
+++ b/solution.py
@@ -476,9 +476,13 @@
     parent_up(y, pc_ref, psolved_ref, mate_rows, far_rows, 0, cols_ref, 0)
 
 
-def parent_last(psolved_in, prates_ref, mate_in, far_in, mate_cols, far_cols, out_ref):
+def parent_merged(mate_cols, far_cols, after_ref, edges_ref):
+    edges_ref[...] = parent_edges(mate_cols, far_cols, 0)
+
+
+def parent_last(psolved_in, prates_ref, edges_ref, mate_in, far_in, out_ref):
     half, vectors = psolved_in.shape[0], psolved_in.shape[1]
-    edges = parent_edges(mate_cols, far_cols, 0)
+    edges = edges_ref[...]
     mate = lambda j: mate_in[8 * j : 8 * j + 8, :]
     far = lambda j: far_in[8 * j : 8 * j + 8, :]
     for i in range(half):
@@ -652,11 +656,20 @@
         3_000_000,
         far_out=True,
     )
+    edges = call(
+        parent_merged,
+        shape(8, LANES),
+        [],
+        [*last_halos[2:], child_out],
+        LONG,
+        100_000,
+        far_in=(2,),
+    )
     parent_out = call(
         parent_last,
         shape(depth * vectors * 2, narrow),
         [],
-        [psolved, prates, *last_halos],
+        [psolved, prates, edges, *last_halos[:2]],
         500_000,
         500_000,
     )

time: 33.9 us -> 34.1 us (level)
    pallas_call x14 -> x15, Pallas kernels: 11.3 us -> 11.4 us  [call(): pl.pallas_call(body, out_shape=outs, in_specs=[FAR if i in far_in else VM...]
  transfers between devices with their start and end apart: 14 -> 14, of which waited for: 7 -> 6; matrix products, arithmetic and copies ran while one was open for 0% -> 0% of each run, Pallas kernels for 22% -> 22%
where the time goes in v12:
time: 34.1 us; the launch traced here: 33.9 us
  starting transfers between devices  16.2 us (48%)
  Pallas kernels  11.4 us (33%)
  waiting for transfers between devices  5.53 us (16%)
  between operations  0.78 us (2%)
    ppermute x12, starting transfers between devices, swapped(): return lax.ppermute(value, axis, pairs)  12.9 us
    pallas_call x15, Pallas kernels, call(): pl.pallas_call(body, out_shape=outs, in_specs=[FAR if i in far_in else VM...  11.4 us
    ppermute x12, waiting for transfers between devices, swapped(): return lax.ppermute(value, axis, pairs)  5.52 us
    ppermute x2, starting transfers between devices, passed_along(): lax.ppermute(value, axis, [(i, (i + steps) % count) for i in range(count)])  3.3 us
  transfers between devices with their start and end apart: 14, of which 6 were waited for; matrix products, arithmetic and copies ran while one was open for 0% of the time, Pallas kernels for 22%

profile of v12, /device:TPU:0, one launch (start us, length us, event | category | flops | bytes accessed | tf_op | source)
XLA Modules:
  0.0 33.9 jit_solution(9722930897209431010)
XLA Ops:
  0.6 2.1 %begin.1 = (f32[128,128]{1,0:T(8,128)S(1)}, f32[32,8,8,128]{3,2,1,0:T(8,128)S(1)}, f32[32,8,128]{2,1,0:T(8,128)S(1)}, f32[32,8,128]{2,1,0:T(8,128)S(1)}, f32[32,...) custom-call(f32[32,8,8,128]{3,2,1,0:T(8,128)} %x_hbm.1, ...), custom_call_target="tpu_custom_call" | custom-call | flops 4000000 | bytes 3000000 | tf_op jit(solution)/shard_map/begin/pallas_call | solution.py:24
  2.7 3.1 %collective-permute-start = (f32[128,128]{1,0:T(8,128)S(1)}, f32[128,128]{1,0:T(8,128)S(1)}, u32[]{:S(2)}, u32[]{:S(2)}) collective-permute-start(f32[128,128]{1,0:T(8,128)S(1)} %get-tuple-element.48), channel_id=1, source_target_pairs={{0,2},{1,3},{2,4},{3,5},{4,6},{5,7},{6,0},{7,1},{8,10},{9,11},{10,... | collective-permute-start | bytes 196616 | tf_op jit(solution)/shard_map/ppermute | solution.py:499
  5.8 0.7 %child_first.1 = (f32[32,8,8,128]{3,2,1,0:T(8,128)S(1)}, f32[256,128]{1,0:T(8,128)S(1)}, f32[256,128]{1,0:T(8,128)S(1)}, f32[32,128]{1,0:T(8,128)S(1)}) custom-call(f32[32,8,8,128]{3,2,1,0:T(8,128)S(1)} %get-tuple-element.37.x_ref, f32[32,8,128]{2,1,0:T(8,128)S(1)} %get-tuple-element.38.a_ref, f32[32,8,128]{2,1,0:T(8,128)S(1)} %get-tuple-element.39.b_ref, ...), custom_call_target="tpu_custom_call" | custom-call | flops 4000000 | bytes 3000000 | tf_op jit(solution)/shard_map/child_first/pallas_call | solution.py:24
  6.5 1.6 %collective-permute-start.4 = (f32[256,128]{1,0:T(8,128)S(1)}, f32[256,128]{1,0:T(8,128)S(1)}, u32[]{:S(2)}, u32[]{:S(2)}) collective-permute-start(f32[256,128]{1,0:T(8,128)S(1)} %get-tuple-element.53), channel_id=1, source_target_pairs={{1,2},{2,1},{3,4},{4,3},{5,6},{6,5},{7,0},{0,7},{9,10},{10,9},{11,... | collective-permute-start | bytes 393224 | tf_op jit(solution)/shard_map/ppermute | solution.py:508
  8.1 2.4 %collective-permute-start.2 = (f32[32,128]{1,0:T(8,128)S(1)}, f32[32,128]{1,0:T(8,128)S(1)}, u32[]{:S(2)}, u32[]{:S(2)}) collective-permute-start(f32[32,128]{1,0:T(8,128)S(1)} %get-tuple-element.44.after_ref), channel_id=1, source_target_pairs={{8,16},{16,8},{24,0},{0,24},{9,17},{17,9},{25,1},{1,25},{10,18},{1... | collective-permute-start | bytes 49160 | tf_op jit(solution)/shard_map/ppermute | solution.py:508
  10.5 0.5 %collective-permute-start.1 = (f32[32,128]{1,0:T(8,128)S(1)}, f32[32,128]{1,0:T(8,128)S(1)}, u32[]{:S(2)}, u32[]{:S(2)}) collective-permute-start(f32[32,128]{1,0:T(8,128)S(1)} %get-tuple-element.44.after_ref), channel_id=1, source_target_pairs={{0,8},{8,0},{16,24},{24,16},{1,9},{9,1},{17,25},{25,17},{2,10},{10... | collective-permute-start | bytes 49160 | tf_op jit(solution)/shard_map/ppermute | solution.py:508
  11.1 1.1 %child_inner.2 = (f32[32,8,8,128]{3,2,1,0:T(8,128)S(1)}, f32[32,8,128]{2,1,0:T(8,128)S(1)}, f32[32,8,128]{2,1,0:T(8,128)S(1)}) custom-call(f32[32,8,8,128]{3,2,1,0:T(8,128)S(1)} %get-tuple-element.41.solved_ref, f32[4,32,8,128]{3,2,1,0:T(8,128)S(1)} %get-tuple-element.42.rates_ref, f32[8,128]{1,0:T(8,128)S(1)} %get-tuple-element.43.land_ref, ...), custom_call_target="tpu_custom_call" | custom-call | flops 10000000 | bytes 4000000 | tf_op jit(solution)/shard_map/child_inner/pallas_call | solution.py:24
  12.4 0.3 collective-permute-done.2.far_cols
  12.7 1.5 %collective-permute-done.1.mate_cols = f32[32,128]{1,0:T(8,128)S(1)} collective-permute-done((f32[32,128]{1,0:T(8,128)S(1)}, f32[32,128]{1,0:T(8,128)S(1)}, u32[]{:S(2)}, u32[]{:S(2)}) %collective-permute-start.1) | collective-permute-done | bytes 16416 | tf_op jit(solution)/shard_map/ppermute | solution.py:508
  14.3 1.2 %child_columns.1 = (f32[128,512]{1,0:T(8,128)S(1)}, f32[32,8,8,128]{3,2,1,0:T(8,128)S(1)}) custom-call(f32[32,8,8,128]{3,2,1,0:T(8,128)S(1)} %get-tuple-element.45.after_ref.inner_ref, f32[32,8,128]{2,1,0:T(8,128)S(1)} %get-tuple-element.46.column_ref, f32[8,128]{1,0:T(8,128)S(1)} %get-tuple-element.47.relax_ref, ...), custom_call_target="tpu_custom_call" | custom-call | flops 10000000 | bytes 3000000 | tf_op jit(solution)/shard_map/child_columns/pallas_call | solution.py:24
  16.1 1.1 %child_second.1 = (f32[32,8,8,128]{3,2,1,0:T(8,128)S(1)}, f32[16,8,128]{2,1,0:T(8,128)S(1)}, f32[320,128]{1,0:T(8,128)S(1)}, f32[320,128]{1,0:T(8,128)S(1)}, f32[40,128]{1,0:T(8,128)S(1)}) custom-call(f32[32,8,8,128]{3,2,1,0:T(8,128)S(1)} %get-tuple-element.50.x_ref, f32[32,8,128]{2,1,0:T(8,128)S(1)} %get-tuple-element.51.row_ref, ...), custom_call_target="tpu_custom_call" | custom-call | flops 8000000 | bytes 3000000 | tf_op jit(solution)/shard_map/child_second/pallas_call | solution.py:24
  17.2 2.1 %collective-permute-start.6 = (f32[320,128]{1,0:T(8,128)S(1)}, f32[320,128]{1,0:T(8,128)S(1)}, u32[]{:S(2)}, u32[]{:S(2)}) collective-permute-start(f32[320,128]{1,0:T(8,128)S(1)} %get-tuple-element.65), channel_id=1, source_target_pairs={{1,2},{2,1},{3,4},{4,3},{5,6},{6,5},{7,0},{0,7},{9,10},{10,9},{11,... | collective-permute-start | bytes 491528 | tf_op jit(solution)/shard_map/ppermute | solution.py:508
  19.3 1.2 %collective-permute-start.8 = (f32[40,128]{1,0:T(8,128)S(1)}, f32[40,128]{1,0:T(8,128)S(1)}, u32[]{:S(2)}, u32[]{:S(2)}) collective-permute-start(f32[40,128]{1,0:T(8,128)S(1)} %get-tuple-element.60.after_ref), channel_id=1, source_target_pairs={{8,16},{16,8},{24,0},{0,24},{9,17},{17,9},{25,1},{1,25},{10,18},{1... | collective-permute-start | bytes 61448 | tf_op jit(solution)/shard_map/ppermute | solution.py:508
  20.5 0.8 %collective-permute-start.7 = (f32[40,128]{1,0:T(8,128)S(1)}, f32[40,128]{1,0:T(8,128)S(1)}, u32[]{:S(2)}, u32[]{:S(2)}) collective-permute-start(f32[40,128]{1,0:T(8,128)S(1)} %get-tuple-element.60.after_ref), channel_id=1, source_target_pairs={{0,8},{8,0},{16,24},{24,16},{1,9},{9,1},{17,25},{25,17},{2,10},{10... | collective-permute-start | bytes 61448 | tf_op jit(solution)/shard_map/ppermute | solution.py:508
  21.3 1.1 %child_inner.3 = (f32[32,8,8,128]{3,2,1,0:T(8,128)S(1)}, f32[32,8,128]{2,1,0:T(8,128)S(1)}, f32[32,8,128]{2,1,0:T(8,128)S(1)}) custom-call(f32[32,8,8,128]{3,2,1,0:T(8,128)S(1)} %get-tuple-element.59.solved_ref, f32[4,32,8,128]{3,2,1,0:T(8,128)S(1)} %get-tuple-element.42.rates_ref, f32[8,128]{1,0:T(8,128)S(1)} %get-tuple-element.43.land_ref, ...), custom_call_target="tpu_custom_call" | custom-call | flops 10000000 | bytes 4000000 | tf_op jit(solution)/shard_map/child_inner/pallas_call | solution.py:24
  22.7 1.3 %collective-permute-done.8.far_cols = f32[40,128]{1,0:T(8,128)S(1)} collective-permute-done((f32[40,128]{1,0:T(8,128)S(1)}, f32[40,128]{1,0:T(8,128)S(1)}, u32[]{:S(2)}, u32[]{:S(2)}) %collective-permute-start.8) | collective-permute-done | bytes 20512 | tf_op jit(solution)/shard_map/ppermute | solution.py:508
  24.3 1.0 %collective-permute-done.6.far_in.far_ref = f32[320,128]{1,0:T(8,128)S(1)} collective-permute-done((f32[320,128]{1,0:T(8,128)S(1)}, f32[320,128]{1,0:T(8,128)S(1)}, u32[]{:S(2)}, u32[]{:S(2)}) %collective-permute-start.6) | collective-permute-done | bytes 163872 | tf_op jit(solution)/shard_map/ppermute | solution.py:508
  25.3 0.4 %parent_second.1 = (f32[16,8,128]{2,1,0:T(8,128)S(1)}, f32[64,128]{1,0:T(8,128)S(1)}, f32[64,128]{1,0:T(8,128)S(1)}, f32[8,128]{1,0:T(8,128)S(1)}) custom-call(f32[16,8,128]{2,1,0:T(8,128)S(1)} %get-tuple-element.66.psolved_in, f32[5,16,128]{2,1,0:T(8,128)S(1)} %parent_rates_masked.1.prates_ref, f32[16,128]{1,0:T(8,128)S(1)} %get-tuple-element.56.pa_ref.after_ref, ...), custom_call_target="tpu_custom_call" | custom-call | flops 1000000 | bytes 500000 | tf_op jit(solution)/shard_map/parent_second/pallas_call | solution.py:24
  25.7 1.1 %collective-permute-start.11 = (f32[8,128]{1,0:T(8,128)S(1)}, f32[8,128]{1,0:T(8,128)S(1)}, u32[]{:S(2)}, u32[]{:S(2)}) collective-permute-start(f32[8,128]{1,0:T(8,128)S(1)} %get-tuple-element.69), channel_id=1, source_target_pairs={{8,16},{16,8},{24,0},{0,24},{9,17},{17,9},{25,1},{1,25},{10,18},{1... | collective-permute-start | bytes 12296 | tf_op jit(solution)/shard_map/ppermute | solution.py:508
  26.9 0.9 %collective-permute-start.10 = (f32[8,128]{1,0:T(8,128)S(1)}, f32[8,128]{1,0:T(8,128)S(1)}, u32[]{:S(2)}, u32[]{:S(2)}) collective-permute-start(f32[8,128]{1,0:T(8,128)S(1)} %get-tuple-element.69), channel_id=1, source_target_pairs={{0,8},{8,0},{16,24},{24,16},{1,9},{9,1},{17,25},{25,17},{2,10},{10... | collective-permute-start | bytes 12296 | tf_op jit(solution)/shard_map/ppermute | solution.py:508
  27.8 2.3 %collective-permute-start.13 = (f32[64,128]{1,0:T(8,128)S(1)}, f32[64,128]{1,0:T(8,128)S(1)}, u32[]{:S(2)}, u32[]{:S(2)}) collective-permute-start(f32[64,128]{1,0:T(8,128)S(1)} %get-tuple-element.71), channel_id=1, source_target_pairs={{1,2},{2,1},{3,4},{4,3},{5,6},{6,5},{7,0},{0,7},{9,10},{10,9},{11,... | collective-permute-start | bytes 98312 | tf_op jit(solution)/shard_map/ppermute | solution.py:508
  30.1 1.6 %child_last.1.after_ref = f32[32,8,8,128]{3,2,1,0:T(8,128)} custom-call(f32[32,8,8,128]{3,2,1,0:T(8,128)S(1)} %get-tuple-element.61.inner_ref.after_ref, f32[32,8,128]{2,1,0:T(8,128)S(1)} %get-tuple-element.62.row_ref, f32[32,8,128]{2,1,0:T(8,128)S(1)} %get-tuple-element.63.column_ref, f32[320,128]{1,0:T(8,128)S(1)} %collective-permute-done.5.mate_in, ...), custom_call_target="tpu_custom_call" | custom-call | flops 4000000 | bytes 3000000 | tf_op jit(solution)/shard_map/child_last/pallas_call | solution.py:24
  31.8 1.1 %collective-permute-done.13.far_in = f32[64,128]{1,0:T(8,128)S(1)} collective-permute-done((f32[64,128]{1,0:T(8,128)S(1)}, f32[64,128]{1,0:T(8,128)S(1)}, u32[]{:S(2)}, u32[]{:S(2)}) %collective-permute-start.13) | collective-permute-done | bytes 32800 | tf_op jit(solution)/shard_map/ppermute | solution.py:508
  32.9 1.0 %parent_last.1 = f32[512,32]{1,0:T(8,128)} custom-call(f32[16,8,128]{2,1,0:T(8,128)S(1)} %get-tuple-element.68.psolved_in, f32[5,16,128]{2,1,0:T(8,128)S(1)} %parent_rates_masked.1.prates_ref, f32[8,128]{1,0:T(8,128)S(1)} %parent_merged.1.edges_ref, f32[64,128]{1,0:T(8,128)S(1)} %collective-permute-done.12.mate_in, f32[64,128]{1,0:T(8,128)S(1)} %collective-permute-done.13.far_in), custom_call_target="tpu_custom_call" | custom-call | flops 500000 | bytes 500000 | tf_op jit(solution)/shard_map/parent_last/pallas_call | solution.py:24
  (25 shorter events, 1.6 us)
Async XLA Ops:
  2.7 9.4 %collective-permute-start = (f32[128,128]{1,0:T(8,128)S(1)}, f32[128,128]{1,0:T(8,128)S(1)}, u32[]{:S(2)}, u32[]{:S(2)}) collective-permute-start(f32[128,128]{1,0:T(8,128)S(1)} %get-tuple-element.48), channel_id=1, source_target_pairs={{0,2},{1,3},{2,4},{3,5},{4,6},{5,7},{6,0},{7,1},{8,10},{9,11},{10,... | collective-permute-start | bytes 196616 | tf_op jit(solution)/shard_map/ppermute | solution.py:499
  6.5 9.0 %collective-permute-start.4 = (f32[256,128]{1,0:T(8,128)S(1)}, f32[256,128]{1,0:T(8,128)S(1)}, u32[]{:S(2)}, u32[]{:S(2)}) collective-permute-start(f32[256,128]{1,0:T(8,128)S(1)} %get-tuple-element.53), channel_id=1, source_target_pairs={{1,2},{2,1},{3,4},{4,3},{5,6},{6,5},{7,0},{0,7},{9,10},{10,9},{11,... | collective-permute-start | bytes 393224 | tf_op jit(solution)/shard_map/ppermute | solution.py:508
  8.1 4.6 %collective-permute-start.2 = (f32[32,128]{1,0:T(8,128)S(1)}, f32[32,128]{1,0:T(8,128)S(1)}, u32[]{:S(2)}, u32[]{:S(2)}) collective-permute-start(f32[32,128]{1,0:T(8,128)S(1)} %get-tuple-element.44.after_ref), channel_id=1, source_target_pairs={{8,16},{16,8},{24,0},{0,24},{9,17},{17,9},{25,1},{1,25},{10,18},{1... | collective-permute-start | bytes 49160 | tf_op jit(solution)/shard_map/ppermute | solution.py:508
  10.5 3.7 %collective-permute-start.1 = (f32[32,128]{1,0:T(8,128)S(1)}, f32[32,128]{1,0:T(8,128)S(1)}, u32[]{:S(2)}, u32[]{:S(2)}) collective-permute-start(f32[32,128]{1,0:T(8,128)S(1)} %get-tuple-element.44.after_ref), channel_id=1, source_target_pairs={{0,8},{8,0},{16,24},{24,16},{1,9},{9,1},{17,25},{25,17},{2,10},{10... | collective-permute-start | bytes 49160 | tf_op jit(solution)/shard_map/ppermute | solution.py:508
  11.1 4.5 %collective-permute-start.3 = (f32[256,128]{1,0:T(8,128)S(1)}, f32[256,128]{1,0:T(8,128)S(1)}, u32[]{:S(2)}, u32[]{:S(2)}) collective-permute-start(f32[256,128]{1,0:T(8,128)S(1)} %get-tuple-element.52), channel_id=1, source_target_pairs={{0,1},{1,0},{2,3},{3,2},{4,5},{5,4},{6,7},{7,6},{8,9},{9,8},{10,11... | collective-permute-start | bytes 393224 | tf_op jit(solution)/shard_map/ppermute | solution.py:508
  11.1 1.1 %copy-start = (f32[32,8,2,32]{3,2,1,0:T(2,128)S(1)}, f32[32,8,2,32]{3,2,1,0:T(2,128)}, u32[]{:S(2)}) copy-start(f32[32,8,2,32]{3,2,1,0:T(2,128)} %param.10) | copy-start | bytes 196612
  11.1 1.1 %copy-start.2 = (f32[32,2,32]{2,1,0:T(2,128)S(1)}, f32[32,2,32]{2,1,0:T(2,128)}, u32[]{:S(2)}) copy-start(f32[32,2,32]{2,1,0:T(2,128)} %param.15) | copy-start | bytes 24580
  15.9 6.5 %collective-permute-start.9 = (f32[128,128]{1,0:T(8,128)S(1)}, f32[128,128]{1,0:T(8,128)S(1)}, u32[]{:S(2)}, u32[]{:S(2)}) collective-permute-start(f32[128,128]{1,0:T(8,128)S(1)} %child_rows.1), channel_id=1, source_target_pairs={{0,2},{1,3},{2,4},{3,5},{4,6},{5,7},{6,0},{7,1},{8,10},{9,11},{10,... | collective-permute-start | bytes 196616 | tf_op jit(solution)/shard_map/ppermute | solution.py:499
  17.2 8.0 %collective-permute-start.6 = (f32[320,128]{1,0:T(8,128)S(1)}, f32[320,128]{1,0:T(8,128)S(1)}, u32[]{:S(2)}, u32[]{:S(2)}) collective-permute-start(f32[320,128]{1,0:T(8,128)S(1)} %get-tuple-element.65), channel_id=1, source_target_pairs={{1,2},{2,1},{3,4},{4,3},{5,6},{6,5},{7,0},{0,7},{9,10},{10,9},{11,... | collective-permute-start | bytes 491528 | tf_op jit(solution)/shard_map/ppermute | solution.py:508
  19.3 4.7 %collective-permute-start.8 = (f32[40,128]{1,0:T(8,128)S(1)}, f32[40,128]{1,0:T(8,128)S(1)}, u32[]{:S(2)}, u32[]{:S(2)}) collective-permute-start(f32[40,128]{1,0:T(8,128)S(1)} %get-tuple-element.60.after_ref), channel_id=1, source_target_pairs={{8,16},{16,8},{24,0},{0,24},{9,17},{17,9},{25,1},{1,25},{10,18},{1... | collective-permute-start | bytes 61448 | tf_op jit(solution)/shard_map/ppermute | solution.py:508
  20.5 3.8 %collective-permute-start.7 = (f32[40,128]{1,0:T(8,128)S(1)}, f32[40,128]{1,0:T(8,128)S(1)}, u32[]{:S(2)}, u32[]{:S(2)}) collective-permute-start(f32[40,128]{1,0:T(8,128)S(1)} %get-tuple-element.60.after_ref), channel_id=1, source_target_pairs={{0,8},{8,0},{16,24},{24,16},{1,9},{9,1},{17,25},{25,17},{2,10},{10... | collective-permute-start | bytes 61448 | tf_op jit(solution)/shard_map/ppermute | solution.py:508
  21.3 4.0 %collective-permute-start.5 = (f32[320,128]{1,0:T(8,128)S(1)}, f32[320,128]{1,0:T(8,128)S(1)}, u32[]{:S(2)}, u32[]{:S(2)}) collective-permute-start(f32[320,128]{1,0:T(8,128)S(1)} %get-tuple-element.64), channel_id=1, source_target_pairs={{0,1},{1,0},{2,3},{3,2},{4,5},{5,4},{6,7},{7,6},{8,9},{9,8},{10,11... | collective-permute-start | bytes 491528 | tf_op jit(solution)/shard_map/ppermute | solution.py:508
  21.3 1.1 %copy-start.1 = (f32[4,32,2,32]{3,2,1,0:T(2,128)S(1)}, f32[4,32,2,32]{3,2,1,0:T(2,128)}, u32[]{:S(2)}) copy-start(f32[4,32,2,32]{3,2,1,0:T(2,128)} %param.14) | copy-start | bytes 98308
  25.7 6.0 %collective-permute-start.11 = (f32[8,128]{1,0:T(8,128)S(1)}, f32[8,128]{1,0:T(8,128)S(1)}, u32[]{:S(2)}, u32[]{:S(2)}) collective-permute-start(f32[8,128]{1,0:T(8,128)S(1)} %get-tuple-element.69), channel_id=1, source_target_pairs={{8,16},{16,8},{24,0},{0,24},{9,17},{17,9},{25,1},{1,25},{10,18},{1... | collective-permute-start | bytes 12296 | tf_op jit(solution)/shard_map/ppermute | solution.py:508
  26.9 4.8 %collective-permute-start.10 = (f32[8,128]{1,0:T(8,128)S(1)}, f32[8,128]{1,0:T(8,128)S(1)}, u32[]{:S(2)}, u32[]{:S(2)}) collective-permute-start(f32[8,128]{1,0:T(8,128)S(1)} %get-tuple-element.69), channel_id=1, source_target_pairs={{0,8},{8,0},{16,24},{24,16},{1,9},{9,1},{17,25},{25,17},{2,10},{10... | collective-permute-start | bytes 12296 | tf_op jit(solution)/shard_map/ppermute | solution.py:508
  27.8 4.0 %collective-permute-start.12 = (f32[64,128]{1,0:T(8,128)S(1)}, f32[64,128]{1,0:T(8,128)S(1)}, u32[]{:S(2)}, u32[]{:S(2)}) collective-permute-start(f32[64,128]{1,0:T(8,128)S(1)} %get-tuple-element.70), channel_id=1, source_target_pairs={{0,1},{1,0},{2,3},{3,2},{4,5},{5,4},{6,7},{7,6},{8,9},{9,8},{10,11... | collective-permute-start | bytes 98312 | tf_op jit(solution)/shard_map/ppermute | solution.py:508
  27.8 5.1 %collective-permute-start.13 = (f32[64,128]{1,0:T(8,128)S(1)}, f32[64,128]{1,0:T(8,128)S(1)}, u32[]{:S(2)}, u32[]{:S(2)}) collective-permute-start(f32[64,128]{1,0:T(8,128)S(1)} %get-tuple-element.71), channel_id=1, source_target_pairs={{1,2},{2,1},{3,4},{4,3},{5,6},{6,5},{7,0},{0,7},{9,10},{10,9},{11,... | collective-permute-start | bytes 98312 | tf_op jit(solution)/shard_map/ppermute | solution.py:508

commit v13 on v11

--- a/solution.py
+++ b/solution.py
@@ -152,7 +152,7 @@
         if group == half // LEVELS - 1:
             last -= 1
         count = last - LEVELS * group + 1
-        state = lax.fori_loop(0, count, lambda step, state, last=last: up(last - step, state), state, unroll=4 if count % 4 == 0 else count)
+        state = lax.fori_loop(0, count, lambda step, state, last=last: up(last - step, state), state, unroll=count)
         keep_columns(group, state[2 * vectors :])
         state = state[: 2 * vectors] + (blank,) * 2
 
@@ -250,7 +250,7 @@
             inner_ref[k, v] = centre * s + across + along
         return 0
 
-    lax.fori_loop(0, depth, level, 0, unroll=4)
+    lax.fori_loop(0, depth, level, 0, unroll=8)
 
 
 def edge_merger(mate_cols, far_cols, merged_ref):
@@ -349,7 +349,7 @@
                 ) + row_rates * row_halo(mate_in, far_in, k, v, vectors, mates)
             return 0
 
-        lax.fori_loop(0, LEVELS, level, 0, unroll=4)
+        lax.fori_loop(0, LEVELS, level, 0, unroll=LEVELS)
         part = pl.ds(LEVELS * group, LEVELS)
         copies.append(pltpu.make_async_copy(out_ref.at[part], out_hbm.at[part], sems.at[group]))
         copies[-1].start()

time: 33.9 us -> 33.7 us (level)
  Pallas kernels: 11.3 us -> 9.98 us
  waiting for transfers between devices: 5.52 us -> 6.63 us
    pallas_call x14, Pallas kernels: 11.3 us -> 9.98 us  [call(): pl.pallas_call(body, out_shape=outs, in_specs=[FAR if i in far_in else VM...]
    ppermute x12, waiting for transfers between devices: 5.51 us -> 6.31 us  [swapped(): return lax.ppermute(value, axis, pairs)]
  transfers between devices with their start and end apart: 14 -> 14, of which waited for: 7 -> 8; matrix products, arithmetic and copies ran while one was open for 0% -> 0% of each run, Pallas kernels for 22% -> 18%
where the time goes in v13:
time: 33.7 us; the launch traced here: 33.5 us
  starting transfers between devices  16 us (47%)
  Pallas kernels  9.98 us (30%)
  waiting for transfers between devices  6.63 us (20%)
  between operations  0.74 us (2%)
    ppermute x12, starting transfers between devices, swapped(): return lax.ppermute(value, axis, pairs)  12.7 us
    pallas_call x14, Pallas kernels, call(): pl.pallas_call(body, out_shape=outs, in_specs=[FAR if i in far_in else VM...  9.98 us
    ppermute x12, waiting for transfers between devices, swapped(): return lax.ppermute(value, axis, pairs)  6.31 us
    ppermute x2, starting transfers between devices, passed_along(): lax.ppermute(value, axis, [(i, (i + steps) % count) for i in range(count)])  3.3 us
  transfers between devices with their start and end apart: 14, of which 8 were waited for; matrix products, arithmetic and copies ran while one was open for 0% of the time, Pallas kernels for 18%

profile of v13, /device:TPU:0, one launch (start us, length us, event | category | flops | bytes accessed | tf_op | source)
XLA Modules:
  0.0 33.5 jit_solution(773721893871467357)
XLA Ops:
  0.6 2.1 %begin.1 = (f32[128,128]{1,0:T(8,128)S(1)}, f32[32,8,8,128]{3,2,1,0:T(8,128)S(1)}, f32[32,8,128]{2,1,0:T(8,128)S(1)}, f32[32,8,128]{2,1,0:T(8,128)S(1)}, f32[32,...) custom-call(f32[32,8,8,128]{3,2,1,0:T(8,128)} %x_hbm.1, ...), custom_call_target="tpu_custom_call" | custom-call | flops 4000000 | bytes 3000000 | tf_op jit(solution)/shard_map/begin/pallas_call | solution.py:24
  2.7 3.1 %collective-permute-start = (f32[128,128]{1,0:T(8,128)S(1)}, f32[128,128]{1,0:T(8,128)S(1)}, u32[]{:S(2)}, u32[]{:S(2)}) collective-permute-start(f32[128,128]{1,0:T(8,128)S(1)} %get-tuple-element.48), channel_id=1, source_target_pairs={{0,2},{1,3},{2,4},{3,5},{4,6},{5,7},{6,0},{7,1},{8,10},{9,11},{10,... | collective-permute-start | bytes 196616 | tf_op jit(solution)/shard_map/ppermute | solution.py:495
  5.8 0.6 %child_first.1 = (f32[32,8,8,128]{3,2,1,0:T(8,128)S(1)}, f32[256,128]{1,0:T(8,128)S(1)}, f32[256,128]{1,0:T(8,128)S(1)}, f32[32,128]{1,0:T(8,128)S(1)}) custom-call(f32[32,8,8,128]{3,2,1,0:T(8,128)S(1)} %get-tuple-element.37.x_ref, f32[32,8,128]{2,1,0:T(8,128)S(1)} %get-tuple-element.38.a_ref, f32[32,8,128]{2,1,0:T(8,128)S(1)} %get-tuple-element.39.b_ref, ...), custom_call_target="tpu_custom_call" | custom-call | flops 4000000 | bytes 3000000 | tf_op jit(solution)/shard_map/child_first/pallas_call | solution.py:24
  6.4 1.5 %collective-permute-start.4 = (f32[256,128]{1,0:T(8,128)S(1)}, f32[256,128]{1,0:T(8,128)S(1)}, u32[]{:S(2)}, u32[]{:S(2)}) collective-permute-start(f32[256,128]{1,0:T(8,128)S(1)} %get-tuple-element.53), channel_id=1, source_target_pairs={{1,2},{2,1},{3,4},{4,3},{5,6},{6,5},{7,0},{0,7},{9,10},{10,9},{11,... | collective-permute-start | bytes 393224 | tf_op jit(solution)/shard_map/ppermute | solution.py:504
  7.9 2.4 %collective-permute-start.2 = (f32[32,128]{1,0:T(8,128)S(1)}, f32[32,128]{1,0:T(8,128)S(1)}, u32[]{:S(2)}, u32[]{:S(2)}) collective-permute-start(f32[32,128]{1,0:T(8,128)S(1)} %get-tuple-element.44.after_ref), channel_id=1, source_target_pairs={{8,16},{16,8},{24,0},{0,24},{9,17},{17,9},{25,1},{1,25},{10,18},{1... | collective-permute-start | bytes 49160 | tf_op jit(solution)/shard_map/ppermute | solution.py:504
  10.4 0.5 %collective-permute-start.1 = (f32[32,128]{1,0:T(8,128)S(1)}, f32[32,128]{1,0:T(8,128)S(1)}, u32[]{:S(2)}, u32[]{:S(2)}) collective-permute-start(f32[32,128]{1,0:T(8,128)S(1)} %get-tuple-element.44.after_ref), channel_id=1, source_target_pairs={{0,8},{8,0},{16,24},{24,16},{1,9},{9,1},{17,25},{25,17},{2,10},{10... | collective-permute-start | bytes 49160 | tf_op jit(solution)/shard_map/ppermute | solution.py:504
  10.9 0.8 %child_inner.2 = (f32[32,8,8,128]{3,2,1,0:T(8,128)S(1)}, f32[32,8,128]{2,1,0:T(8,128)S(1)}, f32[32,8,128]{2,1,0:T(8,128)S(1)}) custom-call(f32[32,8,8,128]{3,2,1,0:T(8,128)S(1)} %get-tuple-element.41.solved_ref, f32[4,32,8,128]{3,2,1,0:T(8,128)S(1)} %get-tuple-element.42.rates_ref, f32[8,128]{1,0:T(8,128)S(1)} %get-tuple-element.43.land_ref, ...), custom_call_target="tpu_custom_call" | custom-call | flops 10000000 | bytes 4000000 | tf_op jit(solution)/shard_map/child_inner/pallas_call | solution.py:24
  12.1 0.5 %collective-permute-done.2.far_cols = f32[32,128]{1,0:T(8,128)S(1)} collective-permute-done((f32[32,128]{1,0:T(8,128)S(1)}, f32[32,128]{1,0:T(8,128)S(1)}, u32[]{:S(2)}, u32[]{:S(2)}) %collective-permute-start.2) | collective-permute-done | bytes 16416 | tf_op jit(solution)/shard_map/ppermute | solution.py:504
  12.6 1.5 %collective-permute-done.1.mate_cols = f32[32,128]{1,0:T(8,128)S(1)} collective-permute-done((f32[32,128]{1,0:T(8,128)S(1)}, f32[32,128]{1,0:T(8,128)S(1)}, u32[]{:S(2)}, u32[]{:S(2)}) %collective-permute-start.1) | collective-permute-done | bytes 16416 | tf_op jit(solution)/shard_map/ppermute | solution.py:504
  14.1 1.2 %child_columns.1 = (f32[128,512]{1,0:T(8,128)S(1)}, f32[32,8,8,128]{3,2,1,0:T(8,128)S(1)}) custom-call(f32[32,8,8,128]{3,2,1,0:T(8,128)S(1)} %get-tuple-element.45.after_ref.inner_ref, f32[32,8,128]{2,1,0:T(8,128)S(1)} %get-tuple-element.46.column_ref, f32[8,128]{1,0:T(8,128)S(1)} %get-tuple-element.47.relax_ref, ...), custom_call_target="tpu_custom_call" | custom-call | flops 10000000 | bytes 3000000 | tf_op jit(solution)/shard_map/child_columns/pallas_call | solution.py:24
  16.0 0.9 %child_second.1 = (f32[32,8,8,128]{3,2,1,0:T(8,128)S(1)}, f32[16,8,128]{2,1,0:T(8,128)S(1)}, f32[320,128]{1,0:T(8,128)S(1)}, f32[320,128]{1,0:T(8,128)S(1)}, f32[40,128]{1,0:T(8,128)S(1)}) custom-call(f32[32,8,8,128]{3,2,1,0:T(8,128)S(1)} %get-tuple-element.50.x_ref, f32[32,8,128]{2,1,0:T(8,128)S(1)} %get-tuple-element.51.row_ref, ...), custom_call_target="tpu_custom_call" | custom-call | flops 8000000 | bytes 3000000 | tf_op jit(solution)/shard_map/child_second/pallas_call | solution.py:24
  16.9 2.1 %collective-permute-start.6 = (f32[320,128]{1,0:T(8,128)S(1)}, f32[320,128]{1,0:T(8,128)S(1)}, u32[]{:S(2)}, u32[]{:S(2)}) collective-permute-start(f32[320,128]{1,0:T(8,128)S(1)} %get-tuple-element.65), channel_id=1, source_target_pairs={{1,2},{2,1},{3,4},{4,3},{5,6},{6,5},{7,0},{0,7},{9,10},{10,9},{11,... | collective-permute-start | bytes 491528 | tf_op jit(solution)/shard_map/ppermute | solution.py:504
  19.0 1.2 %collective-permute-start.8 = (f32[40,128]{1,0:T(8,128)S(1)}, f32[40,128]{1,0:T(8,128)S(1)}, u32[]{:S(2)}, u32[]{:S(2)}) collective-permute-start(f32[40,128]{1,0:T(8,128)S(1)} %get-tuple-element.60.after_ref), channel_id=1, source_target_pairs={{8,16},{16,8},{24,0},{0,24},{9,17},{17,9},{25,1},{1,25},{10,18},{1... | collective-permute-start | bytes 61448 | tf_op jit(solution)/shard_map/ppermute | solution.py:504
  20.2 0.8 %collective-permute-start.7 = (f32[40,128]{1,0:T(8,128)S(1)}, f32[40,128]{1,0:T(8,128)S(1)}, u32[]{:S(2)}, u32[]{:S(2)}) collective-permute-start(f32[40,128]{1,0:T(8,128)S(1)} %get-tuple-element.60.after_ref), channel_id=1, source_target_pairs={{0,8},{8,0},{16,24},{24,16},{1,9},{9,1},{17,25},{25,17},{2,10},{10... | collective-permute-start | bytes 61448 | tf_op jit(solution)/shard_map/ppermute | solution.py:504
  21.0 0.8 %child_inner.3 = (f32[32,8,8,128]{3,2,1,0:T(8,128)S(1)}, f32[32,8,128]{2,1,0:T(8,128)S(1)}, f32[32,8,128]{2,1,0:T(8,128)S(1)}) custom-call(f32[32,8,8,128]{3,2,1,0:T(8,128)S(1)} %get-tuple-element.59.solved_ref, f32[4,32,8,128]{3,2,1,0:T(8,128)S(1)} %get-tuple-element.42.rates_ref, f32[8,128]{1,0:T(8,128)S(1)} %get-tuple-element.43.land_ref, ...), custom_call_target="tpu_custom_call" | custom-call | flops 10000000 | bytes 4000000 | tf_op jit(solution)/shard_map/child_inner/pallas_call | solution.py:24
  22.4 1.3 %collective-permute-done.8.far_cols = f32[40,128]{1,0:T(8,128)S(1)} collective-permute-done((f32[40,128]{1,0:T(8,128)S(1)}, f32[40,128]{1,0:T(8,128)S(1)}, u32[]{:S(2)}, u32[]{:S(2)}) %collective-permute-start.8) | collective-permute-done | bytes 20512 | tf_op jit(solution)/shard_map/ppermute | solution.py:504
  24.0 1.1 %collective-permute-done.6.far_in.far_ref = f32[320,128]{1,0:T(8,128)S(1)} collective-permute-done((f32[320,128]{1,0:T(8,128)S(1)}, f32[320,128]{1,0:T(8,128)S(1)}, u32[]{:S(2)}, u32[]{:S(2)}) %collective-permute-start.6) | collective-permute-done | bytes 163872 | tf_op jit(solution)/shard_map/ppermute | solution.py:504
  25.2 0.4 %parent_second.1 = (f32[16,8,128]{2,1,0:T(8,128)S(1)}, f32[64,128]{1,0:T(8,128)S(1)}, f32[64,128]{1,0:T(8,128)S(1)}, f32[8,128]{1,0:T(8,128)S(1)}) custom-call(f32[16,8,128]{2,1,0:T(8,128)S(1)} %get-tuple-element.66.psolved_in, f32[5,16,128]{2,1,0:T(8,128)S(1)} %parent_rates_masked.1.prates_ref, f32[16,128]{1,0:T(8,128)S(1)} %get-tuple-element.56.pa_ref.after_ref, ...), custom_call_target="tpu_custom_call" | custom-call | flops 1000000 | bytes 500000 | tf_op jit(solution)/shard_map/parent_second/pallas_call | solution.py:24
  25.7 2.1 %collective-permute-start.11 = (f32[64,128]{1,0:T(8,128)S(1)}, f32[64,128]{1,0:T(8,128)S(1)}, u32[]{:S(2)}, u32[]{:S(2)}) collective-permute-start(f32[64,128]{1,0:T(8,128)S(1)} %get-tuple-element.70), channel_id=1, source_target_pairs={{1,2},{2,1},{3,4},{4,3},{5,6},{6,5},{7,0},{0,7},{9,10},{10,9},{11,... | collective-permute-start | bytes 98312 | tf_op jit(solution)/shard_map/ppermute | solution.py:504
  27.8 1.1 %collective-permute-start.13 = (f32[8,128]{1,0:T(8,128)S(1)}, f32[8,128]{1,0:T(8,128)S(1)}, u32[]{:S(2)}, u32[]{:S(2)}) collective-permute-start(f32[8,128]{1,0:T(8,128)S(1)} %get-tuple-element.71), channel_id=1, source_target_pairs={{8,16},{16,8},{24,0},{0,24},{9,17},{17,9},{25,1},{1,25},{10,18},{1... | collective-permute-start | bytes 12296 | tf_op jit(solution)/shard_map/ppermute | solution.py:504
  28.9 0.9 %collective-permute-start.12 = (f32[8,128]{1,0:T(8,128)S(1)}, f32[8,128]{1,0:T(8,128)S(1)}, u32[]{:S(2)}, u32[]{:S(2)}) collective-permute-start(f32[8,128]{1,0:T(8,128)S(1)} %get-tuple-element.71), channel_id=1, source_target_pairs={{0,8},{8,0},{16,24},{24,16},{1,9},{9,1},{17,25},{25,17},{2,10},{10... | collective-permute-start | bytes 12296 | tf_op jit(solution)/shard_map/ppermute | solution.py:504
  29.8 1.2 %child_last.1 = f32[32,8,8,128]{3,2,1,0:T(8,128)} custom-call(f32[32,8,8,128]{3,2,1,0:T(8,128)S(1)} %get-tuple-element.61.inner_ref.after_ref, f32[32,8,128]{2,1,0:T(8,128)S(1)} %get-tuple-element.62.row_ref, f32[32,8,128]{2,1,0:T(8,128)S(1)} %get-tuple-element.63.column_ref, f32[320,128]{1,0:T(8,128)S(1)} %collective-permute-done.5.mate_in, ...), custom_call_target="tpu_custom_call" | custom-call | flops 4000000 | bytes 3000000 | tf_op jit(solution)/shard_map/child_last/pallas_call | solution.py:24
  31.0 1.3 %collective-permute-done.13.far_cols = f32[8,128]{1,0:T(8,128)S(1)} collective-permute-done((f32[8,128]{1,0:T(8,128)S(1)}, f32[8,128]{1,0:T(8,128)S(1)}, u32[]{:S(2)}, u32[]{:S(2)}) %collective-permute-start.13) | collective-permute-done | bytes 4128 | tf_op jit(solution)/shard_map/ppermute | solution.py:504
  32.5 1.0 %parent_last.1 = f32[512,32]{1,0:T(8,128)} custom-call(f32[16,8,128]{2,1,0:T(8,128)S(1)} %get-tuple-element.68.psolved_in, f32[5,16,128]{2,1,0:T(8,128)S(1)} %parent_rates_masked.1.prates_ref, f32[64,128]{1,0:T(8,128)S(1)} %collective-permute-done.10.mate_in, f32[64,128]{1,0:T(8,128)S(1)} %collective-permute-done.11.far_in, ...), custom_call_target="tpu_custom_call" | custom-call | flops 500000 | bytes 500000 | tf_op jit(solution)/shard_map/parent_last/pallas_call | solution.py:24
  (24 shorter events, 2.1 us)
Async XLA Ops:
  2.7 9.0 %collective-permute-start = (f32[128,128]{1,0:T(8,128)S(1)}, f32[128,128]{1,0:T(8,128)S(1)}, u32[]{:S(2)}, u32[]{:S(2)}) collective-permute-start(f32[128,128]{1,0:T(8,128)S(1)} %get-tuple-element.48), channel_id=1, source_target_pairs={{0,2},{1,3},{2,4},{3,5},{4,6},{5,7},{6,0},{7,1},{8,10},{9,11},{10,... | collective-permute-start | bytes 196616 | tf_op jit(solution)/shard_map/ppermute | solution.py:495
  6.4 9.0 %collective-permute-start.4 = (f32[256,128]{1,0:T(8,128)S(1)}, f32[256,128]{1,0:T(8,128)S(1)}, u32[]{:S(2)}, u32[]{:S(2)}) collective-permute-start(f32[256,128]{1,0:T(8,128)S(1)} %get-tuple-element.53), channel_id=1, source_target_pairs={{1,2},{2,1},{3,4},{4,3},{5,6},{6,5},{7,0},{0,7},{9,10},{10,9},{11,... | collective-permute-start | bytes 393224 | tf_op jit(solution)/shard_map/ppermute | solution.py:504
  7.9 4.6 %collective-permute-start.2 = (f32[32,128]{1,0:T(8,128)S(1)}, f32[32,128]{1,0:T(8,128)S(1)}, u32[]{:S(2)}, u32[]{:S(2)}) collective-permute-start(f32[32,128]{1,0:T(8,128)S(1)} %get-tuple-element.44.after_ref), channel_id=1, source_target_pairs={{8,16},{16,8},{24,0},{0,24},{9,17},{17,9},{25,1},{1,25},{10,18},{1... | collective-permute-start | bytes 49160 | tf_op jit(solution)/shard_map/ppermute | solution.py:504
  10.4 3.7 %collective-permute-start.1 = (f32[32,128]{1,0:T(8,128)S(1)}, f32[32,128]{1,0:T(8,128)S(1)}, u32[]{:S(2)}, u32[]{:S(2)}) collective-permute-start(f32[32,128]{1,0:T(8,128)S(1)} %get-tuple-element.44.after_ref), channel_id=1, source_target_pairs={{0,8},{8,0},{16,24},{24,16},{1,9},{9,1},{17,25},{25,17},{2,10},{10... | collective-permute-start | bytes 49160 | tf_op jit(solution)/shard_map/ppermute | solution.py:504
  10.9 4.5 %collective-permute-start.3 = (f32[256,128]{1,0:T(8,128)S(1)}, f32[256,128]{1,0:T(8,128)S(1)}, u32[]{:S(2)}, u32[]{:S(2)}) collective-permute-start(f32[256,128]{1,0:T(8,128)S(1)} %get-tuple-element.52), channel_id=1, source_target_pairs={{0,1},{1,0},{2,3},{3,2},{4,5},{5,4},{6,7},{7,6},{8,9},{9,8},{10,11... | collective-permute-start | bytes 393224 | tf_op jit(solution)/shard_map/ppermute | solution.py:504
  10.9 1.0 %copy-start = (f32[32,8,2,32]{3,2,1,0:T(2,128)S(1)}, f32[32,8,2,32]{3,2,1,0:T(2,128)}, u32[]{:S(2)}) copy-start(f32[32,8,2,32]{3,2,1,0:T(2,128)} %param.10) | copy-start | bytes 196612
  10.9 1.0 %copy-start.2 = (f32[32,2,32]{2,1,0:T(2,128)S(1)}, f32[32,2,32]{2,1,0:T(2,128)}, u32[]{:S(2)}) copy-start(f32[32,2,32]{2,1,0:T(2,128)} %param.15) | copy-start | bytes 24580
  15.8 6.4 %collective-permute-start.9 = (f32[128,128]{1,0:T(8,128)S(1)}, f32[128,128]{1,0:T(8,128)S(1)}, u32[]{:S(2)}, u32[]{:S(2)}) collective-permute-start(f32[128,128]{1,0:T(8,128)S(1)} %child_rows.1), channel_id=1, source_target_pairs={{0,2},{1,3},{2,4},{3,5},{4,6},{5,7},{6,0},{7,1},{8,10},{9,11},{10,... | collective-permute-start | bytes 196616 | tf_op jit(solution)/shard_map/ppermute | solution.py:495
  16.9 8.2 %collective-permute-start.6 = (f32[320,128]{1,0:T(8,128)S(1)}, f32[320,128]{1,0:T(8,128)S(1)}, u32[]{:S(2)}, u32[]{:S(2)}) collective-permute-start(f32[320,128]{1,0:T(8,128)S(1)} %get-tuple-element.65), channel_id=1, source_target_pairs={{1,2},{2,1},{3,4},{4,3},{5,6},{6,5},{7,0},{0,7},{9,10},{10,9},{11,... | collective-permute-start | bytes 491528 | tf_op jit(solution)/shard_map/ppermute | solution.py:504
  19.0 4.7 %collective-permute-start.8 = (f32[40,128]{1,0:T(8,128)S(1)}, f32[40,128]{1,0:T(8,128)S(1)}, u32[]{:S(2)}, u32[]{:S(2)}) collective-permute-start(f32[40,128]{1,0:T(8,128)S(1)} %get-tuple-element.60.after_ref), channel_id=1, source_target_pairs={{8,16},{16,8},{24,0},{0,24},{9,17},{17,9},{25,1},{1,25},{10,18},{1... | collective-permute-start | bytes 61448 | tf_op jit(solution)/shard_map/ppermute | solution.py:504
  20.2 3.8 %collective-permute-start.7 = (f32[40,128]{1,0:T(8,128)S(1)}, f32[40,128]{1,0:T(8,128)S(1)}, u32[]{:S(2)}, u32[]{:S(2)}) collective-permute-start(f32[40,128]{1,0:T(8,128)S(1)} %get-tuple-element.60.after_ref), channel_id=1, source_target_pairs={{0,8},{8,0},{16,24},{24,16},{1,9},{9,1},{17,25},{25,17},{2,10},{10... | collective-permute-start | bytes 61448 | tf_op jit(solution)/shard_map/ppermute | solution.py:504
  21.0 4.2 %collective-permute-start.5 = (f32[320,128]{1,0:T(8,128)S(1)}, f32[320,128]{1,0:T(8,128)S(1)}, u32[]{:S(2)}, u32[]{:S(2)}) collective-permute-start(f32[320,128]{1,0:T(8,128)S(1)} %get-tuple-element.64), channel_id=1, source_target_pairs={{0,1},{1,0},{2,3},{3,2},{4,5},{5,4},{6,7},{7,6},{8,9},{9,8},{10,11... | collective-permute-start | bytes 491528 | tf_op jit(solution)/shard_map/ppermute | solution.py:504
  21.0 1.2 %copy-start.1 = (f32[4,32,2,32]{3,2,1,0:T(2,128)S(1)}, f32[4,32,2,32]{3,2,1,0:T(2,128)}, u32[]{:S(2)}) copy-start(f32[4,32,2,32]{3,2,1,0:T(2,128)} %param.14) | copy-start | bytes 98308
  25.6 6.9 %collective-permute-start.10 = (f32[64,128]{1,0:T(8,128)S(1)}, f32[64,128]{1,0:T(8,128)S(1)}, u32[]{:S(2)}, u32[]{:S(2)}) collective-permute-start(f32[64,128]{1,0:T(8,128)S(1)} %get-tuple-element.69), channel_id=1, source_target_pairs={{0,1},{1,0},{2,3},{3,2},{4,5},{5,4},{6,7},{7,6},{8,9},{9,8},{10,11... | collective-permute-start | bytes 98312 | tf_op jit(solution)/shard_map/ppermute | solution.py:504
  25.7 6.8 %collective-permute-start.11 = (f32[64,128]{1,0:T(8,128)S(1)}, f32[64,128]{1,0:T(8,128)S(1)}, u32[]{:S(2)}, u32[]{:S(2)}) collective-permute-start(f32[64,128]{1,0:T(8,128)S(1)} %get-tuple-element.70), channel_id=1, source_target_pairs={{1,2},{2,1},{3,4},{4,3},{5,6},{6,5},{7,0},{0,7},{9,10},{10,9},{11,... | collective-permute-start | bytes 98312 | tf_op jit(solution)/shard_map/ppermute | solution.py:504
  27.8 4.5 %collective-permute-start.13 = (f32[8,128]{1,0:T(8,128)S(1)}, f32[8,128]{1,0:T(8,128)S(1)}, u32[]{:S(2)}, u32[]{:S(2)}) collective-permute-start(f32[8,128]{1,0:T(8,128)S(1)} %get-tuple-element.71), channel_id=1, source_target_pairs={{8,16},{16,8},{24,0},{0,24},{9,17},{17,9},{25,1},{1,25},{10,18},{1... | collective-permute-start | bytes 12296 | tf_op jit(solution)/shard_map/ppermute | solution.py:504
  28.9 3.6 %collective-permute-start.12 = (f32[8,128]{1,0:T(8,128)S(1)}, f32[8,128]{1,0:T(8,128)S(1)}, u32[]{:S(2)}, u32[]{:S(2)}) collective-permute-start(f32[8,128]{1,0:T(8,128)S(1)} %get-tuple-element.71), channel_id=1, source_target_pairs={{0,8},{8,0},{16,24},{24,16},{1,9},{9,1},{17,25},{25,17},{2,10},{10... | collective-permute-start | bytes 12296 | tf_op jit(solution)/shard_map/ppermute | solution.py:504

commit v14 on v13

--- a/solution.py
+++ b/solution.py
@@ -217,7 +217,7 @@
                 values.append(y)
         return tuple(values)
 
-    carry = lax.fori_loop(0, half, down, (jnp.zeros((8, LANES), F32),) * (2 * vectors), unroll=4)
+    carry = lax.fori_loop(0, half, down, (jnp.zeros((8, LANES), F32),) * (2 * vectors), unroll=8)
     child_up(carry, c_ref, solved_ref, mate_rows, far_rows, cols_ref)
 
 
@@ -250,7 +250,7 @@
             inner_ref[k, v] = centre * s + across + along
         return 0
 
-    lax.fori_loop(0, depth, level, 0, unroll=8)
+    lax.fori_loop(0, depth, level, 0, unroll=16)
 
 
 def edge_merger(mate_cols, far_cols, merged_ref):
@@ -286,14 +286,19 @@
             column_rates = column_ref[k]
             for v in range(vectors):
                 x_ref[k, v] = column_edged(inner_ref, column_rates, edges[side], k, v, base + v)
+        return 0
+
+    def add(i, _):
+        for side, k in ((0, i), (1, depth - 1 - i)):
             block_rows(x_ref, k, weights, sums_ref, i, side)
         return 0
 
     for group in range(half // LEVELS):
         edges = [merged_ref[8 * g : 8 * g + 8, :] for g in (group, groups - 1 - group)]
         lax.fori_loop(
-            LEVELS * group, LEVELS * (group + 1), lambda i, _, edges=edges: level(i, _, edges), 0, unroll=4
+            LEVELS * group, LEVELS * (group + 1), lambda i, _, edges=edges: level(i, _, edges), 0, unroll=LEVELS
         )
+        lax.fori_loop(LEVELS * group, LEVELS * (group + 1), add, 0, unroll=LEVELS)
 
 
 def child_rows(sums_in, row_ref, relax_ref, after_ref, mate_in, far_in, sums_out, sums_ref):

time: 33.7 us -> 33.7 us (level)
  Pallas kernels: 9.98 us -> 9.37 us
  waiting for transfers between devices: 6.63 us -> 7.07 us
    pallas_call x14, Pallas kernels: 9.98 us -> 9.37 us  [call(): pl.pallas_call(body, out_shape=outs, in_specs=[FAR if i in far_in else VM...]
  transfers between devices with their start and end apart: 14 -> 14, of which waited for: 8 -> 8; matrix products, arithmetic and copies ran while one was open for 0% -> 0% of each run, Pallas kernels for 18% -> 17%
where the time goes in v14:
time: 33.7 us; the launch traced here: 33.5 us
  starting transfers between devices  16.1 us (48%)
  Pallas kernels  9.37 us (28%)
  waiting for transfers between devices  7.07 us (21%)
  between operations  0.74 us (2%)
    ppermute x12, starting transfers between devices, swapped(): return lax.ppermute(value, axis, pairs)  12.8 us
    pallas_call x14, Pallas kernels, call(): pl.pallas_call(body, out_shape=outs, in_specs=[FAR if i in far_in else VM...  9.37 us
    ppermute x12, waiting for transfers between devices, swapped(): return lax.ppermute(value, axis, pairs)  6.64 us
    ppermute x2, starting transfers between devices, passed_along(): lax.ppermute(value, axis, [(i, (i + steps) % count) for i in range(count)])  3.3 us
  transfers between devices with their start and end apart: 14, of which 8 were waited for; matrix products, arithmetic and copies ran while one was open for 0% of the time, Pallas kernels for 17%

profile of v14, /device:TPU:0, one launch (start us, length us, event | category | flops | bytes accessed | tf_op | source)
XLA Modules:
  0.0 33.5 jit_solution(4432720864531012717)
XLA Ops:
  0.6 2.1 %begin.1 = (f32[128,128]{1,0:T(8,128)S(1)}, f32[32,8,8,128]{3,2,1,0:T(8,128)S(1)}, f32[32,8,128]{2,1,0:T(8,128)S(1)}, f32[32,8,128]{2,1,0:T(8,128)S(1)}, f32[32,...) custom-call(f32[32,8,8,128]{3,2,1,0:T(8,128)} %x_hbm.1, ...), custom_call_target="tpu_custom_call" | custom-call | flops 4000000 | bytes 3000000 | tf_op jit(solution)/shard_map/begin/pallas_call | solution.py:24
  2.7 3.1 %collective-permute-start = (f32[128,128]{1,0:T(8,128)S(1)}, f32[128,128]{1,0:T(8,128)S(1)}, u32[]{:S(2)}, u32[]{:S(2)}) collective-permute-start(f32[128,128]{1,0:T(8,128)S(1)} %get-tuple-element.48), channel_id=1, source_target_pairs={{0,2},{1,3},{2,4},{3,5},{4,6},{5,7},{6,0},{7,1},{8,10},{9,11},{10,... | collective-permute-start | bytes 196616 | tf_op jit(solution)/shard_map/ppermute | solution.py:500
  5.8 0.6 %child_first.1 = (f32[32,8,8,128]{3,2,1,0:T(8,128)S(1)}, f32[256,128]{1,0:T(8,128)S(1)}, f32[256,128]{1,0:T(8,128)S(1)}, f32[32,128]{1,0:T(8,128)S(1)}) custom-call(f32[32,8,8,128]{3,2,1,0:T(8,128)S(1)} %get-tuple-element.37.x_ref, f32[32,8,128]{2,1,0:T(8,128)S(1)} %get-tuple-element.38.a_ref, f32[32,8,128]{2,1,0:T(8,128)S(1)} %get-tuple-element.39.b_ref, ...), custom_call_target="tpu_custom_call" | custom-call | flops 4000000 | bytes 3000000 | tf_op jit(solution)/shard_map/child_first/pallas_call | solution.py:24
  6.4 1.5 %collective-permute-start.4 = (f32[256,128]{1,0:T(8,128)S(1)}, f32[256,128]{1,0:T(8,128)S(1)}, u32[]{:S(2)}, u32[]{:S(2)}) collective-permute-start(f32[256,128]{1,0:T(8,128)S(1)} %get-tuple-element.53), channel_id=1, source_target_pairs={{1,2},{2,1},{3,4},{4,3},{5,6},{6,5},{7,0},{0,7},{9,10},{10,9},{11,... | collective-permute-start | bytes 393224 | tf_op jit(solution)/shard_map/ppermute | solution.py:509
  7.9 2.4 %collective-permute-start.2 = (f32[32,128]{1,0:T(8,128)S(1)}, f32[32,128]{1,0:T(8,128)S(1)}, u32[]{:S(2)}, u32[]{:S(2)}) collective-permute-start(f32[32,128]{1,0:T(8,128)S(1)} %get-tuple-element.44.after_ref), channel_id=1, source_target_pairs={{8,16},{16,8},{24,0},{0,24},{9,17},{17,9},{25,1},{1,25},{10,18},{1... | collective-permute-start | bytes 49160 | tf_op jit(solution)/shard_map/ppermute | solution.py:509
  10.4 0.5 %collective-permute-start.1 = (f32[32,128]{1,0:T(8,128)S(1)}, f32[32,128]{1,0:T(8,128)S(1)}, u32[]{:S(2)}, u32[]{:S(2)}) collective-permute-start(f32[32,128]{1,0:T(8,128)S(1)} %get-tuple-element.44.after_ref), channel_id=1, source_target_pairs={{0,8},{8,0},{16,24},{24,16},{1,9},{9,1},{17,25},{25,17},{2,10},{10... | collective-permute-start | bytes 49160 | tf_op jit(solution)/shard_map/ppermute | solution.py:509
  10.9 0.7 %child_inner.2 = (f32[32,8,8,128]{3,2,1,0:T(8,128)S(1)}, f32[32,8,128]{2,1,0:T(8,128)S(1)}, f32[32,8,128]{2,1,0:T(8,128)S(1)}) custom-call(f32[32,8,8,128]{3,2,1,0:T(8,128)S(1)} %get-tuple-element.41.solved_ref, f32[4,32,8,128]{3,2,1,0:T(8,128)S(1)} %get-tuple-element.42.rates_ref, f32[8,128]{1,0:T(8,128)S(1)} %get-tuple-element.43.land_ref, ...), custom_call_target="tpu_custom_call" | custom-call | flops 10000000 | bytes 4000000 | tf_op jit(solution)/shard_map/child_inner/pallas_call | solution.py:24
  12.1 0.5 %collective-permute-done.2.far_cols = f32[32,128]{1,0:T(8,128)S(1)} collective-permute-done((f32[32,128]{1,0:T(8,128)S(1)}, f32[32,128]{1,0:T(8,128)S(1)}, u32[]{:S(2)}, u32[]{:S(2)}) %collective-permute-start.2) | collective-permute-done | bytes 16416 | tf_op jit(solution)/shard_map/ppermute | solution.py:509
  12.6 1.5 %collective-permute-done.1.mate_cols = f32[32,128]{1,0:T(8,128)S(1)} collective-permute-done((f32[32,128]{1,0:T(8,128)S(1)}, f32[32,128]{1,0:T(8,128)S(1)}, u32[]{:S(2)}, u32[]{:S(2)}) %collective-permute-start.1) | collective-permute-done | bytes 16416 | tf_op jit(solution)/shard_map/ppermute | solution.py:509
  14.1 0.9 %child_columns.1 = (f32[128,512]{1,0:T(8,128)S(1)}, f32[32,8,8,128]{3,2,1,0:T(8,128)S(1)}) custom-call(f32[32,8,8,128]{3,2,1,0:T(8,128)S(1)} %get-tuple-element.45.after_ref.inner_ref, f32[32,8,128]{2,1,0:T(8,128)S(1)} %get-tuple-element.46.column_ref, f32[8,128]{1,0:T(8,128)S(1)} %get-tuple-element.47.relax_ref, ...), custom_call_target="tpu_custom_call" | custom-call | flops 10000000 | bytes 3000000 | tf_op jit(solution)/shard_map/child_columns/pallas_call | solution.py:24
  15.6 0.9 %child_second.1 = (f32[32,8,8,128]{3,2,1,0:T(8,128)S(1)}, f32[16,8,128]{2,1,0:T(8,128)S(1)}, f32[320,128]{1,0:T(8,128)S(1)}, f32[320,128]{1,0:T(8,128)S(1)}, f32[40,128]{1,0:T(8,128)S(1)}) custom-call(f32[32,8,8,128]{3,2,1,0:T(8,128)S(1)} %get-tuple-element.50.x_ref, f32[32,8,128]{2,1,0:T(8,128)S(1)} %get-tuple-element.51.row_ref, ...), custom_call_target="tpu_custom_call" | custom-call | flops 8000000 | bytes 3000000 | tf_op jit(solution)/shard_map/child_second/pallas_call | solution.py:24
  16.6 2.1 %collective-permute-start.6 = (f32[320,128]{1,0:T(8,128)S(1)}, f32[320,128]{1,0:T(8,128)S(1)}, u32[]{:S(2)}, u32[]{:S(2)}) collective-permute-start(f32[320,128]{1,0:T(8,128)S(1)} %get-tuple-element.65), channel_id=1, source_target_pairs={{1,2},{2,1},{3,4},{4,3},{5,6},{6,5},{7,0},{0,7},{9,10},{10,9},{11,... | collective-permute-start | bytes 491528 | tf_op jit(solution)/shard_map/ppermute | solution.py:509
  18.7 1.2 %collective-permute-start.8 = (f32[40,128]{1,0:T(8,128)S(1)}, f32[40,128]{1,0:T(8,128)S(1)}, u32[]{:S(2)}, u32[]{:S(2)}) collective-permute-start(f32[40,128]{1,0:T(8,128)S(1)} %get-tuple-element.60.after_ref), channel_id=1, source_target_pairs={{8,16},{16,8},{24,0},{0,24},{9,17},{17,9},{25,1},{1,25},{10,18},{1... | collective-permute-start | bytes 61448 | tf_op jit(solution)/shard_map/ppermute | solution.py:509
  19.9 0.8 %collective-permute-start.7 = (f32[40,128]{1,0:T(8,128)S(1)}, f32[40,128]{1,0:T(8,128)S(1)}, u32[]{:S(2)}, u32[]{:S(2)}) collective-permute-start(f32[40,128]{1,0:T(8,128)S(1)} %get-tuple-element.60.after_ref), channel_id=1, source_target_pairs={{0,8},{8,0},{16,24},{24,16},{1,9},{9,1},{17,25},{25,17},{2,10},{10... | collective-permute-start | bytes 61448 | tf_op jit(solution)/shard_map/ppermute | solution.py:509
  20.7 0.7 %child_inner.3 = (f32[32,8,8,128]{3,2,1,0:T(8,128)S(1)}, f32[32,8,128]{2,1,0:T(8,128)S(1)}, f32[32,8,128]{2,1,0:T(8,128)S(1)}) custom-call(f32[32,8,8,128]{3,2,1,0:T(8,128)S(1)} %get-tuple-element.59.solved_ref, f32[4,32,8,128]{3,2,1,0:T(8,128)S(1)} %get-tuple-element.42.rates_ref, f32[8,128]{1,0:T(8,128)S(1)} %get-tuple-element.43.land_ref, ...), custom_call_target="tpu_custom_call" | custom-call | flops 10000000 | bytes 4000000 | tf_op jit(solution)/shard_map/child_inner/pallas_call | solution.py:24
  22.1 1.3 %collective-permute-done.8.far_cols = f32[40,128]{1,0:T(8,128)S(1)} collective-permute-done((f32[40,128]{1,0:T(8,128)S(1)}, f32[40,128]{1,0:T(8,128)S(1)}, u32[]{:S(2)}, u32[]{:S(2)}) %collective-permute-start.8) | collective-permute-done | bytes 20512 | tf_op jit(solution)/shard_map/ppermute | solution.py:509
  23.7 1.1 %collective-permute-done.6.far_in.far_ref = f32[320,128]{1,0:T(8,128)S(1)} collective-permute-done((f32[320,128]{1,0:T(8,128)S(1)}, f32[320,128]{1,0:T(8,128)S(1)}, u32[]{:S(2)}, u32[]{:S(2)}) %collective-permute-start.6) | collective-permute-done | bytes 163872 | tf_op jit(solution)/shard_map/ppermute | solution.py:509
  25.4 2.1 %collective-permute-start.11 = (f32[64,128]{1,0:T(8,128)S(1)}, f32[64,128]{1,0:T(8,128)S(1)}, u32[]{:S(2)}, u32[]{:S(2)}) collective-permute-start(f32[64,128]{1,0:T(8,128)S(1)} %get-tuple-element.70), channel_id=1, source_target_pairs={{1,2},{2,1},{3,4},{4,3},{5,6},{6,5},{7,0},{0,7},{9,10},{10,9},{11,... | collective-permute-start | bytes 98312 | tf_op jit(solution)/shard_map/ppermute | solution.py:509
  27.5 1.4 %collective-permute-start.13 = (f32[8,128]{1,0:T(8,128)S(1)}, f32[8,128]{1,0:T(8,128)S(1)}, u32[]{:S(2)}, u32[]{:S(2)}) collective-permute-start(f32[8,128]{1,0:T(8,128)S(1)} %get-tuple-element.71), channel_id=1, source_target_pairs={{8,16},{16,8},{24,0},{0,24},{9,17},{17,9},{25,1},{1,25},{10,18},{1... | collective-permute-start | bytes 12296 | tf_op jit(solution)/shard_map/ppermute | solution.py:509
  28.9 0.5 %collective-permute-start.12 = (f32[8,128]{1,0:T(8,128)S(1)}, f32[8,128]{1,0:T(8,128)S(1)}, u32[]{:S(2)}, u32[]{:S(2)}) collective-permute-start(f32[8,128]{1,0:T(8,128)S(1)} %get-tuple-element.71), channel_id=1, source_target_pairs={{0,8},{8,0},{16,24},{24,16},{1,9},{9,1},{17,25},{25,17},{2,10},{10... | collective-permute-start | bytes 12296 | tf_op jit(solution)/shard_map/ppermute | solution.py:509
  29.4 1.2 %child_last.1 = f32[32,8,8,128]{3,2,1,0:T(8,128)} custom-call(f32[32,8,8,128]{3,2,1,0:T(8,128)S(1)} %get-tuple-element.61.inner_ref.after_ref, f32[32,8,128]{2,1,0:T(8,128)S(1)} %get-tuple-element.62.row_ref, f32[32,8,128]{2,1,0:T(8,128)S(1)} %get-tuple-element.63.column_ref, f32[320,128]{1,0:T(8,128)S(1)} %collective-permute-done.5.mate_in, ...), custom_call_target="tpu_custom_call" | custom-call | flops 4000000 | bytes 3000000 | tf_op jit(solution)/shard_map/child_last/pallas_call | solution.py:24
  30.7 1.3 %collective-permute-done.13.far_cols = f32[8,128]{1,0:T(8,128)S(1)} collective-permute-done((f32[8,128]{1,0:T(8,128)S(1)}, f32[8,128]{1,0:T(8,128)S(1)}, u32[]{:S(2)}, u32[]{:S(2)}) %collective-permute-start.13) | collective-permute-done | bytes 4128 | tf_op jit(solution)/shard_map/ppermute | solution.py:509
  32.0 0.5 %collective-permute-done.12.mate_cols = f32[8,128]{1,0:T(8,128)S(1)} collective-permute-done((f32[8,128]{1,0:T(8,128)S(1)}, f32[8,128]{1,0:T(8,128)S(1)}, u32[]{:S(2)}, u32[]{:S(2)}) %collective-permute-start.12) | collective-permute-done | bytes 4128 | tf_op jit(solution)/shard_map/ppermute | solution.py:509
  32.5 1.0 %parent_last.1 = f32[512,32]{1,0:T(8,128)} custom-call(f32[16,8,128]{2,1,0:T(8,128)S(1)} %get-tuple-element.68.psolved_in, f32[5,16,128]{2,1,0:T(8,128)S(1)} %parent_rates_masked.1.prates_ref, f32[64,128]{1,0:T(8,128)S(1)} %collective-permute-done.10.mate_in, f32[64,128]{1,0:T(8,128)S(1)} %collective-permute-done.11.far_in, ...), custom_call_target="tpu_custom_call" | custom-call | flops 500000 | bytes 500000 | tf_op jit(solution)/shard_map/parent_last/pallas_call | solution.py:24
  (24 shorter events, 2.6 us)
Async XLA Ops:
  2.7 8.9 %collective-permute-start = (f32[128,128]{1,0:T(8,128)S(1)}, f32[128,128]{1,0:T(8,128)S(1)}, u32[]{:S(2)}, u32[]{:S(2)}) collective-permute-start(f32[128,128]{1,0:T(8,128)S(1)} %get-tuple-element.48), channel_id=1, source_target_pairs={{0,2},{1,3},{2,4},{3,5},{4,6},{5,7},{6,0},{7,1},{8,10},{9,11},{10,... | collective-permute-start | bytes 196616 | tf_op jit(solution)/shard_map/ppermute | solution.py:500
  6.4 8.6 %collective-permute-start.4 = (f32[256,128]{1,0:T(8,128)S(1)}, f32[256,128]{1,0:T(8,128)S(1)}, u32[]{:S(2)}, u32[]{:S(2)}) collective-permute-start(f32[256,128]{1,0:T(8,128)S(1)} %get-tuple-element.53), channel_id=1, source_target_pairs={{1,2},{2,1},{3,4},{4,3},{5,6},{6,5},{7,0},{0,7},{9,10},{10,9},{11,... | collective-permute-start | bytes 393224 | tf_op jit(solution)/shard_map/ppermute | solution.py:509
  7.9 4.6 %collective-permute-start.2 = (f32[32,128]{1,0:T(8,128)S(1)}, f32[32,128]{1,0:T(8,128)S(1)}, u32[]{:S(2)}, u32[]{:S(2)}) collective-permute-start(f32[32,128]{1,0:T(8,128)S(1)} %get-tuple-element.44.after_ref), channel_id=1, source_target_pairs={{8,16},{16,8},{24,0},{0,24},{9,17},{17,9},{25,1},{1,25},{10,18},{1... | collective-permute-start | bytes 49160 | tf_op jit(solution)/shard_map/ppermute | solution.py:509
  10.4 3.7 %collective-permute-start.1 = (f32[32,128]{1,0:T(8,128)S(1)}, f32[32,128]{1,0:T(8,128)S(1)}, u32[]{:S(2)}, u32[]{:S(2)}) collective-permute-start(f32[32,128]{1,0:T(8,128)S(1)} %get-tuple-element.44.after_ref), channel_id=1, source_target_pairs={{0,8},{8,0},{16,24},{24,16},{1,9},{9,1},{17,25},{25,17},{2,10},{10... | collective-permute-start | bytes 49160 | tf_op jit(solution)/shard_map/ppermute | solution.py:509
  10.9 4.2 %collective-permute-start.3 = (f32[256,128]{1,0:T(8,128)S(1)}, f32[256,128]{1,0:T(8,128)S(1)}, u32[]{:S(2)}, u32[]{:S(2)}) collective-permute-start(f32[256,128]{1,0:T(8,128)S(1)} %get-tuple-element.52), channel_id=1, source_target_pairs={{0,1},{1,0},{2,3},{3,2},{4,5},{5,4},{6,7},{7,6},{8,9},{9,8},{10,11... | collective-permute-start | bytes 393224 | tf_op jit(solution)/shard_map/ppermute | solution.py:509
  10.9 1.0 %copy-start = (f32[32,8,2,32]{3,2,1,0:T(2,128)S(1)}, f32[32,8,2,32]{3,2,1,0:T(2,128)}, u32[]{:S(2)}) copy-start(f32[32,8,2,32]{3,2,1,0:T(2,128)} %param.10) | copy-start | bytes 196612
  10.9 1.0 %copy-start.2 = (f32[32,2,32]{2,1,0:T(2,128)S(1)}, f32[32,2,32]{2,1,0:T(2,128)}, u32[]{:S(2)}) copy-start(f32[32,2,32]{2,1,0:T(2,128)} %param.15) | copy-start | bytes 24580
  15.4 6.4 %collective-permute-start.9 = (f32[128,128]{1,0:T(8,128)S(1)}, f32[128,128]{1,0:T(8,128)S(1)}, u32[]{:S(2)}, u32[]{:S(2)}) collective-permute-start(f32[128,128]{1,0:T(8,128)S(1)} %child_rows.1), channel_id=1, source_target_pairs={{0,2},{1,3},{2,4},{3,5},{4,6},{5,7},{6,0},{7,1},{8,10},{9,11},{10,... | collective-permute-start | bytes 196616 | tf_op jit(solution)/shard_map/ppermute | solution.py:500
  16.6 8.2 %collective-permute-start.6 = (f32[320,128]{1,0:T(8,128)S(1)}, f32[320,128]{1,0:T(8,128)S(1)}, u32[]{:S(2)}, u32[]{:S(2)}) collective-permute-start(f32[320,128]{1,0:T(8,128)S(1)} %get-tuple-element.65), channel_id=1, source_target_pairs={{1,2},{2,1},{3,4},{4,3},{5,6},{6,5},{7,0},{0,7},{9,10},{10,9},{11,... | collective-permute-start | bytes 491528 | tf_op jit(solution)/shard_map/ppermute | solution.py:509
  18.7 4.7 %collective-permute-start.8 = (f32[40,128]{1,0:T(8,128)S(1)}, f32[40,128]{1,0:T(8,128)S(1)}, u32[]{:S(2)}, u32[]{:S(2)}) collective-permute-start(f32[40,128]{1,0:T(8,128)S(1)} %get-tuple-element.60.after_ref), channel_id=1, source_target_pairs={{8,16},{16,8},{24,0},{0,24},{9,17},{17,9},{25,1},{1,25},{10,18},{1... | collective-permute-start | bytes 61448 | tf_op jit(solution)/shard_map/ppermute | solution.py:509
  19.9 3.8 %collective-permute-start.7 = (f32[40,128]{1,0:T(8,128)S(1)}, f32[40,128]{1,0:T(8,128)S(1)}, u32[]{:S(2)}, u32[]{:S(2)}) collective-permute-start(f32[40,128]{1,0:T(8,128)S(1)} %get-tuple-element.60.after_ref), channel_id=1, source_target_pairs={{0,8},{8,0},{16,24},{24,16},{1,9},{9,1},{17,25},{25,17},{2,10},{10... | collective-permute-start | bytes 61448 | tf_op jit(solution)/shard_map/ppermute | solution.py:509
  20.7 4.2 %collective-permute-start.5 = (f32[320,128]{1,0:T(8,128)S(1)}, f32[320,128]{1,0:T(8,128)S(1)}, u32[]{:S(2)}, u32[]{:S(2)}) collective-permute-start(f32[320,128]{1,0:T(8,128)S(1)} %get-tuple-element.64), channel_id=1, source_target_pairs={{0,1},{1,0},{2,3},{3,2},{4,5},{5,4},{6,7},{7,6},{8,9},{9,8},{10,11... | collective-permute-start | bytes 491528 | tf_op jit(solution)/shard_map/ppermute | solution.py:509
  20.7 1.1 %copy-start.1 = (f32[4,32,2,32]{3,2,1,0:T(2,128)S(1)}, f32[4,32,2,32]{3,2,1,0:T(2,128)}, u32[]{:S(2)}) copy-start(f32[4,32,2,32]{3,2,1,0:T(2,128)} %param.14) | copy-start | bytes 98308
  25.3 7.2 %collective-permute-start.10 = (f32[64,128]{1,0:T(8,128)S(1)}, f32[64,128]{1,0:T(8,128)S(1)}, u32[]{:S(2)}, u32[]{:S(2)}) collective-permute-start(f32[64,128]{1,0:T(8,128)S(1)} %get-tuple-element.69), channel_id=1, source_target_pairs={{0,1},{1,0},{2,3},{3,2},{4,5},{5,4},{6,7},{7,6},{8,9},{9,8},{10,11... | collective-permute-start | bytes 98312 | tf_op jit(solution)/shard_map/ppermute | solution.py:509
  25.4 7.2 %collective-permute-start.11 = (f32[64,128]{1,0:T(8,128)S(1)}, f32[64,128]{1,0:T(8,128)S(1)}, u32[]{:S(2)}, u32[]{:S(2)}) collective-permute-start(f32[64,128]{1,0:T(8,128)S(1)} %get-tuple-element.70), channel_id=1, source_target_pairs={{1,2},{2,1},{3,4},{4,3},{5,6},{6,5},{7,0},{0,7},{9,10},{10,9},{11,... | collective-permute-start | bytes 98312 | tf_op jit(solution)/shard_map/ppermute | solution.py:509
  27.5 4.5 %collective-permute-start.13 = (f32[8,128]{1,0:T(8,128)S(1)}, f32[8,128]{1,0:T(8,128)S(1)}, u32[]{:S(2)}, u32[]{:S(2)}) collective-permute-start(f32[8,128]{1,0:T(8,128)S(1)} %get-tuple-element.71), channel_id=1, source_target_pairs={{8,16},{16,8},{24,0},{0,24},{9,17},{17,9},{25,1},{1,25},{10,18},{1... | collective-permute-start | bytes 12296 | tf_op jit(solution)/shard_map/ppermute | solution.py:509
  28.9 3.6 %collective-permute-start.12 = (f32[8,128]{1,0:T(8,128)S(1)}, f32[8,128]{1,0:T(8,128)S(1)}, u32[]{:S(2)}, u32[]{:S(2)}) collective-permute-start(f32[8,128]{1,0:T(8,128)S(1)} %get-tuple-element.71), channel_id=1, source_target_pairs={{0,8},{8,0},{16,24},{24,16},{1,9},{9,1},{17,25},{25,17},{2,10},{10... | collective-permute-start | bytes 12296 | tf_op jit(solution)/shard_map/ppermute | solution.py:509

commit v15 on v14

--- a/solution.py
+++ b/solution.py
@@ -217,7 +217,7 @@
                 values.append(y)
         return tuple(values)
 
-    carry = lax.fori_loop(0, half, down, (jnp.zeros((8, LANES), F32),) * (2 * vectors), unroll=8)
+    carry = lax.fori_loop(0, half, down, (jnp.zeros((8, LANES), F32),) * (2 * vectors), unroll=half)
     child_up(carry, c_ref, solved_ref, mate_rows, far_rows, cols_ref)
 
 
@@ -481,11 +481,12 @@
     parent_up(y, pc_ref, psolved_ref, mate_rows, far_rows, 0, cols_ref, 0)
 
 
-def parent_last(psolved_in, prates_ref, mate_in, far_in, mate_cols, far_cols, out_ref):
+def parent_last(psolved_in, prates_ref, mate_in, far_in, mate_cols, far_cols, out_hbm, out_ref, sems):
     half, vectors = psolved_in.shape[0], psolved_in.shape[1]
     edges = parent_edges(mate_cols, far_cols, 0)
     mate = lambda j: mate_in[8 * j : 8 * j + 8, :]
     far = lambda j: far_in[8 * j : 8 * j + 8, :]
+    size, copies = 4, []
     for i in range(half):
         x = parent_transport(psolved_in, prates_ref, mate, far, edges, i)
         for h in range(2):
@@ -493,6 +494,13 @@
                 lo = 64 * h + 32 * r
                 k = 2 * half - 1 - i if h else i
                 out_ref[pl.ds(2 * vectors * k + r, vectors, stride=2), :] = x[:, lo : lo + 32]
+        if i % size == size - 1:
+            for first in (i + 1 - size, 2 * half - 1 - i):
+                part = pl.ds(2 * vectors * first, 2 * vectors * size)
+                copies.append(pltpu.make_async_copy(out_ref.at[part], out_hbm.at[part], sems.at[len(copies)]))
+                copies[-1].start()
+    for copy in copies:
+        copy.wait()
 
 
 def passed_along(value, axis, steps):
@@ -660,10 +668,11 @@
     parent_out = call(
         parent_last,
         shape(depth * vectors * 2, narrow),
-        [],
+        [pltpu.VMEM((depth * vectors * 2, narrow), F32), pltpu.SemaphoreType.DMA((half // 2,))],
         [psolved, prates, *last_halos],
         500_000,
         500_000,
+        far_out=True,
     )
     return (child_out, parent_out.reshape(parent_adjoint.shape))
 

time: 33.7 us -> 33.7 us (level)
  no operation moved by 1% of the time
where the time goes in v15:
time: 33.7 us; the launch traced here: 33.5 us
  starting transfers between devices  16 us (47%)
  Pallas kernels  9.4 us (28%)
  waiting for transfers between devices  7.15 us (21%)
  between operations  0.74 us (2%)
    ppermute x12, starting transfers between devices, swapped(): return lax.ppermute(value, axis, pairs)  12.7 us
    pallas_call x14, Pallas kernels, call(): pl.pallas_call(body, out_shape=outs, in_specs=[FAR if i in far_in else VM...  9.4 us
    ppermute x12, waiting for transfers between devices, swapped(): return lax.ppermute(value, axis, pairs)  6.59 us
    ppermute x2, starting transfers between devices, passed_along(): lax.ppermute(value, axis, [(i, (i + steps) % count) for i in range(count)])  3.3 us
  transfers between devices with their start and end apart: 14, of which 8 were waited for; matrix products, arithmetic and copies ran while one was open for 0% of the time, Pallas kernels for 17%

profile of v15, /device:TPU:0, one launch (start us, length us, event | category | flops | bytes accessed | tf_op | source)
XLA Modules:
  0.0 33.5 jit_solution(15132859756199562247)
XLA Ops:
  0.6 2.1 %begin.1 = (f32[128,128]{1,0:T(8,128)S(1)}, f32[32,8,8,128]{3,2,1,0:T(8,128)S(1)}, f32[32,8,128]{2,1,0:T(8,128)S(1)}, f32[32,8,128]{2,1,0:T(8,128)S(1)}, f32[32,...) custom-call(f32[32,8,8,128]{3,2,1,0:T(8,128)} %x_hbm.1, ...), custom_call_target="tpu_custom_call" | custom-call | flops 4000000 | bytes 3000000 | tf_op jit(solution)/shard_map/begin/pallas_call | solution.py:24
  2.7 3.1 %collective-permute-start = (f32[128,128]{1,0:T(8,128)S(1)}, f32[128,128]{1,0:T(8,128)S(1)}, u32[]{:S(2)}, u32[]{:S(2)}) collective-permute-start(f32[128,128]{1,0:T(8,128)S(1)} %get-tuple-element.48), channel_id=1, source_target_pairs={{0,2},{1,3},{2,4},{3,5},{4,6},{5,7},{6,0},{7,1},{8,10},{9,11},{10,... | collective-permute-start | bytes 196616 | tf_op jit(solution)/shard_map/ppermute | solution.py:508
  5.8 0.6 %child_first.1 = (f32[32,8,8,128]{3,2,1,0:T(8,128)S(1)}, f32[256,128]{1,0:T(8,128)S(1)}, f32[256,128]{1,0:T(8,128)S(1)}, f32[32,128]{1,0:T(8,128)S(1)}) custom-call(f32[32,8,8,128]{3,2,1,0:T(8,128)S(1)} %get-tuple-element.37.x_ref, f32[32,8,128]{2,1,0:T(8,128)S(1)} %get-tuple-element.38.a_ref, f32[32,8,128]{2,1,0:T(8,128)S(1)} %get-tuple-element.39.b_ref, ...), custom_call_target="tpu_custom_call" | custom-call | flops 4000000 | bytes 3000000 | tf_op jit(solution)/shard_map/child_first/pallas_call | solution.py:24
  6.5 1.5 %collective-permute-start.4 = (f32[256,128]{1,0:T(8,128)S(1)}, f32[256,128]{1,0:T(8,128)S(1)}, u32[]{:S(2)}, u32[]{:S(2)}) collective-permute-start(f32[256,128]{1,0:T(8,128)S(1)} %get-tuple-element.53), channel_id=1, source_target_pairs={{1,2},{2,1},{3,4},{4,3},{5,6},{6,5},{7,0},{0,7},{9,10},{10,9},{11,... | collective-permute-start | bytes 393224 | tf_op jit(solution)/shard_map/ppermute | solution.py:517
  8.0 2.4 %collective-permute-start.2 = (f32[32,128]{1,0:T(8,128)S(1)}, f32[32,128]{1,0:T(8,128)S(1)}, u32[]{:S(2)}, u32[]{:S(2)}) collective-permute-start(f32[32,128]{1,0:T(8,128)S(1)} %get-tuple-element.44.after_ref), channel_id=1, source_target_pairs={{8,16},{16,8},{24,0},{0,24},{9,17},{17,9},{25,1},{1,25},{10,18},{1... | collective-permute-start | bytes 49160 | tf_op jit(solution)/shard_map/ppermute | solution.py:517
  10.5 0.5 %collective-permute-start.1 = (f32[32,128]{1,0:T(8,128)S(1)}, f32[32,128]{1,0:T(8,128)S(1)}, u32[]{:S(2)}, u32[]{:S(2)}) collective-permute-start(f32[32,128]{1,0:T(8,128)S(1)} %get-tuple-element.44.after_ref), channel_id=1, source_target_pairs={{0,8},{8,0},{16,24},{24,16},{1,9},{9,1},{17,25},{25,17},{2,10},{10... | collective-permute-start | bytes 49160 | tf_op jit(solution)/shard_map/ppermute | solution.py:517
  11.0 0.7 %child_inner.2 = (f32[32,8,8,128]{3,2,1,0:T(8,128)S(1)}, f32[32,8,128]{2,1,0:T(8,128)S(1)}, f32[32,8,128]{2,1,0:T(8,128)S(1)}) custom-call(f32[32,8,8,128]{3,2,1,0:T(8,128)S(1)} %get-tuple-element.41.solved_ref, f32[4,32,8,128]{3,2,1,0:T(8,128)S(1)} %get-tuple-element.42.rates_ref, f32[8,128]{1,0:T(8,128)S(1)} %get-tuple-element.43.land_ref, ...), custom_call_target="tpu_custom_call" | custom-call | flops 10000000 | bytes 4000000 | tf_op jit(solution)/shard_map/child_inner/pallas_call | solution.py:24
  12.6 1.5 %collective-permute-done.1.mate_cols = f32[32,128]{1,0:T(8,128)S(1)} collective-permute-done((f32[32,128]{1,0:T(8,128)S(1)}, f32[32,128]{1,0:T(8,128)S(1)}, u32[]{:S(2)}, u32[]{:S(2)}) %collective-permute-start.1) | collective-permute-done | bytes 16416 | tf_op jit(solution)/shard_map/ppermute | solution.py:517
  14.2 0.9 %child_columns.1 = (f32[128,512]{1,0:T(8,128)S(1)}, f32[32,8,8,128]{3,2,1,0:T(8,128)S(1)}) custom-call(f32[32,8,8,128]{3,2,1,0:T(8,128)S(1)} %get-tuple-element.45.after_ref.inner_ref, f32[32,8,128]{2,1,0:T(8,128)S(1)} %get-tuple-element.46.column_ref, f32[8,128]{1,0:T(8,128)S(1)} %get-tuple-element.47.relax_ref, ...), custom_call_target="tpu_custom_call" | custom-call | flops 10000000 | bytes 3000000 | tf_op jit(solution)/shard_map/child_columns/pallas_call | solution.py:24
  15.7 0.9 %child_second.1 = (f32[32,8,8,128]{3,2,1,0:T(8,128)S(1)}, f32[16,8,128]{2,1,0:T(8,128)S(1)}, f32[320,128]{1,0:T(8,128)S(1)}, f32[320,128]{1,0:T(8,128)S(1)}, f32[40,128]{1,0:T(8,128)S(1)}) custom-call(f32[32,8,8,128]{3,2,1,0:T(8,128)S(1)} %get-tuple-element.50.x_ref, f32[32,8,128]{2,1,0:T(8,128)S(1)} %get-tuple-element.51.row_ref, ...), custom_call_target="tpu_custom_call" | custom-call | flops 8000000 | bytes 3000000 | tf_op jit(solution)/shard_map/child_second/pallas_call | solution.py:24
  16.6 2.1 %collective-permute-start.6 = (f32[320,128]{1,0:T(8,128)S(1)}, f32[320,128]{1,0:T(8,128)S(1)}, u32[]{:S(2)}, u32[]{:S(2)}) collective-permute-start(f32[320,128]{1,0:T(8,128)S(1)} %get-tuple-element.65), channel_id=1, source_target_pairs={{1,2},{2,1},{3,4},{4,3},{5,6},{6,5},{7,0},{0,7},{9,10},{10,9},{11,... | collective-permute-start | bytes 491528 | tf_op jit(solution)/shard_map/ppermute | solution.py:517
  18.7 1.2 %collective-permute-start.8 = (f32[40,128]{1,0:T(8,128)S(1)}, f32[40,128]{1,0:T(8,128)S(1)}, u32[]{:S(2)}, u32[]{:S(2)}) collective-permute-start(f32[40,128]{1,0:T(8,128)S(1)} %get-tuple-element.60.after_ref), channel_id=1, source_target_pairs={{8,16},{16,8},{24,0},{0,24},{9,17},{17,9},{25,1},{1,25},{10,18},{1... | collective-permute-start | bytes 61448 | tf_op jit(solution)/shard_map/ppermute | solution.py:517
  19.9 0.8 %collective-permute-start.7 = (f32[40,128]{1,0:T(8,128)S(1)}, f32[40,128]{1,0:T(8,128)S(1)}, u32[]{:S(2)}, u32[]{:S(2)}) collective-permute-start(f32[40,128]{1,0:T(8,128)S(1)} %get-tuple-element.60.after_ref), channel_id=1, source_target_pairs={{0,8},{8,0},{16,24},{24,16},{1,9},{9,1},{17,25},{25,17},{2,10},{10... | collective-permute-start | bytes 61448 | tf_op jit(solution)/shard_map/ppermute | solution.py:517
  20.7 0.7 %child_inner.3 = (f32[32,8,8,128]{3,2,1,0:T(8,128)S(1)}, f32[32,8,128]{2,1,0:T(8,128)S(1)}, f32[32,8,128]{2,1,0:T(8,128)S(1)}) custom-call(f32[32,8,8,128]{3,2,1,0:T(8,128)S(1)} %get-tuple-element.59.solved_ref, f32[4,32,8,128]{3,2,1,0:T(8,128)S(1)} %get-tuple-element.42.rates_ref, f32[8,128]{1,0:T(8,128)S(1)} %get-tuple-element.43.land_ref, ...), custom_call_target="tpu_custom_call" | custom-call | flops 10000000 | bytes 4000000 | tf_op jit(solution)/shard_map/child_inner/pallas_call | solution.py:24
  21.4 0.6 %collective-permute-done.9.feed_ref = f32[128,128]{1,0:T(8,128)S(1)} collective-permute-done((f32[128,128]{1,0:T(8,128)S(1)}, f32[128,128]{1,0:T(8,128)S(1)}, u32[]{:S(2)}, u32[]{:S(2)}) %collective-permute-start.9) | collective-permute-done | bytes 65568 | tf_op jit(solution)/shard_map/ppermute | solution.py:508
  22.2 1.2 %collective-permute-done.8.far_cols = f32[40,128]{1,0:T(8,128)S(1)} collective-permute-done((f32[40,128]{1,0:T(8,128)S(1)}, f32[40,128]{1,0:T(8,128)S(1)}, u32[]{:S(2)}, u32[]{:S(2)}) %collective-permute-start.8) | collective-permute-done | bytes 20512 | tf_op jit(solution)/shard_map/ppermute | solution.py:517
  23.7 1.2 %collective-permute-done.6.far_in.far_ref = f32[320,128]{1,0:T(8,128)S(1)} collective-permute-done((f32[320,128]{1,0:T(8,128)S(1)}, f32[320,128]{1,0:T(8,128)S(1)}, u32[]{:S(2)}, u32[]{:S(2)}) %collective-permute-start.6) | collective-permute-done | bytes 163872 | tf_op jit(solution)/shard_map/ppermute | solution.py:517
  25.4 2.0 %collective-permute-start.11 = (f32[64,128]{1,0:T(8,128)S(1)}, f32[64,128]{1,0:T(8,128)S(1)}, u32[]{:S(2)}, u32[]{:S(2)}) collective-permute-start(f32[64,128]{1,0:T(8,128)S(1)} %get-tuple-element.70), channel_id=1, source_target_pairs={{1,2},{2,1},{3,4},{4,3},{5,6},{6,5},{7,0},{0,7},{9,10},{10,9},{11,... | collective-permute-start | bytes 98312 | tf_op jit(solution)/shard_map/ppermute | solution.py:517
  27.5 1.4 %collective-permute-start.13 = (f32[8,128]{1,0:T(8,128)S(1)}, f32[8,128]{1,0:T(8,128)S(1)}, u32[]{:S(2)}, u32[]{:S(2)}) collective-permute-start(f32[8,128]{1,0:T(8,128)S(1)} %get-tuple-element.71), channel_id=1, source_target_pairs={{8,16},{16,8},{24,0},{0,24},{9,17},{17,9},{25,1},{1,25},{10,18},{1... | collective-permute-start | bytes 12296 | tf_op jit(solution)/shard_map/ppermute | solution.py:517
  28.9 0.5 %collective-permute-start.12 = (f32[8,128]{1,0:T(8,128)S(1)}, f32[8,128]{1,0:T(8,128)S(1)}, u32[]{:S(2)}, u32[]{:S(2)}) collective-permute-start(f32[8,128]{1,0:T(8,128)S(1)} %get-tuple-element.71), channel_id=1, source_target_pairs={{0,8},{8,0},{16,24},{24,16},{1,9},{9,1},{17,25},{25,17},{2,10},{10... | collective-permute-start | bytes 12296 | tf_op jit(solution)/shard_map/ppermute | solution.py:517
  29.5 1.2 %child_last.1 = f32[32,8,8,128]{3,2,1,0:T(8,128)} custom-call(f32[32,8,8,128]{3,2,1,0:T(8,128)S(1)} %get-tuple-element.61.inner_ref.after_ref, f32[32,8,128]{2,1,0:T(8,128)S(1)} %get-tuple-element.62.row_ref, f32[32,8,128]{2,1,0:T(8,128)S(1)} %get-tuple-element.63.column_ref, f32[320,128]{1,0:T(8,128)S(1)} %collective-permute-done.5.mate_in, ...), custom_call_target="tpu_custom_call" | custom-call | flops 4000000 | bytes 3000000 | tf_op jit(solution)/shard_map/child_last/pallas_call | solution.py:24
  30.7 1.3 %collective-permute-done.13.far_cols = f32[8,128]{1,0:T(8,128)S(1)} collective-permute-done((f32[8,128]{1,0:T(8,128)S(1)}, f32[8,128]{1,0:T(8,128)S(1)}, u32[]{:S(2)}, u32[]{:S(2)}) %collective-permute-start.13) | collective-permute-done | bytes 4128 | tf_op jit(solution)/shard_map/ppermute | solution.py:517
  32.0 0.5 %collective-permute-done.12.mate_cols = f32[8,128]{1,0:T(8,128)S(1)} collective-permute-done((f32[8,128]{1,0:T(8,128)S(1)}, f32[8,128]{1,0:T(8,128)S(1)}, u32[]{:S(2)}, u32[]{:S(2)}) %collective-permute-start.12) | collective-permute-done | bytes 4128 | tf_op jit(solution)/shard_map/ppermute | solution.py:517
  32.5 1.0 %parent_last.1 = f32[512,32]{1,0:T(8,128)} custom-call(f32[16,8,128]{2,1,0:T(8,128)S(1)} %get-tuple-element.68.psolved_in, f32[5,16,128]{2,1,0:T(8,128)S(1)} %parent_rates_masked.1.prates_ref, f32[64,128]{1,0:T(8,128)S(1)} %collective-permute-done.10.mate_in, f32[64,128]{1,0:T(8,128)S(1)} %collective-permute-done.11.far_in, ...), custom_call_target="tpu_custom_call" | custom-call | flops 500000 | bytes 500000 | tf_op jit(solution)/shard_map/parent_last/pallas_call | solution.py:24
  (24 shorter events, 2.7 us)
Async XLA Ops:
  2.7 8.9 %collective-permute-start = (f32[128,128]{1,0:T(8,128)S(1)}, f32[128,128]{1,0:T(8,128)S(1)}, u32[]{:S(2)}, u32[]{:S(2)}) collective-permute-start(f32[128,128]{1,0:T(8,128)S(1)} %get-tuple-element.48), channel_id=1, source_target_pairs={{0,2},{1,3},{2,4},{3,5},{4,6},{5,7},{6,0},{7,1},{8,10},{9,11},{10,... | collective-permute-start | bytes 196616 | tf_op jit(solution)/shard_map/ppermute | solution.py:508
  6.5 8.6 %collective-permute-start.4 = (f32[256,128]{1,0:T(8,128)S(1)}, f32[256,128]{1,0:T(8,128)S(1)}, u32[]{:S(2)}, u32[]{:S(2)}) collective-permute-start(f32[256,128]{1,0:T(8,128)S(1)} %get-tuple-element.53), channel_id=1, source_target_pairs={{1,2},{2,1},{3,4},{4,3},{5,6},{6,5},{7,0},{0,7},{9,10},{10,9},{11,... | collective-permute-start | bytes 393224 | tf_op jit(solution)/shard_map/ppermute | solution.py:517
  8.0 4.6 %collective-permute-start.2 = (f32[32,128]{1,0:T(8,128)S(1)}, f32[32,128]{1,0:T(8,128)S(1)}, u32[]{:S(2)}, u32[]{:S(2)}) collective-permute-start(f32[32,128]{1,0:T(8,128)S(1)} %get-tuple-element.44.after_ref), channel_id=1, source_target_pairs={{8,16},{16,8},{24,0},{0,24},{9,17},{17,9},{25,1},{1,25},{10,18},{1... | collective-permute-start | bytes 49160 | tf_op jit(solution)/shard_map/ppermute | solution.py:517
  10.5 3.7 %collective-permute-start.1 = (f32[32,128]{1,0:T(8,128)S(1)}, f32[32,128]{1,0:T(8,128)S(1)}, u32[]{:S(2)}, u32[]{:S(2)}) collective-permute-start(f32[32,128]{1,0:T(8,128)S(1)} %get-tuple-element.44.after_ref), channel_id=1, source_target_pairs={{0,8},{8,0},{16,24},{24,16},{1,9},{9,1},{17,25},{25,17},{2,10},{10... | collective-permute-start | bytes 49160 | tf_op jit(solution)/shard_map/ppermute | solution.py:517
  11.0 4.2 %collective-permute-start.3 = (f32[256,128]{1,0:T(8,128)S(1)}, f32[256,128]{1,0:T(8,128)S(1)}, u32[]{:S(2)}, u32[]{:S(2)}) collective-permute-start(f32[256,128]{1,0:T(8,128)S(1)} %get-tuple-element.52), channel_id=1, source_target_pairs={{0,1},{1,0},{2,3},{3,2},{4,5},{5,4},{6,7},{7,6},{8,9},{9,8},{10,11... | collective-permute-start | bytes 393224 | tf_op jit(solution)/shard_map/ppermute | solution.py:517
  11.0 1.0 %copy-start = (f32[32,8,2,32]{3,2,1,0:T(2,128)S(1)}, f32[32,8,2,32]{3,2,1,0:T(2,128)}, u32[]{:S(2)}) copy-start(f32[32,8,2,32]{3,2,1,0:T(2,128)} %param.10) | copy-start | bytes 196612
  11.0 1.0 %copy-start.2 = (f32[32,2,32]{2,1,0:T(2,128)S(1)}, f32[32,2,32]{2,1,0:T(2,128)}, u32[]{:S(2)}) copy-start(f32[32,2,32]{2,1,0:T(2,128)} %param.15) | copy-start | bytes 24580
  15.5 6.5 %collective-permute-start.9 = (f32[128,128]{1,0:T(8,128)S(1)}, f32[128,128]{1,0:T(8,128)S(1)}, u32[]{:S(2)}, u32[]{:S(2)}) collective-permute-start(f32[128,128]{1,0:T(8,128)S(1)} %child_rows.1), channel_id=1, source_target_pairs={{0,2},{1,3},{2,4},{3,5},{4,6},{5,7},{6,0},{7,1},{8,10},{9,11},{10,... | collective-permute-start | bytes 196616 | tf_op jit(solution)/shard_map/ppermute | solution.py:508
  16.6 8.3 %collective-permute-start.6 = (f32[320,128]{1,0:T(8,128)S(1)}, f32[320,128]{1,0:T(8,128)S(1)}, u32[]{:S(2)}, u32[]{:S(2)}) collective-permute-start(f32[320,128]{1,0:T(8,128)S(1)} %get-tuple-element.65), channel_id=1, source_target_pairs={{1,2},{2,1},{3,4},{4,3},{5,6},{6,5},{7,0},{0,7},{9,10},{10,9},{11,... | collective-permute-start | bytes 491528 | tf_op jit(solution)/shard_map/ppermute | solution.py:517
  18.7 4.7 %collective-permute-start.8 = (f32[40,128]{1,0:T(8,128)S(1)}, f32[40,128]{1,0:T(8,128)S(1)}, u32[]{:S(2)}, u32[]{:S(2)}) collective-permute-start(f32[40,128]{1,0:T(8,128)S(1)} %get-tuple-element.60.after_ref), channel_id=1, source_target_pairs={{8,16},{16,8},{24,0},{0,24},{9,17},{17,9},{25,1},{1,25},{10,18},{1... | collective-permute-start | bytes 61448 | tf_op jit(solution)/shard_map/ppermute | solution.py:517
  19.9 3.8 %collective-permute-start.7 = (f32[40,128]{1,0:T(8,128)S(1)}, f32[40,128]{1,0:T(8,128)S(1)}, u32[]{:S(2)}, u32[]{:S(2)}) collective-permute-start(f32[40,128]{1,0:T(8,128)S(1)} %get-tuple-element.60.after_ref), channel_id=1, source_target_pairs={{0,8},{8,0},{16,24},{24,16},{1,9},{9,1},{17,25},{25,17},{2,10},{10... | collective-permute-start | bytes 61448 | tf_op jit(solution)/shard_map/ppermute | solution.py:517
  20.7 4.3 %collective-permute-start.5 = (f32[320,128]{1,0:T(8,128)S(1)}, f32[320,128]{1,0:T(8,128)S(1)}, u32[]{:S(2)}, u32[]{:S(2)}) collective-permute-start(f32[320,128]{1,0:T(8,128)S(1)} %get-tuple-element.64), channel_id=1, source_target_pairs={{0,1},{1,0},{2,3},{3,2},{4,5},{5,4},{6,7},{7,6},{8,9},{9,8},{10,11... | collective-permute-start | bytes 491528 | tf_op jit(solution)/shard_map/ppermute | solution.py:517
  20.7 1.3 %copy-start.1 = (f32[4,32,2,32]{3,2,1,0:T(2,128)S(1)}, f32[4,32,2,32]{3,2,1,0:T(2,128)}, u32[]{:S(2)}) copy-start(f32[4,32,2,32]{3,2,1,0:T(2,128)} %param.14) | copy-start | bytes 98308
  25.4 7.2 %collective-permute-start.10 = (f32[64,128]{1,0:T(8,128)S(1)}, f32[64,128]{1,0:T(8,128)S(1)}, u32[]{:S(2)}, u32[]{:S(2)}) collective-permute-start(f32[64,128]{1,0:T(8,128)S(1)} %get-tuple-element.69), channel_id=1, source_target_pairs={{0,1},{1,0},{2,3},{3,2},{4,5},{5,4},{6,7},{7,6},{8,9},{9,8},{10,11... | collective-permute-start | bytes 98312 | tf_op jit(solution)/shard_map/ppermute | solution.py:517
  25.4 7.1 %collective-permute-start.11 = (f32[64,128]{1,0:T(8,128)S(1)}, f32[64,128]{1,0:T(8,128)S(1)}, u32[]{:S(2)}, u32[]{:S(2)}) collective-permute-start(f32[64,128]{1,0:T(8,128)S(1)} %get-tuple-element.70), channel_id=1, source_target_pairs={{1,2},{2,1},{3,4},{4,3},{5,6},{6,5},{7,0},{0,7},{9,10},{10,9},{11,... | collective-permute-start | bytes 98312 | tf_op jit(solution)/shard_map/ppermute | solution.py:517
  27.5 4.5 %collective-permute-start.13 = (f32[8,128]{1,0:T(8,128)S(1)}, f32[8,128]{1,0:T(8,128)S(1)}, u32[]{:S(2)}, u32[]{:S(2)}) collective-permute-start(f32[8,128]{1,0:T(8,128)S(1)} %get-tuple-element.71), channel_id=1, source_target_pairs={{8,16},{16,8},{24,0},{0,24},{9,17},{17,9},{25,1},{1,25},{10,18},{1... | collective-permute-start | bytes 12296 | tf_op jit(solution)/shard_map/ppermute | solution.py:517
  28.9 3.6 %collective-permute-start.12 = (f32[8,128]{1,0:T(8,128)S(1)}, f32[8,128]{1,0:T(8,128)S(1)}, u32[]{:S(2)}, u32[]{:S(2)}) collective-permute-start(f32[8,128]{1,0:T(8,128)S(1)} %get-tuple-element.71), channel_id=1, source_target_pairs={{0,8},{8,0},{16,24},{24,16},{1,9},{9,1},{17,25},{25,17},{2,10},{10... | collective-permute-start | bytes 12296 | tf_op jit(solution)/shard_map/ppermute | solution.py:517

commit v16 on v14

--- a/solution.py
+++ b/solution.py
@@ -481,9 +481,13 @@
     parent_up(y, pc_ref, psolved_ref, mate_rows, far_rows, 0, cols_ref, 0)
 
 
-def parent_last(psolved_in, prates_ref, mate_in, far_in, mate_cols, far_cols, out_ref):
+def parent_merged(mate_cols, far_cols, far_ref, after_ref, edges_ref):
+    edges_ref[...] = parent_edges(mate_cols, far_cols, 0)
+
+
+def parent_last(psolved_in, prates_ref, edges_ref, mate_in, far_in, out_ref):
     half, vectors = psolved_in.shape[0], psolved_in.shape[1]
-    edges = parent_edges(mate_cols, far_cols, 0)
+    edges = edges_ref[...]
     mate = lambda j: mate_in[8 * j : 8 * j + 8, :]
     far = lambda j: far_in[8 * j : 8 * j + 8, :]
     for i in range(half):
@@ -657,11 +661,20 @@
         3_000_000,
         far_out=True,
     )
+    edges = call(
+        parent_merged,
+        shape(8, LANES),
+        [],
+        [*last_halos[2:], last_halos[1], child_out],
+        LONG,
+        100_000,
+        far_in=(3,),
+    )
     parent_out = call(
         parent_last,
         shape(depth * vectors * 2, narrow),
         [],
-        [psolved, prates, *last_halos],
+        [psolved, prates, edges, *last_halos[:2]],
         500_000,
         500_000,
     )

time: 33.7 us -> 32.6 us (0.967)
  starting transfers between devices: 16.1 us -> 15.2 us
  waiting for transfers between devices: 7.07 us -> 6.72 us
    ppermute x12, starting transfers between devices: 12.8 us -> 11.9 us  [swapped(): return lax.ppermute(value, axis, pairs)]
    ppermute x12, waiting for transfers between devices: 6.64 us -> 6.29 us  [swapped(): return lax.ppermute(value, axis, pairs)]
    pallas_call x14 -> x15, Pallas kernels: 9.37 us -> 9.48 us  [call(): pl.pallas_call(body, out_shape=outs, in_specs=[FAR if i in far_in else VM...]
where the time goes in v16:
time: 32.6 us; the launch traced here: 32.4 us
  starting transfers between devices  15.2 us (47%)
  Pallas kernels  9.48 us (29%)
  waiting for transfers between devices  6.72 us (21%)
  between operations  0.73 us (2%)
    ppermute x12, starting transfers between devices, swapped(): return lax.ppermute(value, axis, pairs)  11.9 us
    pallas_call x15, Pallas kernels, call(): pl.pallas_call(body, out_shape=outs, in_specs=[FAR if i in far_in else VM...  9.48 us
    ppermute x12, waiting for transfers between devices, swapped(): return lax.ppermute(value, axis, pairs)  6.29 us
    ppermute x2, starting transfers between devices, passed_along(): lax.ppermute(value, axis, [(i, (i + steps) % count) for i in range(count)])  3.3 us
  transfers between devices with their start and end apart: 14, of which 8 were waited for; matrix products, arithmetic and copies ran while one was open for 0% of the time, Pallas kernels for 17%

profile of v16, /device:TPU:0, one launch (start us, length us, event | category | flops | bytes accessed | tf_op | source)
XLA Modules:
  0.0 32.4 jit_solution(17114250456371774627)
XLA Ops:
  0.6 2.1 %begin.1 = (f32[128,128]{1,0:T(8,128)S(1)}, f32[32,8,8,128]{3,2,1,0:T(8,128)S(1)}, f32[32,8,128]{2,1,0:T(8,128)S(1)}, f32[32,8,128]{2,1,0:T(8,128)S(1)}, f32[32,...) custom-call(f32[32,8,8,128]{3,2,1,0:T(8,128)} %x_hbm.1, ...), custom_call_target="tpu_custom_call" | custom-call | flops 4000000 | bytes 3000000 | tf_op jit(solution)/shard_map/begin/pallas_call | solution.py:24
  2.7 3.1 %collective-permute-start = (f32[128,128]{1,0:T(8,128)S(1)}, f32[128,128]{1,0:T(8,128)S(1)}, u32[]{:S(2)}, u32[]{:S(2)}) collective-permute-start(f32[128,128]{1,0:T(8,128)S(1)} %get-tuple-element.48), channel_id=1, source_target_pairs={{0,2},{1,3},{2,4},{3,5},{4,6},{5,7},{6,0},{7,1},{8,10},{9,11},{10,... | collective-permute-start | bytes 196616 | tf_op jit(solution)/shard_map/ppermute | solution.py:504
  5.8 0.6 %child_first.1 = (f32[32,8,8,128]{3,2,1,0:T(8,128)S(1)}, f32[256,128]{1,0:T(8,128)S(1)}, f32[256,128]{1,0:T(8,128)S(1)}, f32[32,128]{1,0:T(8,128)S(1)}) custom-call(f32[32,8,8,128]{3,2,1,0:T(8,128)S(1)} %get-tuple-element.37.x_ref, f32[32,8,128]{2,1,0:T(8,128)S(1)} %get-tuple-element.38.a_ref, f32[32,8,128]{2,1,0:T(8,128)S(1)} %get-tuple-element.39.b_ref, ...), custom_call_target="tpu_custom_call" | custom-call | flops 4000000 | bytes 3000000 | tf_op jit(solution)/shard_map/child_first/pallas_call | solution.py:24
  6.4 1.5 %collective-permute-start.4 = (f32[256,128]{1,0:T(8,128)S(1)}, f32[256,128]{1,0:T(8,128)S(1)}, u32[]{:S(2)}, u32[]{:S(2)}) collective-permute-start(f32[256,128]{1,0:T(8,128)S(1)} %get-tuple-element.53), channel_id=1, source_target_pairs={{1,2},{2,1},{3,4},{4,3},{5,6},{6,5},{7,0},{0,7},{9,10},{10,9},{11,... | collective-permute-start | bytes 393224 | tf_op jit(solution)/shard_map/ppermute | solution.py:513
  7.9 2.4 %collective-permute-start.2 = (f32[32,128]{1,0:T(8,128)S(1)}, f32[32,128]{1,0:T(8,128)S(1)}, u32[]{:S(2)}, u32[]{:S(2)}) collective-permute-start(f32[32,128]{1,0:T(8,128)S(1)} %get-tuple-element.44.after_ref), channel_id=1, source_target_pairs={{8,16},{16,8},{24,0},{0,24},{9,17},{17,9},{25,1},{1,25},{10,18},{1... | collective-permute-start | bytes 49160 | tf_op jit(solution)/shard_map/ppermute | solution.py:513
  10.4 0.5 %collective-permute-start.1 = (f32[32,128]{1,0:T(8,128)S(1)}, f32[32,128]{1,0:T(8,128)S(1)}, u32[]{:S(2)}, u32[]{:S(2)}) collective-permute-start(f32[32,128]{1,0:T(8,128)S(1)} %get-tuple-element.44.after_ref), channel_id=1, source_target_pairs={{0,8},{8,0},{16,24},{24,16},{1,9},{9,1},{17,25},{25,17},{2,10},{10... | collective-permute-start | bytes 49160 | tf_op jit(solution)/shard_map/ppermute | solution.py:513
  10.9 0.7 %child_inner.2 = (f32[32,8,8,128]{3,2,1,0:T(8,128)S(1)}, f32[32,8,128]{2,1,0:T(8,128)S(1)}, f32[32,8,128]{2,1,0:T(8,128)S(1)}) custom-call(f32[32,8,8,128]{3,2,1,0:T(8,128)S(1)} %get-tuple-element.41.solved_ref, f32[4,32,8,128]{3,2,1,0:T(8,128)S(1)} %get-tuple-element.42.rates_ref, f32[8,128]{1,0:T(8,128)S(1)} %get-tuple-element.43.land_ref, ...), custom_call_target="tpu_custom_call" | custom-call | flops 10000000 | bytes 4000000 | tf_op jit(solution)/shard_map/child_inner/pallas_call | solution.py:24
  12.1 0.5 %collective-permute-done.2.far_cols = f32[32,128]{1,0:T(8,128)S(1)} collective-permute-done((f32[32,128]{1,0:T(8,128)S(1)}, f32[32,128]{1,0:T(8,128)S(1)}, u32[]{:S(2)}, u32[]{:S(2)}) %collective-permute-start.2) | collective-permute-done | bytes 16416 | tf_op jit(solution)/shard_map/ppermute | solution.py:513
  12.6 1.5 %collective-permute-done.1.mate_cols = f32[32,128]{1,0:T(8,128)S(1)} collective-permute-done((f32[32,128]{1,0:T(8,128)S(1)}, f32[32,128]{1,0:T(8,128)S(1)}, u32[]{:S(2)}, u32[]{:S(2)}) %collective-permute-start.1) | collective-permute-done | bytes 16416 | tf_op jit(solution)/shard_map/ppermute | solution.py:513
  14.1 0.9 %child_columns.1 = (f32[128,512]{1,0:T(8,128)S(1)}, f32[32,8,8,128]{3,2,1,0:T(8,128)S(1)}) custom-call(f32[32,8,8,128]{3,2,1,0:T(8,128)S(1)} %get-tuple-element.45.after_ref.inner_ref, f32[32,8,128]{2,1,0:T(8,128)S(1)} %get-tuple-element.46.column_ref, f32[8,128]{1,0:T(8,128)S(1)} %get-tuple-element.47.relax_ref, ...), custom_call_target="tpu_custom_call" | custom-call | flops 10000000 | bytes 3000000 | tf_op jit(solution)/shard_map/child_columns/pallas_call | solution.py:24
  15.6 0.9 %child_second.1 = (f32[32,8,8,128]{3,2,1,0:T(8,128)S(1)}, f32[16,8,128]{2,1,0:T(8,128)S(1)}, f32[320,128]{1,0:T(8,128)S(1)}, f32[320,128]{1,0:T(8,128)S(1)}, f32[40,128]{1,0:T(8,128)S(1)}) custom-call(f32[32,8,8,128]{3,2,1,0:T(8,128)S(1)} %get-tuple-element.50.x_ref, f32[32,8,128]{2,1,0:T(8,128)S(1)} %get-tuple-element.51.row_ref, ...), custom_call_target="tpu_custom_call" | custom-call | flops 8000000 | bytes 3000000 | tf_op jit(solution)/shard_map/child_second/pallas_call | solution.py:24
  16.6 2.1 %collective-permute-start.6 = (f32[320,128]{1,0:T(8,128)S(1)}, f32[320,128]{1,0:T(8,128)S(1)}, u32[]{:S(2)}, u32[]{:S(2)}) collective-permute-start(f32[320,128]{1,0:T(8,128)S(1)} %get-tuple-element.65), channel_id=1, source_target_pairs={{1,2},{2,1},{3,4},{4,3},{5,6},{6,5},{7,0},{0,7},{9,10},{10,9},{11,... | collective-permute-start | bytes 491528 | tf_op jit(solution)/shard_map/ppermute | solution.py:513
  18.7 1.2 %collective-permute-start.8 = (f32[40,128]{1,0:T(8,128)S(1)}, f32[40,128]{1,0:T(8,128)S(1)}, u32[]{:S(2)}, u32[]{:S(2)}) collective-permute-start(f32[40,128]{1,0:T(8,128)S(1)} %get-tuple-element.60.after_ref), channel_id=1, source_target_pairs={{8,16},{16,8},{24,0},{0,24},{9,17},{17,9},{25,1},{1,25},{10,18},{1... | collective-permute-start | bytes 61448 | tf_op jit(solution)/shard_map/ppermute | solution.py:513
  19.9 0.8 %collective-permute-start.7 = (f32[40,128]{1,0:T(8,128)S(1)}, f32[40,128]{1,0:T(8,128)S(1)}, u32[]{:S(2)}, u32[]{:S(2)}) collective-permute-start(f32[40,128]{1,0:T(8,128)S(1)} %get-tuple-element.60.after_ref), channel_id=1, source_target_pairs={{0,8},{8,0},{16,24},{24,16},{1,9},{9,1},{17,25},{25,17},{2,10},{10... | collective-permute-start | bytes 61448 | tf_op jit(solution)/shard_map/ppermute | solution.py:513
  20.7 0.7 %child_inner.3 = (f32[32,8,8,128]{3,2,1,0:T(8,128)S(1)}, f32[32,8,128]{2,1,0:T(8,128)S(1)}, f32[32,8,128]{2,1,0:T(8,128)S(1)}) custom-call(f32[32,8,8,128]{3,2,1,0:T(8,128)S(1)} %get-tuple-element.59.solved_ref, f32[4,32,8,128]{3,2,1,0:T(8,128)S(1)} %get-tuple-element.42.rates_ref, f32[8,128]{1,0:T(8,128)S(1)} %get-tuple-element.43.land_ref, ...), custom_call_target="tpu_custom_call" | custom-call | flops 10000000 | bytes 4000000 | tf_op jit(solution)/shard_map/child_inner/pallas_call | solution.py:24
  21.4 0.4 %collective-permute-done.9.feed_ref = f32[128,128]{1,0:T(8,128)S(1)} collective-permute-done((f32[128,128]{1,0:T(8,128)S(1)}, f32[128,128]{1,0:T(8,128)S(1)}, u32[]{:S(2)}, u32[]{:S(2)}) %collective-permute-start.9) | collective-permute-done | bytes 65568 | tf_op jit(solution)/shard_map/ppermute | solution.py:504
  22.1 1.3 %collective-permute-done.8.far_cols = f32[40,128]{1,0:T(8,128)S(1)} collective-permute-done((f32[40,128]{1,0:T(8,128)S(1)}, f32[40,128]{1,0:T(8,128)S(1)}, u32[]{:S(2)}, u32[]{:S(2)}) %collective-permute-start.8) | collective-permute-done | bytes 20512 | tf_op jit(solution)/shard_map/ppermute | solution.py:513
  23.7 1.1 %collective-permute-done.6.far_in.far_ref = f32[320,128]{1,0:T(8,128)S(1)} collective-permute-done((f32[320,128]{1,0:T(8,128)S(1)}, f32[320,128]{1,0:T(8,128)S(1)}, u32[]{:S(2)}, u32[]{:S(2)}) %collective-permute-start.6) | collective-permute-done | bytes 163872 | tf_op jit(solution)/shard_map/ppermute | solution.py:513
  25.3 1.3 %collective-permute-start.12 = (f32[64,128]{1,0:T(8,128)S(1)}, f32[64,128]{1,0:T(8,128)S(1)}, u32[]{:S(2)}, u32[]{:S(2)}) collective-permute-start(f32[64,128]{1,0:T(8,128)S(1)} %get-tuple-element.70), channel_id=1, source_target_pairs={{1,2},{2,1},{3,4},{4,3},{5,6},{6,5},{7,0},{0,7},{9,10},{10,9},{11,... | collective-permute-start | bytes 98312 | tf_op jit(solution)/shard_map/ppermute | solution.py:513
  26.6 1.1 %collective-permute-start.11 = (f32[8,128]{1,0:T(8,128)S(1)}, f32[8,128]{1,0:T(8,128)S(1)}, u32[]{:S(2)}, u32[]{:S(2)}) collective-permute-start(f32[8,128]{1,0:T(8,128)S(1)} %get-tuple-element.69), channel_id=1, source_target_pairs={{8,16},{16,8},{24,0},{0,24},{9,17},{17,9},{25,1},{1,25},{10,18},{1... | collective-permute-start | bytes 12296 | tf_op jit(solution)/shard_map/ppermute | solution.py:513
  27.7 0.9 %collective-permute-start.10 = (f32[8,128]{1,0:T(8,128)S(1)}, f32[8,128]{1,0:T(8,128)S(1)}, u32[]{:S(2)}, u32[]{:S(2)}) collective-permute-start(f32[8,128]{1,0:T(8,128)S(1)} %get-tuple-element.69), channel_id=1, source_target_pairs={{0,8},{8,0},{16,24},{24,16},{1,9},{9,1},{17,25},{25,17},{2,10},{10... | collective-permute-start | bytes 12296 | tf_op jit(solution)/shard_map/ppermute | solution.py:513
  28.6 1.2 %child_last.1.after_ref = f32[32,8,8,128]{3,2,1,0:T(8,128)} custom-call(f32[32,8,8,128]{3,2,1,0:T(8,128)S(1)} %get-tuple-element.61.inner_ref.after_ref, f32[32,8,128]{2,1,0:T(8,128)S(1)} %get-tuple-element.62.row_ref, f32[32,8,128]{2,1,0:T(8,128)S(1)} %get-tuple-element.63.column_ref, f32[320,128]{1,0:T(8,128)S(1)} %collective-permute-done.5.mate_in, ...), custom_call_target="tpu_custom_call" | custom-call | flops 4000000 | bytes 3000000 | tf_op jit(solution)/shard_map/child_last/pallas_call | solution.py:24
  29.8 1.3 %collective-permute-done.11.far_cols = f32[8,128]{1,0:T(8,128)S(1)} collective-permute-done((f32[8,128]{1,0:T(8,128)S(1)}, f32[8,128]{1,0:T(8,128)S(1)}, u32[]{:S(2)}, u32[]{:S(2)}) %collective-permute-start.11) | collective-permute-done | bytes 4128 | tf_op jit(solution)/shard_map/ppermute | solution.py:513
  31.4 1.0 %parent_last.1 = f32[512,32]{1,0:T(8,128)} custom-call(f32[16,8,128]{2,1,0:T(8,128)S(1)} %get-tuple-element.68.psolved_in, f32[5,16,128]{2,1,0:T(8,128)S(1)} %parent_rates_masked.1.prates_ref, f32[8,128]{1,0:T(8,128)S(1)} %parent_merged.1.edges_ref, f32[64,128]{1,0:T(8,128)S(1)} %collective-permute-done.13.mate_in, ...), custom_call_target="tpu_custom_call" | custom-call | flops 500000 | bytes 500000 | tf_op jit(solution)/shard_map/parent_last/pallas_call | solution.py:24
  (25 shorter events, 2.3 us)
Async XLA Ops:
  2.7 8.9 %collective-permute-start = (f32[128,128]{1,0:T(8,128)S(1)}, f32[128,128]{1,0:T(8,128)S(1)}, u32[]{:S(2)}, u32[]{:S(2)}) collective-permute-start(f32[128,128]{1,0:T(8,128)S(1)} %get-tuple-element.48), channel_id=1, source_target_pairs={{0,2},{1,3},{2,4},{3,5},{4,6},{5,7},{6,0},{7,1},{8,10},{9,11},{10,... | collective-permute-start | bytes 196616 | tf_op jit(solution)/shard_map/ppermute | solution.py:504
  6.4 8.6 %collective-permute-start.4 = (f32[256,128]{1,0:T(8,128)S(1)}, f32[256,128]{1,0:T(8,128)S(1)}, u32[]{:S(2)}, u32[]{:S(2)}) collective-permute-start(f32[256,128]{1,0:T(8,128)S(1)} %get-tuple-element.53), channel_id=1, source_target_pairs={{1,2},{2,1},{3,4},{4,3},{5,6},{6,5},{7,0},{0,7},{9,10},{10,9},{11,... | collective-permute-start | bytes 393224 | tf_op jit(solution)/shard_map/ppermute | solution.py:513
  7.9 4.6 %collective-permute-start.2 = (f32[32,128]{1,0:T(8,128)S(1)}, f32[32,128]{1,0:T(8,128)S(1)}, u32[]{:S(2)}, u32[]{:S(2)}) collective-permute-start(f32[32,128]{1,0:T(8,128)S(1)} %get-tuple-element.44.after_ref), channel_id=1, source_target_pairs={{8,16},{16,8},{24,0},{0,24},{9,17},{17,9},{25,1},{1,25},{10,18},{1... | collective-permute-start | bytes 49160 | tf_op jit(solution)/shard_map/ppermute | solution.py:513
  10.4 3.7 %collective-permute-start.1 = (f32[32,128]{1,0:T(8,128)S(1)}, f32[32,128]{1,0:T(8,128)S(1)}, u32[]{:S(2)}, u32[]{:S(2)}) collective-permute-start(f32[32,128]{1,0:T(8,128)S(1)} %get-tuple-element.44.after_ref), channel_id=1, source_target_pairs={{0,8},{8,0},{16,24},{24,16},{1,9},{9,1},{17,25},{25,17},{2,10},{10... | collective-permute-start | bytes 49160 | tf_op jit(solution)/shard_map/ppermute | solution.py:513
  10.9 4.2 %collective-permute-start.3 = (f32[256,128]{1,0:T(8,128)S(1)}, f32[256,128]{1,0:T(8,128)S(1)}, u32[]{:S(2)}, u32[]{:S(2)}) collective-permute-start(f32[256,128]{1,0:T(8,128)S(1)} %get-tuple-element.52), channel_id=1, source_target_pairs={{0,1},{1,0},{2,3},{3,2},{4,5},{5,4},{6,7},{7,6},{8,9},{9,8},{10,11... | collective-permute-start | bytes 393224 | tf_op jit(solution)/shard_map/ppermute | solution.py:513
  10.9 1.0 %copy-start = (f32[32,8,2,32]{3,2,1,0:T(2,128)S(1)}, f32[32,8,2,32]{3,2,1,0:T(2,128)}, u32[]{:S(2)}) copy-start(f32[32,8,2,32]{3,2,1,0:T(2,128)} %param.10) | copy-start | bytes 196612
  10.9 1.0 %copy-start.2 = (f32[32,2,32]{2,1,0:T(2,128)S(1)}, f32[32,2,32]{2,1,0:T(2,128)}, u32[]{:S(2)}) copy-start(f32[32,2,32]{2,1,0:T(2,128)} %param.15) | copy-start | bytes 24580
  15.4 6.4 %collective-permute-start.9 = (f32[128,128]{1,0:T(8,128)S(1)}, f32[128,128]{1,0:T(8,128)S(1)}, u32[]{:S(2)}, u32[]{:S(2)}) collective-permute-start(f32[128,128]{1,0:T(8,128)S(1)} %child_rows.1), channel_id=1, source_target_pairs={{0,2},{1,3},{2,4},{3,5},{4,6},{5,7},{6,0},{7,1},{8,10},{9,11},{10,... | collective-permute-start | bytes 196616 | tf_op jit(solution)/shard_map/ppermute | solution.py:504
  16.6 8.2 %collective-permute-start.6 = (f32[320,128]{1,0:T(8,128)S(1)}, f32[320,128]{1,0:T(8,128)S(1)}, u32[]{:S(2)}, u32[]{:S(2)}) collective-permute-start(f32[320,128]{1,0:T(8,128)S(1)} %get-tuple-element.65), channel_id=1, source_target_pairs={{1,2},{2,1},{3,4},{4,3},{5,6},{6,5},{7,0},{0,7},{9,10},{10,9},{11,... | collective-permute-start | bytes 491528 | tf_op jit(solution)/shard_map/ppermute | solution.py:513
  18.7 4.7 %collective-permute-start.8 = (f32[40,128]{1,0:T(8,128)S(1)}, f32[40,128]{1,0:T(8,128)S(1)}, u32[]{:S(2)}, u32[]{:S(2)}) collective-permute-start(f32[40,128]{1,0:T(8,128)S(1)} %get-tuple-element.60.after_ref), channel_id=1, source_target_pairs={{8,16},{16,8},{24,0},{0,24},{9,17},{17,9},{25,1},{1,25},{10,18},{1... | collective-permute-start | bytes 61448 | tf_op jit(solution)/shard_map/ppermute | solution.py:513
  19.9 3.8 %collective-permute-start.7 = (f32[40,128]{1,0:T(8,128)S(1)}, f32[40,128]{1,0:T(8,128)S(1)}, u32[]{:S(2)}, u32[]{:S(2)}) collective-permute-start(f32[40,128]{1,0:T(8,128)S(1)} %get-tuple-element.60.after_ref), channel_id=1, source_target_pairs={{0,8},{8,0},{16,24},{24,16},{1,9},{9,1},{17,25},{25,17},{2,10},{10... | collective-permute-start | bytes 61448 | tf_op jit(solution)/shard_map/ppermute | solution.py:513
  20.7 4.2 %collective-permute-start.5 = (f32[320,128]{1,0:T(8,128)S(1)}, f32[320,128]{1,0:T(8,128)S(1)}, u32[]{:S(2)}, u32[]{:S(2)}) collective-permute-start(f32[320,128]{1,0:T(8,128)S(1)} %get-tuple-element.64), channel_id=1, source_target_pairs={{0,1},{1,0},{2,3},{3,2},{4,5},{5,4},{6,7},{7,6},{8,9},{9,8},{10,11... | collective-permute-start | bytes 491528 | tf_op jit(solution)/shard_map/ppermute | solution.py:513
  20.7 1.1 %copy-start.1 = (f32[4,32,2,32]{3,2,1,0:T(2,128)S(1)}, f32[4,32,2,32]{3,2,1,0:T(2,128)}, u32[]{:S(2)}) copy-start(f32[4,32,2,32]{3,2,1,0:T(2,128)} %param.14) | copy-start | bytes 98308
  25.3 6.0 %collective-permute-start.12 = (f32[64,128]{1,0:T(8,128)S(1)}, f32[64,128]{1,0:T(8,128)S(1)}, u32[]{:S(2)}, u32[]{:S(2)}) collective-permute-start(f32[64,128]{1,0:T(8,128)S(1)} %get-tuple-element.70), channel_id=1, source_target_pairs={{1,2},{2,1},{3,4},{4,3},{5,6},{6,5},{7,0},{0,7},{9,10},{10,9},{11,... | collective-permute-start | bytes 98312 | tf_op jit(solution)/shard_map/ppermute | solution.py:513
  26.6 4.5 %collective-permute-start.11 = (f32[8,128]{1,0:T(8,128)S(1)}, f32[8,128]{1,0:T(8,128)S(1)}, u32[]{:S(2)}, u32[]{:S(2)}) collective-permute-start(f32[8,128]{1,0:T(8,128)S(1)} %get-tuple-element.69), channel_id=1, source_target_pairs={{8,16},{16,8},{24,0},{0,24},{9,17},{17,9},{25,1},{1,25},{10,18},{1... | collective-permute-start | bytes 12296 | tf_op jit(solution)/shard_map/ppermute | solution.py:513
  27.7 3.6 %collective-permute-start.10 = (f32[8,128]{1,0:T(8,128)S(1)}, f32[8,128]{1,0:T(8,128)S(1)}, u32[]{:S(2)}, u32[]{:S(2)}) collective-permute-start(f32[8,128]{1,0:T(8,128)S(1)} %get-tuple-element.69), channel_id=1, source_target_pairs={{0,8},{8,0},{16,24},{24,16},{1,9},{9,1},{17,25},{25,17},{2,10},{10... | collective-permute-start | bytes 12296 | tf_op jit(solution)/shard_map/ppermute | solution.py:513
  28.6 2.8 %collective-permute-start.13 = (f32[64,128]{1,0:T(8,128)S(1)}, f32[64,128]{1,0:T(8,128)S(1)}, u32[]{:S(2)}, u32[]{:S(2)}) collective-permute-start(f32[64,128]{1,0:T(8,128)S(1)} %get-tuple-element.71), channel_id=1, source_target_pairs={{0,1},{1,0},{2,3},{3,2},{4,5},{5,4},{6,7},{7,6},{8,9},{9,8},{10,11... | collective-permute-start | bytes 98312 | tf_op jit(solution)/shard_map/ppermute | solution.py:513
